TPU v7x, 512 devices: a whole 4x8x8 slice. The times are simulated.
512 devices in a mesh: depth: 8 (over z_lo, core), lat: 64 (over z_hi, x, y).
Axes of the slice: x: 4, y: 8, z: 8 (z_hi: 2, z_lo: 4; z = z_hi * 4 + z_lo), core: 2. Of those that a mesh axis runs over, the one named last changes fastest.
Arguments:
- forcing: bfloat16 [8, 2, 16, 16384], P('depth', None, None, 'lat'), may hold values from -6 to 6
- blocks: bfloat16 [8, 768, 2, 128, 128], P('depth', 'lat'), may hold values from -0.15625 to 0.15625
- block_rows: int32 [8, 768], P('depth', 'lat'), may hold values from 0 to 1
- block_cols: int32 [8, 768], P('depth', 'lat'), may hold values from 0 to 5
Outputs:
- down_traces: bfloat16 [8, 2, 16, 16384], P('depth', None, None, 'lat')
- up_traces: bfloat16 [8, 2, 16, 16384], P('depth', None, None, 'lat')
Inputs may be any that keep to these rules, and one draw needn't show every extreme that they name: `block_rows`: a block row index inside the owner's own block rows. `block_cols`: below 2: the previous lateral device's block rows; from 4: the next device's.
All inputs are finite; a program needn't handle non-finite values.
Results may differ from a plain program's by a relative error of at most 0.025.
Values may be sent and summed in bfloat16 or wider, within the bound.
No kernel may reach another device: no remote copies, remote signals or barrier semaphores. Data moves between devices by JAX's collectives and lax.ppermute only.
A program may use at most 64 MiB of HBM per device.

v0:
```python
import jax
import jax.numpy as jnp
from jax import lax
from jax.sharding import PartitionSpec as P


def padded(cells, sides, width):
    for axis, dim in sides:
        count = lax.axis_size(axis)
        ends = count - 1
        head = lax.slice_in_dim(cells, 0, width, axis=dim)
        tail = lax.slice_in_dim(cells, cells.shape[dim] - width, cells.shape[dim], axis=dim)
        cells = jnp.concatenate(
            [
                lax.ppermute(tail, axis, [(i, (i + 1) % count) for i in range(ends)]),
                cells,
                lax.ppermute(head, axis, [((i + 1) % count, i) for i in range(ends)]),
            ],
            axis=dim,
        )
    return cells


def passed_along(value, axis, steps):
    count = lax.axis_size(axis)
    initial, last = (max(0, -steps), min(count, count - steps))
    return lax.ppermute(value, axis, [(source, source + steps) for source in range(initial, last)])


def local(forcing, blocks, block_rows, block_cols):
    sources = forcing.shape[2]
    block_size = blocks.shape[-1]
    row_blocks = forcing.shape[3] // block_size
    local_force = forcing[0].reshape(2, sources, row_blocks, block_size)
    layer_blocks = blocks[0]
    column_index = block_cols[0]
    selector = (block_rows[0][:, None] == jnp.arange(row_blocks, dtype=jnp.int32)[None, :]).astype(
        jnp.float32
    )
    layers = lax.axis_size("depth")

    def apply_layer(field):
        window = padded(field, (("lat", 2),), row_blocks)
        picked = jnp.take(window, column_index, axis=2)
        product = jnp.einsum(
            "bpij,qsbj->pqsbi", layer_blocks, picked, preferred_element_type=jnp.float32
        )
        combined = jnp.stack([product[0, 0] - product[1, 1], product[0, 1] + product[1, 0]])
        summed = jnp.einsum("qsbi,br->qsri", combined, selector, precision=lax.Precision.HIGHEST)
        return summed.astype(jnp.bfloat16)

    incoming = jnp.zeros_like(local_force)
    downward = incoming
    for section in range(layers):
        operand = (local_force.astype(jnp.float32) + incoming.astype(jnp.float32)).astype(
            jnp.bfloat16
        )
        downward = apply_layer(operand)
        if section + 1 < layers:
            incoming = passed_along(downward, "depth", 1)
    from_below = jnp.zeros_like(local_force)
    upward = from_below
    for section in range(layers):
        operand = (
            local_force.astype(jnp.float32)
            + incoming.astype(jnp.float32)
            + from_below.astype(jnp.float32)
        ).astype(jnp.bfloat16)
        upward = apply_layer(operand)
        if section + 1 < layers:
            from_below = passed_along(upward, "depth", -1)
    return (downward.reshape(forcing.shape), upward.reshape(forcing.shape))


def solution(mesh):
    placed = (
        P("depth", None, None, "lat"),
        P("depth", "lat", None, None, None),
        P("depth", "lat"),
        P("depth", "lat"),
    )
    return jax.shard_map(
        local,
        mesh=mesh,
        in_specs=placed,
        out_specs=(P("depth", None, None, "lat"), P("depth", None, None, "lat")),
        check_vma=False,
    )
```

profile of v0, /device:TPU:448, one launch (start us, length us, event | category | flops | bytes accessed | tf_op | source)
XLA Modules:
  0.0 328.0 jit_solution(12758732801648245342)
XLA Ops:
  1.5 6.6 %collective-permute-start.1 = (bf16[2,16,2,128]{3,2,1,0:T(2,128)(2,1)S(1)}, bf16[2,16,2,128]{3,2,1,0:T(2,128)(2,1)S(1)}, u32[]{:S(2)}, u32[]{:S(2)}) collective-permute-start(bf16[2,16,2,128]{3,2,1,0:T(2,128)(2,1)S(1)} %reshape_squeeze.3), channel_id=1, source_target_pairs={{1,0},{2,1},{3,2},{4,3},{5,4},{6,5},{7,6},{8,7},{9,8},{10,9},{11,1... | collective-permute-start | bytes 49160 | tf_op jit(solution)/shard_map/ppermute | solution.py:17
  8.1 1.9 collective-permute-start
  10.1 11.8 %collective-permute-done = bf16[2,16,2,128]{3,2,1,0:T(2,128)(2,1)S(1)} collective-permute-done((bf16[2,16,2,128]{3,2,1,0:T(2,128)(2,1)S(1)}, bf16[2,16,2,128]{3,2,1,0:T(2,128)(2,1)S(1)}, u32[]{:S(2)}, u32[]{:S(2)}) %collective-permute-start) | collective-permute-done | bytes 16416 | tf_op jit(solution)/shard_map/ppermute | solution.py:15
  23.9 1.9 collective-permute-start.2
  25.8 3.1 collective-permute-done.2
  29.0 1.9 collective-permute-start.4
  30.9 3.9 %collective-permute-start.3 = (bf16[2,16,2,128]{3,2,1,0:T(2,128)(2,1)S(1)}, bf16[2,16,2,128]{3,2,1,0:T(2,128)(2,1)S(1)}, u32[]{:S(2)}, u32[]{:S(2)}) collective-permute-start(bf16[2,16,2,128]{3,2,1,0:T(2,128)(2,1)S(1)} %fusion.150), channel_id=1, source_target_pairs={{0,1},{1,2},{2,3},{3,4},{4,5},{5,6},{6,7},{7,8},{8,9},{9,10},{10,1... | collective-permute-start | bytes 49160 | tf_op jit(solution)/shard_map/ppermute | solution.py:15
  34.9 9.8 %collective-permute-done.3 = bf16[2,16,2,128]{3,2,1,0:T(2,128)(2,1)S(1)} collective-permute-done((bf16[2,16,2,128]{3,2,1,0:T(2,128)(2,1)S(1)}, bf16[2,16,2,128]{3,2,1,0:T(2,128)(2,1)S(1)}, u32[]{:S(2)}, u32[]{:S(2)}) %collective-permute-start.3) | collective-permute-done | bytes 16416 | tf_op jit(solution)/shard_map/ppermute | solution.py:15
  46.2 1.9 collective-permute-start.5
  48.1 3.1 collective-permute-done.5
  51.3 1.9 collective-permute-start.7
  53.2 3.9 %collective-permute-start.6 = (bf16[2,16,2,128]{3,2,1,0:T(2,128)(2,1)S(1)}, bf16[2,16,2,128]{3,2,1,0:T(2,128)(2,1)S(1)}, u32[]{:S(2)}, u32[]{:S(2)}) collective-permute-start(bf16[2,16,2,128]{3,2,1,0:T(2,128)(2,1)S(1)} %fusion.151), channel_id=1, source_target_pairs={{0,1},{1,2},{2,3},{3,4},{4,5},{5,6},{6,7},{7,8},{8,9},{9,10},{10,1... | collective-permute-start | bytes 49160 | tf_op jit(solution)/shard_map/ppermute | solution.py:15
  57.1 9.8 %collective-permute-done.6 = bf16[2,16,2,128]{3,2,1,0:T(2,128)(2,1)S(1)} collective-permute-done((bf16[2,16,2,128]{3,2,1,0:T(2,128)(2,1)S(1)}, bf16[2,16,2,128]{3,2,1,0:T(2,128)(2,1)S(1)}, u32[]{:S(2)}, u32[]{:S(2)}) %collective-permute-start.6) | collective-permute-done | bytes 16416 | tf_op jit(solution)/shard_map/ppermute | solution.py:15
  68.5 1.9 collective-permute-start.8
  70.4 3.1 collective-permute-done.8
  73.6 1.9 collective-permute-start.10
  75.5 3.9 %collective-permute-start.9 = (bf16[2,16,2,128]{3,2,1,0:T(2,128)(2,1)S(1)}, bf16[2,16,2,128]{3,2,1,0:T(2,128)(2,1)S(1)}, u32[]{:S(2)}, u32[]{:S(2)}) collective-permute-start(bf16[2,16,2,128]{3,2,1,0:T(2,128)(2,1)S(1)} %fusion.152), channel_id=1, source_target_pairs={{0,1},{1,2},{2,3},{3,4},{4,5},{5,6},{6,7},{7,8},{8,9},{9,10},{10,1... | collective-permute-start | bytes 49160 | tf_op jit(solution)/shard_map/ppermute | solution.py:15
  79.4 9.8 %collective-permute-done.9 = bf16[2,16,2,128]{3,2,1,0:T(2,128)(2,1)S(1)} collective-permute-done((bf16[2,16,2,128]{3,2,1,0:T(2,128)(2,1)S(1)}, bf16[2,16,2,128]{3,2,1,0:T(2,128)(2,1)S(1)}, u32[]{:S(2)}, u32[]{:S(2)}) %collective-permute-start.9) | collective-permute-done | bytes 16416 | tf_op jit(solution)/shard_map/ppermute | solution.py:15
  90.8 1.9 collective-permute-start.11
  92.7 3.1 collective-permute-done.11
  95.8 1.9 collective-permute-start.13
  97.8 3.9 %collective-permute-start.12 = (bf16[2,16,2,128]{3,2,1,0:T(2,128)(2,1)S(1)}, bf16[2,16,2,128]{3,2,1,0:T(2,128)(2,1)S(1)}, u32[]{:S(2)}, u32[]{:S(2)}) collective-permute-start(bf16[2,16,2,128]{3,2,1,0:T(2,128)(2,1)S(1)} %fusion.153), channel_id=1, source_target_pairs={{0,1},{1,2},{2,3},{3,4},{4,5},{5,6},{6,7},{7,8},{8,9},{9,10},{10,1... | collective-permute-start | bytes 49160 | tf_op jit(solution)/shard_map/ppermute | solution.py:15
  101.7 9.8 %collective-permute-done.12 = bf16[2,16,2,128]{3,2,1,0:T(2,128)(2,1)S(1)} collective-permute-done((bf16[2,16,2,128]{3,2,1,0:T(2,128)(2,1)S(1)}, bf16[2,16,2,128]{3,2,1,0:T(2,128)(2,1)S(1)}, u32[]{:S(2)}, u32[]{:S(2)}) %collective-permute-start.12) | collective-permute-done | bytes 16416 | tf_op jit(solution)/shard_map/ppermute | solution.py:15
  113.0 1.9 collective-permute-start.14
  115.0 3.1 collective-permute-done.14
  118.1 1.9 collective-permute-start.16
  120.1 3.9 %collective-permute-start.15 = (bf16[2,16,2,128]{3,2,1,0:T(2,128)(2,1)S(1)}, bf16[2,16,2,128]{3,2,1,0:T(2,128)(2,1)S(1)}, u32[]{:S(2)}, u32[]{:S(2)}) collective-permute-start(bf16[2,16,2,128]{3,2,1,0:T(2,128)(2,1)S(1)} %fusion.154), channel_id=1, source_target_pairs={{0,1},{1,2},{2,3},{3,4},{4,5},{5,6},{6,7},{7,8},{8,9},{9,10},{10,1... | collective-permute-start | bytes 49160 | tf_op jit(solution)/shard_map/ppermute | solution.py:15
  124.0 9.8 %collective-permute-done.15 = bf16[2,16,2,128]{3,2,1,0:T(2,128)(2,1)S(1)} collective-permute-done((bf16[2,16,2,128]{3,2,1,0:T(2,128)(2,1)S(1)}, bf16[2,16,2,128]{3,2,1,0:T(2,128)(2,1)S(1)}, u32[]{:S(2)}, u32[]{:S(2)}) %collective-permute-start.15) | collective-permute-done | bytes 16416 | tf_op jit(solution)/shard_map/ppermute | solution.py:15
  135.3 1.9 collective-permute-start.17
  137.3 3.1 collective-permute-done.17
  140.4 1.9 collective-permute-start.19
  142.3 3.9 %collective-permute-start.18 = (bf16[2,16,2,128]{3,2,1,0:T(2,128)(2,1)S(1)}, bf16[2,16,2,128]{3,2,1,0:T(2,128)(2,1)S(1)}, u32[]{:S(2)}, u32[]{:S(2)}) collective-permute-start(bf16[2,16,2,128]{3,2,1,0:T(2,128)(2,1)S(1)} %fusion.155), channel_id=1, source_target_pairs={{0,1},{1,2},{2,3},{3,4},{4,5},{5,6},{6,7},{7,8},{8,9},{9,10},{10,1... | collective-permute-start | bytes 49160 | tf_op jit(solution)/shard_map/ppermute | solution.py:15
  146.3 9.8 %collective-permute-done.18 = bf16[2,16,2,128]{3,2,1,0:T(2,128)(2,1)S(1)} collective-permute-done((bf16[2,16,2,128]{3,2,1,0:T(2,128)(2,1)S(1)}, bf16[2,16,2,128]{3,2,1,0:T(2,128)(2,1)S(1)}, u32[]{:S(2)}, u32[]{:S(2)}) %collective-permute-start.18) | collective-permute-done | bytes 16416 | tf_op jit(solution)/shard_map/ppermute | solution.py:15
  159.5 3.1 collective-permute-done.20
  162.7 1.9 collective-permute-start.22
  164.6 3.9 %collective-permute-start.21 = (bf16[2,16,2,128]{3,2,1,0:T(2,128)(2,1)S(1)}, bf16[2,16,2,128]{3,2,1,0:T(2,128)(2,1)S(1)}, u32[]{:S(2)}, u32[]{:S(2)}) collective-permute-start(bf16[2,16,2,128]{3,2,1,0:T(2,128)(2,1)S(1)} %fusion.201), channel_id=1, source_target_pairs={{0,1},{1,2},{2,3},{3,4},{4,5},{5,6},{6,7},{7,8},{8,9},{9,10},{10,1... | collective-permute-start | bytes 49160 | tf_op jit(solution)/shard_map/ppermute | solution.py:15
  168.6 9.8 %collective-permute-done.21 = bf16[2,16,2,128]{3,2,1,0:T(2,128)(2,1)S(1)} collective-permute-done((bf16[2,16,2,128]{3,2,1,0:T(2,128)(2,1)S(1)}, bf16[2,16,2,128]{3,2,1,0:T(2,128)(2,1)S(1)}, u32[]{:S(2)}, u32[]{:S(2)}) %collective-permute-start.21) | collective-permute-done | bytes 16416 | tf_op jit(solution)/shard_map/ppermute | solution.py:15
  183.3 1.9 collective-permute-start.25
  185.2 3.9 %collective-permute-start.24 = (bf16[2,16,2,128]{3,2,1,0:T(2,128)(2,1)S(1)}, bf16[2,16,2,128]{3,2,1,0:T(2,128)(2,1)S(1)}, u32[]{:S(2)}, u32[]{:S(2)}) collective-permute-start(bf16[2,16,2,128]{3,2,1,0:T(2,128)(2,1)S(1)} %add_convert_fusion.6), channel_id=1, source_target_pairs={{0,1},{1,2},{2,3},{3,4},{4,5},{5,6},{6,7},{7,8},{8,9},{9,10},{10,1... | collective-permute-start | bytes 49160 | tf_op jit(solution)/shard_map/ppermute | solution.py:15
  189.1 9.8 %collective-permute-done.24 = bf16[2,16,2,128]{3,2,1,0:T(2,128)(2,1)S(1)} collective-permute-done((bf16[2,16,2,128]{3,2,1,0:T(2,128)(2,1)S(1)}, bf16[2,16,2,128]{3,2,1,0:T(2,128)(2,1)S(1)}, u32[]{:S(2)}, u32[]{:S(2)}) %collective-permute-start.24) | collective-permute-done | bytes 16416 | tf_op jit(solution)/shard_map/ppermute | solution.py:15
  200.5 2.5 collective-permute-start.26
  204.4 1.9 collective-permute-start.28
  206.4 3.9 %collective-permute-start.27 = (bf16[2,16,2,128]{3,2,1,0:T(2,128)(2,1)S(1)}, bf16[2,16,2,128]{3,2,1,0:T(2,128)(2,1)S(1)}, u32[]{:S(2)}, u32[]{:S(2)}) collective-permute-start(bf16[2,16,2,128]{3,2,1,0:T(2,128)(2,1)S(1)} %add_convert_fusion.5), channel_id=1, source_target_pairs={{0,1},{1,2},{2,3},{3,4},{4,5},{5,6},{6,7},{7,8},{8,9},{9,10},{10,1... | collective-permute-start | bytes 49160 | tf_op jit(solution)/shard_map/ppermute | solution.py:15
  210.3 9.8 %collective-permute-done.27 = bf16[2,16,2,128]{3,2,1,0:T(2,128)(2,1)S(1)} collective-permute-done((bf16[2,16,2,128]{3,2,1,0:T(2,128)(2,1)S(1)}, bf16[2,16,2,128]{3,2,1,0:T(2,128)(2,1)S(1)}, u32[]{:S(2)}, u32[]{:S(2)}) %collective-permute-start.27) | collective-permute-done | bytes 16416 | tf_op jit(solution)/shard_map/ppermute | solution.py:15
  221.6 2.5 collective-permute-start.29
  225.6 1.9 collective-permute-start.31
  227.5 3.9 %collective-permute-start.30 = (bf16[2,16,2,128]{3,2,1,0:T(2,128)(2,1)S(1)}, bf16[2,16,2,128]{3,2,1,0:T(2,128)(2,1)S(1)}, u32[]{:S(2)}, u32[]{:S(2)}) collective-permute-start(bf16[2,16,2,128]{3,2,1,0:T(2,128)(2,1)S(1)} %add_convert_fusion.4), channel_id=1, source_target_pairs={{0,1},{1,2},{2,3},{3,4},{4,5},{5,6},{6,7},{7,8},{8,9},{9,10},{10,1... | collective-permute-start | bytes 49160 | tf_op jit(solution)/shard_map/ppermute | solution.py:15
  231.4 9.8 %collective-permute-done.30 = bf16[2,16,2,128]{3,2,1,0:T(2,128)(2,1)S(1)} collective-permute-done((bf16[2,16,2,128]{3,2,1,0:T(2,128)(2,1)S(1)}, bf16[2,16,2,128]{3,2,1,0:T(2,128)(2,1)S(1)}, u32[]{:S(2)}, u32[]{:S(2)}) %collective-permute-start.30) | collective-permute-done | bytes 16416 | tf_op jit(solution)/shard_map/ppermute | solution.py:15
  242.8 2.5 collective-permute-start.32
  246.7 1.9 collective-permute-start.34
  248.6 3.9 %collective-permute-start.33 = (bf16[2,16,2,128]{3,2,1,0:T(2,128)(2,1)S(1)}, bf16[2,16,2,128]{3,2,1,0:T(2,128)(2,1)S(1)}, u32[]{:S(2)}, u32[]{:S(2)}) collective-permute-start(bf16[2,16,2,128]{3,2,1,0:T(2,128)(2,1)S(1)} %add_convert_fusion.3), channel_id=1, source_target_pairs={{0,1},{1,2},{2,3},{3,4},{4,5},{5,6},{6,7},{7,8},{8,9},{9,10},{10,1... | collective-permute-start | bytes 49160 | tf_op jit(solution)/shard_map/ppermute | solution.py:15
  252.6 9.8 %collective-permute-done.33 = bf16[2,16,2,128]{3,2,1,0:T(2,128)(2,1)S(1)} collective-permute-done((bf16[2,16,2,128]{3,2,1,0:T(2,128)(2,1)S(1)}, bf16[2,16,2,128]{3,2,1,0:T(2,128)(2,1)S(1)}, u32[]{:S(2)}, u32[]{:S(2)}) %collective-permute-start.33) | collective-permute-done | bytes 16416 | tf_op jit(solution)/shard_map/ppermute | solution.py:15
  263.9 2.5 collective-permute-start.35
  267.8 1.9 collective-permute-start.37
  269.8 3.9 %collective-permute-start.36 = (bf16[2,16,2,128]{3,2,1,0:T(2,128)(2,1)S(1)}, bf16[2,16,2,128]{3,2,1,0:T(2,128)(2,1)S(1)}, u32[]{:S(2)}, u32[]{:S(2)}) collective-permute-start(bf16[2,16,2,128]{3,2,1,0:T(2,128)(2,1)S(1)} %add_convert_fusion.2), channel_id=1, source_target_pairs={{0,1},{1,2},{2,3},{3,4},{4,5},{5,6},{6,7},{7,8},{8,9},{9,10},{10,1... | collective-permute-start | bytes 49160 | tf_op jit(solution)/shard_map/ppermute | solution.py:15
  273.7 9.8 %collective-permute-done.36 = bf16[2,16,2,128]{3,2,1,0:T(2,128)(2,1)S(1)} collective-permute-done((bf16[2,16,2,128]{3,2,1,0:T(2,128)(2,1)S(1)}, bf16[2,16,2,128]{3,2,1,0:T(2,128)(2,1)S(1)}, u32[]{:S(2)}, u32[]{:S(2)}) %collective-permute-start.36) | collective-permute-done | bytes 16416 | tf_op jit(solution)/shard_map/ppermute | solution.py:15
  285.1 2.5 collective-permute-start.38
  289.0 1.9 collective-permute-start.40
  290.9 3.9 %collective-permute-start.39 = (bf16[2,16,2,128]{3,2,1,0:T(2,128)(2,1)S(1)}, bf16[2,16,2,128]{3,2,1,0:T(2,128)(2,1)S(1)}, u32[]{:S(2)}, u32[]{:S(2)}) collective-permute-start(bf16[2,16,2,128]{3,2,1,0:T(2,128)(2,1)S(1)} %add_convert_fusion.1), channel_id=1, source_target_pairs={{0,1},{1,2},{2,3},{3,4},{4,5},{5,6},{6,7},{7,8},{8,9},{9,10},{10,1... | collective-permute-start | bytes 49160 | tf_op jit(solution)/shard_map/ppermute | solution.py:15
  294.9 9.8 %collective-permute-done.39 = bf16[2,16,2,128]{3,2,1,0:T(2,128)(2,1)S(1)} collective-permute-done((bf16[2,16,2,128]{3,2,1,0:T(2,128)(2,1)S(1)}, bf16[2,16,2,128]{3,2,1,0:T(2,128)(2,1)S(1)}, u32[]{:S(2)}, u32[]{:S(2)}) %collective-permute-start.39) | collective-permute-done | bytes 16416 | tf_op jit(solution)/shard_map/ppermute | solution.py:15
  306.2 2.5 collective-permute-start.41
  310.1 1.9 collective-permute-start.43
  312.1 3.9 %collective-permute-start.42 = (bf16[2,16,2,128]{3,2,1,0:T(2,128)(2,1)S(1)}, bf16[2,16,2,128]{3,2,1,0:T(2,128)(2,1)S(1)}, u32[]{:S(2)}, u32[]{:S(2)}) collective-permute-start(bf16[2,16,2,128]{3,2,1,0:T(2,128)(2,1)S(1)} %add_convert_fusion), channel_id=1, source_target_pairs={{0,1},{1,2},{2,3},{3,4},{4,5},{5,6},{6,7},{7,8},{8,9},{9,10},{10,1... | collective-permute-start | bytes 49160 | tf_op jit(solution)/shard_map/ppermute | solution.py:15
  316.6 9.2 %collective-permute-done.42 = bf16[2,16,2,128]{3,2,1,0:T(2,128)(2,1)S(1)} collective-permute-done((bf16[2,16,2,128]{3,2,1,0:T(2,128)(2,1)S(1)}, bf16[2,16,2,128]{3,2,1,0:T(2,128)(2,1)S(1)}, u32[]{:S(2)}, u32[]{:S(2)}) %collective-permute-start.42) | collective-permute-done | bytes 16416 | tf_op jit(solution)/shard_map/ppermute | solution.py:15
  (172 shorter events, 38.7 us)
Async XLA Ops:
  0.6 21.9 %copy-start = (bf16[1,12,2,128,128]{4,3,2,1,0:T(8,128)(2,1)S(1)}, bf16[1,12,2,128,128]{4,3,2,1,0:T(8,128)(2,1)}, u32[]{:S(2)}) copy-start(bf16[1,12,2,128,128]{4,3,2,1,0:T(8,128)(2,1)} %param.7) | copy-start | bytes 2359300
  0.6 9.4 %copy-start.3 = (s32[1,12]{1,0:T(1,128)S(1)}, s32[1,12]{1,0:T(1,128)}, u32[]{:S(2)}) copy-start(s32[1,12]{1,0:T(1,128)} %param.9) | copy-start | bytes 148
  1.5 8.6 %collective-permute-start.1 = (bf16[2,16,2,128]{3,2,1,0:T(2,128)(2,1)S(1)}, bf16[2,16,2,128]{3,2,1,0:T(2,128)(2,1)S(1)}, u32[]{:S(2)}, u32[]{:S(2)}) collective-permute-start(bf16[2,16,2,128]{3,2,1,0:T(2,128)(2,1)S(1)} %reshape_squeeze.3), channel_id=1, source_target_pairs={{1,0},{2,1},{3,2},{4,3},{5,4},{6,5},{7,6},{8,7},{9,8},{10,9},{11,1... | collective-permute-start | bytes 49160 | tf_op jit(solution)/shard_map/ppermute | solution.py:17
  8.1 13.8 %collective-permute-start = (bf16[2,16,2,128]{3,2,1,0:T(2,128)(2,1)S(1)}, bf16[2,16,2,128]{3,2,1,0:T(2,128)(2,1)S(1)}, u32[]{:S(2)}, u32[]{:S(2)}) collective-permute-start(bf16[2,16,2,128]{3,2,1,0:T(2,128)(2,1)S(1)} %reshape_squeeze.3), channel_id=1, source_target_pairs={{0,1},{1,2},{2,3},{3,4},{4,5},{5,6},{6,7},{7,8},{8,9},{9,10},{10,1... | collective-permute-start | bytes 49160 | tf_op jit(solution)/shard_map/ppermute | solution.py:15
  10.1 11.9 %copy-start.2 = (s32[1024]{0:T(1024)}, s32[1024]{0:T(1024)S(1)}, u32[]{:S(2)}) copy-start(s32[1024]{0:T(1024)S(1)} %pad_clamp_fusion) | copy-start | bytes 12292
  23.0 0.7 copy-start.1
  23.9 5.1 %collective-permute-start.2 = (bf16[2,16,2,128]{3,2,1,0:T(2,128)(2,1)S(1)}, bf16[2,16,2,128]{3,2,1,0:T(2,128)(2,1)S(1)}, u32[]{:S(2)}, u32[]{:S(2)}) collective-permute-start(bf16[2,16,2,128]{3,2,1,0:T(2,128)(2,1)S(1)} %fusion), channel_id=1, source_target_pairs={{0,64},{64,128},{128,192},{192,256},{256,320},{320,384},{384,448},... | collective-permute-start | bytes 49160 | tf_op jit(solution)/shard_map/ppermute | solution.py:27
  29.0 5.9 %collective-permute-start.4 = (bf16[2,16,2,128]{3,2,1,0:T(2,128)(2,1)S(1)}, bf16[2,16,2,128]{3,2,1,0:T(2,128)(2,1)S(1)}, u32[]{:S(2)}, u32[]{:S(2)}) collective-permute-start(bf16[2,16,2,128]{3,2,1,0:T(2,128)(2,1)S(1)} %fusion.150), channel_id=1, source_target_pairs={{1,0},{2,1},{3,2},{4,3},{5,4},{6,5},{7,6},{8,7},{9,8},{10,9},{11,1... | collective-permute-start | bytes 49160 | tf_op jit(solution)/shard_map/ppermute | solution.py:17
  30.9 13.8 %collective-permute-start.3 = (bf16[2,16,2,128]{3,2,1,0:T(2,128)(2,1)S(1)}, bf16[2,16,2,128]{3,2,1,0:T(2,128)(2,1)S(1)}, u32[]{:S(2)}, u32[]{:S(2)}) collective-permute-start(bf16[2,16,2,128]{3,2,1,0:T(2,128)(2,1)S(1)} %fusion.150), channel_id=1, source_target_pairs={{0,1},{1,2},{2,3},{3,4},{4,5},{5,6},{6,7},{7,8},{8,9},{9,10},{10,1... | collective-permute-start | bytes 49160 | tf_op jit(solution)/shard_map/ppermute | solution.py:15
  46.2 5.1 %collective-permute-start.5 = (bf16[2,16,2,128]{3,2,1,0:T(2,128)(2,1)S(1)}, bf16[2,16,2,128]{3,2,1,0:T(2,128)(2,1)S(1)}, u32[]{:S(2)}, u32[]{:S(2)}) collective-permute-start(bf16[2,16,2,128]{3,2,1,0:T(2,128)(2,1)S(1)} %fusion.1), channel_id=1, source_target_pairs={{0,64},{64,128},{128,192},{192,256},{256,320},{320,384},{384,448},... | collective-permute-start | bytes 49160 | tf_op jit(solution)/shard_map/ppermute | solution.py:27
  51.3 5.9 %collective-permute-start.7 = (bf16[2,16,2,128]{3,2,1,0:T(2,128)(2,1)S(1)}, bf16[2,16,2,128]{3,2,1,0:T(2,128)(2,1)S(1)}, u32[]{:S(2)}, u32[]{:S(2)}) collective-permute-start(bf16[2,16,2,128]{3,2,1,0:T(2,128)(2,1)S(1)} %fusion.151), channel_id=1, source_target_pairs={{1,0},{2,1},{3,2},{4,3},{5,4},{6,5},{7,6},{8,7},{9,8},{10,9},{11,1... | collective-permute-start | bytes 49160 | tf_op jit(solution)/shard_map/ppermute | solution.py:17
  53.2 13.8 %collective-permute-start.6 = (bf16[2,16,2,128]{3,2,1,0:T(2,128)(2,1)S(1)}, bf16[2,16,2,128]{3,2,1,0:T(2,128)(2,1)S(1)}, u32[]{:S(2)}, u32[]{:S(2)}) collective-permute-start(bf16[2,16,2,128]{3,2,1,0:T(2,128)(2,1)S(1)} %fusion.151), channel_id=1, source_target_pairs={{0,1},{1,2},{2,3},{3,4},{4,5},{5,6},{6,7},{7,8},{8,9},{9,10},{10,1... | collective-permute-start | bytes 49160 | tf_op jit(solution)/shard_map/ppermute | solution.py:15
  68.5 5.1 %collective-permute-start.8 = (bf16[2,16,2,128]{3,2,1,0:T(2,128)(2,1)S(1)}, bf16[2,16,2,128]{3,2,1,0:T(2,128)(2,1)S(1)}, u32[]{:S(2)}, u32[]{:S(2)}) collective-permute-start(bf16[2,16,2,128]{3,2,1,0:T(2,128)(2,1)S(1)} %fusion.2), channel_id=1, source_target_pairs={{0,64},{64,128},{128,192},{192,256},{256,320},{320,384},{384,448},... | collective-permute-start | bytes 49160 | tf_op jit(solution)/shard_map/ppermute | solution.py:27
  73.6 5.9 %collective-permute-start.10 = (bf16[2,16,2,128]{3,2,1,0:T(2,128)(2,1)S(1)}, bf16[2,16,2,128]{3,2,1,0:T(2,128)(2,1)S(1)}, u32[]{:S(2)}, u32[]{:S(2)}) collective-permute-start(bf16[2,16,2,128]{3,2,1,0:T(2,128)(2,1)S(1)} %fusion.152), channel_id=1, source_target_pairs={{1,0},{2,1},{3,2},{4,3},{5,4},{6,5},{7,6},{8,7},{9,8},{10,9},{11,1... | collective-permute-start | bytes 49160 | tf_op jit(solution)/shard_map/ppermute | solution.py:17
  75.5 13.8 %collective-permute-start.9 = (bf16[2,16,2,128]{3,2,1,0:T(2,128)(2,1)S(1)}, bf16[2,16,2,128]{3,2,1,0:T(2,128)(2,1)S(1)}, u32[]{:S(2)}, u32[]{:S(2)}) collective-permute-start(bf16[2,16,2,128]{3,2,1,0:T(2,128)(2,1)S(1)} %fusion.152), channel_id=1, source_target_pairs={{0,1},{1,2},{2,3},{3,4},{4,5},{5,6},{6,7},{7,8},{8,9},{9,10},{10,1... | collective-permute-start | bytes 49160 | tf_op jit(solution)/shard_map/ppermute | solution.py:15
  90.8 5.1 %collective-permute-start.11 = (bf16[2,16,2,128]{3,2,1,0:T(2,128)(2,1)S(1)}, bf16[2,16,2,128]{3,2,1,0:T(2,128)(2,1)S(1)}, u32[]{:S(2)}, u32[]{:S(2)}) collective-permute-start(bf16[2,16,2,128]{3,2,1,0:T(2,128)(2,1)S(1)} %fusion.3), channel_id=1, source_target_pairs={{0,64},{64,128},{128,192},{192,256},{256,320},{320,384},{384,448},... | collective-permute-start | bytes 49160 | tf_op jit(solution)/shard_map/ppermute | solution.py:27
  95.8 5.9 %collective-permute-start.13 = (bf16[2,16,2,128]{3,2,1,0:T(2,128)(2,1)S(1)}, bf16[2,16,2,128]{3,2,1,0:T(2,128)(2,1)S(1)}, u32[]{:S(2)}, u32[]{:S(2)}) collective-permute-start(bf16[2,16,2,128]{3,2,1,0:T(2,128)(2,1)S(1)} %fusion.153), channel_id=1, source_target_pairs={{1,0},{2,1},{3,2},{4,3},{5,4},{6,5},{7,6},{8,7},{9,8},{10,9},{11,1... | collective-permute-start | bytes 49160 | tf_op jit(solution)/shard_map/ppermute | solution.py:17
  97.8 13.8 %collective-permute-start.12 = (bf16[2,16,2,128]{3,2,1,0:T(2,128)(2,1)S(1)}, bf16[2,16,2,128]{3,2,1,0:T(2,128)(2,1)S(1)}, u32[]{:S(2)}, u32[]{:S(2)}) collective-permute-start(bf16[2,16,2,128]{3,2,1,0:T(2,128)(2,1)S(1)} %fusion.153), channel_id=1, source_target_pairs={{0,1},{1,2},{2,3},{3,4},{4,5},{5,6},{6,7},{7,8},{8,9},{9,10},{10,1... | collective-permute-start | bytes 49160 | tf_op jit(solution)/shard_map/ppermute | solution.py:15
  113.0 5.1 %collective-permute-start.14 = (bf16[2,16,2,128]{3,2,1,0:T(2,128)(2,1)S(1)}, bf16[2,16,2,128]{3,2,1,0:T(2,128)(2,1)S(1)}, u32[]{:S(2)}, u32[]{:S(2)}) collective-permute-start(bf16[2,16,2,128]{3,2,1,0:T(2,128)(2,1)S(1)} %fusion.4), channel_id=1, source_target_pairs={{0,64},{64,128},{128,192},{192,256},{256,320},{320,384},{384,448},... | collective-permute-start | bytes 49160 | tf_op jit(solution)/shard_map/ppermute | solution.py:27
  118.1 5.9 %collective-permute-start.16 = (bf16[2,16,2,128]{3,2,1,0:T(2,128)(2,1)S(1)}, bf16[2,16,2,128]{3,2,1,0:T(2,128)(2,1)S(1)}, u32[]{:S(2)}, u32[]{:S(2)}) collective-permute-start(bf16[2,16,2,128]{3,2,1,0:T(2,128)(2,1)S(1)} %fusion.154), channel_id=1, source_target_pairs={{1,0},{2,1},{3,2},{4,3},{5,4},{6,5},{7,6},{8,7},{9,8},{10,9},{11,1... | collective-permute-start | bytes 49160 | tf_op jit(solution)/shard_map/ppermute | solution.py:17
  120.1 13.8 %collective-permute-start.15 = (bf16[2,16,2,128]{3,2,1,0:T(2,128)(2,1)S(1)}, bf16[2,16,2,128]{3,2,1,0:T(2,128)(2,1)S(1)}, u32[]{:S(2)}, u32[]{:S(2)}) collective-permute-start(bf16[2,16,2,128]{3,2,1,0:T(2,128)(2,1)S(1)} %fusion.154), channel_id=1, source_target_pairs={{0,1},{1,2},{2,3},{3,4},{4,5},{5,6},{6,7},{7,8},{8,9},{9,10},{10,1... | collective-permute-start | bytes 49160 | tf_op jit(solution)/shard_map/ppermute | solution.py:15
  135.3 5.1 %collective-permute-start.17 = (bf16[2,16,2,128]{3,2,1,0:T(2,128)(2,1)S(1)}, bf16[2,16,2,128]{3,2,1,0:T(2,128)(2,1)S(1)}, u32[]{:S(2)}, u32[]{:S(2)}) collective-permute-start(bf16[2,16,2,128]{3,2,1,0:T(2,128)(2,1)S(1)} %fusion.5), channel_id=1, source_target_pairs={{0,64},{64,128},{128,192},{192,256},{256,320},{320,384},{384,448},... | collective-permute-start | bytes 49160 | tf_op jit(solution)/shard_map/ppermute | solution.py:27
  140.4 5.9 %collective-permute-start.19 = (bf16[2,16,2,128]{3,2,1,0:T(2,128)(2,1)S(1)}, bf16[2,16,2,128]{3,2,1,0:T(2,128)(2,1)S(1)}, u32[]{:S(2)}, u32[]{:S(2)}) collective-permute-start(bf16[2,16,2,128]{3,2,1,0:T(2,128)(2,1)S(1)} %fusion.155), channel_id=1, source_target_pairs={{1,0},{2,1},{3,2},{4,3},{5,4},{6,5},{7,6},{8,7},{9,8},{10,9},{11,1... | collective-permute-start | bytes 49160 | tf_op jit(solution)/shard_map/ppermute | solution.py:17
  142.3 13.8 %collective-permute-start.18 = (bf16[2,16,2,128]{3,2,1,0:T(2,128)(2,1)S(1)}, bf16[2,16,2,128]{3,2,1,0:T(2,128)(2,1)S(1)}, u32[]{:S(2)}, u32[]{:S(2)}) collective-permute-start(bf16[2,16,2,128]{3,2,1,0:T(2,128)(2,1)S(1)} %fusion.155), channel_id=1, source_target_pairs={{0,1},{1,2},{2,3},{3,4},{4,5},{5,6},{6,7},{7,8},{8,9},{9,10},{10,1... | collective-permute-start | bytes 49160 | tf_op jit(solution)/shard_map/ppermute | solution.py:15
  157.6 5.1 %collective-permute-start.20 = (bf16[2,16,2,128]{3,2,1,0:T(2,128)(2,1)S(1)}, bf16[2,16,2,128]{3,2,1,0:T(2,128)(2,1)S(1)}, u32[]{:S(2)}, u32[]{:S(2)}) collective-permute-start(bf16[2,16,2,128]{3,2,1,0:T(2,128)(2,1)S(1)} %fusion.6), channel_id=1, source_target_pairs={{0,64},{64,128},{128,192},{192,256},{256,320},{320,384},{384,448},... | collective-permute-start | bytes 49160 | tf_op jit(solution)/shard_map/ppermute | solution.py:27
  162.7 5.9 %collective-permute-start.22 = (bf16[2,16,2,128]{3,2,1,0:T(2,128)(2,1)S(1)}, bf16[2,16,2,128]{3,2,1,0:T(2,128)(2,1)S(1)}, u32[]{:S(2)}, u32[]{:S(2)}) collective-permute-start(bf16[2,16,2,128]{3,2,1,0:T(2,128)(2,1)S(1)} %fusion.201), channel_id=1, source_target_pairs={{1,0},{2,1},{3,2},{4,3},{5,4},{6,5},{7,6},{8,7},{9,8},{10,9},{11,1... | collective-permute-start | bytes 49160 | tf_op jit(solution)/shard_map/ppermute | solution.py:17
  164.6 13.8 %collective-permute-start.21 = (bf16[2,16,2,128]{3,2,1,0:T(2,128)(2,1)S(1)}, bf16[2,16,2,128]{3,2,1,0:T(2,128)(2,1)S(1)}, u32[]{:S(2)}, u32[]{:S(2)}) collective-permute-start(bf16[2,16,2,128]{3,2,1,0:T(2,128)(2,1)S(1)} %fusion.201), channel_id=1, source_target_pairs={{0,1},{1,2},{2,3},{3,4},{4,5},{5,6},{6,7},{7,8},{8,9},{9,10},{10,1... | collective-permute-start | bytes 49160 | tf_op jit(solution)/shard_map/ppermute | solution.py:15
  179.9 3.4 %collective-permute-start.23 = (bf16[2,16,2,128]{3,2,1,0:T(2,128)(2,1)S(1)}, bf16[2,16,2,128]{3,2,1,0:T(2,128)(2,1)S(1)}, u32[]{:S(2)}, u32[]{:S(2)}) collective-permute-start(bf16[2,16,2,128]{3,2,1,0:T(2,128)(2,1)S(1)} %fusion.7), channel_id=1, source_target_pairs={{64,0},{128,64},{192,128},{256,192},{320,256},{384,320},{448,384},... | collective-permute-start | bytes 49160 | tf_op jit(solution)/shard_map/ppermute | solution.py:27
  183.3 5.9 %collective-permute-start.25 = (bf16[2,16,2,128]{3,2,1,0:T(2,128)(2,1)S(1)}, bf16[2,16,2,128]{3,2,1,0:T(2,128)(2,1)S(1)}, u32[]{:S(2)}, u32[]{:S(2)}) collective-permute-start(bf16[2,16,2,128]{3,2,1,0:T(2,128)(2,1)S(1)} %add_convert_fusion.6), channel_id=1, source_target_pairs={{1,0},{2,1},{3,2},{4,3},{5,4},{6,5},{7,6},{8,7},{9,8},{10,9},{11,1... | collective-permute-start | bytes 49160 | tf_op jit(solution)/shard_map/ppermute | solution.py:17
  185.2 13.8 %collective-permute-start.24 = (bf16[2,16,2,128]{3,2,1,0:T(2,128)(2,1)S(1)}, bf16[2,16,2,128]{3,2,1,0:T(2,128)(2,1)S(1)}, u32[]{:S(2)}, u32[]{:S(2)}) collective-permute-start(bf16[2,16,2,128]{3,2,1,0:T(2,128)(2,1)S(1)} %add_convert_fusion.6), channel_id=1, source_target_pairs={{0,1},{1,2},{2,3},{3,4},{4,5},{5,6},{6,7},{7,8},{8,9},{9,10},{10,1... | collective-permute-start | bytes 49160 | tf_op jit(solution)/shard_map/ppermute | solution.py:15
  200.5 3.9 %collective-permute-start.26 = (bf16[2,16,2,128]{3,2,1,0:T(2,128)(2,1)S(1)}, bf16[2,16,2,128]{3,2,1,0:T(2,128)(2,1)S(1)}, u32[]{:S(2)}, u32[]{:S(2)}) collective-permute-start(bf16[2,16,2,128]{3,2,1,0:T(2,128)(2,1)S(1)} %fusion.8), channel_id=1, source_target_pairs={{64,0},{128,64},{192,128},{256,192},{320,256},{384,320},{448,384},... | collective-permute-start | bytes 49160 | tf_op jit(solution)/shard_map/ppermute | solution.py:27
  204.4 5.9 %collective-permute-start.28 = (bf16[2,16,2,128]{3,2,1,0:T(2,128)(2,1)S(1)}, bf16[2,16,2,128]{3,2,1,0:T(2,128)(2,1)S(1)}, u32[]{:S(2)}, u32[]{:S(2)}) collective-permute-start(bf16[2,16,2,128]{3,2,1,0:T(2,128)(2,1)S(1)} %add_convert_fusion.5), channel_id=1, source_target_pairs={{1,0},{2,1},{3,2},{4,3},{5,4},{6,5},{7,6},{8,7},{9,8},{10,9},{11,1... | collective-permute-start | bytes 49160 | tf_op jit(solution)/shard_map/ppermute | solution.py:17
  206.4 13.8 %collective-permute-start.27 = (bf16[2,16,2,128]{3,2,1,0:T(2,128)(2,1)S(1)}, bf16[2,16,2,128]{3,2,1,0:T(2,128)(2,1)S(1)}, u32[]{:S(2)}, u32[]{:S(2)}) collective-permute-start(bf16[2,16,2,128]{3,2,1,0:T(2,128)(2,1)S(1)} %add_convert_fusion.5), channel_id=1, source_target_pairs={{0,1},{1,2},{2,3},{3,4},{4,5},{5,6},{6,7},{7,8},{8,9},{9,10},{10,1... | collective-permute-start | bytes 49160 | tf_op jit(solution)/shard_map/ppermute | solution.py:15
  221.6 3.9 %collective-permute-start.29 = (bf16[2,16,2,128]{3,2,1,0:T(2,128)(2,1)S(1)}, bf16[2,16,2,128]{3,2,1,0:T(2,128)(2,1)S(1)}, u32[]{:S(2)}, u32[]{:S(2)}) collective-permute-start(bf16[2,16,2,128]{3,2,1,0:T(2,128)(2,1)S(1)} %fusion.9), channel_id=1, source_target_pairs={{64,0},{128,64},{192,128},{256,192},{320,256},{384,320},{448,384},... | collective-permute-start | bytes 49160 | tf_op jit(solution)/shard_map/ppermute | solution.py:27
  225.6 5.9 %collective-permute-start.31 = (bf16[2,16,2,128]{3,2,1,0:T(2,128)(2,1)S(1)}, bf16[2,16,2,128]{3,2,1,0:T(2,128)(2,1)S(1)}, u32[]{:S(2)}, u32[]{:S(2)}) collective-permute-start(bf16[2,16,2,128]{3,2,1,0:T(2,128)(2,1)S(1)} %add_convert_fusion.4), channel_id=1, source_target_pairs={{1,0},{2,1},{3,2},{4,3},{5,4},{6,5},{7,6},{8,7},{9,8},{10,9},{11,1... | collective-permute-start | bytes 49160 | tf_op jit(solution)/shard_map/ppermute | solution.py:17
  227.5 13.8 %collective-permute-start.30 = (bf16[2,16,2,128]{3,2,1,0:T(2,128)(2,1)S(1)}, bf16[2,16,2,128]{3,2,1,0:T(2,128)(2,1)S(1)}, u32[]{:S(2)}, u32[]{:S(2)}) collective-permute-start(bf16[2,16,2,128]{3,2,1,0:T(2,128)(2,1)S(1)} %add_convert_fusion.4), channel_id=1, source_target_pairs={{0,1},{1,2},{2,3},{3,4},{4,5},{5,6},{6,7},{7,8},{8,9},{9,10},{10,1... | collective-permute-start | bytes 49160 | tf_op jit(solution)/shard_map/ppermute | solution.py:15
  242.8 3.9 %collective-permute-start.32 = (bf16[2,16,2,128]{3,2,1,0:T(2,128)(2,1)S(1)}, bf16[2,16,2,128]{3,2,1,0:T(2,128)(2,1)S(1)}, u32[]{:S(2)}, u32[]{:S(2)}) collective-permute-start(bf16[2,16,2,128]{3,2,1,0:T(2,128)(2,1)S(1)} %fusion.10), channel_id=1, source_target_pairs={{64,0},{128,64},{192,128},{256,192},{320,256},{384,320},{448,384},... | collective-permute-start | bytes 49160 | tf_op jit(solution)/shard_map/ppermute | solution.py:27
  246.7 5.9 %collective-permute-start.34 = (bf16[2,16,2,128]{3,2,1,0:T(2,128)(2,1)S(1)}, bf16[2,16,2,128]{3,2,1,0:T(2,128)(2,1)S(1)}, u32[]{:S(2)}, u32[]{:S(2)}) collective-permute-start(bf16[2,16,2,128]{3,2,1,0:T(2,128)(2,1)S(1)} %add_convert_fusion.3), channel_id=1, source_target_pairs={{1,0},{2,1},{3,2},{4,3},{5,4},{6,5},{7,6},{8,7},{9,8},{10,9},{11,1... | collective-permute-start | bytes 49160 | tf_op jit(solution)/shard_map/ppermute | solution.py:17
  248.6 13.8 %collective-permute-start.33 = (bf16[2,16,2,128]{3,2,1,0:T(2,128)(2,1)S(1)}, bf16[2,16,2,128]{3,2,1,0:T(2,128)(2,1)S(1)}, u32[]{:S(2)}, u32[]{:S(2)}) collective-permute-start(bf16[2,16,2,128]{3,2,1,0:T(2,128)(2,1)S(1)} %add_convert_fusion.3), channel_id=1, source_target_pairs={{0,1},{1,2},{2,3},{3,4},{4,5},{5,6},{6,7},{7,8},{8,9},{9,10},{10,1... | collective-permute-start | bytes 49160 | tf_op jit(solution)/shard_map/ppermute | solution.py:15
  263.9 3.9 %collective-permute-start.35 = (bf16[2,16,2,128]{3,2,1,0:T(2,128)(2,1)S(1)}, bf16[2,16,2,128]{3,2,1,0:T(2,128)(2,1)S(1)}, u32[]{:S(2)}, u32[]{:S(2)}) collective-permute-start(bf16[2,16,2,128]{3,2,1,0:T(2,128)(2,1)S(1)} %fusion.11), channel_id=1, source_target_pairs={{64,0},{128,64},{192,128},{256,192},{320,256},{384,320},{448,384},... | collective-permute-start | bytes 49160 | tf_op jit(solution)/shard_map/ppermute | solution.py:27
  267.8 5.9 %collective-permute-start.37 = (bf16[2,16,2,128]{3,2,1,0:T(2,128)(2,1)S(1)}, bf16[2,16,2,128]{3,2,1,0:T(2,128)(2,1)S(1)}, u32[]{:S(2)}, u32[]{:S(2)}) collective-permute-start(bf16[2,16,2,128]{3,2,1,0:T(2,128)(2,1)S(1)} %add_convert_fusion.2), channel_id=1, source_target_pairs={{1,0},{2,1},{3,2},{4,3},{5,4},{6,5},{7,6},{8,7},{9,8},{10,9},{11,1... | collective-permute-start | bytes 49160 | tf_op jit(solution)/shard_map/ppermute | solution.py:17
  269.8 13.8 %collective-permute-start.36 = (bf16[2,16,2,128]{3,2,1,0:T(2,128)(2,1)S(1)}, bf16[2,16,2,128]{3,2,1,0:T(2,128)(2,1)S(1)}, u32[]{:S(2)}, u32[]{:S(2)}) collective-permute-start(bf16[2,16,2,128]{3,2,1,0:T(2,128)(2,1)S(1)} %add_convert_fusion.2), channel_id=1, source_target_pairs={{0,1},{1,2},{2,3},{3,4},{4,5},{5,6},{6,7},{7,8},{8,9},{9,10},{10,1... | collective-permute-start | bytes 49160 | tf_op jit(solution)/shard_map/ppermute | solution.py:15
  285.1 3.9 %collective-permute-start.38 = (bf16[2,16,2,128]{3,2,1,0:T(2,128)(2,1)S(1)}, bf16[2,16,2,128]{3,2,1,0:T(2,128)(2,1)S(1)}, u32[]{:S(2)}, u32[]{:S(2)}) collective-permute-start(bf16[2,16,2,128]{3,2,1,0:T(2,128)(2,1)S(1)} %fusion.12), channel_id=1, source_target_pairs={{64,0},{128,64},{192,128},{256,192},{320,256},{384,320},{448,384},... | collective-permute-start | bytes 49160 | tf_op jit(solution)/shard_map/ppermute | solution.py:27
  289.0 5.9 %collective-permute-start.40 = (bf16[2,16,2,128]{3,2,1,0:T(2,128)(2,1)S(1)}, bf16[2,16,2,128]{3,2,1,0:T(2,128)(2,1)S(1)}, u32[]{:S(2)}, u32[]{:S(2)}) collective-permute-start(bf16[2,16,2,128]{3,2,1,0:T(2,128)(2,1)S(1)} %add_convert_fusion.1), channel_id=1, source_target_pairs={{1,0},{2,1},{3,2},{4,3},{5,4},{6,5},{7,6},{8,7},{9,8},{10,9},{11,1... | collective-permute-start | bytes 49160 | tf_op jit(solution)/shard_map/ppermute | solution.py:17
  290.9 13.8 %collective-permute-start.39 = (bf16[2,16,2,128]{3,2,1,0:T(2,128)(2,1)S(1)}, bf16[2,16,2,128]{3,2,1,0:T(2,128)(2,1)S(1)}, u32[]{:S(2)}, u32[]{:S(2)}) collective-permute-start(bf16[2,16,2,128]{3,2,1,0:T(2,128)(2,1)S(1)} %add_convert_fusion.1), channel_id=1, source_target_pairs={{0,1},{1,2},{2,3},{3,4},{4,5},{5,6},{6,7},{7,8},{8,9},{9,10},{10,1... | collective-permute-start | bytes 49160 | tf_op jit(solution)/shard_map/ppermute | solution.py:15
  306.2 3.9 %collective-permute-start.41 = (bf16[2,16,2,128]{3,2,1,0:T(2,128)(2,1)S(1)}, bf16[2,16,2,128]{3,2,1,0:T(2,128)(2,1)S(1)}, u32[]{:S(2)}, u32[]{:S(2)}) collective-permute-start(bf16[2,16,2,128]{3,2,1,0:T(2,128)(2,1)S(1)} %fusion.13), channel_id=1, source_target_pairs={{64,0},{128,64},{192,128},{256,192},{320,256},{384,320},{448,384},... | collective-permute-start | bytes 49160 | tf_op jit(solution)/shard_map/ppermute | solution.py:27
  310.1 6.5 %collective-permute-start.43 = (bf16[2,16,2,128]{3,2,1,0:T(2,128)(2,1)S(1)}, bf16[2,16,2,128]{3,2,1,0:T(2,128)(2,1)S(1)}, u32[]{:S(2)}, u32[]{:S(2)}) collective-permute-start(bf16[2,16,2,128]{3,2,1,0:T(2,128)(2,1)S(1)} %add_convert_fusion), channel_id=1, source_target_pairs={{1,0},{2,1},{3,2},{4,3},{5,4},{6,5},{7,6},{8,7},{9,8},{10,9},{11,1... | collective-permute-start | bytes 49160 | tf_op jit(solution)/shard_map/ppermute | solution.py:17
  312.1 13.8 %collective-permute-start.42 = (bf16[2,16,2,128]{3,2,1,0:T(2,128)(2,1)S(1)}, bf16[2,16,2,128]{3,2,1,0:T(2,128)(2,1)S(1)}, u32[]{:S(2)}, u32[]{:S(2)}) collective-permute-start(bf16[2,16,2,128]{3,2,1,0:T(2,128)(2,1)S(1)} %add_convert_fusion), channel_id=1, source_target_pairs={{0,1},{1,2},{2,3},{3,4},{4,5},{5,6},{6,7},{7,8},{8,9},{9,10},{10,1... | collective-permute-start | bytes 49160 | tf_op jit(solution)/shard_map/ppermute | solution.py:15
where the time goes:
time: 330 us; the launch traced here: 328 us
  waiting for transfers between devices  181 us (55%)
  starting transfers between devices  120 us (36%)
  local copies, waits for them, and re-layouts  13.1 us (4%)
  matrix products  9.91 us (3%)
    ppermute x15, waiting for transfers between devices, padded(): lax.ppermute(tail, axis, [(i, (i + 1) % count) for i in range(ends)])  149 us
    ppermute x15, starting transfers between devices, padded(): lax.ppermute(tail, axis, [(i, (i + 1) % count) for i in range(ends)])  56.7 us
    ppermute x15, starting transfers between devices, padded(): lax.ppermute(head, axis, [((i + 1) % count, i) for i in range(ends)])  33.6 us
    ppermute x14, waiting for transfers between devices, passed_along(): lax.ppermute(value, axis, [(source, source + steps) for source in range(i...  31.9 us
    ppermute x14, starting transfers between devices, passed_along(): lax.ppermute(value, axis, [(source, source + steps) for source in range(i...  30.2 us
    gather x15, local copies, waits for them, and re-layouts, apply_layer(): picked = jnp.take(window, column_index, axis=2)  10.2 us
  transfers between devices with their start and end apart: 44, of which 29 were waited for; matrix products, arithmetic and copies ran while one was open for 0% of the time, Pallas kernels for 0%

commit v1 on v0

v1 whole, which is shorter than its diff:
```python
import functools

import jax
import jax.numpy as jnp
from jax import lax
from jax.experimental import pallas as pl
from jax.experimental.pallas import tpu as pltpu
from jax.sharding import PartitionSpec as P

AXES = ("depth", "lat")
FAR, NEAR, SAME = range(3)
PARAMS = pltpu.CompilerParams(vmem_limit_bytes=16 * 2**20)


def gather_kernel(rows_ref, cols_ref, blocks_ref, dense_ref, total_ref):
    count, parts, size, _ = blocks_ref.shape
    rows, slots = total_ref.shape[:2]
    total_ref[...] = jnp.zeros_like(total_ref)
    for b in range(count):
        total_ref[rows_ref[0, b], cols_ref[0, b]] += blocks_ref[b].astype(jnp.float32)
    for r in range(rows):
        for s in range(slots):
            for p in range(parts):
                column = (p * rows + r) * size
                dense_ref[s * size : (s + 1) * size, column : column + size] = (
                    total_ref[r, s, p].T.astype(jnp.bfloat16)
                )


def applied(order, first_ref, second_ref, third_ref, dense_ref):
    sources, width = first_ref.shape[1:]
    refs = dict(zip(order, (first_ref, second_ref, third_ref)))
    window = jnp.concatenate(
        [refs[part][...].reshape(2 * sources, width) for part in (FAR, SAME, NEAR)], axis=1
    )
    product = jnp.dot(window, dense_ref[...], preferred_element_type=jnp.float32)
    by_real, by_imag = product[:, :width], product[:, width:]
    real = by_real[:sources] - by_imag[sources:]
    imag = by_real[sources:] + by_imag[:sources]
    return real, imag


def down_kernel(layer, order, first_ref, second_ref, third_ref, dense_ref, kept_ref, next_ref, send_ref, down_ref):
    down_ref[...] = kept_ref[...]

    @pl.when(lax.axis_index("depth") == layer)
    def _():
        for part, total in enumerate(applied(order, first_ref, second_ref, third_ref, dense_ref)):
            trace = total.astype(jnp.bfloat16).astype(jnp.float32)
            down_ref[part] = total
            send_ref[part] = (next_ref[part].astype(jnp.float32) + trace).astype(jnp.bfloat16)


def turn_kernel(layer, order, first_ref, second_ref, third_ref, dense_ref, kept_ref, send_ref, down_ref):
    down_ref[...] = kept_ref[...]

    @pl.when(lax.axis_index("depth") == layer)
    def _():
        for part, total in enumerate(applied(order, first_ref, second_ref, third_ref, dense_ref)):
            down_ref[part] = total
            send_ref[part] = total.astype(jnp.bfloat16)


def up_kernel(layer, order, first_ref, second_ref, third_ref, dense_ref, down_ref, kept_ref, send_ref, up_ref):
    up_ref[...] = kept_ref[...]

    @pl.when(lax.axis_index("depth") == layer)
    def _():
        for part, total in enumerate(applied(order, first_ref, second_ref, third_ref, dense_ref)):
            total = down_ref[part] + total
            up_ref[part] = total
            send_ref[part] = total.astype(jnp.bfloat16)


def vmem(count):
    return [pl.BlockSpec(memory_space=pltpu.VMEM)] * count


def local(forcing, blocks, block_rows, block_cols):
    layers, lats = lax.axis_size("depth"), lax.axis_size("lat")
    field = forcing[0]
    _, sources, width = field.shape
    count, parts, size, _ = blocks.shape[1:]
    rows = width // size

    def sent(value, moves):
        pairs = [
            (k * lats + j, to_k * lats + to_j)
            for k, j, to_k, to_j in moves
            if 0 <= to_k < layers and 0 <= to_j < lats
        ]
        return lax.ppermute(value, AXES, pairs)

    def beside(j, odd):
        return j + 1 if (j % 2 == 1) == odd else j - 1

    def far(value, k, to_k):
        return sent(value, [(k, j, to_k, beside(j, True)) for j in range(lats)])

    def near(value, k, to_k):
        return sent(value, [(k, j, to_k, beside(j, False)) for j in range(lats)])

    def same(value, k, to_k):
        return sent(value, [(k, j, to_k, j) for j in range(lats)])

    following = sent(field, [(k, j, k - 1, j) for k in range(1, layers) for j in range(lats)])

    left_is_far = lax.axis_index("lat") % 2 == 0
    cols = jnp.where(left_is_far, block_cols, 2 * rows - block_cols // rows * rows + block_cols % rows)
    dense = pl.pallas_call(
        gather_kernel,
        out_shape=jax.ShapeDtypeStruct((3 * width, parts * width), jnp.bfloat16),
        in_specs=[pl.BlockSpec(memory_space=pltpu.SMEM)] * 2 + vmem(1),
        out_specs=pl.BlockSpec(memory_space=pltpu.VMEM),
        scratch_shapes=[pltpu.VMEM((rows, 3 * rows, parts, size, size), jnp.float32)],
        compiler_params=PARAMS,
        name="dense",
    )(block_rows, cols, blocks[0])

    half = jax.ShapeDtypeStruct(field.shape, jnp.bfloat16)
    full = jax.ShapeDtypeStruct(field.shape, jnp.float32)

    def step(kernel, layer, order, *operands):
        return pl.pallas_call(
            functools.partial(kernel, layer, order),
            out_shape=(half, full),
            in_specs=vmem(len(operands)),
            out_specs=tuple(vmem(2)),
            compiler_params=PARAMS,
            name=f"{kernel.__name__}{layer}",
        )(*operands)

    def moved(value, k, to_k, order):
        parts = {FAR: far, NEAR: near, SAME: same}
        return [parts[part](value, k, to_k) for part in order]

    last = layers - 1
    down = jnp.zeros(field.shape, jnp.float32)
    order, window = (FAR, NEAR, SAME), [far(field, 0, 0), near(field, 0, 0), field]
    for layer in range(last):
        send, down = step(down_kernel, layer, order, *window, dense, down, following)
        order = (SAME, FAR, NEAR) if layer == 2 else (FAR, NEAR, SAME)
        window = moved(send, layer, layer + 1, order)
    send, down = step(turn_kernel, last, order, *window, dense, down)
    up = down
    for layer in reversed(range(last)):
        window = moved(send, layer + 1, layer, order)
        send, up = step(up_kernel, layer, order, *window, dense, down, up)
    down, up = down.astype(jnp.bfloat16), up.astype(jnp.bfloat16)
    return (down.reshape(forcing.shape), up.reshape(forcing.shape))


def solution(mesh):
    placed = (
        P("depth", None, None, "lat"),
        P("depth", "lat", None, None, None),
        P("depth", "lat"),
        P("depth", "lat"),
    )
    return jax.shard_map(
        local,
        mesh=mesh,
        in_specs=placed,
        out_specs=(P("depth", None, None, "lat"), P("depth", None, None, "lat")),
        check_vma=False,
    )
```

time: 330 us -> 250 us (0.76)
  the two profiles are of different devices: /device:TPU:448 before, /device:TPU:62 now
where the time goes in v1:
time: 250 us; the launch traced here: 249 us
  starting transfers between devices  207 us (83%)
  waiting for transfers between devices  34.3 us (14%)
  local copies, waits for them, and re-layouts  2.78 us (1%)
    ppermute x45, starting transfers between devices, sent(): return lax.ppermute(value, AXES, pairs)  207 us
    ppermute x45, waiting for transfers between devices, sent(): return lax.ppermute(value, AXES, pairs)  34.3 us
  transfers between devices with their start and end apart: 45, of which 4 were waited for; matrix products, arithmetic and copies ran while one was open for 0% of the time, Pallas kernels for 0%

profile of v1, /device:TPU:62, one launch (start us, length us, event | category | flops | bytes accessed | tf_op | source)
XLA Modules:
  0.0 248.8 jit_solution(3052996938316665483)
XLA Ops:
  0.6 17.5 %collective-permute-start.2 = (bf16[2,16,256]{2,1,0:T(8,128)(2,1)}, bf16[2,16,256]{2,1,0:T(8,128)(2,1)S(1)}, u32[]{:S(2)}, u32[]{:S(2)}) collective-permute-start(bf16[2,16,256]{2,1,0:T(8,128)(2,1)} %bitcast.7), channel_id=1, source_target_pairs={{64,0},{65,1},{66,2},{67,3},{68,4},{69,5},{70,6},{71,7},{72,8},{73... | collective-permute-start | bytes 49160 | tf_op jit(solution)/shard_map/ppermute | solution.py:92
  18.1 8.9 %collective-permute-start = (bf16[2,16,256]{2,1,0:T(8,128)(2,1)}, bf16[2,16,256]{2,1,0:T(8,128)(2,1)S(1)}, u32[]{:S(2)}, u32[]{:S(2)}) collective-permute-start(bf16[2,16,256]{2,1,0:T(8,128)(2,1)} %bitcast.8), channel_id=1, source_target_pairs={{1,2},{2,1},{3,4},{4,3},{5,6},{6,5},{7,8},{8,7},{9,10},{10,9},{11,... | collective-permute-start | bytes 49160 | tf_op jit(solution)/shard_map/ppermute | solution.py:92
  27.0 1.9 collective-permute-start.1
  29.0 0.6 copy-done.3
  29.6 0.0 copy-start.2
  29.6 0.6 copy-done.2
  30.3 1.1 copy-done
  31.4 1.1 dense.1.dense_ref
  32.5 0.0 copy-start.1
  32.5 0.0 collective-permute-done.2.next_ref
  32.5 0.0 collective-permute-done.first_ref
  32.5 0.3 collective-permute-done.1.second_ref
  32.8 0.3 copy-done.1
  33.2 0.2 down_kernel0.1
  33.4 1.3 collective-permute-start.3
  34.7 1.3 collective-permute-start.4
  36.0 1.3 collective-permute-start.5
  37.3 0.0 collective-permute-done.3.first_ref
  37.3 0.1 collective-permute-done.4.second_ref
  37.5 0.7 collective-permute-done.5.third_ref
  38.2 0.7 collective-permute-start.6
  38.8 0.7 collective-permute-start.7
  39.5 0.7 collective-permute-start.8
  40.2 0.0 collective-permute-done.7.second_ref
  40.2 0.7 collective-permute-start.10
  40.9 0.7 collective-permute-start.11
  41.6 0.7 collective-permute-start.9
  42.3 0.7 collective-permute-start.12
  42.9 0.7 collective-permute-start.13
  43.6 0.7 collective-permute-start.14
  44.3 0.7 collective-permute-start.15
  45.0 0.7 collective-permute-start.16
  45.7 0.7 collective-permute-start.17
  46.4 0.7 collective-permute-start.18
  47.1 34.1 %collective-permute-start.19 = (bf16[2,16,256]{2,1,0:T(8,128)(2,1)S(1)}, bf16[2,16,256]{2,1,0:T(8,128)(2,1)S(1)}, u32[]{:S(2)}, u32[]{:S(2)}) collective-permute-start(bf16[2,16,256]{2,1,0:T(8,128)(2,1)S(1)} %get-tuple-element.41), channel_id=1, source_target_pairs={{320,385},{321,384},{322,387},{323,386},{324,389},{325,388},{326,3... | collective-permute-start | bytes 49160 | tf_op jit(solution)/shard_map/ppermute | solution.py:92
  81.2 16.1 %collective-permute-start.20 = (bf16[2,16,256]{2,1,0:T(8,128)(2,1)S(1)}, bf16[2,16,256]{2,1,0:T(8,128)(2,1)S(1)}, u32[]{:S(2)}, u32[]{:S(2)}) collective-permute-start(bf16[2,16,256]{2,1,0:T(8,128)(2,1)S(1)} %get-tuple-element.41), channel_id=1, source_target_pairs={{320,384},{321,385},{322,386},{323,387},{324,388},{325,389},{326,3... | collective-permute-start | bytes 49160 | tf_op jit(solution)/shard_map/ppermute | solution.py:92
  97.3 0.7 collective-permute-start.21
  98.0 18.6 %collective-permute-start.22 = (bf16[2,16,256]{2,1,0:T(8,128)(2,1)S(1)}, bf16[2,16,256]{2,1,0:T(8,128)(2,1)S(1)}, u32[]{:S(2)}, u32[]{:S(2)}) collective-permute-start(bf16[2,16,256]{2,1,0:T(8,128)(2,1)S(1)} %get-tuple-element.43), channel_id=1, source_target_pairs={{384,449},{385,448},{386,451},{387,450},{388,453},{389,452},{390,4... | collective-permute-start | bytes 49160 | tf_op jit(solution)/shard_map/ppermute | solution.py:92
  116.6 16.1 %collective-permute-start.23 = (bf16[2,16,256]{2,1,0:T(8,128)(2,1)S(1)}, bf16[2,16,256]{2,1,0:T(8,128)(2,1)S(1)}, u32[]{:S(2)}, u32[]{:S(2)}) collective-permute-start(bf16[2,16,256]{2,1,0:T(8,128)(2,1)S(1)} %get-tuple-element.43), channel_id=1, source_target_pairs={{384,448},{385,449},{386,450},{387,451},{388,452},{389,453},{390,4... | collective-permute-start | bytes 49160 | tf_op jit(solution)/shard_map/ppermute | solution.py:92
  132.7 0.7 collective-permute-start.24
  133.4 18.0 %collective-permute-start.25 = (bf16[2,16,256]{2,1,0:T(8,128)(2,1)S(1)}, bf16[2,16,256]{2,1,0:T(8,128)(2,1)S(1)}, u32[]{:S(2)}, u32[]{:S(2)}) collective-permute-start(bf16[2,16,256]{2,1,0:T(8,128)(2,1)S(1)} %get-tuple-element.46), channel_id=1, source_target_pairs={{448,385},{449,384},{450,387},{451,386},{452,389},{453,388},{454,3... | collective-permute-start | bytes 49160 | tf_op jit(solution)/shard_map/ppermute | solution.py:92
  151.3 16.1 %collective-permute-start.26 = (bf16[2,16,256]{2,1,0:T(8,128)(2,1)S(1)}, bf16[2,16,256]{2,1,0:T(8,128)(2,1)S(1)}, u32[]{:S(2)}, u32[]{:S(2)}) collective-permute-start(bf16[2,16,256]{2,1,0:T(8,128)(2,1)S(1)} %get-tuple-element.46), channel_id=1, source_target_pairs={{448,384},{449,385},{450,386},{451,387},{452,388},{453,389},{454,3... | collective-permute-start | bytes 49160 | tf_op jit(solution)/shard_map/ppermute | solution.py:92
  167.5 0.7 collective-permute-start.27
  168.1 17.3 %collective-permute-start.28 = (bf16[2,16,256]{2,1,0:T(8,128)(2,1)S(1)}, bf16[2,16,256]{2,1,0:T(8,128)(2,1)S(1)}, u32[]{:S(2)}, u32[]{:S(2)}) collective-permute-start(bf16[2,16,256]{2,1,0:T(8,128)(2,1)S(1)} %get-tuple-element.47), channel_id=1, source_target_pairs={{384,321},{385,320},{386,323},{387,322},{388,325},{389,324},{390,3... | collective-permute-start | bytes 49160 | tf_op jit(solution)/shard_map/ppermute | solution.py:92
  185.4 16.1 %collective-permute-start.29 = (bf16[2,16,256]{2,1,0:T(8,128)(2,1)S(1)}, bf16[2,16,256]{2,1,0:T(8,128)(2,1)S(1)}, u32[]{:S(2)}, u32[]{:S(2)}) collective-permute-start(bf16[2,16,256]{2,1,0:T(8,128)(2,1)S(1)} %get-tuple-element.47), channel_id=1, source_target_pairs={{384,320},{385,321},{386,322},{387,323},{388,324},{389,325},{390,3... | collective-permute-start | bytes 49160 | tf_op jit(solution)/shard_map/ppermute | solution.py:92
  201.6 0.7 collective-permute-start.30
  202.2 0.7 collective-permute-start.31
  202.9 0.7 collective-permute-start.32
  203.6 0.7 collective-permute-start.33
  204.3 0.7 collective-permute-start.34
  205.0 0.7 collective-permute-start.35
  205.7 0.7 collective-permute-start.36
  206.4 0.7 collective-permute-start.37
  207.0 0.7 collective-permute-start.38
  207.8 0.7 collective-permute-start.39
  208.4 0.7 collective-permute-start.40
  209.1 0.7 collective-permute-start.41
  209.8 1.3 collective-permute-start.42
  211.1 1.3 collective-permute-start.43
  212.4 1.3 collective-permute-start.44
  213.7 0.6 convert_bitcast_fusion.1
  214.3 33.0 %collective-permute-done.42.first_ref = bf16[2,16,256]{2,1,0:T(8,128)(2,1)S(1)} collective-permute-done((bf16[2,16,256]{2,1,0:T(8,128)(2,1)S(1)}, bf16[2,16,256]{2,1,0:T(8,128)(2,1)S(1)}, u32[]{:S(2)}, u32[]{:S(2)}) %collective-permute-start.42) | collective-permute-done | bytes 16416 | tf_op jit(solution)/shard_map/ppermute | solution.py:92
  247.4 0.9 up_kernel0.1
  248.2 0.6 convert_bitcast_fusion
  (54 shorter events, 0.3 us)
Async XLA Ops:
  0.6 31.9 %collective-permute-start.2 = (bf16[2,16,256]{2,1,0:T(8,128)(2,1)}, bf16[2,16,256]{2,1,0:T(8,128)(2,1)S(1)}, u32[]{:S(2)}, u32[]{:S(2)}) collective-permute-start(bf16[2,16,256]{2,1,0:T(8,128)(2,1)} %bitcast.7), channel_id=1, source_target_pairs={{64,0},{65,1},{66,2},{67,3},{68,4},{69,5},{70,6},{71,7},{72,8},{73... | collective-permute-start | bytes 49160 | tf_op jit(solution)/shard_map/ppermute | solution.py:92
  18.1 14.4 %collective-permute-start = (bf16[2,16,256]{2,1,0:T(8,128)(2,1)}, bf16[2,16,256]{2,1,0:T(8,128)(2,1)S(1)}, u32[]{:S(2)}, u32[]{:S(2)}) collective-permute-start(bf16[2,16,256]{2,1,0:T(8,128)(2,1)} %bitcast.8), channel_id=1, source_target_pairs={{1,2},{2,1},{3,4},{4,3},{5,6},{6,5},{7,8},{8,7},{9,10},{10,9},{11,... | collective-permute-start | bytes 49160 | tf_op jit(solution)/shard_map/ppermute | solution.py:92
  27.0 5.8 %collective-permute-start.1 = (bf16[2,16,256]{2,1,0:T(8,128)(2,1)}, bf16[2,16,256]{2,1,0:T(8,128)(2,1)S(1)}, u32[]{:S(2)}, u32[]{:S(2)}) collective-permute-start(bf16[2,16,256]{2,1,0:T(8,128)(2,1)} %bitcast.9), channel_id=1, source_target_pairs={{0,1},{1,0},{2,3},{3,2},{4,5},{5,4},{6,7},{7,6},{8,9},{9,8},{10,11... | collective-permute-start | bytes 49160 | tf_op jit(solution)/shard_map/ppermute | solution.py:92
  28.9 0.7 copy-start.3
  29.6 0.7 copy-start.2
  30.3 1.1 copy-start
  32.5 0.7 copy-start.1
  33.4 3.9 %collective-permute-start.3 = (bf16[2,16,256]{2,1,0:T(8,128)(2,1)S(1)}, bf16[2,16,256]{2,1,0:T(8,128)(2,1)S(1)}, u32[]{:S(2)}, u32[]{:S(2)}) collective-permute-start(bf16[2,16,256]{2,1,0:T(8,128)(2,1)S(1)} %get-tuple-element.31), channel_id=1, source_target_pairs={{1,66},{2,65},{3,68},{4,67},{5,70},{6,69},{7,72},{8,71},{9,74},{10... | collective-permute-start | bytes 49160 | tf_op jit(solution)/shard_map/ppermute | solution.py:92
  34.7 2.7 %collective-permute-start.4 = (bf16[2,16,256]{2,1,0:T(8,128)(2,1)S(1)}, bf16[2,16,256]{2,1,0:T(8,128)(2,1)S(1)}, u32[]{:S(2)}, u32[]{:S(2)}) collective-permute-start(bf16[2,16,256]{2,1,0:T(8,128)(2,1)S(1)} %get-tuple-element.31), channel_id=1, source_target_pairs={{0,65},{1,64},{2,67},{3,66},{4,69},{5,68},{6,71},{7,70},{8,73},{9,... | collective-permute-start | bytes 49160 | tf_op jit(solution)/shard_map/ppermute | solution.py:92
  36.0 2.1 collective-permute-start.5
  38.2 2.0 collective-permute-start.6
  38.8 1.4 collective-permute-start.7
  39.5 0.7 collective-permute-start.8
  40.2 2.0 collective-permute-start.10
  40.9 1.4 collective-permute-start.11
  41.6 0.7 collective-permute-start.9
  42.3 2.0 collective-permute-start.12
  42.9 1.4 collective-permute-start.13
  43.6 0.7 collective-permute-start.14
  44.3 2.0 collective-permute-start.15
  45.0 1.4 collective-permute-start.16
  45.7 0.7 collective-permute-start.17
  46.4 50.9 %collective-permute-start.18 = (bf16[2,16,256]{2,1,0:T(8,128)(2,1)S(1)}, bf16[2,16,256]{2,1,0:T(8,128)(2,1)S(1)}, u32[]{:S(2)}, u32[]{:S(2)}) collective-permute-start(bf16[2,16,256]{2,1,0:T(8,128)(2,1)S(1)} %get-tuple-element.41), channel_id=1, source_target_pairs={{321,386},{322,385},{323,388},{324,387},{325,390},{326,389},{327,3... | collective-permute-start | bytes 49160 | tf_op jit(solution)/shard_map/ppermute | solution.py:92
  47.1 50.2 %collective-permute-start.19 = (bf16[2,16,256]{2,1,0:T(8,128)(2,1)S(1)}, bf16[2,16,256]{2,1,0:T(8,128)(2,1)S(1)}, u32[]{:S(2)}, u32[]{:S(2)}) collective-permute-start(bf16[2,16,256]{2,1,0:T(8,128)(2,1)S(1)} %get-tuple-element.41), channel_id=1, source_target_pairs={{320,385},{321,384},{322,387},{323,386},{324,389},{325,388},{326,3... | collective-permute-start | bytes 49160 | tf_op jit(solution)/shard_map/ppermute | solution.py:92
  81.2 16.1 %collective-permute-start.20 = (bf16[2,16,256]{2,1,0:T(8,128)(2,1)S(1)}, bf16[2,16,256]{2,1,0:T(8,128)(2,1)S(1)}, u32[]{:S(2)}, u32[]{:S(2)}) collective-permute-start(bf16[2,16,256]{2,1,0:T(8,128)(2,1)S(1)} %get-tuple-element.41), channel_id=1, source_target_pairs={{320,384},{321,385},{322,386},{323,387},{324,388},{325,389},{326,3... | collective-permute-start | bytes 49160 | tf_op jit(solution)/shard_map/ppermute | solution.py:92
  97.3 35.3 %collective-permute-start.21 = (bf16[2,16,256]{2,1,0:T(8,128)(2,1)S(1)}, bf16[2,16,256]{2,1,0:T(8,128)(2,1)S(1)}, u32[]{:S(2)}, u32[]{:S(2)}) collective-permute-start(bf16[2,16,256]{2,1,0:T(8,128)(2,1)S(1)} %get-tuple-element.43), channel_id=1, source_target_pairs={{385,450},{386,449},{387,452},{388,451},{389,454},{390,453},{391,4... | collective-permute-start | bytes 49160 | tf_op jit(solution)/shard_map/ppermute | solution.py:92
  98.0 34.7 %collective-permute-start.22 = (bf16[2,16,256]{2,1,0:T(8,128)(2,1)S(1)}, bf16[2,16,256]{2,1,0:T(8,128)(2,1)S(1)}, u32[]{:S(2)}, u32[]{:S(2)}) collective-permute-start(bf16[2,16,256]{2,1,0:T(8,128)(2,1)S(1)} %get-tuple-element.43), channel_id=1, source_target_pairs={{384,449},{385,448},{386,451},{387,450},{388,453},{389,452},{390,4... | collective-permute-start | bytes 49160 | tf_op jit(solution)/shard_map/ppermute | solution.py:92
  116.6 16.1 %collective-permute-start.23 = (bf16[2,16,256]{2,1,0:T(8,128)(2,1)S(1)}, bf16[2,16,256]{2,1,0:T(8,128)(2,1)S(1)}, u32[]{:S(2)}, u32[]{:S(2)}) collective-permute-start(bf16[2,16,256]{2,1,0:T(8,128)(2,1)S(1)} %get-tuple-element.43), channel_id=1, source_target_pairs={{384,448},{385,449},{386,450},{387,451},{388,452},{389,453},{390,4... | collective-permute-start | bytes 49160 | tf_op jit(solution)/shard_map/ppermute | solution.py:92
  132.7 34.7 %collective-permute-start.24 = (bf16[2,16,256]{2,1,0:T(8,128)(2,1)S(1)}, bf16[2,16,256]{2,1,0:T(8,128)(2,1)S(1)}, u32[]{:S(2)}, u32[]{:S(2)}) collective-permute-start(bf16[2,16,256]{2,1,0:T(8,128)(2,1)S(1)} %get-tuple-element.46), channel_id=1, source_target_pairs={{449,386},{450,385},{451,388},{452,387},{453,390},{454,389},{455,3... | collective-permute-start | bytes 49160 | tf_op jit(solution)/shard_map/ppermute | solution.py:92
  133.4 34.0 %collective-permute-start.25 = (bf16[2,16,256]{2,1,0:T(8,128)(2,1)S(1)}, bf16[2,16,256]{2,1,0:T(8,128)(2,1)S(1)}, u32[]{:S(2)}, u32[]{:S(2)}) collective-permute-start(bf16[2,16,256]{2,1,0:T(8,128)(2,1)S(1)} %get-tuple-element.46), channel_id=1, source_target_pairs={{448,385},{449,384},{450,387},{451,386},{452,389},{453,388},{454,3... | collective-permute-start | bytes 49160 | tf_op jit(solution)/shard_map/ppermute | solution.py:92
  151.3 16.1 %collective-permute-start.26 = (bf16[2,16,256]{2,1,0:T(8,128)(2,1)S(1)}, bf16[2,16,256]{2,1,0:T(8,128)(2,1)S(1)}, u32[]{:S(2)}, u32[]{:S(2)}) collective-permute-start(bf16[2,16,256]{2,1,0:T(8,128)(2,1)S(1)} %get-tuple-element.46), channel_id=1, source_target_pairs={{448,384},{449,385},{450,386},{451,387},{452,388},{453,389},{454,3... | collective-permute-start | bytes 49160 | tf_op jit(solution)/shard_map/ppermute | solution.py:92
  167.5 34.0 %collective-permute-start.27 = (bf16[2,16,256]{2,1,0:T(8,128)(2,1)S(1)}, bf16[2,16,256]{2,1,0:T(8,128)(2,1)S(1)}, u32[]{:S(2)}, u32[]{:S(2)}) collective-permute-start(bf16[2,16,256]{2,1,0:T(8,128)(2,1)S(1)} %get-tuple-element.47), channel_id=1, source_target_pairs={{385,322},{386,321},{387,324},{388,323},{389,326},{390,325},{391,3... | collective-permute-start | bytes 49160 | tf_op jit(solution)/shard_map/ppermute | solution.py:92
  168.1 33.4 %collective-permute-start.28 = (bf16[2,16,256]{2,1,0:T(8,128)(2,1)S(1)}, bf16[2,16,256]{2,1,0:T(8,128)(2,1)S(1)}, u32[]{:S(2)}, u32[]{:S(2)}) collective-permute-start(bf16[2,16,256]{2,1,0:T(8,128)(2,1)S(1)} %get-tuple-element.47), channel_id=1, source_target_pairs={{384,321},{385,320},{386,323},{387,322},{388,325},{389,324},{390,3... | collective-permute-start | bytes 49160 | tf_op jit(solution)/shard_map/ppermute | solution.py:92
  185.4 16.1 %collective-permute-start.29 = (bf16[2,16,256]{2,1,0:T(8,128)(2,1)S(1)}, bf16[2,16,256]{2,1,0:T(8,128)(2,1)S(1)}, u32[]{:S(2)}, u32[]{:S(2)}) collective-permute-start(bf16[2,16,256]{2,1,0:T(8,128)(2,1)S(1)} %get-tuple-element.47), channel_id=1, source_target_pairs={{384,320},{385,321},{386,322},{387,323},{388,324},{389,325},{390,3... | collective-permute-start | bytes 49160 | tf_op jit(solution)/shard_map/ppermute | solution.py:92
  201.6 2.0 collective-permute-start.30
  202.2 1.4 collective-permute-start.31
  202.9 0.7 collective-permute-start.32
  203.6 2.0 collective-permute-start.33
  204.3 1.4 collective-permute-start.34
  205.0 0.7 collective-permute-start.35
  205.7 2.0 collective-permute-start.36
  206.4 1.4 collective-permute-start.37
  207.0 0.7 collective-permute-start.38
  207.8 2.0 collective-permute-start.39
  208.4 1.4 collective-permute-start.40
  209.1 0.7 collective-permute-start.41
  209.8 37.5 %collective-permute-start.42 = (bf16[2,16,256]{2,1,0:T(8,128)(2,1)S(1)}, bf16[2,16,256]{2,1,0:T(8,128)(2,1)S(1)}, u32[]{:S(2)}, u32[]{:S(2)}) collective-permute-start(bf16[2,16,256]{2,1,0:T(8,128)(2,1)S(1)} %get-tuple-element.57), channel_id=1, source_target_pairs={{65,2},{66,1},{67,4},{68,3},{69,6},{70,5},{71,8},{72,7},{73,10},{7... | collective-permute-start | bytes 49160 | tf_op jit(solution)/shard_map/ppermute | solution.py:92
  211.1 36.2 %collective-permute-start.43 = (bf16[2,16,256]{2,1,0:T(8,128)(2,1)S(1)}, bf16[2,16,256]{2,1,0:T(8,128)(2,1)S(1)}, u32[]{:S(2)}, u32[]{:S(2)}) collective-permute-start(bf16[2,16,256]{2,1,0:T(8,128)(2,1)S(1)} %get-tuple-element.57), channel_id=1, source_target_pairs={{64,1},{65,0},{66,3},{67,2},{68,5},{69,4},{70,7},{71,6},{72,9},{73... | collective-permute-start | bytes 49160 | tf_op jit(solution)/shard_map/ppermute | solution.py:92
  212.4 34.9 %collective-permute-start.44 = (bf16[2,16,256]{2,1,0:T(8,128)(2,1)S(1)}, bf16[2,16,256]{2,1,0:T(8,128)(2,1)S(1)}, u32[]{:S(2)}, u32[]{:S(2)}) collective-permute-start(bf16[2,16,256]{2,1,0:T(8,128)(2,1)S(1)} %get-tuple-element.57), channel_id=1, source_target_pairs={{64,0},{65,1},{66,2},{67,3},{68,4},{69,5},{70,6},{71,7},{72,8},{73... | collective-permute-start | bytes 49160 | tf_op jit(solution)/shard_map/ppermute | solution.py:92

commit v2 on v1

--- a/solution.py
+++ b/solution.py
@@ -97,11 +97,15 @@
     def far(value, k, to_k):
         return sent(value, [(k, j, to_k, beside(j, True)) for j in range(lats)])
 
+    def rounds(k, to_k):
+        half = layers // 2
+        return [(i, i + to_k - k) for i in range(k % half, layers, half)]
+
     def near(value, k, to_k):
-        return sent(value, [(k, j, to_k, beside(j, False)) for j in range(lats)])
+        return sent(value, [(i, j, to_i, beside(j, False)) for i, to_i in rounds(k, to_k) for j in range(lats)])
 
     def same(value, k, to_k):
-        return sent(value, [(k, j, to_k, j) for j in range(lats)])
+        return sent(value, [(i, j, to_i, j) for i, to_i in rounds(k, to_k) for j in range(lats)])
 
     following = sent(field, [(k, j, k - 1, j) for k in range(1, layers) for j in range(lats)])
 
@@ -136,7 +140,7 @@
 
     last = layers - 1
     down = jnp.zeros(field.shape, jnp.float32)
-    order, window = (FAR, NEAR, SAME), [far(field, 0, 0), near(field, 0, 0), field]
+    order, window = (FAR, NEAR, SAME), [far(field, 0, 0), sent(field, [(0, j, 0, beside(j, False)) for j in range(lats)]), field]
     for layer in range(last):
         send, down = step(down_kernel, layer, order, *window, dense, down, following)
         order = (SAME, FAR, NEAR) if layer == 2 else (FAR, NEAR, SAME)

time: 250 us -> 131 us (0.52)
  starting transfers between devices: 207 us -> 54.8 us
  waiting for transfers between devices: 34.3 us -> 67.2 us
    ppermute x45, starting transfers between devices: 207 us -> 54.8 us  [sent(): return lax.ppermute(value, AXES, pairs)]
    ppermute x45, waiting for transfers between devices: 34.3 us -> 67.2 us  [sent(): return lax.ppermute(value, AXES, pairs)]
  transfers between devices with their start and end apart: 45 -> 45, of which waited for: 4 -> 6; matrix products, arithmetic and copies ran while one was open for 0% -> 0% of each run, Pallas kernels for 0% -> 1%
where the time goes in v2:
time: 131 us; the launch traced here: 130 us
  waiting for transfers between devices  67.2 us (51%)
  starting transfers between devices  54.8 us (42%)
  local copies, waits for them, and re-layouts  2.78 us (2%)
  Pallas kernels  2.33 us (2%)
  between operations  1.41 us (1%)
    ppermute x45, waiting for transfers between devices, sent(): return lax.ppermute(value, AXES, pairs)  67.2 us
    ppermute x45, starting transfers between devices, sent(): return lax.ppermute(value, AXES, pairs)  54.8 us
    unnamed x8, local copies, waits for them, and re-layouts  2.78 us
  transfers between devices with their start and end apart: 45, of which 6 were waited for; matrix products, arithmetic and copies ran while one was open for 0% of the time, Pallas kernels for 1%

profile of v2, /device:TPU:62, one launch (start us, length us, event | category | flops | bytes accessed | tf_op | source)
XLA Modules:
  0.0 129.8 jit_solution(2121696516515689637)
XLA Ops:
  0.6 1.3 collective-permute-start.2
  1.9 10.0 %collective-permute-start = (bf16[2,16,256]{2,1,0:T(8,128)(2,1)}, bf16[2,16,256]{2,1,0:T(8,128)(2,1)S(1)}, u32[]{:S(2)}, u32[]{:S(2)}) collective-permute-start(bf16[2,16,256]{2,1,0:T(8,128)(2,1)} %bitcast.8), channel_id=1, source_target_pairs={{1,2},{2,1},{3,4},{4,3},{5,6},{6,5},{7,8},{8,7},{9,10},{10,9},{11,... | collective-permute-start | bytes 49160 | tf_op jit(solution)/shard_map/ppermute | solution.py:92
  12.0 1.9 %collective-permute-start.1 = (bf16[2,16,256]{2,1,0:T(8,128)(2,1)}, bf16[2,16,256]{2,1,0:T(8,128)(2,1)S(1)}, u32[]{:S(2)}, u32[]{:S(2)}) collective-permute-start(bf16[2,16,256]{2,1,0:T(8,128)(2,1)} %bitcast.9), channel_id=1, source_target_pairs={{0,1},{1,0},{2,3},{3,2},{4,5},{5,4},{6,7},{7,6},{8,9},{9,8},{10,11... | collective-permute-start | bytes 49160 | tf_op jit(solution)/shard_map/ppermute | solution.py:92
  13.9 0.6 copy-done.3
  14.6 0.0 copy-start.2
  14.6 0.6 copy-done.2
  15.2 1.1 copy-done
  16.4 1.1 dense.1.dense_ref
  17.4 0.0 copy-start.1
  17.5 0.3 collective-permute-done.1.second_ref
  17.8 0.3 copy-done.1
  18.2 0.2 down_kernel0.1
  18.4 1.3 collective-permute-start.3
  19.7 1.3 collective-permute-start.4
  21.0 1.3 collective-permute-start.5
  22.3 0.0 collective-permute-done.3.first_ref
  22.3 0.1 collective-permute-done.4.second_ref
  22.4 0.7 collective-permute-done.5.third_ref
  23.1 0.7 collective-permute-start.6
  23.8 0.7 collective-permute-start.7
  24.5 0.7 collective-permute-start.8
  25.1 0.0 collective-permute-done.7.second_ref
  25.2 0.7 collective-permute-start.10
  25.9 0.7 collective-permute-start.11
  26.5 0.7 collective-permute-start.9
  27.3 0.7 collective-permute-start.12
  27.9 0.7 collective-permute-start.13
  28.6 0.7 collective-permute-start.14
  29.3 0.7 collective-permute-start.15
  30.0 6.8 %collective-permute-start.16 = (bf16[2,16,256]{2,1,0:T(8,128)(2,1)S(1)}, bf16[2,16,256]{2,1,0:T(8,128)(2,1)S(1)}, u32[]{:S(2)}, u32[]{:S(2)}) collective-permute-start(bf16[2,16,256]{2,1,0:T(8,128)(2,1)S(1)} %get-tuple-element.39), channel_id=1, source_target_pairs={{0,65},{1,64},{2,67},{3,66},{4,69},{5,68},{6,71},{7,70},{8,73},{9,... | collective-permute-start | bytes 49160 | tf_op jit(solution)/shard_map/ppermute | solution.py:92
  36.8 3.3 %collective-permute-start.17 = (bf16[2,16,256]{2,1,0:T(8,128)(2,1)S(1)}, bf16[2,16,256]{2,1,0:T(8,128)(2,1)S(1)}, u32[]{:S(2)}, u32[]{:S(2)}) collective-permute-start(bf16[2,16,256]{2,1,0:T(8,128)(2,1)S(1)} %get-tuple-element.39), channel_id=1, source_target_pairs={{0,64},{1,65},{2,66},{3,67},{4,68},{5,69},{6,70},{7,71},{8,72},{9,... | collective-permute-start | bytes 49160 | tf_op jit(solution)/shard_map/ppermute | solution.py:92
  40.1 0.8 collective-permute-done.17.third_ref
  40.9 0.7 collective-permute-start.18
  41.6 0.7 collective-permute-start.19
  42.3 0.7 collective-permute-start.20
  43.0 0.7 collective-permute-start.21
  43.7 0.7 collective-permute-start.22
  44.3 0.7 collective-permute-start.23
  45.1 0.7 collective-permute-start.24
  45.7 0.7 collective-permute-start.25
  46.4 0.7 collective-permute-start.26
  47.1 0.7 collective-permute-start.27
  47.8 0.7 collective-permute-start.28
  48.5 0.7 collective-permute-start.29
  49.2 0.7 collective-permute-start.30
  49.9 1.3 collective-permute-start.31
  51.2 1.3 collective-permute-start.32
  52.5 19.9 %collective-permute-done.31.second_ref = bf16[2,16,256]{2,1,0:T(8,128)(2,1)S(1)} collective-permute-done((bf16[2,16,256]{2,1,0:T(8,128)(2,1)S(1)}, bf16[2,16,256]{2,1,0:T(8,128)(2,1)S(1)}, u32[]{:S(2)}, u32[]{:S(2)}) %collective-permute-start.31) | collective-permute-done | bytes 16416 | tf_op jit(solution)/shard_map/ppermute | solution.py:92
  72.4 0.7 collective-permute-start.33
  73.0 0.7 collective-permute-start.34
  73.7 0.7 collective-permute-start.35
  74.4 0.7 collective-permute-start.36
  75.1 0.7 collective-permute-start.37
  75.8 0.7 collective-permute-start.38
  76.5 0.7 collective-permute-start.39
  77.2 0.7 collective-permute-start.40
  77.8 0.7 collective-permute-start.41
  78.6 1.3 collective-permute-start.42
  79.9 1.3 collective-permute-start.43
  81.2 1.3 collective-permute-start.44
  82.5 0.6 convert_bitcast_fusion.1
  83.1 45.3 %collective-permute-done.42.first_ref = bf16[2,16,256]{2,1,0:T(8,128)(2,1)S(1)} collective-permute-done((bf16[2,16,256]{2,1,0:T(8,128)(2,1)S(1)}, bf16[2,16,256]{2,1,0:T(8,128)(2,1)S(1)}, u32[]{:S(2)}, u32[]{:S(2)}) %collective-permute-start.42) | collective-permute-done | bytes 16416 | tf_op jit(solution)/shard_map/ppermute | solution.py:92
  128.3 0.9 up_kernel0.1
  129.2 0.6 convert_bitcast_fusion
  (54 shorter events, 0.3 us)
Async XLA Ops:
  0.6 16.8 %collective-permute-start.2 = (bf16[2,16,256]{2,1,0:T(8,128)(2,1)}, bf16[2,16,256]{2,1,0:T(8,128)(2,1)S(1)}, u32[]{:S(2)}, u32[]{:S(2)}) collective-permute-start(bf16[2,16,256]{2,1,0:T(8,128)(2,1)} %bitcast.7), channel_id=1, source_target_pairs={{64,0},{65,1},{66,2},{67,3},{68,4},{69,5},{70,6},{71,7},{72,8},{73... | collective-permute-start | bytes 49160 | tf_op jit(solution)/shard_map/ppermute | solution.py:92
  1.9 15.5 %collective-permute-start = (bf16[2,16,256]{2,1,0:T(8,128)(2,1)}, bf16[2,16,256]{2,1,0:T(8,128)(2,1)S(1)}, u32[]{:S(2)}, u32[]{:S(2)}) collective-permute-start(bf16[2,16,256]{2,1,0:T(8,128)(2,1)} %bitcast.8), channel_id=1, source_target_pairs={{1,2},{2,1},{3,4},{4,3},{5,6},{6,5},{7,8},{8,7},{9,10},{10,9},{11,... | collective-permute-start | bytes 49160 | tf_op jit(solution)/shard_map/ppermute | solution.py:92
  12.0 5.8 %collective-permute-start.1 = (bf16[2,16,256]{2,1,0:T(8,128)(2,1)}, bf16[2,16,256]{2,1,0:T(8,128)(2,1)S(1)}, u32[]{:S(2)}, u32[]{:S(2)}) collective-permute-start(bf16[2,16,256]{2,1,0:T(8,128)(2,1)} %bitcast.9), channel_id=1, source_target_pairs={{0,1},{1,0},{2,3},{3,2},{4,5},{5,4},{6,7},{7,6},{8,9},{9,8},{10,11... | collective-permute-start | bytes 49160 | tf_op jit(solution)/shard_map/ppermute | solution.py:92
  13.9 0.7 copy-start.3
  14.6 0.7 copy-start.2
  15.2 1.1 copy-start
  17.4 0.7 copy-start.1
  18.4 3.9 %collective-permute-start.3 = (bf16[2,16,256]{2,1,0:T(8,128)(2,1)S(1)}, bf16[2,16,256]{2,1,0:T(8,128)(2,1)S(1)}, u32[]{:S(2)}, u32[]{:S(2)}) collective-permute-start(bf16[2,16,256]{2,1,0:T(8,128)(2,1)S(1)} %get-tuple-element.31), channel_id=1, source_target_pairs={{1,66},{2,65},{3,68},{4,67},{5,70},{6,69},{7,72},{8,71},{9,74},{10... | collective-permute-start | bytes 49160 | tf_op jit(solution)/shard_map/ppermute | solution.py:92
  19.7 2.7 %collective-permute-start.4 = (bf16[2,16,256]{2,1,0:T(8,128)(2,1)S(1)}, bf16[2,16,256]{2,1,0:T(8,128)(2,1)S(1)}, u32[]{:S(2)}, u32[]{:S(2)}) collective-permute-start(bf16[2,16,256]{2,1,0:T(8,128)(2,1)S(1)} %get-tuple-element.31), channel_id=1, source_target_pairs={{0,65},{1,64},{2,67},{3,66},{4,69},{5,68},{6,71},{7,70},{8,73},{9,... | collective-permute-start | bytes 49160 | tf_op jit(solution)/shard_map/ppermute | solution.py:92
  21.0 2.1 %collective-permute-start.5 = (bf16[2,16,256]{2,1,0:T(8,128)(2,1)S(1)}, bf16[2,16,256]{2,1,0:T(8,128)(2,1)S(1)}, u32[]{:S(2)}, u32[]{:S(2)}) collective-permute-start(bf16[2,16,256]{2,1,0:T(8,128)(2,1)S(1)} %get-tuple-element.31), channel_id=1, source_target_pairs={{0,64},{1,65},{2,66},{3,67},{4,68},{5,69},{6,70},{7,71},{8,72},{9,... | collective-permute-start | bytes 49160 | tf_op jit(solution)/shard_map/ppermute | solution.py:92
  23.1 2.0 %collective-permute-start.6 = (bf16[2,16,256]{2,1,0:T(8,128)(2,1)S(1)}, bf16[2,16,256]{2,1,0:T(8,128)(2,1)S(1)}, u32[]{:S(2)}, u32[]{:S(2)}) collective-permute-start(bf16[2,16,256]{2,1,0:T(8,128)(2,1)S(1)} %get-tuple-element.33), channel_id=1, source_target_pairs={{65,130},{66,129},{67,132},{68,131},{69,134},{70,133},{71,136},{72... | collective-permute-start | bytes 49160 | tf_op jit(solution)/shard_map/ppermute | solution.py:92
  23.8 1.4 %collective-permute-start.7 = (bf16[2,16,256]{2,1,0:T(8,128)(2,1)S(1)}, bf16[2,16,256]{2,1,0:T(8,128)(2,1)S(1)}, u32[]{:S(2)}, u32[]{:S(2)}) collective-permute-start(bf16[2,16,256]{2,1,0:T(8,128)(2,1)S(1)} %get-tuple-element.33), channel_id=1, source_target_pairs={{64,129},{65,128},{66,131},{67,130},{68,133},{69,132},{70,135},{71... | collective-permute-start | bytes 49160 | tf_op jit(solution)/shard_map/ppermute | solution.py:92
  24.5 0.7 collective-permute-start.8
  25.2 2.0 %collective-permute-start.10 = (bf16[2,16,256]{2,1,0:T(8,128)(2,1)S(1)}, bf16[2,16,256]{2,1,0:T(8,128)(2,1)S(1)}, u32[]{:S(2)}, u32[]{:S(2)}) collective-permute-start(bf16[2,16,256]{2,1,0:T(8,128)(2,1)S(1)} %get-tuple-element.35), channel_id=1, source_target_pairs={{129,194},{130,193},{131,196},{132,195},{133,198},{134,197},{135,2... | collective-permute-start | bytes 49160 | tf_op jit(solution)/shard_map/ppermute | solution.py:92
  25.9 1.4 %collective-permute-start.11 = (bf16[2,16,256]{2,1,0:T(8,128)(2,1)S(1)}, bf16[2,16,256]{2,1,0:T(8,128)(2,1)S(1)}, u32[]{:S(2)}, u32[]{:S(2)}) collective-permute-start(bf16[2,16,256]{2,1,0:T(8,128)(2,1)S(1)} %get-tuple-element.35), channel_id=1, source_target_pairs={{128,193},{129,192},{130,195},{131,194},{132,197},{133,196},{134,1... | collective-permute-start | bytes 49160 | tf_op jit(solution)/shard_map/ppermute | solution.py:92
  26.5 0.7 collective-permute-start.9
  27.3 2.0 %collective-permute-start.12 = (bf16[2,16,256]{2,1,0:T(8,128)(2,1)S(1)}, bf16[2,16,256]{2,1,0:T(8,128)(2,1)S(1)}, u32[]{:S(2)}, u32[]{:S(2)}) collective-permute-start(bf16[2,16,256]{2,1,0:T(8,128)(2,1)S(1)} %get-tuple-element.37), channel_id=1, source_target_pairs={{193,258},{194,257},{195,260},{196,259},{197,262},{198,261},{199,2... | collective-permute-start | bytes 49160 | tf_op jit(solution)/shard_map/ppermute | solution.py:92
  27.9 1.4 %collective-permute-start.13 = (bf16[2,16,256]{2,1,0:T(8,128)(2,1)S(1)}, bf16[2,16,256]{2,1,0:T(8,128)(2,1)S(1)}, u32[]{:S(2)}, u32[]{:S(2)}) collective-permute-start(bf16[2,16,256]{2,1,0:T(8,128)(2,1)S(1)} %get-tuple-element.37), channel_id=1, source_target_pairs={{192,257},{193,256},{194,259},{195,258},{196,261},{197,260},{198,2... | collective-permute-start | bytes 49160 | tf_op jit(solution)/shard_map/ppermute | solution.py:92
  28.6 0.7 collective-permute-start.14
  29.3 10.8 %collective-permute-start.15 = (bf16[2,16,256]{2,1,0:T(8,128)(2,1)S(1)}, bf16[2,16,256]{2,1,0:T(8,128)(2,1)S(1)}, u32[]{:S(2)}, u32[]{:S(2)}) collective-permute-start(bf16[2,16,256]{2,1,0:T(8,128)(2,1)S(1)} %get-tuple-element.39), channel_id=1, source_target_pairs={{257,322},{258,321},{259,324},{260,323},{261,326},{262,325},{263,3... | collective-permute-start | bytes 49160 | tf_op jit(solution)/shard_map/ppermute | solution.py:92
  30.0 10.1 %collective-permute-start.16 = (bf16[2,16,256]{2,1,0:T(8,128)(2,1)S(1)}, bf16[2,16,256]{2,1,0:T(8,128)(2,1)S(1)}, u32[]{:S(2)}, u32[]{:S(2)}) collective-permute-start(bf16[2,16,256]{2,1,0:T(8,128)(2,1)S(1)} %get-tuple-element.39), channel_id=1, source_target_pairs={{0,65},{1,64},{2,67},{3,66},{4,69},{5,68},{6,71},{7,70},{8,73},{9,... | collective-permute-start | bytes 49160 | tf_op jit(solution)/shard_map/ppermute | solution.py:92
  36.8 4.1 %collective-permute-start.17 = (bf16[2,16,256]{2,1,0:T(8,128)(2,1)S(1)}, bf16[2,16,256]{2,1,0:T(8,128)(2,1)S(1)}, u32[]{:S(2)}, u32[]{:S(2)}) collective-permute-start(bf16[2,16,256]{2,1,0:T(8,128)(2,1)S(1)} %get-tuple-element.39), channel_id=1, source_target_pairs={{0,64},{1,65},{2,66},{3,67},{4,68},{5,69},{6,70},{7,71},{8,72},{9,... | collective-permute-start | bytes 49160 | tf_op jit(solution)/shard_map/ppermute | solution.py:92
  40.9 2.0 %collective-permute-start.18 = (bf16[2,16,256]{2,1,0:T(8,128)(2,1)S(1)}, bf16[2,16,256]{2,1,0:T(8,128)(2,1)S(1)}, u32[]{:S(2)}, u32[]{:S(2)}) collective-permute-start(bf16[2,16,256]{2,1,0:T(8,128)(2,1)S(1)} %get-tuple-element.41), channel_id=1, source_target_pairs={{321,386},{322,385},{323,388},{324,387},{325,390},{326,389},{327,3... | collective-permute-start | bytes 49160 | tf_op jit(solution)/shard_map/ppermute | solution.py:92
  41.6 1.4 %collective-permute-start.19 = (bf16[2,16,256]{2,1,0:T(8,128)(2,1)S(1)}, bf16[2,16,256]{2,1,0:T(8,128)(2,1)S(1)}, u32[]{:S(2)}, u32[]{:S(2)}) collective-permute-start(bf16[2,16,256]{2,1,0:T(8,128)(2,1)S(1)} %get-tuple-element.41), channel_id=1, source_target_pairs={{64,129},{65,128},{66,131},{67,130},{68,133},{69,132},{70,135},{71... | collective-permute-start | bytes 49160 | tf_op jit(solution)/shard_map/ppermute | solution.py:92
  42.3 0.7 collective-permute-start.20
  43.0 2.0 %collective-permute-start.21 = (bf16[2,16,256]{2,1,0:T(8,128)(2,1)S(1)}, bf16[2,16,256]{2,1,0:T(8,128)(2,1)S(1)}, u32[]{:S(2)}, u32[]{:S(2)}) collective-permute-start(bf16[2,16,256]{2,1,0:T(8,128)(2,1)S(1)} %get-tuple-element.43), channel_id=1, source_target_pairs={{385,450},{386,449},{387,452},{388,451},{389,454},{390,453},{391,4... | collective-permute-start | bytes 49160 | tf_op jit(solution)/shard_map/ppermute | solution.py:92
  43.7 1.4 %collective-permute-start.22 = (bf16[2,16,256]{2,1,0:T(8,128)(2,1)S(1)}, bf16[2,16,256]{2,1,0:T(8,128)(2,1)S(1)}, u32[]{:S(2)}, u32[]{:S(2)}) collective-permute-start(bf16[2,16,256]{2,1,0:T(8,128)(2,1)S(1)} %get-tuple-element.43), channel_id=1, source_target_pairs={{128,193},{129,192},{130,195},{131,194},{132,197},{133,196},{134,1... | collective-permute-start | bytes 49160 | tf_op jit(solution)/shard_map/ppermute | solution.py:92
  44.3 0.7 collective-permute-start.23
  45.1 2.0 %collective-permute-start.24 = (bf16[2,16,256]{2,1,0:T(8,128)(2,1)S(1)}, bf16[2,16,256]{2,1,0:T(8,128)(2,1)S(1)}, u32[]{:S(2)}, u32[]{:S(2)}) collective-permute-start(bf16[2,16,256]{2,1,0:T(8,128)(2,1)S(1)} %get-tuple-element.46), channel_id=1, source_target_pairs={{449,386},{450,385},{451,388},{452,387},{453,390},{454,389},{455,3... | collective-permute-start | bytes 49160 | tf_op jit(solution)/shard_map/ppermute | solution.py:92
  45.7 1.4 %collective-permute-start.25 = (bf16[2,16,256]{2,1,0:T(8,128)(2,1)S(1)}, bf16[2,16,256]{2,1,0:T(8,128)(2,1)S(1)}, u32[]{:S(2)}, u32[]{:S(2)}) collective-permute-start(bf16[2,16,256]{2,1,0:T(8,128)(2,1)S(1)} %get-tuple-element.46), channel_id=1, source_target_pairs={{192,129},{193,128},{194,131},{195,130},{196,133},{197,132},{198,1... | collective-permute-start | bytes 49160 | tf_op jit(solution)/shard_map/ppermute | solution.py:92
  46.4 0.7 collective-permute-start.26
  47.1 2.0 %collective-permute-start.27 = (bf16[2,16,256]{2,1,0:T(8,128)(2,1)S(1)}, bf16[2,16,256]{2,1,0:T(8,128)(2,1)S(1)}, u32[]{:S(2)}, u32[]{:S(2)}) collective-permute-start(bf16[2,16,256]{2,1,0:T(8,128)(2,1)S(1)} %get-tuple-element.47), channel_id=1, source_target_pairs={{385,322},{386,321},{387,324},{388,323},{389,326},{390,325},{391,3... | collective-permute-start | bytes 49160 | tf_op jit(solution)/shard_map/ppermute | solution.py:92
  47.8 1.4 %collective-permute-start.28 = (bf16[2,16,256]{2,1,0:T(8,128)(2,1)S(1)}, bf16[2,16,256]{2,1,0:T(8,128)(2,1)S(1)}, u32[]{:S(2)}, u32[]{:S(2)}) collective-permute-start(bf16[2,16,256]{2,1,0:T(8,128)(2,1)S(1)} %get-tuple-element.47), channel_id=1, source_target_pairs={{128,65},{129,64},{130,67},{131,66},{132,69},{133,68},{134,71},{13... | collective-permute-start | bytes 49160 | tf_op jit(solution)/shard_map/ppermute | solution.py:92
  48.5 0.7 collective-permute-start.29
  49.2 3.3 %collective-permute-start.30 = (bf16[2,16,256]{2,1,0:T(8,128)(2,1)S(1)}, bf16[2,16,256]{2,1,0:T(8,128)(2,1)S(1)}, u32[]{:S(2)}, u32[]{:S(2)}) collective-permute-start(bf16[2,16,256]{2,1,0:T(8,128)(2,1)S(1)} %get-tuple-element.49), channel_id=1, source_target_pairs={{321,258},{322,257},{323,260},{324,259},{325,262},{326,261},{327,2... | collective-permute-start | bytes 49160 | tf_op jit(solution)/shard_map/ppermute | solution.py:92
  49.9 22.5 %collective-permute-start.31 = (bf16[2,16,256]{2,1,0:T(8,128)(2,1)S(1)}, bf16[2,16,256]{2,1,0:T(8,128)(2,1)S(1)}, u32[]{:S(2)}, u32[]{:S(2)}) collective-permute-start(bf16[2,16,256]{2,1,0:T(8,128)(2,1)S(1)} %get-tuple-element.49), channel_id=1, source_target_pairs={{64,1},{65,0},{66,3},{67,2},{68,5},{69,4},{70,7},{71,6},{72,9},{73... | collective-permute-start | bytes 49160 | tf_op jit(solution)/shard_map/ppermute | solution.py:92
  51.2 21.2 %collective-permute-start.32 = (bf16[2,16,256]{2,1,0:T(8,128)(2,1)S(1)}, bf16[2,16,256]{2,1,0:T(8,128)(2,1)S(1)}, u32[]{:S(2)}, u32[]{:S(2)}) collective-permute-start(bf16[2,16,256]{2,1,0:T(8,128)(2,1)S(1)} %get-tuple-element.49), channel_id=1, source_target_pairs={{64,0},{65,1},{66,2},{67,3},{68,4},{69,5},{70,6},{71,7},{72,8},{73... | collective-permute-start | bytes 49160 | tf_op jit(solution)/shard_map/ppermute | solution.py:92
  72.4 2.0 %collective-permute-start.33 = (bf16[2,16,256]{2,1,0:T(8,128)(2,1)S(1)}, bf16[2,16,256]{2,1,0:T(8,128)(2,1)S(1)}, u32[]{:S(2)}, u32[]{:S(2)}) collective-permute-start(bf16[2,16,256]{2,1,0:T(8,128)(2,1)S(1)} %get-tuple-element.51), channel_id=1, source_target_pairs={{257,194},{258,193},{259,196},{260,195},{261,198},{262,197},{263,2... | collective-permute-start | bytes 49160 | tf_op jit(solution)/shard_map/ppermute | solution.py:92
  73.0 1.4 %collective-permute-start.34 = (bf16[2,16,256]{2,1,0:T(8,128)(2,1)S(1)}, bf16[2,16,256]{2,1,0:T(8,128)(2,1)S(1)}, u32[]{:S(2)}, u32[]{:S(2)}) collective-permute-start(bf16[2,16,256]{2,1,0:T(8,128)(2,1)S(1)} %get-tuple-element.51), channel_id=1, source_target_pairs={{256,193},{257,192},{258,195},{259,194},{260,197},{261,196},{262,1... | collective-permute-start | bytes 49160 | tf_op jit(solution)/shard_map/ppermute | solution.py:92
  73.7 0.7 collective-permute-start.35
  74.4 2.0 %collective-permute-start.36 = (bf16[2,16,256]{2,1,0:T(8,128)(2,1)S(1)}, bf16[2,16,256]{2,1,0:T(8,128)(2,1)S(1)}, u32[]{:S(2)}, u32[]{:S(2)}) collective-permute-start(bf16[2,16,256]{2,1,0:T(8,128)(2,1)S(1)} %get-tuple-element.53), channel_id=1, source_target_pairs={{193,130},{194,129},{195,132},{196,131},{197,134},{198,133},{199,1... | collective-permute-start | bytes 49160 | tf_op jit(solution)/shard_map/ppermute | solution.py:92
  75.1 1.4 %collective-permute-start.37 = (bf16[2,16,256]{2,1,0:T(8,128)(2,1)S(1)}, bf16[2,16,256]{2,1,0:T(8,128)(2,1)S(1)}, u32[]{:S(2)}, u32[]{:S(2)}) collective-permute-start(bf16[2,16,256]{2,1,0:T(8,128)(2,1)S(1)} %get-tuple-element.53), channel_id=1, source_target_pairs={{192,129},{193,128},{194,131},{195,130},{196,133},{197,132},{198,1... | collective-permute-start | bytes 49160 | tf_op jit(solution)/shard_map/ppermute | solution.py:92
  75.8 0.7 collective-permute-start.38
  76.5 2.0 %collective-permute-start.39 = (bf16[2,16,256]{2,1,0:T(8,128)(2,1)S(1)}, bf16[2,16,256]{2,1,0:T(8,128)(2,1)S(1)}, u32[]{:S(2)}, u32[]{:S(2)}) collective-permute-start(bf16[2,16,256]{2,1,0:T(8,128)(2,1)S(1)} %get-tuple-element.55), channel_id=1, source_target_pairs={{129,66},{130,65},{131,68},{132,67},{133,70},{134,69},{135,72},{13... | collective-permute-start | bytes 49160 | tf_op jit(solution)/shard_map/ppermute | solution.py:92
  77.2 1.4 %collective-permute-start.40 = (bf16[2,16,256]{2,1,0:T(8,128)(2,1)S(1)}, bf16[2,16,256]{2,1,0:T(8,128)(2,1)S(1)}, u32[]{:S(2)}, u32[]{:S(2)}) collective-permute-start(bf16[2,16,256]{2,1,0:T(8,128)(2,1)S(1)} %get-tuple-element.55), channel_id=1, source_target_pairs={{128,65},{129,64},{130,67},{131,66},{132,69},{133,68},{134,71},{13... | collective-permute-start | bytes 49160 | tf_op jit(solution)/shard_map/ppermute | solution.py:92
  77.8 0.7 collective-permute-start.41
  78.6 49.8 %collective-permute-start.42 = (bf16[2,16,256]{2,1,0:T(8,128)(2,1)S(1)}, bf16[2,16,256]{2,1,0:T(8,128)(2,1)S(1)}, u32[]{:S(2)}, u32[]{:S(2)}) collective-permute-start(bf16[2,16,256]{2,1,0:T(8,128)(2,1)S(1)} %get-tuple-element.57), channel_id=1, source_target_pairs={{65,2},{66,1},{67,4},{68,3},{69,6},{70,5},{71,8},{72,7},{73,10},{7... | collective-permute-start | bytes 49160 | tf_op jit(solution)/shard_map/ppermute | solution.py:92
  79.9 48.5 %collective-permute-start.43 = (bf16[2,16,256]{2,1,0:T(8,128)(2,1)S(1)}, bf16[2,16,256]{2,1,0:T(8,128)(2,1)S(1)}, u32[]{:S(2)}, u32[]{:S(2)}) collective-permute-start(bf16[2,16,256]{2,1,0:T(8,128)(2,1)S(1)} %get-tuple-element.57), channel_id=1, source_target_pairs={{64,1},{65,0},{66,3},{67,2},{68,5},{69,4},{70,7},{71,6},{72,9},{73... | collective-permute-start | bytes 49160 | tf_op jit(solution)/shard_map/ppermute | solution.py:92
  81.2 47.2 %collective-permute-start.44 = (bf16[2,16,256]{2,1,0:T(8,128)(2,1)S(1)}, bf16[2,16,256]{2,1,0:T(8,128)(2,1)S(1)}, u32[]{:S(2)}, u32[]{:S(2)}) collective-permute-start(bf16[2,16,256]{2,1,0:T(8,128)(2,1)S(1)} %get-tuple-element.57), channel_id=1, source_target_pairs={{64,0},{65,1},{66,2},{67,3},{68,4},{69,5},{70,6},{71,7},{72,8},{73... | collective-permute-start | bytes 49160 | tf_op jit(solution)/shard_map/ppermute | solution.py:92

commit v3 on v1

v3 whole, which is shorter than its diff:
```python
import functools

import jax
import jax.numpy as jnp
from jax import lax
from jax.experimental import pallas as pl
from jax.experimental.pallas import tpu as pltpu
from jax.sharding import PartitionSpec as P

AXES = ("depth", "lat")
PARAMS = pltpu.CompilerParams(vmem_limit_bytes=24 * 2**20)


def dense_kernel(rows_ref, cols_ref, blocks_ref, dense_ref, total_ref):
    count, parts, size, _ = blocks_ref.shape
    rows, slots = total_ref.shape[:2]
    total_ref[...] = jnp.zeros_like(total_ref)
    for b in range(count):
        total_ref[rows_ref[0, b], cols_ref[0, b]] += blocks_ref[b].astype(jnp.float32)
    for r in range(rows):
        for s in range(slots):
            for p in range(parts):
                column = (p * rows + r) * size
                dense_ref[s * size : (s + 1) * size, column : column + size] = (
                    total_ref[r, s, p].T.astype(jnp.bfloat16)
                )


def hold_kernel(field_ref, *refs):
    refs[-1][...] = field_ref[...]


def later_kernel(layers, dense_ref, _after, copy_ref):
    layer = lax.axis_index("depth")

    @pl.when(functools.reduce(jnp.logical_or, [layer == k for k in layers]))
    def _():
        copy_ref[...] = dense_ref[...]


def up_kernel(layer, far_ref, near_ref, same_ref, dense_ref, down_ref, kept_ref, up_ref):
    up_ref[...] = kept_ref[...]

    @pl.when(lax.axis_index("depth") == layer)
    def _():
        window = (far_ref[...], same_ref[...], near_ref[...])
        up_ref[...] = plus(down_ref[...], applied(window, dense_ref))


def applied(window, dense_ref):
    sources, width = window[0].shape[1:]
    flat = jnp.concatenate([part.reshape(2 * sources, width) for part in window], axis=1)
    product = jnp.dot(flat, dense_ref[...], preferred_element_type=jnp.float32)
    by_real, by_imag = product[:, :width], product[:, width:]
    real = by_real[:sources] - by_imag[sources:]
    imag = by_real[sources:] + by_imag[:sources]
    return jnp.stack([real, imag])


def plus(field, trace):
    return (field.astype(jnp.float32) + trace.astype(jnp.float32)).astype(jnp.bfloat16)


def three(outer, far_ref, near_ref, same_ref, dense_refs, pairs_ref):
    first_ref, second_ref = outer
    place = lax.axis_index("lat") % 4
    first_is_far = (place == 0) | (place == 3)

    @pl.when(first_is_far)
    def _():
        pairs_ref[0] = first_ref[...]
        pairs_ref[1] = second_ref[...]

    @pl.when(jnp.logical_not(first_is_far))
    def _():
        pairs_ref[0] = second_ref[...]
        pairs_ref[1] = first_ref[...]

    far, near, same = far_ref[...], near_ref[...], same_ref[...]
    return (
        applied((same, far, pairs_ref[0]), dense_refs[0]),
        applied((far, same, near), dense_refs[1]),
        applied((pairs_ref[1], near, same), dense_refs[2]),
    )


def down_kernel(layer, next_ref, far_ref, near_ref, same_ref, dense_ref, kept_ref, sent_ref, send_ref, down_ref):
    down_ref[...] = kept_ref[...]
    send_ref[...] = sent_ref[...]

    @pl.when(lax.axis_index("depth") == layer)
    def _():
        window = (far_ref[...], same_ref[...], near_ref[...])
        trace = applied(window, dense_ref).astype(jnp.bfloat16)
        down_ref[...] = trace
        send_ref[...] = plus(next_ref[...], trace)


def down_two_kernel(
    layer, first_ref, far_ref, second_ref, near_ref, same_ref, other_far_ref, other_same_ref, other_near_ref,
    dense_ref, field_far_ref, field_ref, field_near_ref, kept_ref, down_ref, both_ref, pairs_ref,
):
    down_ref[...] = kept_ref[...]

    @pl.when(lax.axis_index("depth") == layer)
    def _():
        others = (other_far_ref, other_same_ref, other_near_ref)
        traces = [
            total.astype(jnp.bfloat16)
            for total in three((first_ref, second_ref), far_ref, near_ref, same_ref, others, pairs_ref)
        ]
        fields = (field_far_ref[...], field_ref[...], field_near_ref[...])
        window = [plus(field, trace) for field, trace in zip(fields, traces)]
        trace = applied(window, dense_ref).astype(jnp.bfloat16)
        down_ref[...] = trace
        both_ref[1] = traces[1]

    both_ref[0] = down_ref[...]


def turn_kernel(layer, far_ref, near_ref, both_ref, dense_ref, wait_ref, kept_ref, send_ref, up_ref, down_ref):
    up_ref[...] = kept_ref[...]
    down_ref[...] = kept_ref[...]

    @pl.when(lax.axis_index("depth") == layer)
    def _():
        down_ref[...] = both_ref[1]
        window = (far_ref[0], both_ref[0], near_ref[0])
        trace = plus(both_ref[1], applied(window, dense_ref))
        up_ref[...] = trace
        send_ref[...] = plus(wait_ref[...], trace)


def up_two_kernel(
    layer, waits, first_ref, far_ref, second_ref, near_ref, same_ref, other_far_ref, other_same_ref, other_near_ref,
    dense_ref, down_ref, wait_ref, kept_ref, other_ref, send_ref, up_ref, back_ref, pairs_ref,
):
    up_ref[...] = kept_ref[...]
    back_ref[...] = other_ref[...]

    @pl.when(lax.axis_index("depth") == layer)
    def _():
        others = (other_far_ref, other_same_ref, other_near_ref)
        totals = three((first_ref, second_ref), far_ref, near_ref, same_ref, others, pairs_ref)
        window = [total.astype(jnp.bfloat16) for total in totals]
        back_ref[...] = window[1]
        trace = plus(down_ref[...], applied(window, dense_ref))
        up_ref[...] = trace
        send_ref[...] = plus(wait_ref[...], trace) if waits else trace


def end_kernel(layers, up_ref, returned_ref, out_ref):
    layer = lax.axis_index("depth")
    elsewhere = functools.reduce(jnp.logical_or, [layer == k for k in layers])

    @pl.when(elsewhere)
    def _():
        out_ref[...] = returned_ref[...]

    @pl.when(jnp.logical_not(elsewhere))
    def _():
        out_ref[...] = up_ref[...]


def vmem(count):
    return [pl.BlockSpec(memory_space=pltpu.VMEM)] * count


def local(forcing, blocks, block_rows, block_cols):
    layers, lats = lax.axis_size("depth"), lax.axis_size("lat")
    field = forcing[0]
    _, sources, width = field.shape
    count, parts, size, _ = blocks.shape[1:]
    rows = width // size
    top = layers - 1

    def sent(value, steps, place):
        pairs = [
            (k * lats + j, to_k * lats + place(j))
            for k, to_k in steps
            for j in range(lats)
            if 0 <= place(j) < lats
        ]
        return lax.ppermute(value, AXES, pairs)

    def far(j):
        return j + 1 if j % 2 else j - 1

    def near(j):
        return j - 1 if j % 2 else j + 1

    def same(j):
        return j

    def first(j):
        return j + 2 if j % 4 > 1 else j - 2

    def second(j):
        return j - 2 if j % 4 > 1 else j + 2

    rounds = [(k, k + 1) for k in range(top - 2)]
    rounds += [(top - 2, top), (top, top - 1)] + [(k, k - 2) for k in range(top - 1, 2, -2)] + [(2, 1), (1, 0)]
    wide, narrow = {step: [step] for step in rounds}, {step: [step] for step in rounds}
    if layers == 8:
        for shared in ([(0, 1), (3, 4)], [(1, 2), (4, 5)], [(2, 3), (7, 6)]):
            narrow |= {step: shared for step in shared}
        for shared in ([(5, 7), (4, 2)],):
            narrow |= {step: shared for step in shared}
            wide |= {step: shared for step in shared}

    def moved(value, k, to_k):
        step = narrow[k, to_k]
        return sent(value, [(k, to_k)], far), sent(value, step, near), sent(value, step, same)

    def moved_two(value, k, to_k):
        outer, inner = wide[k, to_k], narrow[k, to_k]
        return (
            sent(value, outer, first),
            sent(value, outer, far),
            sent(value, outer, second),
            sent(value, inner, near),
            sent(value, inner, same),
        )

    following = sent(field, [(k, k - 1) for k in range(1, layers)], same)
    beside = [(0, 0), (top, top)]
    field_far, field_near = sent(field, beside, far), sent(field, beside, near)

    left_is_far = lax.axis_index("lat") % 2 == 0
    cols = jnp.where(left_is_far, block_cols, 2 * rows - block_cols // rows * rows + block_cols % rows)
    matrix = jax.ShapeDtypeStruct((3 * width, parts * width), jnp.bfloat16)
    dense = pl.pallas_call(
        dense_kernel,
        out_shape=matrix,
        in_specs=[pl.BlockSpec(memory_space=pltpu.SMEM)] * 2 + vmem(1),
        out_specs=pl.BlockSpec(memory_space=pltpu.VMEM),
        scratch_shapes=[pltpu.VMEM((rows, 3 * rows, parts, size, size), jnp.float32)],
        compiler_params=PARAMS,
        name="dense",
    )(block_rows, cols, blocks[0])

    one = jax.ShapeDtypeStruct(field.shape, jnp.bfloat16)
    two = jax.ShapeDtypeStruct((2, *field.shape), jnp.bfloat16)

    def step(kernel, out_shape, layer, *operands, pairs=False):
        return pl.pallas_call(
            functools.partial(kernel, *layer),
            out_shape=out_shape,
            in_specs=vmem(len(operands)),
            out_specs=tuple(vmem(len(out_shape))),
            scratch_shapes=[pltpu.VMEM(two.shape, two.dtype)] if pairs else [],
            compiler_params=PARAMS,
            name=kernel.__name__,
        )(*operands)

    def hold(value, *others):
        return pl.pallas_call(
            hold_kernel,
            out_shape=one,
            in_specs=vmem(1) + [pl.BlockSpec(memory_space=pl.ANY)] * len(others),
            out_specs=pl.BlockSpec(memory_space=pltpu.VMEM),
            compiler_params=PARAMS,
            name="hold",
        )(value, *others)

    ups = [(k + 1, k) for k in range(2, top - 1, 2)]
    given = [*ups, (top - 1, top)]
    send = down = jnp.zeros(field.shape, jnp.bfloat16)
    window = (field_far, field_near, field)
    for layer in range(top - 1):
        if layer == 1:
            following = hold(following, other_same)
        if layer == 4:
            following = hold(following, other_far, other_near)
        send, down = step(down_kernel, (one, one), (layer,), following, *window, dense, down, send)
        if layer == 0:
            [copy] = step(later_kernel, (matrix,), ([k for k, _ in given],), dense, send)
            other_far, other_near, other_same = (sent(copy, given, place) for place in (far, near, same))
        if layer == top - 3:
            wait = sent(send, [(k, k + 2) for k in range(2, top - 2, 2)], same)
        if layer + 1 < top - 1:
            window = moved(send, layer, layer + 1)
    window = moved_two(send, top - 2, top)
    down, both = step(
        down_two_kernel, (one, two), (top,), *window, other_far, other_same, other_near, dense,
        field_far, field, field_near, down, pairs=True,
    )
    window = moved(both, top, top - 1)
    send, up, down = step(turn_kernel, (one,) * 3, (top - 1,), *window, dense, wait, down)
    back = jnp.zeros(field.shape, jnp.bfloat16)
    for layer in range(top - 3, 1, -2):
        window = moved_two(send, layer + 2, layer)
        send, up, back = step(
            up_two_kernel, (one,) * 3, (layer, layer > 2), *window, other_far, other_same, other_near, dense,
            down, wait, up, back, pairs=True,
        )
    returned = sent(back, [(to_k, k) for k, to_k in ups], same)
    [up] = step(up_kernel, (one,), (1,), *moved(send, 2, 1), dense, down, up)
    [up] = step(end_kernel, (one,), ([k for k, _ in ups],), up, returned)
    [up] = step(up_kernel, (one,), (0,), *moved(up, 1, 0), dense, down, up)
    return (down.reshape(forcing.shape), up.reshape(forcing.shape))


def solution(mesh):
    placed = (
        P("depth", None, None, "lat"),
        P("depth", "lat", None, None, None),
        P("depth", "lat"),
        P("depth", "lat"),
    )
    return jax.shard_map(
        local,
        mesh=mesh,
        in_specs=placed,
        out_specs=(P("depth", None, None, "lat"), P("depth", None, None, "lat")),
        check_vma=False,
    )
```

time: 250 us -> 118 us (0.47)
  starting transfers between devices: 207 us -> 55.6 us
  waiting for transfers between devices: 34.3 us -> 53.5 us
    ppermute x45 -> x47, starting transfers between devices: 207 us -> 55.6 us  [sent(): return lax.ppermute(value, AXES, pairs)]
    ppermute x45 -> x47, waiting for transfers between devices: 34.3 us -> 53.5 us  [sent(): return lax.ppermute(value, AXES, pairs)]
  transfers between devices with their start and end apart: 45 -> 47, of which waited for: 4 -> 5; matrix products, arithmetic and copies ran while one was open for 0% -> 0% of each run, Pallas kernels for 0% -> 1%
where the time goes in v3:
time: 118 us; the launch traced here: 117 us
  starting transfers between devices  55.6 us (47%)
  waiting for transfers between devices  53.5 us (45%)
  local copies, waits for them, and re-layouts  3.5 us (3%)
  Pallas kernels  2.95 us (2%)
  between operations  1.47 us (1%)
    ppermute x47, starting transfers between devices, sent(): return lax.ppermute(value, AXES, pairs)  55.6 us
    ppermute x47, waiting for transfers between devices, sent(): return lax.ppermute(value, AXES, pairs)  53.5 us
    unnamed x12, local copies, waits for them, and re-layouts  3.49 us
  transfers between devices with their start and end apart: 47, of which 5 were waited for; matrix products, arithmetic and copies ran while one was open for 0% of the time, Pallas kernels for 1%

profile of v3, /device:TPU:62, one launch (start us, length us, event | category | flops | bytes accessed | tf_op | source)
XLA Modules:
  0.0 117.0 jit_solution(3494043799902900736)
XLA Ops:
  0.6 1.3 %collective-permute-start = (bf16[2,16,256]{2,1,0:T(8,128)(2,1)}, bf16[2,16,256]{2,1,0:T(8,128)(2,1)S(1)}, u32[]{:S(2)}, u32[]{:S(2)}) collective-permute-start(bf16[2,16,256]{2,1,0:T(8,128)(2,1)} %bitcast.6), channel_id=1, source_target_pairs={{64,0},{65,1},{66,2},{67,3},{68,4},{69,5},{70,6},{71,7},{72,8},{73... | collective-permute-start | bytes 49160 | tf_op jit(solution)/shard_map/ppermute | solution.py:184
  1.9 10.0 %collective-permute-start.1 = (bf16[2,16,256]{2,1,0:T(8,128)(2,1)}, bf16[2,16,256]{2,1,0:T(8,128)(2,1)S(1)}, u32[]{:S(2)}, u32[]{:S(2)}) collective-permute-start(bf16[2,16,256]{2,1,0:T(8,128)(2,1)} %bitcast.7), channel_id=1, source_target_pairs={{1,2},{2,1},{3,4},{4,3},{5,6},{6,5},{7,8},{8,7},{9,10},{10,9},{11,... | collective-permute-start | bytes 49160 | tf_op jit(solution)/shard_map/ppermute | solution.py:184
  12.0 1.9 %collective-permute-start.2 = (bf16[2,16,256]{2,1,0:T(8,128)(2,1)}, bf16[2,16,256]{2,1,0:T(8,128)(2,1)S(1)}, u32[]{:S(2)}, u32[]{:S(2)}) collective-permute-start(bf16[2,16,256]{2,1,0:T(8,128)(2,1)} %bitcast.8), channel_id=1, source_target_pairs={{0,1},{1,0},{2,3},{3,2},{4,5},{5,4},{6,7},{7,6},{8,9},{9,8},{10,11... | collective-permute-start | bytes 49160 | tf_op jit(solution)/shard_map/ppermute | solution.py:184
  13.9 0.6 copy-done.5
  14.6 0.0 copy-start.4
  14.6 0.6 copy-done.4
  15.2 1.1 copy-done
  16.4 1.1 dense.1.dense_ref
  17.4 0.0 copy-start.3
  17.5 0.3 collective-permute-done.2.near_ref.field_near_ref
  17.8 0.3 copy-done.3
  18.2 0.2 down_kernel.6
  18.4 0.7 collective-permute-start.3
  19.2 0.7 collective-permute-start.4
  19.9 0.7 collective-permute-start.5
  20.6 1.3 %collective-permute-start.6 = (bf16[2,16,256]{2,1,0:T(8,128)(2,1)S(1)}, bf16[2,16,256]{2,1,0:T(8,128)(2,1)S(1)}, u32[]{:S(2)}, u32[]{:S(2)}) collective-permute-start(bf16[2,16,256]{2,1,0:T(8,128)(2,1)S(1)} %get-tuple-element.25._after.sent_ref), channel_id=1, source_target_pairs={{1,66},{2,65},{3,68},{4,67},{5,70},{6,69},{7,72},{8,71},{9,74},{10... | collective-permute-start | bytes 49160 | tf_op jit(solution)/shard_map/ppermute | solution.py:184
  21.9 1.3 %collective-permute-start.7 = (bf16[2,16,256]{2,1,0:T(8,128)(2,1)S(1)}, bf16[2,16,256]{2,1,0:T(8,128)(2,1)S(1)}, u32[]{:S(2)}, u32[]{:S(2)}) collective-permute-start(bf16[2,16,256]{2,1,0:T(8,128)(2,1)S(1)} %get-tuple-element.25._after.sent_ref), channel_id=1, source_target_pairs={{0,65},{1,64},{2,67},{3,66},{4,69},{5,68},{6,71},{7,70},{8,73},{9,... | collective-permute-start | bytes 49160 | tf_op jit(solution)/shard_map/ppermute | solution.py:184
  23.2 1.3 %collective-permute-start.8 = (bf16[2,16,256]{2,1,0:T(8,128)(2,1)S(1)}, bf16[2,16,256]{2,1,0:T(8,128)(2,1)S(1)}, u32[]{:S(2)}, u32[]{:S(2)}) collective-permute-start(bf16[2,16,256]{2,1,0:T(8,128)(2,1)S(1)} %get-tuple-element.25._after.sent_ref), channel_id=1, source_target_pairs={{0,64},{1,65},{2,66},{3,67},{4,68},{5,69},{6,70},{7,71},{8,72},{9,... | collective-permute-start | bytes 49160 | tf_op jit(solution)/shard_map/ppermute | solution.py:184
  24.5 0.1 collective-permute-done.7.near_ref
  24.6 0.7 collective-permute-done.8.same_ref
  25.3 0.7 collective-permute-start.9
  26.0 0.7 collective-permute-start.10
  26.7 0.7 collective-permute-start.11
  27.4 0.7 collective-permute-start.12
  28.1 0.7 collective-permute-start.13
  28.7 0.7 collective-permute-start.14
  29.5 0.7 collective-permute-start.15
  30.1 6.8 %collective-permute-start.16 = (bf16[2,16,256]{2,1,0:T(8,128)(2,1)S(1)}, bf16[2,16,256]{2,1,0:T(8,128)(2,1)S(1)}, u32[]{:S(2)}, u32[]{:S(2)}) collective-permute-start(bf16[2,16,256]{2,1,0:T(8,128)(2,1)S(1)} %get-tuple-element.31.sent_ref), channel_id=1, source_target_pairs={{0,65},{1,64},{2,67},{3,66},{4,69},{5,68},{6,71},{7,70},{8,73},{9,... | collective-permute-start | bytes 49160 | tf_op jit(solution)/shard_map/ppermute | solution.py:184
  36.9 3.7 %collective-permute-start.17 = (bf16[2,16,256]{2,1,0:T(8,128)(2,1)S(1)}, bf16[2,16,256]{2,1,0:T(8,128)(2,1)S(1)}, u32[]{:S(2)}, u32[]{:S(2)}) collective-permute-start(bf16[2,16,256]{2,1,0:T(8,128)(2,1)S(1)} %get-tuple-element.31.sent_ref), channel_id=1, source_target_pairs={{0,64},{1,65},{2,66},{3,67},{4,68},{5,69},{6,70},{7,71},{8,72},{9,... | collective-permute-start | bytes 49160 | tf_op jit(solution)/shard_map/ppermute | solution.py:184
  40.7 0.8 collective-permute-done.17.same_ref
  41.5 0.7 collective-permute-start.18
  42.1 0.7 collective-permute-start.19
  42.8 0.7 collective-permute-start.20
  43.5 0.7 collective-permute-start.21
  44.2 0.7 collective-permute-start.22
  44.9 0.7 collective-permute-start.23
  45.6 0.7 collective-permute-start.24
  46.2 0.7 collective-permute-start.25
  47.0 0.7 collective-permute-start.26
  47.6 0.7 collective-permute-start.27
  48.3 0.7 collective-permute-start.28
  49.0 0.7 collective-permute-start.29
  49.7 0.6 turn_kernel.1
  50.3 0.7 collective-permute-start.30
  51.0 0.7 collective-permute-start.31
  51.7 0.7 collective-permute-start.32
  52.3 0.7 collective-permute-start.33
  53.0 0.7 collective-permute-start.34
  53.7 0.0 copy-start.1
  53.7 0.7 copy-done.1
  54.4 0.8 collective-permute-start.35
  55.2 0.7 collective-permute-start.36
  55.9 0.7 collective-permute-start.37
  56.6 0.7 collective-permute-start.38
  57.2 0.7 collective-permute-start.39
  58.0 0.7 collective-permute-start.40
  58.7 0.7 collective-permute-start.41
  59.3 0.7 collective-permute-start.42
  60.0 0.7 collective-permute-start.43
  60.8 1.3 %collective-permute-start.44 = (bf16[2,16,256]{2,1,0:T(8,128)(2,1)S(1)}, bf16[2,16,256]{2,1,0:T(8,128)(2,1)S(1)}, u32[]{:S(2)}, u32[]{:S(2)}) collective-permute-start(bf16[2,16,256]{2,1,0:T(8,128)(2,1)S(1)} %end_kernel.1.kept_ref), channel_id=1, source_target_pairs={{65,2},{66,1},{67,4},{68,3},{69,6},{70,5},{71,8},{72,7},{73,10},{7... | collective-permute-start | bytes 49160 | tf_op jit(solution)/shard_map/ppermute | solution.py:184
  62.1 1.3 %collective-permute-start.45 = (bf16[2,16,256]{2,1,0:T(8,128)(2,1)S(1)}, bf16[2,16,256]{2,1,0:T(8,128)(2,1)S(1)}, u32[]{:S(2)}, u32[]{:S(2)}) collective-permute-start(bf16[2,16,256]{2,1,0:T(8,128)(2,1)S(1)} %end_kernel.1.kept_ref), channel_id=1, source_target_pairs={{64,1},{65,0},{66,3},{67,2},{68,5},{69,4},{70,7},{71,6},{72,9},{73... | collective-permute-start | bytes 49160 | tf_op jit(solution)/shard_map/ppermute | solution.py:184
  63.4 1.3 %collective-permute-start.46 = (bf16[2,16,256]{2,1,0:T(8,128)(2,1)S(1)}, bf16[2,16,256]{2,1,0:T(8,128)(2,1)S(1)}, u32[]{:S(2)}, u32[]{:S(2)}) collective-permute-start(bf16[2,16,256]{2,1,0:T(8,128)(2,1)S(1)} %end_kernel.1.kept_ref), channel_id=1, source_target_pairs={{64,0},{65,1},{66,2},{67,3},{68,4},{69,5},{70,6},{71,7},{72,8},{73... | collective-permute-start | bytes 49160 | tf_op jit(solution)/shard_map/ppermute | solution.py:184
  64.7 51.4 %collective-permute-done.44.far_ref = bf16[2,16,256]{2,1,0:T(8,128)(2,1)S(1)} collective-permute-done((bf16[2,16,256]{2,1,0:T(8,128)(2,1)S(1)}, bf16[2,16,256]{2,1,0:T(8,128)(2,1)S(1)}, u32[]{:S(2)}, u32[]{:S(2)}) %collective-permute-start.44) | collective-permute-done | bytes 16416 | tf_op jit(solution)/shard_map/ppermute | solution.py:184
  116.1 0.9 up_kernel.3
  (61 shorter events, 0.3 us)
Async XLA Ops:
  0.6 16.8 %collective-permute-start = (bf16[2,16,256]{2,1,0:T(8,128)(2,1)}, bf16[2,16,256]{2,1,0:T(8,128)(2,1)S(1)}, u32[]{:S(2)}, u32[]{:S(2)}) collective-permute-start(bf16[2,16,256]{2,1,0:T(8,128)(2,1)} %bitcast.6), channel_id=1, source_target_pairs={{64,0},{65,1},{66,2},{67,3},{68,4},{69,5},{70,6},{71,7},{72,8},{73... | collective-permute-start | bytes 49160 | tf_op jit(solution)/shard_map/ppermute | solution.py:184
  1.9 15.5 %collective-permute-start.1 = (bf16[2,16,256]{2,1,0:T(8,128)(2,1)}, bf16[2,16,256]{2,1,0:T(8,128)(2,1)S(1)}, u32[]{:S(2)}, u32[]{:S(2)}) collective-permute-start(bf16[2,16,256]{2,1,0:T(8,128)(2,1)} %bitcast.7), channel_id=1, source_target_pairs={{1,2},{2,1},{3,4},{4,3},{5,6},{6,5},{7,8},{8,7},{9,10},{10,9},{11,... | collective-permute-start | bytes 49160 | tf_op jit(solution)/shard_map/ppermute | solution.py:184
  12.0 5.8 %collective-permute-start.2 = (bf16[2,16,256]{2,1,0:T(8,128)(2,1)}, bf16[2,16,256]{2,1,0:T(8,128)(2,1)S(1)}, u32[]{:S(2)}, u32[]{:S(2)}) collective-permute-start(bf16[2,16,256]{2,1,0:T(8,128)(2,1)} %bitcast.8), channel_id=1, source_target_pairs={{0,1},{1,0},{2,3},{3,2},{4,5},{5,4},{6,7},{7,6},{8,9},{9,8},{10,11... | collective-permute-start | bytes 49160 | tf_op jit(solution)/shard_map/ppermute | solution.py:184
  13.9 0.7 copy-start.5
  14.6 0.7 copy-start.4
  15.2 1.1 copy-start
  17.4 0.7 copy-start.3
  18.4 4.8 %collective-permute-start.3 = (bf16[768,512]{1,0:T(8,128)(2,1)S(1)}, bf16[768,512]{1,0:T(8,128)(2,1)S(1)}, u32[]{:S(2)}, u32[]{:S(2)}) collective-permute-start(bf16[768,512]{1,0:T(8,128)(2,1)S(1)} %later_kernel.1), channel_id=1, source_target_pairs={{192,128},{193,129},{194,130},{195,131},{196,132},{197,133},{198,1... | collective-permute-start | bytes 2359304 | tf_op jit(solution)/shard_map/ppermute | solution.py:184
  19.2 21.5 %collective-permute-start.4 = (bf16[768,512]{1,0:T(8,128)(2,1)S(1)}, bf16[768,512]{1,0:T(8,128)(2,1)S(1)}, u32[]{:S(2)}, u32[]{:S(2)}) collective-permute-start(bf16[768,512]{1,0:T(8,128)(2,1)S(1)} %later_kernel.1), channel_id=1, source_target_pairs={{193,130},{194,129},{195,132},{196,131},{197,134},{198,133},{199,1... | collective-permute-start | bytes 2359304 | tf_op jit(solution)/shard_map/ppermute | solution.py:184
  19.9 20.8 %collective-permute-start.5 = (bf16[768,512]{1,0:T(8,128)(2,1)S(1)}, bf16[768,512]{1,0:T(8,128)(2,1)S(1)}, u32[]{:S(2)}, u32[]{:S(2)}) collective-permute-start(bf16[768,512]{1,0:T(8,128)(2,1)S(1)} %later_kernel.1), channel_id=1, source_target_pairs={{192,129},{193,128},{194,131},{195,130},{196,133},{197,132},{198,1... | collective-permute-start | bytes 2359304 | tf_op jit(solution)/shard_map/ppermute | solution.py:184
  20.6 3.9 %collective-permute-start.6 = (bf16[2,16,256]{2,1,0:T(8,128)(2,1)S(1)}, bf16[2,16,256]{2,1,0:T(8,128)(2,1)S(1)}, u32[]{:S(2)}, u32[]{:S(2)}) collective-permute-start(bf16[2,16,256]{2,1,0:T(8,128)(2,1)S(1)} %get-tuple-element.25._after.sent_ref), channel_id=1, source_target_pairs={{1,66},{2,65},{3,68},{4,67},{5,70},{6,69},{7,72},{8,71},{9,74},{10... | collective-permute-start | bytes 49160 | tf_op jit(solution)/shard_map/ppermute | solution.py:184
  21.9 2.7 %collective-permute-start.7 = (bf16[2,16,256]{2,1,0:T(8,128)(2,1)S(1)}, bf16[2,16,256]{2,1,0:T(8,128)(2,1)S(1)}, u32[]{:S(2)}, u32[]{:S(2)}) collective-permute-start(bf16[2,16,256]{2,1,0:T(8,128)(2,1)S(1)} %get-tuple-element.25._after.sent_ref), channel_id=1, source_target_pairs={{0,65},{1,64},{2,67},{3,66},{4,69},{5,68},{6,71},{7,70},{8,73},{9,... | collective-permute-start | bytes 49160 | tf_op jit(solution)/shard_map/ppermute | solution.py:184
  23.2 2.1 %collective-permute-start.8 = (bf16[2,16,256]{2,1,0:T(8,128)(2,1)S(1)}, bf16[2,16,256]{2,1,0:T(8,128)(2,1)S(1)}, u32[]{:S(2)}, u32[]{:S(2)}) collective-permute-start(bf16[2,16,256]{2,1,0:T(8,128)(2,1)S(1)} %get-tuple-element.25._after.sent_ref), channel_id=1, source_target_pairs={{0,64},{1,65},{2,66},{3,67},{4,68},{5,69},{6,70},{7,71},{8,72},{9,... | collective-permute-start | bytes 49160 | tf_op jit(solution)/shard_map/ppermute | solution.py:184
  25.3 2.0 %collective-permute-start.9 = (bf16[2,16,256]{2,1,0:T(8,128)(2,1)S(1)}, bf16[2,16,256]{2,1,0:T(8,128)(2,1)S(1)}, u32[]{:S(2)}, u32[]{:S(2)}) collective-permute-start(bf16[2,16,256]{2,1,0:T(8,128)(2,1)S(1)} %get-tuple-element.27.sent_ref), channel_id=1, source_target_pairs={{65,130},{66,129},{67,132},{68,131},{69,134},{70,133},{71,136},{72... | collective-permute-start | bytes 49160 | tf_op jit(solution)/shard_map/ppermute | solution.py:184
  26.0 1.4 %collective-permute-start.10 = (bf16[2,16,256]{2,1,0:T(8,128)(2,1)S(1)}, bf16[2,16,256]{2,1,0:T(8,128)(2,1)S(1)}, u32[]{:S(2)}, u32[]{:S(2)}) collective-permute-start(bf16[2,16,256]{2,1,0:T(8,128)(2,1)S(1)} %get-tuple-element.27.sent_ref), channel_id=1, source_target_pairs={{64,129},{65,128},{66,131},{67,130},{68,133},{69,132},{70,135},{71... | collective-permute-start | bytes 49160 | tf_op jit(solution)/shard_map/ppermute | solution.py:184
  26.7 0.7 collective-permute-start.11
  27.4 2.0 %collective-permute-start.12 = (bf16[2,16,256]{2,1,0:T(8,128)(2,1)S(1)}, bf16[2,16,256]{2,1,0:T(8,128)(2,1)S(1)}, u32[]{:S(2)}, u32[]{:S(2)}) collective-permute-start(bf16[2,16,256]{2,1,0:T(8,128)(2,1)S(1)} %get-tuple-element.29.sent_ref), channel_id=1, source_target_pairs={{129,194},{130,193},{131,196},{132,195},{133,198},{134,197},{135,2... | collective-permute-start | bytes 49160 | tf_op jit(solution)/shard_map/ppermute | solution.py:184
  28.1 1.4 %collective-permute-start.13 = (bf16[2,16,256]{2,1,0:T(8,128)(2,1)S(1)}, bf16[2,16,256]{2,1,0:T(8,128)(2,1)S(1)}, u32[]{:S(2)}, u32[]{:S(2)}) collective-permute-start(bf16[2,16,256]{2,1,0:T(8,128)(2,1)S(1)} %get-tuple-element.29.sent_ref), channel_id=1, source_target_pairs={{128,193},{129,192},{130,195},{131,194},{132,197},{133,196},{134,1... | collective-permute-start | bytes 49160 | tf_op jit(solution)/shard_map/ppermute | solution.py:184
  28.7 0.7 collective-permute-start.14
  29.5 11.2 %collective-permute-start.15 = (bf16[2,16,256]{2,1,0:T(8,128)(2,1)S(1)}, bf16[2,16,256]{2,1,0:T(8,128)(2,1)S(1)}, u32[]{:S(2)}, u32[]{:S(2)}) collective-permute-start(bf16[2,16,256]{2,1,0:T(8,128)(2,1)S(1)} %get-tuple-element.31.sent_ref), channel_id=1, source_target_pairs={{193,258},{194,257},{195,260},{196,259},{197,262},{198,261},{199,2... | collective-permute-start | bytes 49160 | tf_op jit(solution)/shard_map/ppermute | solution.py:184
  30.1 10.6 %collective-permute-start.16 = (bf16[2,16,256]{2,1,0:T(8,128)(2,1)S(1)}, bf16[2,16,256]{2,1,0:T(8,128)(2,1)S(1)}, u32[]{:S(2)}, u32[]{:S(2)}) collective-permute-start(bf16[2,16,256]{2,1,0:T(8,128)(2,1)S(1)} %get-tuple-element.31.sent_ref), channel_id=1, source_target_pairs={{0,65},{1,64},{2,67},{3,66},{4,69},{5,68},{6,71},{7,70},{8,73},{9,... | collective-permute-start | bytes 49160 | tf_op jit(solution)/shard_map/ppermute | solution.py:184
  36.9 4.6 %collective-permute-start.17 = (bf16[2,16,256]{2,1,0:T(8,128)(2,1)S(1)}, bf16[2,16,256]{2,1,0:T(8,128)(2,1)S(1)}, u32[]{:S(2)}, u32[]{:S(2)}) collective-permute-start(bf16[2,16,256]{2,1,0:T(8,128)(2,1)S(1)} %get-tuple-element.31.sent_ref), channel_id=1, source_target_pairs={{0,64},{1,65},{2,66},{3,67},{4,68},{5,69},{6,70},{7,71},{8,72},{9,... | collective-permute-start | bytes 49160 | tf_op jit(solution)/shard_map/ppermute | solution.py:184
  41.5 2.0 %collective-permute-start.18 = (bf16[2,16,256]{2,1,0:T(8,128)(2,1)S(1)}, bf16[2,16,256]{2,1,0:T(8,128)(2,1)S(1)}, u32[]{:S(2)}, u32[]{:S(2)}) collective-permute-start(bf16[2,16,256]{2,1,0:T(8,128)(2,1)S(1)} %get-tuple-element.33.sent_ref), channel_id=1, source_target_pairs={{257,322},{258,321},{259,324},{260,323},{261,326},{262,325},{263,3... | collective-permute-start | bytes 49160 | tf_op jit(solution)/shard_map/ppermute | solution.py:184
  42.1 1.4 %collective-permute-start.19 = (bf16[2,16,256]{2,1,0:T(8,128)(2,1)S(1)}, bf16[2,16,256]{2,1,0:T(8,128)(2,1)S(1)}, u32[]{:S(2)}, u32[]{:S(2)}) collective-permute-start(bf16[2,16,256]{2,1,0:T(8,128)(2,1)S(1)} %get-tuple-element.33.sent_ref), channel_id=1, source_target_pairs={{64,129},{65,128},{66,131},{67,130},{68,133},{69,132},{70,135},{71... | collective-permute-start | bytes 49160 | tf_op jit(solution)/shard_map/ppermute | solution.py:184
  42.8 0.7 collective-permute-start.20
  43.5 3.4 %collective-permute-start.21 = (bf16[2,16,256]{2,1,0:T(8,128)(2,1)S(1)}, bf16[2,16,256]{2,1,0:T(8,128)(2,1)S(1)}, u32[]{:S(2)}, u32[]{:S(2)}) collective-permute-start(bf16[2,16,256]{2,1,0:T(8,128)(2,1)S(1)} %get-tuple-element.35), channel_id=1, source_target_pairs={{322,452},{323,453},{324,450},{325,451},{326,456},{327,457},{328,4... | collective-permute-start | bytes 49160 | tf_op jit(solution)/shard_map/ppermute | solution.py:184
  44.2 2.7 %collective-permute-start.22 = (bf16[2,16,256]{2,1,0:T(8,128)(2,1)S(1)}, bf16[2,16,256]{2,1,0:T(8,128)(2,1)S(1)}, u32[]{:S(2)}, u32[]{:S(2)}) collective-permute-start(bf16[2,16,256]{2,1,0:T(8,128)(2,1)S(1)} %get-tuple-element.35), channel_id=1, source_target_pairs={{321,450},{322,449},{323,452},{324,451},{325,454},{326,453},{327,4... | collective-permute-start | bytes 49160 | tf_op jit(solution)/shard_map/ppermute | solution.py:184
  44.9 2.0 %collective-permute-start.23 = (bf16[2,16,256]{2,1,0:T(8,128)(2,1)S(1)}, bf16[2,16,256]{2,1,0:T(8,128)(2,1)S(1)}, u32[]{:S(2)}, u32[]{:S(2)}) collective-permute-start(bf16[2,16,256]{2,1,0:T(8,128)(2,1)S(1)} %get-tuple-element.35), channel_id=1, source_target_pairs={{320,450},{321,451},{322,448},{323,449},{324,454},{325,455},{326,4... | collective-permute-start | bytes 49160 | tf_op jit(solution)/shard_map/ppermute | solution.py:184
  45.6 1.4 %collective-permute-start.24 = (bf16[2,16,256]{2,1,0:T(8,128)(2,1)S(1)}, bf16[2,16,256]{2,1,0:T(8,128)(2,1)S(1)}, u32[]{:S(2)}, u32[]{:S(2)}) collective-permute-start(bf16[2,16,256]{2,1,0:T(8,128)(2,1)S(1)} %get-tuple-element.35), channel_id=1, source_target_pairs={{320,449},{321,448},{322,451},{323,450},{324,453},{325,452},{326,4... | collective-permute-start | bytes 49160 | tf_op jit(solution)/shard_map/ppermute | solution.py:184
  46.2 0.7 collective-permute-start.25
  47.0 2.7 %collective-permute-start.26 = (bf16[2,2,16,256]{3,2,1,0:T(8,128)(2,1)S(1)}, bf16[2,2,16,256]{3,2,1,0:T(8,128)(2,1)S(1)}, u32[]{:S(2)}, u32[]{:S(2)}) collective-permute-start(bf16[2,2,16,256]{3,2,1,0:T(8,128)(2,1)S(1)} %get-tuple-element.37), channel_id=1, source_target_pairs={{449,386},{450,385},{451,388},{452,387},{453,390},{454,389},{455,3... | collective-permute-start | bytes 98312 | tf_op jit(solution)/shard_map/ppermute | solution.py:184
  47.6 2.0 %collective-permute-start.27 = (bf16[2,2,16,256]{3,2,1,0:T(8,128)(2,1)S(1)}, bf16[2,2,16,256]{3,2,1,0:T(8,128)(2,1)S(1)}, u32[]{:S(2)}, u32[]{:S(2)}) collective-permute-start(bf16[2,2,16,256]{3,2,1,0:T(8,128)(2,1)S(1)} %get-tuple-element.37), channel_id=1, source_target_pairs={{128,193},{129,192},{130,195},{131,194},{132,197},{133,196},{134,1... | collective-permute-start | bytes 98312 | tf_op jit(solution)/shard_map/ppermute | solution.py:184
  48.3 1.4 %collective-permute-start.28 = (bf16[2,2,16,256]{3,2,1,0:T(8,128)(2,1)S(1)}, bf16[2,2,16,256]{3,2,1,0:T(8,128)(2,1)S(1)}, u32[]{:S(2)}, u32[]{:S(2)}) collective-permute-start(bf16[2,2,16,256]{3,2,1,0:T(8,128)(2,1)S(1)} %get-tuple-element.37), channel_id=1, source_target_pairs={{128,192},{129,193},{130,194},{131,195},{132,196},{133,197},{134,1... | collective-permute-start | bytes 98312 | tf_op jit(solution)/shard_map/ppermute | solution.py:184
  49.0 0.7 collective-permute-start.29
  50.3 3.3 %collective-permute-start.30 = (bf16[2,16,256]{2,1,0:T(8,128)(2,1)S(1)}, bf16[2,16,256]{2,1,0:T(8,128)(2,1)S(1)}, u32[]{:S(2)}, u32[]{:S(2)}) collective-permute-start(bf16[2,16,256]{2,1,0:T(8,128)(2,1)S(1)} %get-tuple-element.40), channel_id=1, source_target_pairs={{386,260},{387,261},{388,258},{389,259},{390,264},{391,265},{392,2... | collective-permute-start | bytes 49160 | tf_op jit(solution)/shard_map/ppermute | solution.py:184
  51.0 2.7 %collective-permute-start.31 = (bf16[2,16,256]{2,1,0:T(8,128)(2,1)S(1)}, bf16[2,16,256]{2,1,0:T(8,128)(2,1)S(1)}, u32[]{:S(2)}, u32[]{:S(2)}) collective-permute-start(bf16[2,16,256]{2,1,0:T(8,128)(2,1)S(1)} %get-tuple-element.40), channel_id=1, source_target_pairs={{385,258},{386,257},{387,260},{388,259},{389,262},{390,261},{391,2... | collective-permute-start | bytes 49160 | tf_op jit(solution)/shard_map/ppermute | solution.py:184
  51.7 2.0 %collective-permute-start.32 = (bf16[2,16,256]{2,1,0:T(8,128)(2,1)S(1)}, bf16[2,16,256]{2,1,0:T(8,128)(2,1)S(1)}, u32[]{:S(2)}, u32[]{:S(2)}) collective-permute-start(bf16[2,16,256]{2,1,0:T(8,128)(2,1)S(1)} %get-tuple-element.40), channel_id=1, source_target_pairs={{384,258},{385,259},{386,256},{387,257},{388,262},{389,263},{390,2... | collective-permute-start | bytes 49160 | tf_op jit(solution)/shard_map/ppermute | solution.py:184
  52.3 1.4 %collective-permute-start.33 = (bf16[2,16,256]{2,1,0:T(8,128)(2,1)S(1)}, bf16[2,16,256]{2,1,0:T(8,128)(2,1)S(1)}, u32[]{:S(2)}, u32[]{:S(2)}) collective-permute-start(bf16[2,16,256]{2,1,0:T(8,128)(2,1)S(1)} %get-tuple-element.40), channel_id=1, source_target_pairs={{384,257},{385,256},{386,259},{387,258},{388,261},{389,260},{390,2... | collective-permute-start | bytes 49160 | tf_op jit(solution)/shard_map/ppermute | solution.py:184
  53.0 0.7 collective-permute-start.34
  53.7 0.7 copy-start.1
  54.4 3.5 %copy-start.2 = (bf16[2,16,256]{2,1,0:T(8,128)(2,1)S(1)}, bf16[2,16,256]{2,1,0:T(8,128)(2,1)}, u32[]{:S(2)}) copy-start(bf16[2,16,256]{2,1,0:T(8,128)(2,1)} %get-tuple-element.39.down_ref) | copy-start | bytes 49156
  54.4 3.5 %collective-permute-start.35 = (bf16[2,16,256]{2,1,0:T(8,128)(2,1)S(1)}, bf16[2,16,256]{2,1,0:T(8,128)(2,1)S(1)}, u32[]{:S(2)}, u32[]{:S(2)}) collective-permute-start(bf16[2,16,256]{2,1,0:T(8,128)(2,1)S(1)} %get-tuple-element.42), channel_id=1, source_target_pairs={{322,452},{323,453},{324,450},{325,451},{326,456},{327,457},{328,4... | collective-permute-start | bytes 49160 | tf_op jit(solution)/shard_map/ppermute | solution.py:184
  55.2 2.7 %collective-permute-start.36 = (bf16[2,16,256]{2,1,0:T(8,128)(2,1)S(1)}, bf16[2,16,256]{2,1,0:T(8,128)(2,1)S(1)}, u32[]{:S(2)}, u32[]{:S(2)}) collective-permute-start(bf16[2,16,256]{2,1,0:T(8,128)(2,1)S(1)} %get-tuple-element.42), channel_id=1, source_target_pairs={{321,450},{322,449},{323,452},{324,451},{325,454},{326,453},{327,4... | collective-permute-start | bytes 49160 | tf_op jit(solution)/shard_map/ppermute | solution.py:184
  55.9 2.0 %collective-permute-start.37 = (bf16[2,16,256]{2,1,0:T(8,128)(2,1)S(1)}, bf16[2,16,256]{2,1,0:T(8,128)(2,1)S(1)}, u32[]{:S(2)}, u32[]{:S(2)}) collective-permute-start(bf16[2,16,256]{2,1,0:T(8,128)(2,1)S(1)} %get-tuple-element.42), channel_id=1, source_target_pairs={{320,450},{321,451},{322,448},{323,449},{324,454},{325,455},{326,4... | collective-permute-start | bytes 49160 | tf_op jit(solution)/shard_map/ppermute | solution.py:184
  56.6 1.4 %collective-permute-start.38 = (bf16[2,16,256]{2,1,0:T(8,128)(2,1)S(1)}, bf16[2,16,256]{2,1,0:T(8,128)(2,1)S(1)}, u32[]{:S(2)}, u32[]{:S(2)}) collective-permute-start(bf16[2,16,256]{2,1,0:T(8,128)(2,1)S(1)} %get-tuple-element.42), channel_id=1, source_target_pairs={{320,449},{321,448},{322,451},{323,450},{324,453},{325,452},{326,4... | collective-permute-start | bytes 49160 | tf_op jit(solution)/shard_map/ppermute | solution.py:184
  57.2 0.7 collective-permute-start.39
  58.0 2.7 %collective-permute-start.40 = (bf16[2,16,256]{2,1,0:T(8,128)(2,1)S(1)}, bf16[2,16,256]{2,1,0:T(8,128)(2,1)S(1)}, u32[]{:S(2)}, u32[]{:S(2)}) collective-permute-start(bf16[2,16,256]{2,1,0:T(8,128)(2,1)S(1)} %get-tuple-element.45), channel_id=1, source_target_pairs={{129,66},{130,65},{131,68},{132,67},{133,70},{134,69},{135,72},{13... | collective-permute-start | bytes 49160 | tf_op jit(solution)/shard_map/ppermute | solution.py:184
  58.7 2.0 %collective-permute-start.41 = (bf16[2,16,256]{2,1,0:T(8,128)(2,1)S(1)}, bf16[2,16,256]{2,1,0:T(8,128)(2,1)S(1)}, u32[]{:S(2)}, u32[]{:S(2)}) collective-permute-start(bf16[2,16,256]{2,1,0:T(8,128)(2,1)S(1)} %get-tuple-element.45), channel_id=1, source_target_pairs={{128,65},{129,64},{130,67},{131,66},{132,69},{133,68},{134,71},{13... | collective-permute-start | bytes 49160 | tf_op jit(solution)/shard_map/ppermute | solution.py:184
  59.3 1.4 %collective-permute-start.42 = (bf16[2,16,256]{2,1,0:T(8,128)(2,1)S(1)}, bf16[2,16,256]{2,1,0:T(8,128)(2,1)S(1)}, u32[]{:S(2)}, u32[]{:S(2)}) collective-permute-start(bf16[2,16,256]{2,1,0:T(8,128)(2,1)S(1)} %get-tuple-element.45), channel_id=1, source_target_pairs={{128,64},{129,65},{130,66},{131,67},{132,68},{133,69},{134,70},{13... | collective-permute-start | bytes 49160 | tf_op jit(solution)/shard_map/ppermute | solution.py:184
  60.0 0.7 collective-permute-start.43
  60.8 55.3 %collective-permute-start.44 = (bf16[2,16,256]{2,1,0:T(8,128)(2,1)S(1)}, bf16[2,16,256]{2,1,0:T(8,128)(2,1)S(1)}, u32[]{:S(2)}, u32[]{:S(2)}) collective-permute-start(bf16[2,16,256]{2,1,0:T(8,128)(2,1)S(1)} %end_kernel.1.kept_ref), channel_id=1, source_target_pairs={{65,2},{66,1},{67,4},{68,3},{69,6},{70,5},{71,8},{72,7},{73,10},{7... | collective-permute-start | bytes 49160 | tf_op jit(solution)/shard_map/ppermute | solution.py:184
  62.1 54.1 %collective-permute-start.45 = (bf16[2,16,256]{2,1,0:T(8,128)(2,1)S(1)}, bf16[2,16,256]{2,1,0:T(8,128)(2,1)S(1)}, u32[]{:S(2)}, u32[]{:S(2)}) collective-permute-start(bf16[2,16,256]{2,1,0:T(8,128)(2,1)S(1)} %end_kernel.1.kept_ref), channel_id=1, source_target_pairs={{64,1},{65,0},{66,3},{67,2},{68,5},{69,4},{70,7},{71,6},{72,9},{73... | collective-permute-start | bytes 49160 | tf_op jit(solution)/shard_map/ppermute | solution.py:184
  63.4 52.8 %collective-permute-start.46 = (bf16[2,16,256]{2,1,0:T(8,128)(2,1)S(1)}, bf16[2,16,256]{2,1,0:T(8,128)(2,1)S(1)}, u32[]{:S(2)}, u32[]{:S(2)}) collective-permute-start(bf16[2,16,256]{2,1,0:T(8,128)(2,1)S(1)} %end_kernel.1.kept_ref), channel_id=1, source_target_pairs={{64,0},{65,1},{66,2},{67,3},{68,4},{69,5},{70,6},{71,7},{72,8},{73... | collective-permute-start | bytes 49160 | tf_op jit(solution)/shard_map/ppermute | solution.py:184

commit v4 on v3

--- a/solution.py
+++ b/solution.py
@@ -98,9 +98,11 @@
 
 def down_two_kernel(
     layer, first_ref, far_ref, second_ref, near_ref, same_ref, other_far_ref, other_same_ref, other_near_ref,
-    dense_ref, field_far_ref, field_ref, field_near_ref, kept_ref, down_ref, both_ref, pairs_ref,
+    dense_ref, field_far_ref, field_ref, field_near_ref, next_ref, kept_ref, sent_ref,
+    send_ref, down_ref, wait_ref, both_ref, pairs_ref,
 ):
     down_ref[...] = kept_ref[...]
+    wait_ref[...] = sent_ref[...]
 
     @pl.when(lax.axis_index("depth") == layer)
     def _():
@@ -113,9 +115,10 @@
         window = [plus(field, trace) for field, trace in zip(fields, traces)]
         trace = applied(window, dense_ref).astype(jnp.bfloat16)
         down_ref[...] = trace
+        send_ref[...] = plus(next_ref[...], trace)
+        wait_ref[...] = window[1]
+        both_ref[0] = trace
         both_ref[1] = traces[1]
-
-    both_ref[0] = down_ref[...]
 
 
 def turn_kernel(layer, far_ref, near_ref, both_ref, dense_ref, wait_ref, kept_ref, send_ref, up_ref, down_ref):
@@ -132,11 +135,12 @@
 
 
 def up_two_kernel(
-    layer, waits, first_ref, far_ref, second_ref, near_ref, same_ref, other_far_ref, other_same_ref, other_near_ref,
-    dense_ref, down_ref, wait_ref, kept_ref, other_ref, send_ref, up_ref, back_ref, pairs_ref,
+    layer, lone, first_ref, far_ref, second_ref, near_ref, same_ref, other_far_ref, other_same_ref, other_near_ref,
+    dense_ref, down_ref, below_ref, wait_ref, kept_ref, other_ref, send_ref, up_ref, back_ref, trace_ref, pairs_ref,
 ):
     up_ref[...] = kept_ref[...]
     back_ref[...] = other_ref[...]
+    trace_ref[...] = down_ref[...]
 
     @pl.when(lax.axis_index("depth") == layer)
     def _():
@@ -144,9 +148,11 @@
         totals = three((first_ref, second_ref), far_ref, near_ref, same_ref, others, pairs_ref)
         window = [total.astype(jnp.bfloat16) for total in totals]
         back_ref[...] = window[1]
-        trace = plus(down_ref[...], applied(window, dense_ref))
+        below = down_ref[...] if lone else below_ref[...]
+        trace_ref[...] = below
+        trace = plus(below, applied(window, dense_ref))
         up_ref[...] = trace
-        send_ref[...] = plus(wait_ref[...], trace) if waits else trace
+        send_ref[...] = trace if lone else plus(wait_ref[...], trace)
 
 
 def end_kernel(layers, up_ref, returned_ref, out_ref):
@@ -172,7 +178,7 @@
     _, sources, width = field.shape
     count, parts, size, _ = blocks.shape[1:]
     rows = width // size
-    top = layers - 1
+    top, split = layers - 1, layers // 2 - 1
 
     def sent(value, steps, place):
         pairs = [
@@ -198,19 +204,18 @@
     def second(j):
         return j - 2 if j % 4 > 1 else j + 2
 
-    rounds = [(k, k + 1) for k in range(top - 2)]
-    rounds += [(top - 2, top), (top, top - 1)] + [(k, k - 2) for k in range(top - 1, 2, -2)] + [(2, 1), (1, 0)]
+    rounds = [(k, k + 1) for k in range(split)] + [(k, k + 2) for k in range(split, top, 2)]
+    rounds += [(top, top - 1)] + [(k, k - 2) for k in range(top - 1, 2, -2)] + [(2, 1), (1, 0)]
     wide, narrow = {step: [step] for step in rounds}, {step: [step] for step in rounds}
     if layers == 8:
-        for shared in ([(0, 1), (3, 4)], [(1, 2), (4, 5)], [(2, 3), (7, 6)]):
-            narrow |= {step: shared for step in shared}
-        for shared in ([(5, 7), (4, 2)],):
+        narrow |= {step: [(2, 3), (7, 6)] for step in ((2, 3), (7, 6))}
+        for shared in ([(5, 7), (4, 2)], [(3, 5), (6, 4)]):
             narrow |= {step: shared for step in shared}
             wide |= {step: shared for step in shared}
 
-    def moved(value, k, to_k):
+    def moved(value, k, to_k, halos=()):
         step = narrow[k, to_k]
-        return sent(value, [(k, to_k)], far), sent(value, step, near), sent(value, step, same)
+        return sent(value, [(k, to_k), *halos], far), sent(value, [*step, *halos], near), sent(value, step, same)
 
     def moved_two(value, k, to_k):
         outer, inner = wide[k, to_k], narrow[k, to_k]
@@ -223,8 +228,6 @@
         )
 
     following = sent(field, [(k, k - 1) for k in range(1, layers)], same)
-    beside = [(0, 0), (top, top)]
-    field_far, field_near = sent(field, beside, far), sent(field, beside, near)
 
     left_is_far = lax.axis_index("lat") % 2 == 0
     cols = jnp.where(left_is_far, block_cols, 2 * rows - block_cols // rows * rows + block_cols % rows)
@@ -264,35 +267,39 @@
         )(value, *others)
 
     ups = [(k + 1, k) for k in range(2, top - 1, 2)]
-    given = [*ups, (top - 1, top)]
-    send = down = jnp.zeros(field.shape, jnp.bfloat16)
-    window = (field_far, field_near, field)
-    for layer in range(top - 1):
+    downs = [(k, k + 1) for k in range(split + 1, top, 2)]
+    given = [*ups, *downs]
+    send, down = field, jnp.zeros(field.shape, jnp.bfloat16)
+    window = (sent(field, [(0, 0)], far), sent(field, [(0, 0)], near), field)
+    for layer in range(split + 1):
         if layer == 1:
             following = hold(following, other_same)
-        if layer == 4:
+        if layer == split:
             following = hold(following, other_far, other_near)
         send, down = step(down_kernel, (one, one), (layer,), following, *window, dense, down, send)
         if layer == 0:
             [copy] = step(later_kernel, (matrix,), ([k for k, _ in given],), dense, send)
             other_far, other_near, other_same = (sent(copy, given, place) for place in (far, near, same))
-        if layer == top - 3:
-            wait = sent(send, [(k, k + 2) for k in range(2, top - 2, 2)], same)
-        if layer + 1 < top - 1:
-            window = moved(send, layer, layer + 1)
-    window = moved_two(send, top - 2, top)
-    down, both = step(
-        down_two_kernel, (one, two), (top,), *window, other_far, other_same, other_near, dense,
-        field_far, field, field_near, down, pairs=True,
-    )
+        if layer < split:
+            window = moved(send, layer, layer + 1, [(k, k) for _, k in downs] if layer == 1 else ())
+        if layer == 1:
+            field_far, field_near, _ = window
+    for layer in range(split + 2, top + 1, 2):
+        window = moved_two(send, layer - 2, layer)
+        send, down, kept, both = step(
+            down_two_kernel, (one, one, one, two), (layer,), *window, other_far, other_same, other_near, dense,
+            field_far, field, field_near, following, down, send, pairs=True,
+        )
+        if layer < top:
+            wait, below = sent(kept, [(2, 4), (5, 6)], same), sent(both[1], [(5, 4)], same)
     window = moved(both, top, top - 1)
     send, up, down = step(turn_kernel, (one,) * 3, (top - 1,), *window, dense, wait, down)
     back = jnp.zeros(field.shape, jnp.bfloat16)
     for layer in range(top - 3, 1, -2):
         window = moved_two(send, layer + 2, layer)
-        send, up, back = step(
-            up_two_kernel, (one,) * 3, (layer, layer > 2), *window, other_far, other_same, other_near, dense,
-            down, wait, up, back, pairs=True,
+        send, up, back, down = step(
+            up_two_kernel, (one,) * 4, (layer, layer == 2), *window, other_far, other_same, other_near, dense,
+            down, below, wait, up, back, pairs=True,
         )
     returned = sent(back, [(to_k, k) for k, to_k in ups], same)
     [up] = step(up_kernel, (one,), (1,), *moved(send, 2, 1), dense, down, up)

time: 118 us -> 117 us (level)
  starting transfers between devices: 55.6 us -> 46.3 us
  waiting for transfers between devices: 53.5 us -> 61.4 us
    ppermute x47, starting transfers between devices: 55.6 us -> 46.3 us  [sent(): return lax.ppermute(value, AXES, pairs)]
    ppermute x47, waiting for transfers between devices: 53.5 us -> 61.4 us  [sent(): return lax.ppermute(value, AXES, pairs)]
    pallas_call x14 -> x13, Pallas kernels: 1.88 us -> 2.5 us  [step(): pl.pallas_call(functools.partial(kernel, *layer), out_shape=out_shape, in...]
  transfers between devices with their start and end apart: 47 -> 47, of which waited for: 5 -> 4; matrix products, arithmetic and copies ran while one was open for 0% -> 0% of each run, Pallas kernels for 1% -> 2%
where the time goes in v4:
time: 117 us; the launch traced here: 116 us
  waiting for transfers between devices  61.4 us (52%)
  starting transfers between devices  46.3 us (40%)
  Pallas kernels  3.57 us (3%)
  local copies, waits for them, and re-layouts  3.5 us (3%)
  between operations  1.47 us (1%)
    ppermute x47, waiting for transfers between devices, sent(): return lax.ppermute(value, AXES, pairs)  61.4 us
    ppermute x47, starting transfers between devices, sent(): return lax.ppermute(value, AXES, pairs)  46.3 us
    unnamed x12, local copies, waits for them, and re-layouts  3.49 us
    pallas_call x13, Pallas kernels, step(): pl.pallas_call(functools.partial(kernel, *layer), out_shape=out_shape, in...  2.5 us
  transfers between devices with their start and end apart: 47, of which 4 were waited for; matrix products, arithmetic and copies ran while one was open for 0% of the time, Pallas kernels for 2%

profile of v4, /device:TPU:62, one launch (start us, length us, event | category | flops | bytes accessed | tf_op | source)
XLA Modules:
  0.0 116.2 jit_solution(423806053316726428)
XLA Ops:
  0.6 1.3 %collective-permute-start = (bf16[2,16,256]{2,1,0:T(8,128)(2,1)}, bf16[2,16,256]{2,1,0:T(8,128)(2,1)S(1)}, u32[]{:S(2)}, u32[]{:S(2)}) collective-permute-start(bf16[2,16,256]{2,1,0:T(8,128)(2,1)} %bitcast.7), channel_id=1, source_target_pairs={{64,0},{65,1},{66,2},{67,3},{68,4},{69,5},{70,6},{71,7},{72,8},{73... | collective-permute-start | bytes 49160 | tf_op jit(solution)/shard_map/ppermute | solution.py:190
  1.9 10.0 %collective-permute-start.1 = (bf16[2,16,256]{2,1,0:T(8,128)(2,1)}, bf16[2,16,256]{2,1,0:T(8,128)(2,1)S(1)}, u32[]{:S(2)}, u32[]{:S(2)}) collective-permute-start(bf16[2,16,256]{2,1,0:T(8,128)(2,1)} %bitcast.8), channel_id=1, source_target_pairs={{1,2},{2,1},{3,4},{4,3},{5,6},{6,5},{7,8},{8,7},{9,10},{10,9},{11,... | collective-permute-start | bytes 49160 | tf_op jit(solution)/shard_map/ppermute | solution.py:190
  12.0 1.9 %collective-permute-start.2 = (bf16[2,16,256]{2,1,0:T(8,128)(2,1)}, bf16[2,16,256]{2,1,0:T(8,128)(2,1)S(1)}, u32[]{:S(2)}, u32[]{:S(2)}) collective-permute-start(bf16[2,16,256]{2,1,0:T(8,128)(2,1)} %bitcast.9), channel_id=1, source_target_pairs={{0,1},{1,0},{2,3},{3,2},{4,5},{5,4},{6,7},{7,6},{8,9},{9,8},{10,11... | collective-permute-start | bytes 49160 | tf_op jit(solution)/shard_map/ppermute | solution.py:190
  13.9 0.6 copy-done.5
  14.6 0.0 copy-start.4
  14.6 0.6 copy-done.4
  15.2 1.1 copy-done
  16.4 1.1 dense.1.dense_ref
  17.4 0.0 copy-start.1
  17.5 0.3 collective-permute-done.2.near_ref
  17.8 0.3 copy-done.1
  18.2 0.2 down_kernel.4
  18.4 0.7 collective-permute-start.3
  19.2 0.7 collective-permute-start.4
  19.9 0.7 collective-permute-start.5
  20.6 1.3 %collective-permute-start.6 = (bf16[2,16,256]{2,1,0:T(8,128)(2,1)S(1)}, bf16[2,16,256]{2,1,0:T(8,128)(2,1)S(1)}, u32[]{:S(2)}, u32[]{:S(2)}) collective-permute-start(bf16[2,16,256]{2,1,0:T(8,128)(2,1)S(1)} %get-tuple-element.27._after.sent_ref), channel_id=1, source_target_pairs={{1,66},{2,65},{3,68},{4,67},{5,70},{6,69},{7,72},{8,71},{9,74},{10... | collective-permute-start | bytes 49160 | tf_op jit(solution)/shard_map/ppermute | solution.py:190
  21.9 1.3 %collective-permute-start.7 = (bf16[2,16,256]{2,1,0:T(8,128)(2,1)S(1)}, bf16[2,16,256]{2,1,0:T(8,128)(2,1)S(1)}, u32[]{:S(2)}, u32[]{:S(2)}) collective-permute-start(bf16[2,16,256]{2,1,0:T(8,128)(2,1)S(1)} %get-tuple-element.27._after.sent_ref), channel_id=1, source_target_pairs={{0,65},{1,64},{2,67},{3,66},{4,69},{5,68},{6,71},{7,70},{8,73},{9,... | collective-permute-start | bytes 49160 | tf_op jit(solution)/shard_map/ppermute | solution.py:190
  23.2 1.3 %collective-permute-start.8 = (bf16[2,16,256]{2,1,0:T(8,128)(2,1)S(1)}, bf16[2,16,256]{2,1,0:T(8,128)(2,1)S(1)}, u32[]{:S(2)}, u32[]{:S(2)}) collective-permute-start(bf16[2,16,256]{2,1,0:T(8,128)(2,1)S(1)} %get-tuple-element.27._after.sent_ref), channel_id=1, source_target_pairs={{0,64},{1,65},{2,66},{3,67},{4,68},{5,69},{6,70},{7,71},{8,72},{9,... | collective-permute-start | bytes 49160 | tf_op jit(solution)/shard_map/ppermute | solution.py:190
  24.5 0.1 collective-permute-done.7.near_ref
  24.6 0.7 collective-permute-done.8.same_ref
  25.3 0.7 collective-permute-start.9
  26.0 0.7 collective-permute-start.10
  26.7 0.7 collective-permute-start.11
  27.4 0.7 collective-permute-start.12
  28.1 0.7 collective-permute-start.13
  28.7 0.7 collective-permute-start.14
  29.5 0.7 collective-permute-start.15
  30.2 0.7 collective-permute-start.16
  30.8 0.7 collective-permute-start.17
  31.5 0.7 collective-permute-start.18
  32.2 0.7 collective-permute-start.19
  32.9 0.7 collective-permute-start.20
  33.6 0.7 collective-permute-start.21
  34.3 0.7 collective-permute-start.22
  34.9 0.7 collective-permute-start.23
  35.6 0.7 collective-permute-start.24
  36.3 0.7 collective-permute-start.28
  37.0 0.6 down_two_kernel.3
  37.6 0.7 collective-permute-start.25
  38.3 0.7 collective-permute-start.26
  39.0 0.7 collective-permute-start.27
  39.6 0.7 collective-permute-start.34
  40.4 0.7 collective-permute-start.29
  41.0 0.7 collective-permute-start.30
  41.7 0.7 collective-permute-start.31
  42.4 0.7 collective-permute-start.32
  43.1 0.7 collective-permute-start.33
  43.8 0.7 collective-permute-start.35
  44.5 0.7 collective-permute-start.36
  45.2 0.7 collective-permute-start.37
  45.8 0.7 collective-permute-start.38
  46.5 0.7 collective-permute-start.39
  47.2 0.6 up_two_kernel.3
  47.8 0.7 collective-permute-start.40
  48.5 0.7 collective-permute-start.41
  49.2 0.7 collective-permute-start.42
  49.8 0.7 collective-permute-start.43
  50.5 0.0 copy-start.2
  50.6 0.7 copy-done.2
  51.3 1.3 %collective-permute-start.44 = (bf16[2,16,256]{2,1,0:T(8,128)(2,1)S(1)}, bf16[2,16,256]{2,1,0:T(8,128)(2,1)S(1)}, u32[]{:S(2)}, u32[]{:S(2)}) collective-permute-start(bf16[2,16,256]{2,1,0:T(8,128)(2,1)S(1)} %end_kernel.1.kept_ref), channel_id=1, source_target_pairs={{65,2},{66,1},{67,4},{68,3},{69,6},{70,5},{71,8},{72,7},{73,10},{7... | collective-permute-start | bytes 49160 | tf_op jit(solution)/shard_map/ppermute | solution.py:190
  52.6 1.3 %collective-permute-start.45 = (bf16[2,16,256]{2,1,0:T(8,128)(2,1)S(1)}, bf16[2,16,256]{2,1,0:T(8,128)(2,1)S(1)}, u32[]{:S(2)}, u32[]{:S(2)}) collective-permute-start(bf16[2,16,256]{2,1,0:T(8,128)(2,1)S(1)} %end_kernel.1.kept_ref), channel_id=1, source_target_pairs={{64,1},{65,0},{66,3},{67,2},{68,5},{69,4},{70,7},{71,6},{72,9},{73... | collective-permute-start | bytes 49160 | tf_op jit(solution)/shard_map/ppermute | solution.py:190
  53.9 1.3 %collective-permute-start.46 = (bf16[2,16,256]{2,1,0:T(8,128)(2,1)S(1)}, bf16[2,16,256]{2,1,0:T(8,128)(2,1)S(1)}, u32[]{:S(2)}, u32[]{:S(2)}) collective-permute-start(bf16[2,16,256]{2,1,0:T(8,128)(2,1)S(1)} %end_kernel.1.kept_ref), channel_id=1, source_target_pairs={{64,0},{65,1},{66,2},{67,3},{68,4},{69,5},{70,6},{71,7},{72,8},{73... | collective-permute-start | bytes 49160 | tf_op jit(solution)/shard_map/ppermute | solution.py:190
  55.2 60.1 %collective-permute-done.44.far_ref = bf16[2,16,256]{2,1,0:T(8,128)(2,1)S(1)} collective-permute-done((bf16[2,16,256]{2,1,0:T(8,128)(2,1)S(1)}, bf16[2,16,256]{2,1,0:T(8,128)(2,1)S(1)}, u32[]{:S(2)}, u32[]{:S(2)}) %collective-permute-start.44) | collective-permute-done | bytes 16416 | tf_op jit(solution)/shard_map/ppermute | solution.py:190
  115.3 0.9 up_kernel.3
  (61 shorter events, 0.3 us)
Async XLA Ops:
  0.6 16.8 %collective-permute-start = (bf16[2,16,256]{2,1,0:T(8,128)(2,1)}, bf16[2,16,256]{2,1,0:T(8,128)(2,1)S(1)}, u32[]{:S(2)}, u32[]{:S(2)}) collective-permute-start(bf16[2,16,256]{2,1,0:T(8,128)(2,1)} %bitcast.7), channel_id=1, source_target_pairs={{64,0},{65,1},{66,2},{67,3},{68,4},{69,5},{70,6},{71,7},{72,8},{73... | collective-permute-start | bytes 49160 | tf_op jit(solution)/shard_map/ppermute | solution.py:190
  1.9 15.5 %collective-permute-start.1 = (bf16[2,16,256]{2,1,0:T(8,128)(2,1)}, bf16[2,16,256]{2,1,0:T(8,128)(2,1)S(1)}, u32[]{:S(2)}, u32[]{:S(2)}) collective-permute-start(bf16[2,16,256]{2,1,0:T(8,128)(2,1)} %bitcast.8), channel_id=1, source_target_pairs={{1,2},{2,1},{3,4},{4,3},{5,6},{6,5},{7,8},{8,7},{9,10},{10,9},{11,... | collective-permute-start | bytes 49160 | tf_op jit(solution)/shard_map/ppermute | solution.py:190
  12.0 5.8 %collective-permute-start.2 = (bf16[2,16,256]{2,1,0:T(8,128)(2,1)}, bf16[2,16,256]{2,1,0:T(8,128)(2,1)S(1)}, u32[]{:S(2)}, u32[]{:S(2)}) collective-permute-start(bf16[2,16,256]{2,1,0:T(8,128)(2,1)} %bitcast.9), channel_id=1, source_target_pairs={{0,1},{1,0},{2,3},{3,2},{4,5},{5,4},{6,7},{7,6},{8,9},{9,8},{10,11... | collective-permute-start | bytes 49160 | tf_op jit(solution)/shard_map/ppermute | solution.py:190
  13.9 0.7 copy-start.5
  14.6 0.7 copy-start.4
  15.2 1.1 copy-start
  17.4 0.7 copy-start.1
  18.4 4.8 %collective-permute-start.3 = (bf16[768,512]{1,0:T(8,128)(2,1)S(1)}, bf16[768,512]{1,0:T(8,128)(2,1)S(1)}, u32[]{:S(2)}, u32[]{:S(2)}) collective-permute-start(bf16[768,512]{1,0:T(8,128)(2,1)S(1)} %later_kernel.1), channel_id=1, source_target_pairs={{192,128},{193,129},{194,130},{195,131},{196,132},{197,133},{198,1... | collective-permute-start | bytes 2359304 | tf_op jit(solution)/shard_map/ppermute | solution.py:190
  19.2 10.2 %collective-permute-start.4 = (bf16[768,512]{1,0:T(8,128)(2,1)S(1)}, bf16[768,512]{1,0:T(8,128)(2,1)S(1)}, u32[]{:S(2)}, u32[]{:S(2)}) collective-permute-start(bf16[768,512]{1,0:T(8,128)(2,1)S(1)} %later_kernel.1), channel_id=1, source_target_pairs={{193,130},{194,129},{195,132},{196,131},{197,134},{198,133},{199,1... | collective-permute-start | bytes 2359304 | tf_op jit(solution)/shard_map/ppermute | solution.py:190
  19.9 9.5 %collective-permute-start.5 = (bf16[768,512]{1,0:T(8,128)(2,1)S(1)}, bf16[768,512]{1,0:T(8,128)(2,1)S(1)}, u32[]{:S(2)}, u32[]{:S(2)}) collective-permute-start(bf16[768,512]{1,0:T(8,128)(2,1)S(1)} %later_kernel.1), channel_id=1, source_target_pairs={{192,129},{193,128},{194,131},{195,130},{196,133},{197,132},{198,1... | collective-permute-start | bytes 2359304 | tf_op jit(solution)/shard_map/ppermute | solution.py:190
  20.6 3.9 %collective-permute-start.6 = (bf16[2,16,256]{2,1,0:T(8,128)(2,1)S(1)}, bf16[2,16,256]{2,1,0:T(8,128)(2,1)S(1)}, u32[]{:S(2)}, u32[]{:S(2)}) collective-permute-start(bf16[2,16,256]{2,1,0:T(8,128)(2,1)S(1)} %get-tuple-element.27._after.sent_ref), channel_id=1, source_target_pairs={{1,66},{2,65},{3,68},{4,67},{5,70},{6,69},{7,72},{8,71},{9,74},{10... | collective-permute-start | bytes 49160 | tf_op jit(solution)/shard_map/ppermute | solution.py:190
  21.9 2.7 %collective-permute-start.7 = (bf16[2,16,256]{2,1,0:T(8,128)(2,1)S(1)}, bf16[2,16,256]{2,1,0:T(8,128)(2,1)S(1)}, u32[]{:S(2)}, u32[]{:S(2)}) collective-permute-start(bf16[2,16,256]{2,1,0:T(8,128)(2,1)S(1)} %get-tuple-element.27._after.sent_ref), channel_id=1, source_target_pairs={{0,65},{1,64},{2,67},{3,66},{4,69},{5,68},{6,71},{7,70},{8,73},{9,... | collective-permute-start | bytes 49160 | tf_op jit(solution)/shard_map/ppermute | solution.py:190
  23.2 2.1 %collective-permute-start.8 = (bf16[2,16,256]{2,1,0:T(8,128)(2,1)S(1)}, bf16[2,16,256]{2,1,0:T(8,128)(2,1)S(1)}, u32[]{:S(2)}, u32[]{:S(2)}) collective-permute-start(bf16[2,16,256]{2,1,0:T(8,128)(2,1)S(1)} %get-tuple-element.27._after.sent_ref), channel_id=1, source_target_pairs={{0,64},{1,65},{2,66},{3,67},{4,68},{5,69},{6,70},{7,71},{8,72},{9,... | collective-permute-start | bytes 49160 | tf_op jit(solution)/shard_map/ppermute | solution.py:190
  25.3 2.0 %collective-permute-start.9 = (bf16[2,16,256]{2,1,0:T(8,128)(2,1)S(1)}, bf16[2,16,256]{2,1,0:T(8,128)(2,1)S(1)}, u32[]{:S(2)}, u32[]{:S(2)}) collective-permute-start(bf16[2,16,256]{2,1,0:T(8,128)(2,1)S(1)} %get-tuple-element.29.sent_ref), channel_id=1, source_target_pairs={{65,130},{66,129},{67,132},{68,131},{69,134},{70,133},{71,136},{72... | collective-permute-start | bytes 49160 | tf_op jit(solution)/shard_map/ppermute | solution.py:190
  26.0 1.4 %collective-permute-start.10 = (bf16[2,16,256]{2,1,0:T(8,128)(2,1)S(1)}, bf16[2,16,256]{2,1,0:T(8,128)(2,1)S(1)}, u32[]{:S(2)}, u32[]{:S(2)}) collective-permute-start(bf16[2,16,256]{2,1,0:T(8,128)(2,1)S(1)} %get-tuple-element.29.sent_ref), channel_id=1, source_target_pairs={{64,129},{65,128},{66,131},{67,130},{68,133},{69,132},{70,135},{71... | collective-permute-start | bytes 49160 | tf_op jit(solution)/shard_map/ppermute | solution.py:190
  26.7 0.7 collective-permute-start.11
  27.4 2.0 %collective-permute-start.12 = (bf16[2,16,256]{2,1,0:T(8,128)(2,1)S(1)}, bf16[2,16,256]{2,1,0:T(8,128)(2,1)S(1)}, u32[]{:S(2)}, u32[]{:S(2)}) collective-permute-start(bf16[2,16,256]{2,1,0:T(8,128)(2,1)S(1)} %get-tuple-element.31.sent_ref), channel_id=1, source_target_pairs={{129,194},{130,193},{131,196},{132,195},{133,198},{134,197},{135,2... | collective-permute-start | bytes 49160 | tf_op jit(solution)/shard_map/ppermute | solution.py:190
  28.1 1.4 %collective-permute-start.13 = (bf16[2,16,256]{2,1,0:T(8,128)(2,1)S(1)}, bf16[2,16,256]{2,1,0:T(8,128)(2,1)S(1)}, u32[]{:S(2)}, u32[]{:S(2)}) collective-permute-start(bf16[2,16,256]{2,1,0:T(8,128)(2,1)S(1)} %get-tuple-element.31.sent_ref), channel_id=1, source_target_pairs={{128,193},{129,192},{130,195},{131,194},{132,197},{133,196},{134,1... | collective-permute-start | bytes 49160 | tf_op jit(solution)/shard_map/ppermute | solution.py:190
  28.7 0.7 collective-permute-start.14
  29.5 3.4 %collective-permute-start.15 = (bf16[2,16,256]{2,1,0:T(8,128)(2,1)S(1)}, bf16[2,16,256]{2,1,0:T(8,128)(2,1)S(1)}, u32[]{:S(2)}, u32[]{:S(2)}) collective-permute-start(bf16[2,16,256]{2,1,0:T(8,128)(2,1)S(1)} %get-tuple-element.33.sent_ref), channel_id=1, source_target_pairs={{194,324},{195,325},{196,322},{197,323},{198,328},{199,329},{200,3... | collective-permute-start | bytes 49160 | tf_op jit(solution)/shard_map/ppermute | solution.py:190
  30.2 2.7 %collective-permute-start.16 = (bf16[2,16,256]{2,1,0:T(8,128)(2,1)S(1)}, bf16[2,16,256]{2,1,0:T(8,128)(2,1)S(1)}, u32[]{:S(2)}, u32[]{:S(2)}) collective-permute-start(bf16[2,16,256]{2,1,0:T(8,128)(2,1)S(1)} %get-tuple-element.33.sent_ref), channel_id=1, source_target_pairs={{193,322},{194,321},{195,324},{196,323},{197,326},{198,325},{199,3... | collective-permute-start | bytes 49160 | tf_op jit(solution)/shard_map/ppermute | solution.py:190
  30.8 2.0 %collective-permute-start.17 = (bf16[2,16,256]{2,1,0:T(8,128)(2,1)S(1)}, bf16[2,16,256]{2,1,0:T(8,128)(2,1)S(1)}, u32[]{:S(2)}, u32[]{:S(2)}) collective-permute-start(bf16[2,16,256]{2,1,0:T(8,128)(2,1)S(1)} %get-tuple-element.33.sent_ref), channel_id=1, source_target_pairs={{192,322},{193,323},{194,320},{195,321},{196,326},{197,327},{198,3... | collective-permute-start | bytes 49160 | tf_op jit(solution)/shard_map/ppermute | solution.py:190
  31.5 1.4 %collective-permute-start.18 = (bf16[2,16,256]{2,1,0:T(8,128)(2,1)S(1)}, bf16[2,16,256]{2,1,0:T(8,128)(2,1)S(1)}, u32[]{:S(2)}, u32[]{:S(2)}) collective-permute-start(bf16[2,16,256]{2,1,0:T(8,128)(2,1)S(1)} %get-tuple-element.33.sent_ref), channel_id=1, source_target_pairs={{192,321},{193,320},{194,323},{195,322},{196,325},{197,324},{198,3... | collective-permute-start | bytes 49160 | tf_op jit(solution)/shard_map/ppermute | solution.py:190
  32.2 0.7 collective-permute-start.19
  32.9 3.4 %collective-permute-start.20 = (bf16[2,16,256]{2,1,0:T(8,128)(2,1)S(1)}, bf16[2,16,256]{2,1,0:T(8,128)(2,1)S(1)}, u32[]{:S(2)}, u32[]{:S(2)}) collective-permute-start(bf16[2,16,256]{2,1,0:T(8,128)(2,1)S(1)} %get-tuple-element.35.sent_ref), channel_id=1, source_target_pairs={{322,452},{323,453},{324,450},{325,451},{326,456},{327,457},{328,4... | collective-permute-start | bytes 49160 | tf_op jit(solution)/shard_map/ppermute | solution.py:190
  33.6 3.4 %collective-permute-start.21 = (bf16[2,16,256]{2,1,0:T(8,128)(2,1)S(1)}, bf16[2,16,256]{2,1,0:T(8,128)(2,1)S(1)}, u32[]{:S(2)}, u32[]{:S(2)}) collective-permute-start(bf16[2,16,256]{2,1,0:T(8,128)(2,1)S(1)} %get-tuple-element.35.sent_ref), channel_id=1, source_target_pairs={{321,450},{322,449},{323,452},{324,451},{325,454},{326,453},{327,4... | collective-permute-start | bytes 49160 | tf_op jit(solution)/shard_map/ppermute | solution.py:190
  34.3 2.7 %collective-permute-start.22 = (bf16[2,16,256]{2,1,0:T(8,128)(2,1)S(1)}, bf16[2,16,256]{2,1,0:T(8,128)(2,1)S(1)}, u32[]{:S(2)}, u32[]{:S(2)}) collective-permute-start(bf16[2,16,256]{2,1,0:T(8,128)(2,1)S(1)} %get-tuple-element.35.sent_ref), channel_id=1, source_target_pairs={{320,450},{321,451},{322,448},{323,449},{324,454},{325,455},{326,4... | collective-permute-start | bytes 49160 | tf_op jit(solution)/shard_map/ppermute | solution.py:190
  34.9 2.0 %collective-permute-start.23 = (bf16[2,16,256]{2,1,0:T(8,128)(2,1)S(1)}, bf16[2,16,256]{2,1,0:T(8,128)(2,1)S(1)}, u32[]{:S(2)}, u32[]{:S(2)}) collective-permute-start(bf16[2,16,256]{2,1,0:T(8,128)(2,1)S(1)} %get-tuple-element.35.sent_ref), channel_id=1, source_target_pairs={{320,449},{321,448},{322,451},{323,450},{324,453},{325,452},{326,4... | collective-permute-start | bytes 49160 | tf_op jit(solution)/shard_map/ppermute | solution.py:190
  35.6 1.4 %collective-permute-start.24 = (bf16[2,16,256]{2,1,0:T(8,128)(2,1)S(1)}, bf16[2,16,256]{2,1,0:T(8,128)(2,1)S(1)}, u32[]{:S(2)}, u32[]{:S(2)}) collective-permute-start(bf16[2,16,256]{2,1,0:T(8,128)(2,1)S(1)} %get-tuple-element.35.sent_ref), channel_id=1, source_target_pairs={{320,448},{321,449},{322,450},{323,451},{324,452},{325,453},{326,4... | collective-permute-start | bytes 49160 | tf_op jit(solution)/shard_map/ppermute | solution.py:190
  36.3 4.0 %collective-permute-start.28 = (bf16[2,16,256]{2,1,0:T(8,128)(2,1)S(1)}, bf16[2,16,256]{2,1,0:T(8,128)(2,1)S(1)}, u32[]{:S(2)}, u32[]{:S(2)}) collective-permute-start(bf16[2,16,256]{2,1,0:T(8,128)(2,1)S(1)} %get-tuple-element.38), channel_id=1, source_target_pairs={{128,256},{129,257},{130,258},{131,259},{132,260},{133,261},{134,2... | collective-permute-start | bytes 49160 | tf_op jit(solution)/shard_map/ppermute | solution.py:190
  37.6 2.7 %collective-permute-start.25 = (bf16[2,2,16,256]{3,2,1,0:T(8,128)(2,1)S(1)}, bf16[2,2,16,256]{3,2,1,0:T(8,128)(2,1)S(1)}, u32[]{:S(2)}, u32[]{:S(2)}) collective-permute-start(bf16[2,2,16,256]{3,2,1,0:T(8,128)(2,1)S(1)} %get-tuple-element.37), channel_id=1, source_target_pairs={{449,386},{450,385},{451,388},{452,387},{453,390},{454,389},{455,3... | collective-permute-start | bytes 98312 | tf_op jit(solution)/shard_map/ppermute | solution.py:190
  38.3 2.0 %collective-permute-start.26 = (bf16[2,2,16,256]{3,2,1,0:T(8,128)(2,1)S(1)}, bf16[2,2,16,256]{3,2,1,0:T(8,128)(2,1)S(1)}, u32[]{:S(2)}, u32[]{:S(2)}) collective-permute-start(bf16[2,2,16,256]{3,2,1,0:T(8,128)(2,1)S(1)} %get-tuple-element.37), channel_id=1, source_target_pairs={{128,193},{129,192},{130,195},{131,194},{132,197},{133,196},{134,1... | collective-permute-start | bytes 98312 | tf_op jit(solution)/shard_map/ppermute | solution.py:190
  39.0 1.4 %collective-permute-start.27 = (bf16[2,2,16,256]{3,2,1,0:T(8,128)(2,1)S(1)}, bf16[2,2,16,256]{3,2,1,0:T(8,128)(2,1)S(1)}, u32[]{:S(2)}, u32[]{:S(2)}) collective-permute-start(bf16[2,2,16,256]{3,2,1,0:T(8,128)(2,1)S(1)} %get-tuple-element.37), channel_id=1, source_target_pairs={{128,192},{129,193},{130,194},{131,195},{132,196},{133,197},{134,1... | collective-permute-start | bytes 98312 | tf_op jit(solution)/shard_map/ppermute | solution.py:190
  39.6 3.4 %collective-permute-start.34 = (bf16[2,16,256]{2,1,0:T(8,128)(2,1)S(1)}, bf16[2,16,256]{2,1,0:T(8,128)(2,1)S(1)}, u32[]{:S(2)}, u32[]{:S(2)}) collective-permute-start(bf16[2,16,256]{2,1,0:T(8,128)(2,1)S(1)} %slice_bitcast_fusion), channel_id=1, source_target_pairs={{320,256},{321,257},{322,258},{323,259},{324,260},{325,261},{326,2... | collective-permute-start | bytes 49160 | tf_op jit(solution)/shard_map/ppermute | solution.py:190
  40.4 3.4 %collective-permute-start.29 = (bf16[2,16,256]{2,1,0:T(8,128)(2,1)S(1)}, bf16[2,16,256]{2,1,0:T(8,128)(2,1)S(1)}, u32[]{:S(2)}, u32[]{:S(2)}) collective-permute-start(bf16[2,16,256]{2,1,0:T(8,128)(2,1)S(1)} %get-tuple-element.40), channel_id=1, source_target_pairs={{194,324},{195,325},{196,322},{197,323},{198,328},{199,329},{200,3... | collective-permute-start | bytes 49160 | tf_op jit(solution)/shard_map/ppermute | solution.py:190
  41.0 2.7 %collective-permute-start.30 = (bf16[2,16,256]{2,1,0:T(8,128)(2,1)S(1)}, bf16[2,16,256]{2,1,0:T(8,128)(2,1)S(1)}, u32[]{:S(2)}, u32[]{:S(2)}) collective-permute-start(bf16[2,16,256]{2,1,0:T(8,128)(2,1)S(1)} %get-tuple-element.40), channel_id=1, source_target_pairs={{193,322},{194,321},{195,324},{196,323},{197,326},{198,325},{199,3... | collective-permute-start | bytes 49160 | tf_op jit(solution)/shard_map/ppermute | solution.py:190
  41.7 2.0 %collective-permute-start.31 = (bf16[2,16,256]{2,1,0:T(8,128)(2,1)S(1)}, bf16[2,16,256]{2,1,0:T(8,128)(2,1)S(1)}, u32[]{:S(2)}, u32[]{:S(2)}) collective-permute-start(bf16[2,16,256]{2,1,0:T(8,128)(2,1)S(1)} %get-tuple-element.40), channel_id=1, source_target_pairs={{192,322},{193,323},{194,320},{195,321},{196,326},{197,327},{198,3... | collective-permute-start | bytes 49160 | tf_op jit(solution)/shard_map/ppermute | solution.py:190
  42.4 1.4 %collective-permute-start.32 = (bf16[2,16,256]{2,1,0:T(8,128)(2,1)S(1)}, bf16[2,16,256]{2,1,0:T(8,128)(2,1)S(1)}, u32[]{:S(2)}, u32[]{:S(2)}) collective-permute-start(bf16[2,16,256]{2,1,0:T(8,128)(2,1)S(1)} %get-tuple-element.40), channel_id=1, source_target_pairs={{192,321},{193,320},{194,323},{195,322},{196,325},{197,324},{198,3... | collective-permute-start | bytes 49160 | tf_op jit(solution)/shard_map/ppermute | solution.py:190
  43.1 0.7 collective-permute-start.33
  43.8 3.4 %collective-permute-start.35 = (bf16[2,16,256]{2,1,0:T(8,128)(2,1)S(1)}, bf16[2,16,256]{2,1,0:T(8,128)(2,1)S(1)}, u32[]{:S(2)}, u32[]{:S(2)}) collective-permute-start(bf16[2,16,256]{2,1,0:T(8,128)(2,1)S(1)} %get-tuple-element.44), channel_id=1, source_target_pairs={{322,452},{323,453},{324,450},{325,451},{326,456},{327,457},{328,4... | collective-permute-start | bytes 49160 | tf_op jit(solution)/shard_map/ppermute | solution.py:190
  44.5 2.7 %collective-permute-start.36 = (bf16[2,16,256]{2,1,0:T(8,128)(2,1)S(1)}, bf16[2,16,256]{2,1,0:T(8,128)(2,1)S(1)}, u32[]{:S(2)}, u32[]{:S(2)}) collective-permute-start(bf16[2,16,256]{2,1,0:T(8,128)(2,1)S(1)} %get-tuple-element.44), channel_id=1, source_target_pairs={{321,450},{322,449},{323,452},{324,451},{325,454},{326,453},{327,4... | collective-permute-start | bytes 49160 | tf_op jit(solution)/shard_map/ppermute | solution.py:190
  45.2 2.0 %collective-permute-start.37 = (bf16[2,16,256]{2,1,0:T(8,128)(2,1)S(1)}, bf16[2,16,256]{2,1,0:T(8,128)(2,1)S(1)}, u32[]{:S(2)}, u32[]{:S(2)}) collective-permute-start(bf16[2,16,256]{2,1,0:T(8,128)(2,1)S(1)} %get-tuple-element.44), channel_id=1, source_target_pairs={{320,450},{321,451},{322,448},{323,449},{324,454},{325,455},{326,4... | collective-permute-start | bytes 49160 | tf_op jit(solution)/shard_map/ppermute | solution.py:190
  45.8 1.4 %collective-permute-start.38 = (bf16[2,16,256]{2,1,0:T(8,128)(2,1)S(1)}, bf16[2,16,256]{2,1,0:T(8,128)(2,1)S(1)}, u32[]{:S(2)}, u32[]{:S(2)}) collective-permute-start(bf16[2,16,256]{2,1,0:T(8,128)(2,1)S(1)} %get-tuple-element.44), channel_id=1, source_target_pairs={{320,449},{321,448},{322,451},{323,450},{324,453},{325,452},{326,4... | collective-permute-start | bytes 49160 | tf_op jit(solution)/shard_map/ppermute | solution.py:190
  46.5 0.7 collective-permute-start.39
  47.8 2.7 %collective-permute-start.40 = (bf16[2,16,256]{2,1,0:T(8,128)(2,1)S(1)}, bf16[2,16,256]{2,1,0:T(8,128)(2,1)S(1)}, u32[]{:S(2)}, u32[]{:S(2)}) collective-permute-start(bf16[2,16,256]{2,1,0:T(8,128)(2,1)S(1)} %get-tuple-element.49), channel_id=1, source_target_pairs={{129,66},{130,65},{131,68},{132,67},{133,70},{134,69},{135,72},{13... | collective-permute-start | bytes 49160 | tf_op jit(solution)/shard_map/ppermute | solution.py:190
  48.5 2.0 %collective-permute-start.41 = (bf16[2,16,256]{2,1,0:T(8,128)(2,1)S(1)}, bf16[2,16,256]{2,1,0:T(8,128)(2,1)S(1)}, u32[]{:S(2)}, u32[]{:S(2)}) collective-permute-start(bf16[2,16,256]{2,1,0:T(8,128)(2,1)S(1)} %get-tuple-element.49), channel_id=1, source_target_pairs={{128,65},{129,64},{130,67},{131,66},{132,69},{133,68},{134,71},{13... | collective-permute-start | bytes 49160 | tf_op jit(solution)/shard_map/ppermute | solution.py:190
  49.2 1.4 %collective-permute-start.42 = (bf16[2,16,256]{2,1,0:T(8,128)(2,1)S(1)}, bf16[2,16,256]{2,1,0:T(8,128)(2,1)S(1)}, u32[]{:S(2)}, u32[]{:S(2)}) collective-permute-start(bf16[2,16,256]{2,1,0:T(8,128)(2,1)S(1)} %get-tuple-element.49), channel_id=1, source_target_pairs={{128,64},{129,65},{130,66},{131,67},{132,68},{133,69},{134,70},{13... | collective-permute-start | bytes 49160 | tf_op jit(solution)/shard_map/ppermute | solution.py:190
  49.8 1.4 %collective-permute-start.43 = (bf16[2,16,256]{2,1,0:T(8,128)(2,1)S(1)}, bf16[2,16,256]{2,1,0:T(8,128)(2,1)S(1)}, u32[]{:S(2)}, u32[]{:S(2)}) collective-permute-start(bf16[2,16,256]{2,1,0:T(8,128)(2,1)S(1)} %get-tuple-element.51), channel_id=1, source_target_pairs={{128,192},{129,193},{130,194},{131,195},{132,196},{133,197},{134,1... | collective-permute-start | bytes 49160 | tf_op jit(solution)/shard_map/ppermute | solution.py:190
  50.5 0.7 copy-start.2
  51.3 64.1 %copy-start.3 = (bf16[2,16,256]{2,1,0:T(8,128)(2,1)S(1)}, bf16[2,16,256]{2,1,0:T(8,128)(2,1)}, u32[]{:S(2)}) copy-start(bf16[2,16,256]{2,1,0:T(8,128)(2,1)} %get-tuple-element.48.down_ref) | copy-start | bytes 49156
  51.3 64.0 %collective-permute-start.44 = (bf16[2,16,256]{2,1,0:T(8,128)(2,1)S(1)}, bf16[2,16,256]{2,1,0:T(8,128)(2,1)S(1)}, u32[]{:S(2)}, u32[]{:S(2)}) collective-permute-start(bf16[2,16,256]{2,1,0:T(8,128)(2,1)S(1)} %end_kernel.1.kept_ref), channel_id=1, source_target_pairs={{65,2},{66,1},{67,4},{68,3},{69,6},{70,5},{71,8},{72,7},{73,10},{7... | collective-permute-start | bytes 49160 | tf_op jit(solution)/shard_map/ppermute | solution.py:190
  52.6 62.7 %collective-permute-start.45 = (bf16[2,16,256]{2,1,0:T(8,128)(2,1)S(1)}, bf16[2,16,256]{2,1,0:T(8,128)(2,1)S(1)}, u32[]{:S(2)}, u32[]{:S(2)}) collective-permute-start(bf16[2,16,256]{2,1,0:T(8,128)(2,1)S(1)} %end_kernel.1.kept_ref), channel_id=1, source_target_pairs={{64,1},{65,0},{66,3},{67,2},{68,5},{69,4},{70,7},{71,6},{72,9},{73... | collective-permute-start | bytes 49160 | tf_op jit(solution)/shard_map/ppermute | solution.py:190
  53.9 61.4 %collective-permute-start.46 = (bf16[2,16,256]{2,1,0:T(8,128)(2,1)S(1)}, bf16[2,16,256]{2,1,0:T(8,128)(2,1)S(1)}, u32[]{:S(2)}, u32[]{:S(2)}) collective-permute-start(bf16[2,16,256]{2,1,0:T(8,128)(2,1)S(1)} %end_kernel.1.kept_ref), channel_id=1, source_target_pairs={{64,0},{65,1},{66,2},{67,3},{68,4},{69,5},{70,6},{71,7},{72,8},{73... | collective-permute-start | bytes 49160 | tf_op jit(solution)/shard_map/ppermute | solution.py:190

commit v5 on v4

--- a/solution.py
+++ b/solution.py
@@ -30,12 +30,15 @@
     refs[-1][...] = field_ref[...]
 
 
-def later_kernel(layers, dense_ref, _after, copy_ref):
+def later_kernel(layers, dense_ref, next_ref, _after, load_ref):
     layer = lax.axis_index("depth")
+    depth, width = dense_ref.shape[0], next_ref.shape[2]
 
     @pl.when(functools.reduce(jnp.logical_or, [layer == k for k in layers]))
     def _():
-        copy_ref[...] = dense_ref[...]
+        load_ref[:depth] = dense_ref[...]
+        load_ref[depth:, :width] = next_ref[0]
+        load_ref[depth:, width:] = next_ref[1]
 
 
 def up_kernel(layer, far_ref, near_ref, same_ref, dense_ref, down_ref, kept_ref, up_ref):
@@ -50,7 +53,7 @@
 def applied(window, dense_ref):
     sources, width = window[0].shape[1:]
     flat = jnp.concatenate([part.reshape(2 * sources, width) for part in window], axis=1)
-    product = jnp.dot(flat, dense_ref[...], preferred_element_type=jnp.float32)
+    product = jnp.dot(flat, dense_ref[: flat.shape[1]], preferred_element_type=jnp.float32)
     by_real, by_imag = product[:, :width], product[:, width:]
     real = by_real[:sources] - by_imag[sources:]
     imag = by_real[sources:] + by_imag[:sources]
@@ -98,11 +101,12 @@
 
 def down_two_kernel(
     layer, first_ref, far_ref, second_ref, near_ref, same_ref, other_far_ref, other_same_ref, other_near_ref,
-    dense_ref, field_far_ref, field_ref, field_near_ref, next_ref, kept_ref, sent_ref,
-    send_ref, down_ref, wait_ref, both_ref, pairs_ref,
+    dense_ref, field_ref, next_ref, kept_ref, sent_ref, down_ref, both_ref, *rest,
 ):
+    *more_refs, pairs_ref = rest
     down_ref[...] = kept_ref[...]
-    wait_ref[...] = sent_ref[...]
+    for ref in more_refs[1:]:
+        ref[...] = sent_ref[...]
 
     @pl.when(lax.axis_index("depth") == layer)
     def _():
@@ -111,12 +115,18 @@
             total.astype(jnp.bfloat16)
             for total in three((first_ref, second_ref), far_ref, near_ref, same_ref, others, pairs_ref)
         ]
-        fields = (field_far_ref[...], field_ref[...], field_near_ref[...])
+        depth, width = dense_ref.shape[0], field_ref.shape[2]
+        beside = [
+            jnp.stack([ref[depth:, :width], ref[depth:, width:]]) for ref in (other_far_ref, other_near_ref)
+        ]
+        fields = (beside[0], field_ref[...], beside[1])
         window = [plus(field, trace) for field, trace in zip(fields, traces)]
         trace = applied(window, dense_ref).astype(jnp.bfloat16)
         down_ref[...] = trace
-        send_ref[...] = plus(next_ref[...], trace)
-        wait_ref[...] = window[1]
+        if more_refs:
+            send_ref, wait_ref = more_refs
+            send_ref[...] = plus(next_ref[...], trace)
+            wait_ref[...] = window[1]
         both_ref[0] = trace
         both_ref[1] = traces[1]
 
@@ -136,11 +146,10 @@
 
 def up_two_kernel(
     layer, lone, first_ref, far_ref, second_ref, near_ref, same_ref, other_far_ref, other_same_ref, other_near_ref,
-    dense_ref, down_ref, below_ref, wait_ref, kept_ref, other_ref, send_ref, up_ref, back_ref, trace_ref, pairs_ref,
+    dense_ref, down_ref, below_ref, wait_ref, kept_ref, other_ref, send_ref, up_ref, back_ref, pairs_ref,
 ):
     up_ref[...] = kept_ref[...]
     back_ref[...] = other_ref[...]
-    trace_ref[...] = down_ref[...]
 
     @pl.when(lax.axis_index("depth") == layer)
     def _():
@@ -149,23 +158,33 @@
         window = [total.astype(jnp.bfloat16) for total in totals]
         back_ref[...] = window[1]
         below = down_ref[...] if lone else below_ref[...]
-        trace_ref[...] = below
         trace = plus(below, applied(window, dense_ref))
         up_ref[...] = trace
         send_ref[...] = trace if lone else plus(wait_ref[...], trace)
 
 
-def end_kernel(layers, up_ref, returned_ref, out_ref):
+def chosen_kernel(layers, up_ref, returned_ref, out_ref):
     layer = lax.axis_index("depth")
-    elsewhere = functools.reduce(jnp.logical_or, [layer == k for k in layers])
-
-    @pl.when(elsewhere)
+    out_ref[...] = up_ref[...]
+
+    @pl.when(functools.reduce(jnp.logical_or, [layer == k for k in layers]))
     def _():
         out_ref[...] = returned_ref[...]
 
-    @pl.when(jnp.logical_not(elsewhere))
-    def _():
-        out_ref[...] = up_ref[...]
+
+def last_kernel(passed, far_ref, near_ref, same_ref, dense_ref, down_ref, below_ref, kept_ref, up_out_ref, down_out_ref):
+    layer = lax.axis_index("depth")
+    up_out_ref[...] = kept_ref[...]
+    down_out_ref[...] = down_ref[...]
+
+    @pl.when(layer == passed)
+    def _():
+        down_out_ref[...] = below_ref[...]
+
+    @pl.when(layer == 0)
+    def _():
+        window = (far_ref[...], same_ref[...], near_ref[...])
+        up_out_ref[...] = plus(down_ref[...], applied(window, dense_ref))
 
 
 def vmem(count):
@@ -213,9 +232,9 @@
             narrow |= {step: shared for step in shared}
             wide |= {step: shared for step in shared}
 
-    def moved(value, k, to_k, halos=()):
+    def moved(value, k, to_k):
         step = narrow[k, to_k]
-        return sent(value, [(k, to_k), *halos], far), sent(value, [*step, *halos], near), sent(value, step, same)
+        return sent(value, [(k, to_k)], far), sent(value, step, near), sent(value, step, same)
 
     def moved_two(value, k, to_k):
         outer, inner = wide[k, to_k], narrow[k, to_k]
@@ -232,6 +251,7 @@
     left_is_far = lax.axis_index("lat") % 2 == 0
     cols = jnp.where(left_is_far, block_cols, 2 * rows - block_cols // rows * rows + block_cols % rows)
     matrix = jax.ShapeDtypeStruct((3 * width, parts * width), jnp.bfloat16)
+    payload = jax.ShapeDtypeStruct((3 * width + sources, parts * width), jnp.bfloat16)
     dense = pl.pallas_call(
         dense_kernel,
         out_shape=matrix,
@@ -277,34 +297,33 @@
         if layer == split:
             following = hold(following, other_far, other_near)
         send, down = step(down_kernel, (one, one), (layer,), following, *window, dense, down, send)
+        if layer < split:
+            window = moved(send, layer, layer + 1)
         if layer == 0:
-            [copy] = step(later_kernel, (matrix,), ([k for k, _ in given],), dense, send)
-            other_far, other_near, other_same = (sent(copy, given, place) for place in (far, near, same))
-        if layer < split:
-            window = moved(send, layer, layer + 1, [(k, k) for _, k in downs] if layer == 1 else ())
-        if layer == 1:
-            field_far, field_near, _ = window
+            [load] = step(later_kernel, (payload,), ([k for k, _ in given],), dense, following, send)
+            other_far, other_near, other_same = (sent(load, given, place) for place in (far, near, same))
     for layer in range(split + 2, top + 1, 2):
         window = moved_two(send, layer - 2, layer)
-        send, down, kept, both = step(
-            down_two_kernel, (one, one, one, two), (layer,), *window, other_far, other_same, other_near, dense,
-            field_far, field, field_near, following, down, send, pairs=True,
+        down, both, *more = step(
+            down_two_kernel, (one, two, one, one)[: 4 if layer < top else 2], (layer,), *window,
+            other_far, other_same, other_near, dense, field, following, down, send, pairs=True,
         )
         if layer < top:
+            send, kept = more
             wait, below = sent(kept, [(2, 4), (5, 6)], same), sent(both[1], [(5, 4)], same)
     window = moved(both, top, top - 1)
     send, up, down = step(turn_kernel, (one,) * 3, (top - 1,), *window, dense, wait, down)
     back = jnp.zeros(field.shape, jnp.bfloat16)
     for layer in range(top - 3, 1, -2):
         window = moved_two(send, layer + 2, layer)
-        send, up, back, down = step(
-            up_two_kernel, (one,) * 4, (layer, layer == 2), *window, other_far, other_same, other_near, dense,
+        send, up, back = step(
+            up_two_kernel, (one,) * 3, (layer, layer == 2), *window, other_far, other_same, other_near, dense,
             down, below, wait, up, back, pairs=True,
         )
     returned = sent(back, [(to_k, k) for k, to_k in ups], same)
     [up] = step(up_kernel, (one,), (1,), *moved(send, 2, 1), dense, down, up)
-    [up] = step(end_kernel, (one,), ([k for k, _ in ups],), up, returned)
-    [up] = step(up_kernel, (one,), (0,), *moved(up, 1, 0), dense, down, up)
+    [up] = step(chosen_kernel, (one,), ([k for k, _ in ups],), up, returned)
+    up, down = step(last_kernel, (one, one), (split + 1,), *moved(up, 1, 0), dense, down, below, up)
     return (down.reshape(forcing.shape), up.reshape(forcing.shape))
 
 

time: 117 us -> 115 us (0.983)
  Pallas kernels: 3.57 us -> 2.37 us
    pallas_call x13, Pallas kernels: 2.5 us -> 1.3 us  [step(): pl.pallas_call(functools.partial(kernel, *layer), out_shape=out_shape, in...]
    unnamed x12 -> x8, local copies, waits for them, and re-layouts: 3.49 us -> 2.78 us
  transfers between devices with their start and end apart: 47 -> 47, of which waited for: 4 -> 4; matrix products, arithmetic and copies ran while one was open for 0% -> 0% of each run, Pallas kernels for 2% -> 1%
where the time goes in v5:
time: 115 us; the launch traced here: 114 us
  waiting for transfers between devices  60.7 us (53%)
  starting transfers between devices  46.3 us (40%)
  local copies, waits for them, and re-layouts  2.78 us (2%)
  Pallas kernels  2.37 us (2%)
  between operations  1.48 us (1%)
    ppermute x47, waiting for transfers between devices, sent(): return lax.ppermute(value, AXES, pairs)  60.7 us
    ppermute x47, starting transfers between devices, sent(): return lax.ppermute(value, AXES, pairs)  46.3 us
    unnamed x8, local copies, waits for them, and re-layouts  2.78 us
  transfers between devices with their start and end apart: 47, of which 4 were waited for; matrix products, arithmetic and copies ran while one was open for 0% of the time, Pallas kernels for 1%

profile of v5, /device:TPU:62, one launch (start us, length us, event | category | flops | bytes accessed | tf_op | source)
XLA Modules:
  0.0 113.7 jit_solution(13494846569609251279)
XLA Ops:
  0.6 1.3 %collective-permute-start = (bf16[2,16,256]{2,1,0:T(8,128)(2,1)}, bf16[2,16,256]{2,1,0:T(8,128)(2,1)S(1)}, u32[]{:S(2)}, u32[]{:S(2)}) collective-permute-start(bf16[2,16,256]{2,1,0:T(8,128)(2,1)} %bitcast.7), channel_id=1, source_target_pairs={{64,0},{65,1},{66,2},{67,3},{68,4},{69,5},{70,6},{71,7},{72,8},{73... | collective-permute-start | bytes 49160 | tf_op jit(solution)/shard_map/ppermute | solution.py:209
  1.9 10.0 %collective-permute-start.1 = (bf16[2,16,256]{2,1,0:T(8,128)(2,1)}, bf16[2,16,256]{2,1,0:T(8,128)(2,1)S(1)}, u32[]{:S(2)}, u32[]{:S(2)}) collective-permute-start(bf16[2,16,256]{2,1,0:T(8,128)(2,1)} %bitcast.8), channel_id=1, source_target_pairs={{1,2},{2,1},{3,4},{4,3},{5,6},{6,5},{7,8},{8,7},{9,10},{10,9},{11,... | collective-permute-start | bytes 49160 | tf_op jit(solution)/shard_map/ppermute | solution.py:209
  12.0 1.9 %collective-permute-start.2 = (bf16[2,16,256]{2,1,0:T(8,128)(2,1)}, bf16[2,16,256]{2,1,0:T(8,128)(2,1)S(1)}, u32[]{:S(2)}, u32[]{:S(2)}) collective-permute-start(bf16[2,16,256]{2,1,0:T(8,128)(2,1)} %bitcast.9), channel_id=1, source_target_pairs={{0,1},{1,0},{2,3},{3,2},{4,5},{5,4},{6,7},{7,6},{8,9},{9,8},{10,11... | collective-permute-start | bytes 49160 | tf_op jit(solution)/shard_map/ppermute | solution.py:209
  13.9 0.6 copy-done.3
  14.6 0.0 copy-start.2
  14.6 0.6 copy-done.2
  15.2 1.1 copy-done
  16.4 1.1 dense.1.dense_ref
  17.4 0.0 copy-start.1
  17.5 0.3 collective-permute-done.2.near_ref
  17.8 0.3 copy-done.1
  18.2 0.2 down_kernel.4
  18.4 0.7 collective-permute-start.3
  19.2 0.7 collective-permute-start.4
  19.9 0.7 collective-permute-start.5
  20.6 1.3 %collective-permute-start.6 = (bf16[2,16,256]{2,1,0:T(8,128)(2,1)S(1)}, bf16[2,16,256]{2,1,0:T(8,128)(2,1)S(1)}, u32[]{:S(2)}, u32[]{:S(2)}) collective-permute-start(bf16[2,16,256]{2,1,0:T(8,128)(2,1)S(1)} %get-tuple-element.27._after.sent_ref), channel_id=1, source_target_pairs={{1,66},{2,65},{3,68},{4,67},{5,70},{6,69},{7,72},{8,71},{9,74},{10... | collective-permute-start | bytes 49160 | tf_op jit(solution)/shard_map/ppermute | solution.py:209
  21.9 1.3 %collective-permute-start.7 = (bf16[2,16,256]{2,1,0:T(8,128)(2,1)S(1)}, bf16[2,16,256]{2,1,0:T(8,128)(2,1)S(1)}, u32[]{:S(2)}, u32[]{:S(2)}) collective-permute-start(bf16[2,16,256]{2,1,0:T(8,128)(2,1)S(1)} %get-tuple-element.27._after.sent_ref), channel_id=1, source_target_pairs={{0,65},{1,64},{2,67},{3,66},{4,69},{5,68},{6,71},{7,70},{8,73},{9,... | collective-permute-start | bytes 49160 | tf_op jit(solution)/shard_map/ppermute | solution.py:209
  23.2 0.0 collective-permute-done.3.refs_0_.other_same_ref
  23.2 1.3 %collective-permute-start.8 = (bf16[2,16,256]{2,1,0:T(8,128)(2,1)S(1)}, bf16[2,16,256]{2,1,0:T(8,128)(2,1)S(1)}, u32[]{:S(2)}, u32[]{:S(2)}) collective-permute-start(bf16[2,16,256]{2,1,0:T(8,128)(2,1)S(1)} %get-tuple-element.27._after.sent_ref), channel_id=1, source_target_pairs={{0,64},{1,65},{2,66},{3,67},{4,68},{5,69},{6,70},{7,71},{8,72},{9,... | collective-permute-start | bytes 49160 | tf_op jit(solution)/shard_map/ppermute | solution.py:209
  24.5 0.0 collective-permute-done.6.far_ref
  24.5 0.1 collective-permute-done.7.near_ref
  24.6 0.7 collective-permute-done.8.same_ref
  25.3 0.7 collective-permute-start.9
  26.0 0.7 collective-permute-start.10
  26.7 0.7 collective-permute-start.11
  27.3 0.0 collective-permute-done.9.far_ref
  27.3 0.0 collective-permute-done.10.near_ref
  27.4 0.7 collective-permute-start.12
  28.1 0.7 collective-permute-start.13
  28.7 0.7 collective-permute-start.14
  29.5 0.7 collective-permute-start.15
  30.2 0.7 collective-permute-start.16
  30.8 0.7 collective-permute-start.17
  31.5 0.7 collective-permute-start.18
  32.2 0.7 collective-permute-start.19
  32.9 0.7 collective-permute-start.20
  33.6 0.7 collective-permute-start.21
  34.3 0.7 collective-permute-start.22
  34.9 0.7 collective-permute-start.23
  35.6 0.7 collective-permute-start.24
  36.3 0.7 collective-permute-start.28
  37.0 0.7 collective-permute-start.25
  37.7 0.7 collective-permute-start.26
  38.4 0.7 collective-permute-start.27
  39.0 0.7 collective-permute-start.34
  39.8 0.7 collective-permute-start.29
  40.5 0.7 collective-permute-start.30
  41.1 0.7 collective-permute-start.31
  41.8 0.7 collective-permute-start.32
  42.5 0.7 collective-permute-start.33
  43.2 0.7 collective-permute-start.35
  43.9 0.7 collective-permute-start.36
  44.6 0.7 collective-permute-start.37
  45.2 0.7 collective-permute-start.38
  45.9 0.7 collective-permute-start.39
  46.7 0.7 collective-permute-start.40
  47.3 0.7 collective-permute-start.41
  48.0 0.7 collective-permute-start.42
  48.7 0.7 collective-permute-start.43
  49.4 1.3 %collective-permute-start.44 = (bf16[2,16,256]{2,1,0:T(8,128)(2,1)S(1)}, bf16[2,16,256]{2,1,0:T(8,128)(2,1)S(1)}, u32[]{:S(2)}, u32[]{:S(2)}) collective-permute-start(bf16[2,16,256]{2,1,0:T(8,128)(2,1)S(1)} %chosen_kernel.1.kept_ref), channel_id=1, source_target_pairs={{65,2},{66,1},{67,4},{68,3},{69,6},{70,5},{71,8},{72,7},{73,10},{7... | collective-permute-start | bytes 49160 | tf_op jit(solution)/shard_map/ppermute | solution.py:209
  50.7 1.3 %collective-permute-start.45 = (bf16[2,16,256]{2,1,0:T(8,128)(2,1)S(1)}, bf16[2,16,256]{2,1,0:T(8,128)(2,1)S(1)}, u32[]{:S(2)}, u32[]{:S(2)}) collective-permute-start(bf16[2,16,256]{2,1,0:T(8,128)(2,1)S(1)} %chosen_kernel.1.kept_ref), channel_id=1, source_target_pairs={{64,1},{65,0},{66,3},{67,2},{68,5},{69,4},{70,7},{71,6},{72,9},{73... | collective-permute-start | bytes 49160 | tf_op jit(solution)/shard_map/ppermute | solution.py:209
  52.0 1.3 %collective-permute-start.46 = (bf16[2,16,256]{2,1,0:T(8,128)(2,1)S(1)}, bf16[2,16,256]{2,1,0:T(8,128)(2,1)S(1)}, u32[]{:S(2)}, u32[]{:S(2)}) collective-permute-start(bf16[2,16,256]{2,1,0:T(8,128)(2,1)S(1)} %chosen_kernel.1.kept_ref), channel_id=1, source_target_pairs={{64,0},{65,1},{66,2},{67,3},{68,4},{69,5},{70,6},{71,7},{72,8},{73... | collective-permute-start | bytes 49160 | tf_op jit(solution)/shard_map/ppermute | solution.py:209
  53.3 59.5 %collective-permute-done.44.far_ref = bf16[2,16,256]{2,1,0:T(8,128)(2,1)S(1)} collective-permute-done((bf16[2,16,256]{2,1,0:T(8,128)(2,1)S(1)}, bf16[2,16,256]{2,1,0:T(8,128)(2,1)S(1)}, u32[]{:S(2)}, u32[]{:S(2)}) %collective-permute-start.44) | collective-permute-done | bytes 16416 | tf_op jit(solution)/shard_map/ppermute | solution.py:209
  112.8 0.9 last_kernel.1
  (57 shorter events, 0.3 us)
Async XLA Ops:
  0.6 16.8 %collective-permute-start = (bf16[2,16,256]{2,1,0:T(8,128)(2,1)}, bf16[2,16,256]{2,1,0:T(8,128)(2,1)S(1)}, u32[]{:S(2)}, u32[]{:S(2)}) collective-permute-start(bf16[2,16,256]{2,1,0:T(8,128)(2,1)} %bitcast.7), channel_id=1, source_target_pairs={{64,0},{65,1},{66,2},{67,3},{68,4},{69,5},{70,6},{71,7},{72,8},{73... | collective-permute-start | bytes 49160 | tf_op jit(solution)/shard_map/ppermute | solution.py:209
  1.9 15.5 %collective-permute-start.1 = (bf16[2,16,256]{2,1,0:T(8,128)(2,1)}, bf16[2,16,256]{2,1,0:T(8,128)(2,1)S(1)}, u32[]{:S(2)}, u32[]{:S(2)}) collective-permute-start(bf16[2,16,256]{2,1,0:T(8,128)(2,1)} %bitcast.8), channel_id=1, source_target_pairs={{1,2},{2,1},{3,4},{4,3},{5,6},{6,5},{7,8},{8,7},{9,10},{10,9},{11,... | collective-permute-start | bytes 49160 | tf_op jit(solution)/shard_map/ppermute | solution.py:209
  12.0 5.8 %collective-permute-start.2 = (bf16[2,16,256]{2,1,0:T(8,128)(2,1)}, bf16[2,16,256]{2,1,0:T(8,128)(2,1)S(1)}, u32[]{:S(2)}, u32[]{:S(2)}) collective-permute-start(bf16[2,16,256]{2,1,0:T(8,128)(2,1)} %bitcast.9), channel_id=1, source_target_pairs={{0,1},{1,0},{2,3},{3,2},{4,5},{5,4},{6,7},{7,6},{8,9},{9,8},{10,11... | collective-permute-start | bytes 49160 | tf_op jit(solution)/shard_map/ppermute | solution.py:209
  13.9 0.7 copy-start.3
  14.6 0.7 copy-start.2
  15.2 1.1 copy-start
  17.4 0.7 copy-start.1
  18.4 4.8 %collective-permute-start.3 = (bf16[784,512]{1,0:T(8,128)(2,1)S(1)}, bf16[784,512]{1,0:T(8,128)(2,1)S(1)}, u32[]{:S(2)}, u32[]{:S(2)}) collective-permute-start(bf16[784,512]{1,0:T(8,128)(2,1)S(1)} %later_kernel.1), channel_id=1, source_target_pairs={{192,128},{193,129},{194,130},{195,131},{196,132},{197,133},{198,1... | collective-permute-start | bytes 2408456 | tf_op jit(solution)/shard_map/ppermute | solution.py:209
  19.2 10.2 %collective-permute-start.4 = (bf16[784,512]{1,0:T(8,128)(2,1)S(1)}, bf16[784,512]{1,0:T(8,128)(2,1)S(1)}, u32[]{:S(2)}, u32[]{:S(2)}) collective-permute-start(bf16[784,512]{1,0:T(8,128)(2,1)S(1)} %later_kernel.1), channel_id=1, source_target_pairs={{193,130},{194,129},{195,132},{196,131},{197,134},{198,133},{199,1... | collective-permute-start | bytes 2408456 | tf_op jit(solution)/shard_map/ppermute | solution.py:209
  19.9 9.5 %collective-permute-start.5 = (bf16[784,512]{1,0:T(8,128)(2,1)S(1)}, bf16[784,512]{1,0:T(8,128)(2,1)S(1)}, u32[]{:S(2)}, u32[]{:S(2)}) collective-permute-start(bf16[784,512]{1,0:T(8,128)(2,1)S(1)} %later_kernel.1), channel_id=1, source_target_pairs={{192,129},{193,128},{194,131},{195,130},{196,133},{197,132},{198,1... | collective-permute-start | bytes 2408456 | tf_op jit(solution)/shard_map/ppermute | solution.py:209
  20.6 3.9 %collective-permute-start.6 = (bf16[2,16,256]{2,1,0:T(8,128)(2,1)S(1)}, bf16[2,16,256]{2,1,0:T(8,128)(2,1)S(1)}, u32[]{:S(2)}, u32[]{:S(2)}) collective-permute-start(bf16[2,16,256]{2,1,0:T(8,128)(2,1)S(1)} %get-tuple-element.27._after.sent_ref), channel_id=1, source_target_pairs={{1,66},{2,65},{3,68},{4,67},{5,70},{6,69},{7,72},{8,71},{9,74},{10... | collective-permute-start | bytes 49160 | tf_op jit(solution)/shard_map/ppermute | solution.py:209
  21.9 2.7 %collective-permute-start.7 = (bf16[2,16,256]{2,1,0:T(8,128)(2,1)S(1)}, bf16[2,16,256]{2,1,0:T(8,128)(2,1)S(1)}, u32[]{:S(2)}, u32[]{:S(2)}) collective-permute-start(bf16[2,16,256]{2,1,0:T(8,128)(2,1)S(1)} %get-tuple-element.27._after.sent_ref), channel_id=1, source_target_pairs={{0,65},{1,64},{2,67},{3,66},{4,69},{5,68},{6,71},{7,70},{8,73},{9,... | collective-permute-start | bytes 49160 | tf_op jit(solution)/shard_map/ppermute | solution.py:209
  23.2 2.1 %collective-permute-start.8 = (bf16[2,16,256]{2,1,0:T(8,128)(2,1)S(1)}, bf16[2,16,256]{2,1,0:T(8,128)(2,1)S(1)}, u32[]{:S(2)}, u32[]{:S(2)}) collective-permute-start(bf16[2,16,256]{2,1,0:T(8,128)(2,1)S(1)} %get-tuple-element.27._after.sent_ref), channel_id=1, source_target_pairs={{0,64},{1,65},{2,66},{3,67},{4,68},{5,69},{6,70},{7,71},{8,72},{9,... | collective-permute-start | bytes 49160 | tf_op jit(solution)/shard_map/ppermute | solution.py:209
  25.3 2.0 %collective-permute-start.9 = (bf16[2,16,256]{2,1,0:T(8,128)(2,1)S(1)}, bf16[2,16,256]{2,1,0:T(8,128)(2,1)S(1)}, u32[]{:S(2)}, u32[]{:S(2)}) collective-permute-start(bf16[2,16,256]{2,1,0:T(8,128)(2,1)S(1)} %get-tuple-element.29.sent_ref), channel_id=1, source_target_pairs={{65,130},{66,129},{67,132},{68,131},{69,134},{70,133},{71,136},{72... | collective-permute-start | bytes 49160 | tf_op jit(solution)/shard_map/ppermute | solution.py:209
  26.0 1.4 %collective-permute-start.10 = (bf16[2,16,256]{2,1,0:T(8,128)(2,1)S(1)}, bf16[2,16,256]{2,1,0:T(8,128)(2,1)S(1)}, u32[]{:S(2)}, u32[]{:S(2)}) collective-permute-start(bf16[2,16,256]{2,1,0:T(8,128)(2,1)S(1)} %get-tuple-element.29.sent_ref), channel_id=1, source_target_pairs={{64,129},{65,128},{66,131},{67,130},{68,133},{69,132},{70,135},{71... | collective-permute-start | bytes 49160 | tf_op jit(solution)/shard_map/ppermute | solution.py:209
  26.7 0.7 collective-permute-start.11
  27.4 2.0 %collective-permute-start.12 = (bf16[2,16,256]{2,1,0:T(8,128)(2,1)S(1)}, bf16[2,16,256]{2,1,0:T(8,128)(2,1)S(1)}, u32[]{:S(2)}, u32[]{:S(2)}) collective-permute-start(bf16[2,16,256]{2,1,0:T(8,128)(2,1)S(1)} %get-tuple-element.31.sent_ref), channel_id=1, source_target_pairs={{129,194},{130,193},{131,196},{132,195},{133,198},{134,197},{135,2... | collective-permute-start | bytes 49160 | tf_op jit(solution)/shard_map/ppermute | solution.py:209
  28.1 1.4 %collective-permute-start.13 = (bf16[2,16,256]{2,1,0:T(8,128)(2,1)S(1)}, bf16[2,16,256]{2,1,0:T(8,128)(2,1)S(1)}, u32[]{:S(2)}, u32[]{:S(2)}) collective-permute-start(bf16[2,16,256]{2,1,0:T(8,128)(2,1)S(1)} %get-tuple-element.31.sent_ref), channel_id=1, source_target_pairs={{128,193},{129,192},{130,195},{131,194},{132,197},{133,196},{134,1... | collective-permute-start | bytes 49160 | tf_op jit(solution)/shard_map/ppermute | solution.py:209
  28.7 0.7 collective-permute-start.14
  29.5 3.4 %collective-permute-start.15 = (bf16[2,16,256]{2,1,0:T(8,128)(2,1)S(1)}, bf16[2,16,256]{2,1,0:T(8,128)(2,1)S(1)}, u32[]{:S(2)}, u32[]{:S(2)}) collective-permute-start(bf16[2,16,256]{2,1,0:T(8,128)(2,1)S(1)} %get-tuple-element.33.sent_ref), channel_id=1, source_target_pairs={{194,324},{195,325},{196,322},{197,323},{198,328},{199,329},{200,3... | collective-permute-start | bytes 49160 | tf_op jit(solution)/shard_map/ppermute | solution.py:209
  30.2 2.7 %collective-permute-start.16 = (bf16[2,16,256]{2,1,0:T(8,128)(2,1)S(1)}, bf16[2,16,256]{2,1,0:T(8,128)(2,1)S(1)}, u32[]{:S(2)}, u32[]{:S(2)}) collective-permute-start(bf16[2,16,256]{2,1,0:T(8,128)(2,1)S(1)} %get-tuple-element.33.sent_ref), channel_id=1, source_target_pairs={{193,322},{194,321},{195,324},{196,323},{197,326},{198,325},{199,3... | collective-permute-start | bytes 49160 | tf_op jit(solution)/shard_map/ppermute | solution.py:209
  30.8 2.0 %collective-permute-start.17 = (bf16[2,16,256]{2,1,0:T(8,128)(2,1)S(1)}, bf16[2,16,256]{2,1,0:T(8,128)(2,1)S(1)}, u32[]{:S(2)}, u32[]{:S(2)}) collective-permute-start(bf16[2,16,256]{2,1,0:T(8,128)(2,1)S(1)} %get-tuple-element.33.sent_ref), channel_id=1, source_target_pairs={{192,322},{193,323},{194,320},{195,321},{196,326},{197,327},{198,3... | collective-permute-start | bytes 49160 | tf_op jit(solution)/shard_map/ppermute | solution.py:209
  31.5 1.4 %collective-permute-start.18 = (bf16[2,16,256]{2,1,0:T(8,128)(2,1)S(1)}, bf16[2,16,256]{2,1,0:T(8,128)(2,1)S(1)}, u32[]{:S(2)}, u32[]{:S(2)}) collective-permute-start(bf16[2,16,256]{2,1,0:T(8,128)(2,1)S(1)} %get-tuple-element.33.sent_ref), channel_id=1, source_target_pairs={{192,321},{193,320},{194,323},{195,322},{196,325},{197,324},{198,3... | collective-permute-start | bytes 49160 | tf_op jit(solution)/shard_map/ppermute | solution.py:209
  32.2 0.7 collective-permute-start.19
  32.9 3.4 %collective-permute-start.20 = (bf16[2,16,256]{2,1,0:T(8,128)(2,1)S(1)}, bf16[2,16,256]{2,1,0:T(8,128)(2,1)S(1)}, u32[]{:S(2)}, u32[]{:S(2)}) collective-permute-start(bf16[2,16,256]{2,1,0:T(8,128)(2,1)S(1)} %get-tuple-element.35.sent_ref), channel_id=1, source_target_pairs={{322,452},{323,453},{324,450},{325,451},{326,456},{327,457},{328,4... | collective-permute-start | bytes 49160 | tf_op jit(solution)/shard_map/ppermute | solution.py:209
  33.6 3.4 %collective-permute-start.21 = (bf16[2,16,256]{2,1,0:T(8,128)(2,1)S(1)}, bf16[2,16,256]{2,1,0:T(8,128)(2,1)S(1)}, u32[]{:S(2)}, u32[]{:S(2)}) collective-permute-start(bf16[2,16,256]{2,1,0:T(8,128)(2,1)S(1)} %get-tuple-element.35.sent_ref), channel_id=1, source_target_pairs={{321,450},{322,449},{323,452},{324,451},{325,454},{326,453},{327,4... | collective-permute-start | bytes 49160 | tf_op jit(solution)/shard_map/ppermute | solution.py:209
  34.3 2.7 %collective-permute-start.22 = (bf16[2,16,256]{2,1,0:T(8,128)(2,1)S(1)}, bf16[2,16,256]{2,1,0:T(8,128)(2,1)S(1)}, u32[]{:S(2)}, u32[]{:S(2)}) collective-permute-start(bf16[2,16,256]{2,1,0:T(8,128)(2,1)S(1)} %get-tuple-element.35.sent_ref), channel_id=1, source_target_pairs={{320,450},{321,451},{322,448},{323,449},{324,454},{325,455},{326,4... | collective-permute-start | bytes 49160 | tf_op jit(solution)/shard_map/ppermute | solution.py:209
  34.9 2.0 %collective-permute-start.23 = (bf16[2,16,256]{2,1,0:T(8,128)(2,1)S(1)}, bf16[2,16,256]{2,1,0:T(8,128)(2,1)S(1)}, u32[]{:S(2)}, u32[]{:S(2)}) collective-permute-start(bf16[2,16,256]{2,1,0:T(8,128)(2,1)S(1)} %get-tuple-element.35.sent_ref), channel_id=1, source_target_pairs={{320,449},{321,448},{322,451},{323,450},{324,453},{325,452},{326,4... | collective-permute-start | bytes 49160 | tf_op jit(solution)/shard_map/ppermute | solution.py:209
  35.6 1.4 %collective-permute-start.24 = (bf16[2,16,256]{2,1,0:T(8,128)(2,1)S(1)}, bf16[2,16,256]{2,1,0:T(8,128)(2,1)S(1)}, u32[]{:S(2)}, u32[]{:S(2)}) collective-permute-start(bf16[2,16,256]{2,1,0:T(8,128)(2,1)S(1)} %get-tuple-element.35.sent_ref), channel_id=1, source_target_pairs={{320,448},{321,449},{322,450},{323,451},{324,452},{325,453},{326,4... | collective-permute-start | bytes 49160 | tf_op jit(solution)/shard_map/ppermute | solution.py:209
  36.3 3.4 %collective-permute-start.28 = (bf16[2,16,256]{2,1,0:T(8,128)(2,1)S(1)}, bf16[2,16,256]{2,1,0:T(8,128)(2,1)S(1)}, u32[]{:S(2)}, u32[]{:S(2)}) collective-permute-start(bf16[2,16,256]{2,1,0:T(8,128)(2,1)S(1)} %get-tuple-element.38), channel_id=1, source_target_pairs={{128,256},{129,257},{130,258},{131,259},{132,260},{133,261},{134,2... | collective-permute-start | bytes 49160 | tf_op jit(solution)/shard_map/ppermute | solution.py:209
  37.0 2.7 %collective-permute-start.25 = (bf16[2,2,16,256]{3,2,1,0:T(8,128)(2,1)S(1)}, bf16[2,2,16,256]{3,2,1,0:T(8,128)(2,1)S(1)}, u32[]{:S(2)}, u32[]{:S(2)}) collective-permute-start(bf16[2,2,16,256]{3,2,1,0:T(8,128)(2,1)S(1)} %get-tuple-element.37), channel_id=1, source_target_pairs={{449,386},{450,385},{451,388},{452,387},{453,390},{454,389},{455,3... | collective-permute-start | bytes 98312 | tf_op jit(solution)/shard_map/ppermute | solution.py:209
  37.7 2.0 %collective-permute-start.26 = (bf16[2,2,16,256]{3,2,1,0:T(8,128)(2,1)S(1)}, bf16[2,2,16,256]{3,2,1,0:T(8,128)(2,1)S(1)}, u32[]{:S(2)}, u32[]{:S(2)}) collective-permute-start(bf16[2,2,16,256]{3,2,1,0:T(8,128)(2,1)S(1)} %get-tuple-element.37), channel_id=1, source_target_pairs={{128,193},{129,192},{130,195},{131,194},{132,197},{133,196},{134,1... | collective-permute-start | bytes 98312 | tf_op jit(solution)/shard_map/ppermute | solution.py:209
  38.4 1.4 %collective-permute-start.27 = (bf16[2,2,16,256]{3,2,1,0:T(8,128)(2,1)S(1)}, bf16[2,2,16,256]{3,2,1,0:T(8,128)(2,1)S(1)}, u32[]{:S(2)}, u32[]{:S(2)}) collective-permute-start(bf16[2,2,16,256]{3,2,1,0:T(8,128)(2,1)S(1)} %get-tuple-element.37), channel_id=1, source_target_pairs={{128,192},{129,193},{130,194},{131,195},{132,196},{133,197},{134,1... | collective-permute-start | bytes 98312 | tf_op jit(solution)/shard_map/ppermute | solution.py:209
  39.0 3.4 %collective-permute-start.34 = (bf16[2,16,256]{2,1,0:T(8,128)(2,1)S(1)}, bf16[2,16,256]{2,1,0:T(8,128)(2,1)S(1)}, u32[]{:S(2)}, u32[]{:S(2)}) collective-permute-start(bf16[2,16,256]{2,1,0:T(8,128)(2,1)S(1)} %slice_bitcast_fusion), channel_id=1, source_target_pairs={{320,256},{321,257},{322,258},{323,259},{324,260},{325,261},{326,2... | collective-permute-start | bytes 49160 | tf_op jit(solution)/shard_map/ppermute | solution.py:209
  39.8 3.4 %collective-permute-start.29 = (bf16[2,16,256]{2,1,0:T(8,128)(2,1)S(1)}, bf16[2,16,256]{2,1,0:T(8,128)(2,1)S(1)}, u32[]{:S(2)}, u32[]{:S(2)}) collective-permute-start(bf16[2,16,256]{2,1,0:T(8,128)(2,1)S(1)} %get-tuple-element.40), channel_id=1, source_target_pairs={{194,324},{195,325},{196,322},{197,323},{198,328},{199,329},{200,3... | collective-permute-start | bytes 49160 | tf_op jit(solution)/shard_map/ppermute | solution.py:209
  40.5 2.7 %collective-permute-start.30 = (bf16[2,16,256]{2,1,0:T(8,128)(2,1)S(1)}, bf16[2,16,256]{2,1,0:T(8,128)(2,1)S(1)}, u32[]{:S(2)}, u32[]{:S(2)}) collective-permute-start(bf16[2,16,256]{2,1,0:T(8,128)(2,1)S(1)} %get-tuple-element.40), channel_id=1, source_target_pairs={{193,322},{194,321},{195,324},{196,323},{197,326},{198,325},{199,3... | collective-permute-start | bytes 49160 | tf_op jit(solution)/shard_map/ppermute | solution.py:209
  41.1 2.0 %collective-permute-start.31 = (bf16[2,16,256]{2,1,0:T(8,128)(2,1)S(1)}, bf16[2,16,256]{2,1,0:T(8,128)(2,1)S(1)}, u32[]{:S(2)}, u32[]{:S(2)}) collective-permute-start(bf16[2,16,256]{2,1,0:T(8,128)(2,1)S(1)} %get-tuple-element.40), channel_id=1, source_target_pairs={{192,322},{193,323},{194,320},{195,321},{196,326},{197,327},{198,3... | collective-permute-start | bytes 49160 | tf_op jit(solution)/shard_map/ppermute | solution.py:209
  41.8 1.4 %collective-permute-start.32 = (bf16[2,16,256]{2,1,0:T(8,128)(2,1)S(1)}, bf16[2,16,256]{2,1,0:T(8,128)(2,1)S(1)}, u32[]{:S(2)}, u32[]{:S(2)}) collective-permute-start(bf16[2,16,256]{2,1,0:T(8,128)(2,1)S(1)} %get-tuple-element.40), channel_id=1, source_target_pairs={{192,321},{193,320},{194,323},{195,322},{196,325},{197,324},{198,3... | collective-permute-start | bytes 49160 | tf_op jit(solution)/shard_map/ppermute | solution.py:209
  42.5 0.7 collective-permute-start.33
  43.2 3.4 %collective-permute-start.35 = (bf16[2,16,256]{2,1,0:T(8,128)(2,1)S(1)}, bf16[2,16,256]{2,1,0:T(8,128)(2,1)S(1)}, u32[]{:S(2)}, u32[]{:S(2)}) collective-permute-start(bf16[2,16,256]{2,1,0:T(8,128)(2,1)S(1)} %get-tuple-element.44), channel_id=1, source_target_pairs={{322,452},{323,453},{324,450},{325,451},{326,456},{327,457},{328,4... | collective-permute-start | bytes 49160 | tf_op jit(solution)/shard_map/ppermute | solution.py:209
  43.9 2.7 %collective-permute-start.36 = (bf16[2,16,256]{2,1,0:T(8,128)(2,1)S(1)}, bf16[2,16,256]{2,1,0:T(8,128)(2,1)S(1)}, u32[]{:S(2)}, u32[]{:S(2)}) collective-permute-start(bf16[2,16,256]{2,1,0:T(8,128)(2,1)S(1)} %get-tuple-element.44), channel_id=1, source_target_pairs={{321,450},{322,449},{323,452},{324,451},{325,454},{326,453},{327,4... | collective-permute-start | bytes 49160 | tf_op jit(solution)/shard_map/ppermute | solution.py:209
  44.6 2.0 %collective-permute-start.37 = (bf16[2,16,256]{2,1,0:T(8,128)(2,1)S(1)}, bf16[2,16,256]{2,1,0:T(8,128)(2,1)S(1)}, u32[]{:S(2)}, u32[]{:S(2)}) collective-permute-start(bf16[2,16,256]{2,1,0:T(8,128)(2,1)S(1)} %get-tuple-element.44), channel_id=1, source_target_pairs={{320,450},{321,451},{322,448},{323,449},{324,454},{325,455},{326,4... | collective-permute-start | bytes 49160 | tf_op jit(solution)/shard_map/ppermute | solution.py:209
  45.2 1.4 %collective-permute-start.38 = (bf16[2,16,256]{2,1,0:T(8,128)(2,1)S(1)}, bf16[2,16,256]{2,1,0:T(8,128)(2,1)S(1)}, u32[]{:S(2)}, u32[]{:S(2)}) collective-permute-start(bf16[2,16,256]{2,1,0:T(8,128)(2,1)S(1)} %get-tuple-element.44), channel_id=1, source_target_pairs={{320,449},{321,448},{322,451},{323,450},{324,453},{325,452},{326,4... | collective-permute-start | bytes 49160 | tf_op jit(solution)/shard_map/ppermute | solution.py:209
  45.9 0.7 collective-permute-start.39
  46.7 2.7 %collective-permute-start.40 = (bf16[2,16,256]{2,1,0:T(8,128)(2,1)S(1)}, bf16[2,16,256]{2,1,0:T(8,128)(2,1)S(1)}, u32[]{:S(2)}, u32[]{:S(2)}) collective-permute-start(bf16[2,16,256]{2,1,0:T(8,128)(2,1)S(1)} %get-tuple-element.47), channel_id=1, source_target_pairs={{129,66},{130,65},{131,68},{132,67},{133,70},{134,69},{135,72},{13... | collective-permute-start | bytes 49160 | tf_op jit(solution)/shard_map/ppermute | solution.py:209
  47.3 2.0 %collective-permute-start.41 = (bf16[2,16,256]{2,1,0:T(8,128)(2,1)S(1)}, bf16[2,16,256]{2,1,0:T(8,128)(2,1)S(1)}, u32[]{:S(2)}, u32[]{:S(2)}) collective-permute-start(bf16[2,16,256]{2,1,0:T(8,128)(2,1)S(1)} %get-tuple-element.47), channel_id=1, source_target_pairs={{128,65},{129,64},{130,67},{131,66},{132,69},{133,68},{134,71},{13... | collective-permute-start | bytes 49160 | tf_op jit(solution)/shard_map/ppermute | solution.py:209
  48.0 1.4 %collective-permute-start.42 = (bf16[2,16,256]{2,1,0:T(8,128)(2,1)S(1)}, bf16[2,16,256]{2,1,0:T(8,128)(2,1)S(1)}, u32[]{:S(2)}, u32[]{:S(2)}) collective-permute-start(bf16[2,16,256]{2,1,0:T(8,128)(2,1)S(1)} %get-tuple-element.47), channel_id=1, source_target_pairs={{128,64},{129,65},{130,66},{131,67},{132,68},{133,69},{134,70},{13... | collective-permute-start | bytes 49160 | tf_op jit(solution)/shard_map/ppermute | solution.py:209
  48.7 0.7 collective-permute-start.43
  49.4 63.4 %collective-permute-start.44 = (bf16[2,16,256]{2,1,0:T(8,128)(2,1)S(1)}, bf16[2,16,256]{2,1,0:T(8,128)(2,1)S(1)}, u32[]{:S(2)}, u32[]{:S(2)}) collective-permute-start(bf16[2,16,256]{2,1,0:T(8,128)(2,1)S(1)} %chosen_kernel.1.kept_ref), channel_id=1, source_target_pairs={{65,2},{66,1},{67,4},{68,3},{69,6},{70,5},{71,8},{72,7},{73,10},{7... | collective-permute-start | bytes 49160 | tf_op jit(solution)/shard_map/ppermute | solution.py:209
  50.7 62.1 %collective-permute-start.45 = (bf16[2,16,256]{2,1,0:T(8,128)(2,1)S(1)}, bf16[2,16,256]{2,1,0:T(8,128)(2,1)S(1)}, u32[]{:S(2)}, u32[]{:S(2)}) collective-permute-start(bf16[2,16,256]{2,1,0:T(8,128)(2,1)S(1)} %chosen_kernel.1.kept_ref), channel_id=1, source_target_pairs={{64,1},{65,0},{66,3},{67,2},{68,5},{69,4},{70,7},{71,6},{72,9},{73... | collective-permute-start | bytes 49160 | tf_op jit(solution)/shard_map/ppermute | solution.py:209
  52.0 60.8 %collective-permute-start.46 = (bf16[2,16,256]{2,1,0:T(8,128)(2,1)S(1)}, bf16[2,16,256]{2,1,0:T(8,128)(2,1)S(1)}, u32[]{:S(2)}, u32[]{:S(2)}) collective-permute-start(bf16[2,16,256]{2,1,0:T(8,128)(2,1)S(1)} %chosen_kernel.1.kept_ref), channel_id=1, source_target_pairs={{64,0},{65,1},{66,2},{67,3},{68,4},{69,5},{70,6},{71,7},{72,8},{73... | collective-permute-start | bytes 49160 | tf_op jit(solution)/shard_map/ppermute | solution.py:209

commit v6 on v5

--- a/solution.py
+++ b/solution.py
@@ -87,7 +87,9 @@
     )
 
 
-def down_kernel(layer, next_ref, far_ref, near_ref, same_ref, dense_ref, kept_ref, sent_ref, send_ref, down_ref):
+def down_kernel(layer, shift, next_ref, *refs):
+    *window_refs, dense_ref, kept_ref, sent_ref, send_ref, down_ref = refs
+    far_ref, near_ref, same_ref = window_refs[-shift:] + window_refs[:-shift] if shift else window_refs
     down_ref[...] = kept_ref[...]
     send_ref[...] = sent_ref[...]
 
@@ -295,14 +297,17 @@
         if layer == 1:
             following = hold(following, other_same)
         if layer == split:
-            following = hold(following, other_far, other_near)
-        send, down = step(down_kernel, (one, one), (layer,), following, *window, dense, down, send)
+            following = hold(following, other_near)
+        shift = 1 if layer == 2 else 0
+        parts = [*window[shift:], *window[:shift]]
+        send, down = step(down_kernel, (one, one), (layer, shift), following, *parts, dense, down, send)
         if layer < split:
             window = moved(send, layer, layer + 1)
         if layer == 0:
             [load] = step(later_kernel, (payload,), ([k for k, _ in given],), dense, following, send)
             other_far, other_near, other_same = (sent(load, given, place) for place in (far, near, same))
     for layer in range(split + 2, top + 1, 2):
+        following = hold(following, other_far) if layer < top else following
         window = moved_two(send, layer - 2, layer)
         down, both, *more = step(
             down_two_kernel, (one, two, one, one)[: 4 if layer < top else 2], (layer,), *window,

time: 115 us -> 109 us (0.948)
  waiting for transfers between devices: 60.7 us -> 55.5 us
    ppermute x47, waiting for transfers between devices: 60.7 us -> 55.5 us  [sent(): return lax.ppermute(value, AXES, pairs)]
where the time goes in v6:
time: 109 us; the launch traced here: 108 us
  waiting for transfers between devices  55.5 us (51%)
  starting transfers between devices  46.3 us (42%)
  local copies, waits for them, and re-layouts  2.78 us (3%)
  Pallas kernels  2.37 us (2%)
  between operations  1.49 us (1%)
    ppermute x47, waiting for transfers between devices, sent(): return lax.ppermute(value, AXES, pairs)  55.5 us
    ppermute x47, starting transfers between devices, sent(): return lax.ppermute(value, AXES, pairs)  46.3 us
    unnamed x8, local copies, waits for them, and re-layouts  2.78 us
  transfers between devices with their start and end apart: 47, of which 4 were waited for; matrix products, arithmetic and copies ran while one was open for 0% of the time, Pallas kernels for 1%

profile of v6, /device:TPU:62, one launch (start us, length us, event | category | flops | bytes accessed | tf_op | source)
XLA Modules:
  0.0 108.4 jit_solution(15166738523582963462)
XLA Ops:
  0.6 1.3 %collective-permute-start = (bf16[2,16,256]{2,1,0:T(8,128)(2,1)}, bf16[2,16,256]{2,1,0:T(8,128)(2,1)S(1)}, u32[]{:S(2)}, u32[]{:S(2)}) collective-permute-start(bf16[2,16,256]{2,1,0:T(8,128)(2,1)} %bitcast.7), channel_id=1, source_target_pairs={{64,0},{65,1},{66,2},{67,3},{68,4},{69,5},{70,6},{71,7},{72,8},{73... | collective-permute-start | bytes 49160 | tf_op jit(solution)/shard_map/ppermute | solution.py:211
  1.9 10.0 %collective-permute-start.1 = (bf16[2,16,256]{2,1,0:T(8,128)(2,1)}, bf16[2,16,256]{2,1,0:T(8,128)(2,1)S(1)}, u32[]{:S(2)}, u32[]{:S(2)}) collective-permute-start(bf16[2,16,256]{2,1,0:T(8,128)(2,1)} %bitcast.8), channel_id=1, source_target_pairs={{1,2},{2,1},{3,4},{4,3},{5,6},{6,5},{7,8},{8,7},{9,10},{10,9},{11,... | collective-permute-start | bytes 49160 | tf_op jit(solution)/shard_map/ppermute | solution.py:211
  12.0 1.9 %collective-permute-start.2 = (bf16[2,16,256]{2,1,0:T(8,128)(2,1)}, bf16[2,16,256]{2,1,0:T(8,128)(2,1)S(1)}, u32[]{:S(2)}, u32[]{:S(2)}) collective-permute-start(bf16[2,16,256]{2,1,0:T(8,128)(2,1)} %bitcast.9), channel_id=1, source_target_pairs={{0,1},{1,0},{2,3},{3,2},{4,5},{5,4},{6,7},{7,6},{8,9},{9,8},{10,11... | collective-permute-start | bytes 49160 | tf_op jit(solution)/shard_map/ppermute | solution.py:211
  13.9 0.6 copy-done.3
  14.6 0.0 copy-start.2
  14.6 0.6 copy-done.2
  15.2 1.1 %copy-done = bf16[1,12,2,128,128]{4,3,2,1,0:T(8,128)(2,1)S(1)} copy-done((bf16[1,12,2,128,128]{4,3,2,1,0:T(8,128)(2,1)S(1)}, bf16[1,12,2,128,128]{4,3,2,1,0:T(8,128)(2,1)}, u32[]{:S(2)}) %copy-start) | copy-done | bytes 786456
  16.4 1.1 dense.1.refs_3_.dense_ref
  17.4 0.0 copy-start.1
  17.5 0.0 collective-permute-done.1.refs_0_
  17.5 0.3 collective-permute-done.2.refs_1_
  17.8 0.3 copy-done.1
  18.2 0.2 down_kernel.4
  18.4 0.7 collective-permute-start.3
  19.2 0.7 collective-permute-start.4
  19.9 0.7 collective-permute-start.19
  20.6 1.3 %collective-permute-start.5 = (bf16[2,16,256]{2,1,0:T(8,128)(2,1)S(1)}, bf16[2,16,256]{2,1,0:T(8,128)(2,1)S(1)}, u32[]{:S(2)}, u32[]{:S(2)}) collective-permute-start(bf16[2,16,256]{2,1,0:T(8,128)(2,1)S(1)} %get-tuple-element.27._after.refs_5_), channel_id=1, source_target_pairs={{1,66},{2,65},{3,68},{4,67},{5,70},{6,69},{7,72},{8,71},{9,74},{10... | collective-permute-start | bytes 49160 | tf_op jit(solution)/shard_map/ppermute | solution.py:211
  21.9 1.3 %collective-permute-start.6 = (bf16[2,16,256]{2,1,0:T(8,128)(2,1)S(1)}, bf16[2,16,256]{2,1,0:T(8,128)(2,1)S(1)}, u32[]{:S(2)}, u32[]{:S(2)}) collective-permute-start(bf16[2,16,256]{2,1,0:T(8,128)(2,1)S(1)} %get-tuple-element.27._after.refs_5_), channel_id=1, source_target_pairs={{0,65},{1,64},{2,67},{3,66},{4,69},{5,68},{6,71},{7,70},{8,73},{9,... | collective-permute-start | bytes 49160 | tf_op jit(solution)/shard_map/ppermute | solution.py:211
  23.2 0.0 collective-permute-done.3.refs_0_.other_same_ref
  23.2 1.3 %collective-permute-start.7 = (bf16[2,16,256]{2,1,0:T(8,128)(2,1)S(1)}, bf16[2,16,256]{2,1,0:T(8,128)(2,1)S(1)}, u32[]{:S(2)}, u32[]{:S(2)}) collective-permute-start(bf16[2,16,256]{2,1,0:T(8,128)(2,1)S(1)} %get-tuple-element.27._after.refs_5_), channel_id=1, source_target_pairs={{0,64},{1,65},{2,66},{3,67},{4,68},{5,69},{6,70},{7,71},{8,72},{9,... | collective-permute-start | bytes 49160 | tf_op jit(solution)/shard_map/ppermute | solution.py:211
  24.5 0.1 collective-permute-done.6.refs_1_
  24.6 0.7 collective-permute-done.7.refs_2_
  25.3 0.7 collective-permute-start.10
  26.0 0.7 collective-permute-start.8
  26.7 0.7 collective-permute-start.9
  27.3 0.0 collective-permute-done.10.refs_2_
  27.4 0.0 collective-permute-done.9.refs_1_
  27.4 0.7 collective-permute-start.11
  28.1 0.7 collective-permute-start.12
  28.7 0.7 collective-permute-start.13
  29.5 0.7 collective-permute-start.14
  30.2 0.7 collective-permute-start.15
  30.8 0.7 collective-permute-start.16
  31.5 0.7 collective-permute-start.17
  32.2 0.7 collective-permute-start.18
  32.9 0.7 collective-permute-start.20
  33.6 0.7 collective-permute-start.21
  34.3 0.7 collective-permute-start.22
  34.9 0.7 collective-permute-start.23
  35.6 0.7 collective-permute-start.24
  36.3 0.7 collective-permute-start.28
  37.0 0.7 collective-permute-start.25
  37.7 0.7 collective-permute-start.26
  38.4 0.7 collective-permute-start.27
  39.1 0.7 collective-permute-start.34
  39.8 0.7 collective-permute-start.29
  40.5 0.7 collective-permute-start.30
  41.1 0.7 collective-permute-start.31
  41.8 0.7 collective-permute-start.32
  42.5 0.7 collective-permute-start.33
  43.2 0.7 collective-permute-start.35
  43.9 0.7 collective-permute-start.36
  44.6 0.7 collective-permute-start.37
  45.2 0.7 collective-permute-start.38
  45.9 0.7 collective-permute-start.39
  46.7 0.7 collective-permute-start.40
  47.3 0.7 collective-permute-start.41
  48.0 0.7 collective-permute-start.42
  48.7 0.7 collective-permute-start.43
  49.4 1.3 %collective-permute-start.44 = (bf16[2,16,256]{2,1,0:T(8,128)(2,1)S(1)}, bf16[2,16,256]{2,1,0:T(8,128)(2,1)S(1)}, u32[]{:S(2)}, u32[]{:S(2)}) collective-permute-start(bf16[2,16,256]{2,1,0:T(8,128)(2,1)S(1)} %chosen_kernel.1.kept_ref), channel_id=1, source_target_pairs={{65,2},{66,1},{67,4},{68,3},{69,6},{70,5},{71,8},{72,7},{73,10},{7... | collective-permute-start | bytes 49160 | tf_op jit(solution)/shard_map/ppermute | solution.py:211
  50.7 1.3 %collective-permute-start.45 = (bf16[2,16,256]{2,1,0:T(8,128)(2,1)S(1)}, bf16[2,16,256]{2,1,0:T(8,128)(2,1)S(1)}, u32[]{:S(2)}, u32[]{:S(2)}) collective-permute-start(bf16[2,16,256]{2,1,0:T(8,128)(2,1)S(1)} %chosen_kernel.1.kept_ref), channel_id=1, source_target_pairs={{64,1},{65,0},{66,3},{67,2},{68,5},{69,4},{70,7},{71,6},{72,9},{73... | collective-permute-start | bytes 49160 | tf_op jit(solution)/shard_map/ppermute | solution.py:211
  52.0 1.3 %collective-permute-start.46 = (bf16[2,16,256]{2,1,0:T(8,128)(2,1)S(1)}, bf16[2,16,256]{2,1,0:T(8,128)(2,1)S(1)}, u32[]{:S(2)}, u32[]{:S(2)}) collective-permute-start(bf16[2,16,256]{2,1,0:T(8,128)(2,1)S(1)} %chosen_kernel.1.kept_ref), channel_id=1, source_target_pairs={{64,0},{65,1},{66,2},{67,3},{68,4},{69,5},{70,6},{71,7},{72,8},{73... | collective-permute-start | bytes 49160 | tf_op jit(solution)/shard_map/ppermute | solution.py:211
  53.3 54.2 %collective-permute-done.44.far_ref = bf16[2,16,256]{2,1,0:T(8,128)(2,1)S(1)} collective-permute-done((bf16[2,16,256]{2,1,0:T(8,128)(2,1)S(1)}, bf16[2,16,256]{2,1,0:T(8,128)(2,1)S(1)}, u32[]{:S(2)}, u32[]{:S(2)}) %collective-permute-start.44) | collective-permute-done | bytes 16416 | tf_op jit(solution)/shard_map/ppermute | solution.py:211
  107.6 0.9 last_kernel.1
  (58 shorter events, 0.3 us)
Async XLA Ops:
  0.6 16.8 %collective-permute-start = (bf16[2,16,256]{2,1,0:T(8,128)(2,1)}, bf16[2,16,256]{2,1,0:T(8,128)(2,1)S(1)}, u32[]{:S(2)}, u32[]{:S(2)}) collective-permute-start(bf16[2,16,256]{2,1,0:T(8,128)(2,1)} %bitcast.7), channel_id=1, source_target_pairs={{64,0},{65,1},{66,2},{67,3},{68,4},{69,5},{70,6},{71,7},{72,8},{73... | collective-permute-start | bytes 49160 | tf_op jit(solution)/shard_map/ppermute | solution.py:211
  1.9 15.5 %collective-permute-start.1 = (bf16[2,16,256]{2,1,0:T(8,128)(2,1)}, bf16[2,16,256]{2,1,0:T(8,128)(2,1)S(1)}, u32[]{:S(2)}, u32[]{:S(2)}) collective-permute-start(bf16[2,16,256]{2,1,0:T(8,128)(2,1)} %bitcast.8), channel_id=1, source_target_pairs={{1,2},{2,1},{3,4},{4,3},{5,6},{6,5},{7,8},{8,7},{9,10},{10,9},{11,... | collective-permute-start | bytes 49160 | tf_op jit(solution)/shard_map/ppermute | solution.py:211
  12.0 5.8 %collective-permute-start.2 = (bf16[2,16,256]{2,1,0:T(8,128)(2,1)}, bf16[2,16,256]{2,1,0:T(8,128)(2,1)S(1)}, u32[]{:S(2)}, u32[]{:S(2)}) collective-permute-start(bf16[2,16,256]{2,1,0:T(8,128)(2,1)} %bitcast.9), channel_id=1, source_target_pairs={{0,1},{1,0},{2,3},{3,2},{4,5},{5,4},{6,7},{7,6},{8,9},{9,8},{10,11... | collective-permute-start | bytes 49160 | tf_op jit(solution)/shard_map/ppermute | solution.py:211
  13.9 0.7 copy-start.3
  14.6 0.7 copy-start.2
  15.2 1.1 %copy-start = (bf16[1,12,2,128,128]{4,3,2,1,0:T(8,128)(2,1)S(1)}, bf16[1,12,2,128,128]{4,3,2,1,0:T(8,128)(2,1)}, u32[]{:S(2)}) copy-start(bf16[1,12,2,128,128]{4,3,2,1,0:T(8,128)(2,1)} %param.5) | copy-start | bytes 2359300
  17.4 0.7 copy-start.1
  18.4 4.8 %collective-permute-start.3 = (bf16[784,512]{1,0:T(8,128)(2,1)S(1)}, bf16[784,512]{1,0:T(8,128)(2,1)S(1)}, u32[]{:S(2)}, u32[]{:S(2)}) collective-permute-start(bf16[784,512]{1,0:T(8,128)(2,1)S(1)} %later_kernel.1), channel_id=1, source_target_pairs={{192,128},{193,129},{194,130},{195,131},{196,132},{197,133},{198,1... | collective-permute-start | bytes 2408456 | tf_op jit(solution)/shard_map/ppermute | solution.py:211
  19.2 10.2 %collective-permute-start.4 = (bf16[784,512]{1,0:T(8,128)(2,1)S(1)}, bf16[784,512]{1,0:T(8,128)(2,1)S(1)}, u32[]{:S(2)}, u32[]{:S(2)}) collective-permute-start(bf16[784,512]{1,0:T(8,128)(2,1)S(1)} %later_kernel.1), channel_id=1, source_target_pairs={{192,129},{193,128},{194,131},{195,130},{196,133},{197,132},{198,1... | collective-permute-start | bytes 2408456 | tf_op jit(solution)/shard_map/ppermute | solution.py:211
  19.9 12.3 %collective-permute-start.19 = (bf16[784,512]{1,0:T(8,128)(2,1)S(1)}, bf16[784,512]{1,0:T(8,128)(2,1)S(1)}, u32[]{:S(2)}, u32[]{:S(2)}) collective-permute-start(bf16[784,512]{1,0:T(8,128)(2,1)S(1)} %later_kernel.1), channel_id=1, source_target_pairs={{193,130},{194,129},{195,132},{196,131},{197,134},{198,133},{199,1... | collective-permute-start | bytes 2408456 | tf_op jit(solution)/shard_map/ppermute | solution.py:211
  20.6 3.9 %collective-permute-start.5 = (bf16[2,16,256]{2,1,0:T(8,128)(2,1)S(1)}, bf16[2,16,256]{2,1,0:T(8,128)(2,1)S(1)}, u32[]{:S(2)}, u32[]{:S(2)}) collective-permute-start(bf16[2,16,256]{2,1,0:T(8,128)(2,1)S(1)} %get-tuple-element.27._after.refs_5_), channel_id=1, source_target_pairs={{1,66},{2,65},{3,68},{4,67},{5,70},{6,69},{7,72},{8,71},{9,74},{10... | collective-permute-start | bytes 49160 | tf_op jit(solution)/shard_map/ppermute | solution.py:211
  21.9 2.7 %collective-permute-start.6 = (bf16[2,16,256]{2,1,0:T(8,128)(2,1)S(1)}, bf16[2,16,256]{2,1,0:T(8,128)(2,1)S(1)}, u32[]{:S(2)}, u32[]{:S(2)}) collective-permute-start(bf16[2,16,256]{2,1,0:T(8,128)(2,1)S(1)} %get-tuple-element.27._after.refs_5_), channel_id=1, source_target_pairs={{0,65},{1,64},{2,67},{3,66},{4,69},{5,68},{6,71},{7,70},{8,73},{9,... | collective-permute-start | bytes 49160 | tf_op jit(solution)/shard_map/ppermute | solution.py:211
  23.2 2.1 %collective-permute-start.7 = (bf16[2,16,256]{2,1,0:T(8,128)(2,1)S(1)}, bf16[2,16,256]{2,1,0:T(8,128)(2,1)S(1)}, u32[]{:S(2)}, u32[]{:S(2)}) collective-permute-start(bf16[2,16,256]{2,1,0:T(8,128)(2,1)S(1)} %get-tuple-element.27._after.refs_5_), channel_id=1, source_target_pairs={{0,64},{1,65},{2,66},{3,67},{4,68},{5,69},{6,70},{7,71},{8,72},{9,... | collective-permute-start | bytes 49160 | tf_op jit(solution)/shard_map/ppermute | solution.py:211
  25.3 2.0 %collective-permute-start.10 = (bf16[2,16,256]{2,1,0:T(8,128)(2,1)S(1)}, bf16[2,16,256]{2,1,0:T(8,128)(2,1)S(1)}, u32[]{:S(2)}, u32[]{:S(2)}) collective-permute-start(bf16[2,16,256]{2,1,0:T(8,128)(2,1)S(1)} %get-tuple-element.29.refs_5_), channel_id=1, source_target_pairs={{65,130},{66,129},{67,132},{68,131},{69,134},{70,133},{71,136},{72... | collective-permute-start | bytes 49160 | tf_op jit(solution)/shard_map/ppermute | solution.py:211
  26.0 1.4 %collective-permute-start.8 = (bf16[2,16,256]{2,1,0:T(8,128)(2,1)S(1)}, bf16[2,16,256]{2,1,0:T(8,128)(2,1)S(1)}, u32[]{:S(2)}, u32[]{:S(2)}) collective-permute-start(bf16[2,16,256]{2,1,0:T(8,128)(2,1)S(1)} %get-tuple-element.29.refs_5_), channel_id=1, source_target_pairs={{64,129},{65,128},{66,131},{67,130},{68,133},{69,132},{70,135},{71... | collective-permute-start | bytes 49160 | tf_op jit(solution)/shard_map/ppermute | solution.py:211
  26.7 0.7 collective-permute-start.9
  27.4 2.0 %collective-permute-start.11 = (bf16[2,16,256]{2,1,0:T(8,128)(2,1)S(1)}, bf16[2,16,256]{2,1,0:T(8,128)(2,1)S(1)}, u32[]{:S(2)}, u32[]{:S(2)}) collective-permute-start(bf16[2,16,256]{2,1,0:T(8,128)(2,1)S(1)} %get-tuple-element.31.refs_5_), channel_id=1, source_target_pairs={{129,194},{130,193},{131,196},{132,195},{133,198},{134,197},{135,2... | collective-permute-start | bytes 49160 | tf_op jit(solution)/shard_map/ppermute | solution.py:211
  28.1 1.4 %collective-permute-start.12 = (bf16[2,16,256]{2,1,0:T(8,128)(2,1)S(1)}, bf16[2,16,256]{2,1,0:T(8,128)(2,1)S(1)}, u32[]{:S(2)}, u32[]{:S(2)}) collective-permute-start(bf16[2,16,256]{2,1,0:T(8,128)(2,1)S(1)} %get-tuple-element.31.refs_5_), channel_id=1, source_target_pairs={{128,193},{129,192},{130,195},{131,194},{132,197},{133,196},{134,1... | collective-permute-start | bytes 49160 | tf_op jit(solution)/shard_map/ppermute | solution.py:211
  28.7 0.7 collective-permute-start.13
  29.5 3.4 %collective-permute-start.14 = (bf16[2,16,256]{2,1,0:T(8,128)(2,1)S(1)}, bf16[2,16,256]{2,1,0:T(8,128)(2,1)S(1)}, u32[]{:S(2)}, u32[]{:S(2)}) collective-permute-start(bf16[2,16,256]{2,1,0:T(8,128)(2,1)S(1)} %get-tuple-element.33.sent_ref), channel_id=1, source_target_pairs={{194,324},{195,325},{196,322},{197,323},{198,328},{199,329},{200,3... | collective-permute-start | bytes 49160 | tf_op jit(solution)/shard_map/ppermute | solution.py:211
  30.2 2.7 %collective-permute-start.15 = (bf16[2,16,256]{2,1,0:T(8,128)(2,1)S(1)}, bf16[2,16,256]{2,1,0:T(8,128)(2,1)S(1)}, u32[]{:S(2)}, u32[]{:S(2)}) collective-permute-start(bf16[2,16,256]{2,1,0:T(8,128)(2,1)S(1)} %get-tuple-element.33.sent_ref), channel_id=1, source_target_pairs={{193,322},{194,321},{195,324},{196,323},{197,326},{198,325},{199,3... | collective-permute-start | bytes 49160 | tf_op jit(solution)/shard_map/ppermute | solution.py:211
  30.8 2.1 %collective-permute-start.16 = (bf16[2,16,256]{2,1,0:T(8,128)(2,1)S(1)}, bf16[2,16,256]{2,1,0:T(8,128)(2,1)S(1)}, u32[]{:S(2)}, u32[]{:S(2)}) collective-permute-start(bf16[2,16,256]{2,1,0:T(8,128)(2,1)S(1)} %get-tuple-element.33.sent_ref), channel_id=1, source_target_pairs={{192,322},{193,323},{194,320},{195,321},{196,326},{197,327},{198,3... | collective-permute-start | bytes 49160 | tf_op jit(solution)/shard_map/ppermute | solution.py:211
  31.5 1.4 %collective-permute-start.17 = (bf16[2,16,256]{2,1,0:T(8,128)(2,1)S(1)}, bf16[2,16,256]{2,1,0:T(8,128)(2,1)S(1)}, u32[]{:S(2)}, u32[]{:S(2)}) collective-permute-start(bf16[2,16,256]{2,1,0:T(8,128)(2,1)S(1)} %get-tuple-element.33.sent_ref), channel_id=1, source_target_pairs={{192,321},{193,320},{194,323},{195,322},{196,325},{197,324},{198,3... | collective-permute-start | bytes 49160 | tf_op jit(solution)/shard_map/ppermute | solution.py:211
  32.2 0.7 collective-permute-start.18
  32.9 3.4 %collective-permute-start.20 = (bf16[2,16,256]{2,1,0:T(8,128)(2,1)S(1)}, bf16[2,16,256]{2,1,0:T(8,128)(2,1)S(1)}, u32[]{:S(2)}, u32[]{:S(2)}) collective-permute-start(bf16[2,16,256]{2,1,0:T(8,128)(2,1)S(1)} %get-tuple-element.35.sent_ref), channel_id=1, source_target_pairs={{322,452},{323,453},{324,450},{325,451},{326,456},{327,457},{328,4... | collective-permute-start | bytes 49160 | tf_op jit(solution)/shard_map/ppermute | solution.py:211
  33.6 3.4 %collective-permute-start.21 = (bf16[2,16,256]{2,1,0:T(8,128)(2,1)S(1)}, bf16[2,16,256]{2,1,0:T(8,128)(2,1)S(1)}, u32[]{:S(2)}, u32[]{:S(2)}) collective-permute-start(bf16[2,16,256]{2,1,0:T(8,128)(2,1)S(1)} %get-tuple-element.35.sent_ref), channel_id=1, source_target_pairs={{321,450},{322,449},{323,452},{324,451},{325,454},{326,453},{327,4... | collective-permute-start | bytes 49160 | tf_op jit(solution)/shard_map/ppermute | solution.py:211
  34.3 2.7 %collective-permute-start.22 = (bf16[2,16,256]{2,1,0:T(8,128)(2,1)S(1)}, bf16[2,16,256]{2,1,0:T(8,128)(2,1)S(1)}, u32[]{:S(2)}, u32[]{:S(2)}) collective-permute-start(bf16[2,16,256]{2,1,0:T(8,128)(2,1)S(1)} %get-tuple-element.35.sent_ref), channel_id=1, source_target_pairs={{320,450},{321,451},{322,448},{323,449},{324,454},{325,455},{326,4... | collective-permute-start | bytes 49160 | tf_op jit(solution)/shard_map/ppermute | solution.py:211
  34.9 2.0 %collective-permute-start.23 = (bf16[2,16,256]{2,1,0:T(8,128)(2,1)S(1)}, bf16[2,16,256]{2,1,0:T(8,128)(2,1)S(1)}, u32[]{:S(2)}, u32[]{:S(2)}) collective-permute-start(bf16[2,16,256]{2,1,0:T(8,128)(2,1)S(1)} %get-tuple-element.35.sent_ref), channel_id=1, source_target_pairs={{320,449},{321,448},{322,451},{323,450},{324,453},{325,452},{326,4... | collective-permute-start | bytes 49160 | tf_op jit(solution)/shard_map/ppermute | solution.py:211
  35.6 1.4 %collective-permute-start.24 = (bf16[2,16,256]{2,1,0:T(8,128)(2,1)S(1)}, bf16[2,16,256]{2,1,0:T(8,128)(2,1)S(1)}, u32[]{:S(2)}, u32[]{:S(2)}) collective-permute-start(bf16[2,16,256]{2,1,0:T(8,128)(2,1)S(1)} %get-tuple-element.35.sent_ref), channel_id=1, source_target_pairs={{320,448},{321,449},{322,450},{323,451},{324,452},{325,453},{326,4... | collective-permute-start | bytes 49160 | tf_op jit(solution)/shard_map/ppermute | solution.py:211
  36.3 3.4 %collective-permute-start.28 = (bf16[2,16,256]{2,1,0:T(8,128)(2,1)S(1)}, bf16[2,16,256]{2,1,0:T(8,128)(2,1)S(1)}, u32[]{:S(2)}, u32[]{:S(2)}) collective-permute-start(bf16[2,16,256]{2,1,0:T(8,128)(2,1)S(1)} %get-tuple-element.38), channel_id=1, source_target_pairs={{128,256},{129,257},{130,258},{131,259},{132,260},{133,261},{134,2... | collective-permute-start | bytes 49160 | tf_op jit(solution)/shard_map/ppermute | solution.py:211
  37.0 2.7 %collective-permute-start.25 = (bf16[2,2,16,256]{3,2,1,0:T(8,128)(2,1)S(1)}, bf16[2,2,16,256]{3,2,1,0:T(8,128)(2,1)S(1)}, u32[]{:S(2)}, u32[]{:S(2)}) collective-permute-start(bf16[2,2,16,256]{3,2,1,0:T(8,128)(2,1)S(1)} %get-tuple-element.37), channel_id=1, source_target_pairs={{449,386},{450,385},{451,388},{452,387},{453,390},{454,389},{455,3... | collective-permute-start | bytes 98312 | tf_op jit(solution)/shard_map/ppermute | solution.py:211
  37.7 2.0 %collective-permute-start.26 = (bf16[2,2,16,256]{3,2,1,0:T(8,128)(2,1)S(1)}, bf16[2,2,16,256]{3,2,1,0:T(8,128)(2,1)S(1)}, u32[]{:S(2)}, u32[]{:S(2)}) collective-permute-start(bf16[2,2,16,256]{3,2,1,0:T(8,128)(2,1)S(1)} %get-tuple-element.37), channel_id=1, source_target_pairs={{128,193},{129,192},{130,195},{131,194},{132,197},{133,196},{134,1... | collective-permute-start | bytes 98312 | tf_op jit(solution)/shard_map/ppermute | solution.py:211
  38.4 1.4 %collective-permute-start.27 = (bf16[2,2,16,256]{3,2,1,0:T(8,128)(2,1)S(1)}, bf16[2,2,16,256]{3,2,1,0:T(8,128)(2,1)S(1)}, u32[]{:S(2)}, u32[]{:S(2)}) collective-permute-start(bf16[2,2,16,256]{3,2,1,0:T(8,128)(2,1)S(1)} %get-tuple-element.37), channel_id=1, source_target_pairs={{128,192},{129,193},{130,194},{131,195},{132,196},{133,197},{134,1... | collective-permute-start | bytes 98312 | tf_op jit(solution)/shard_map/ppermute | solution.py:211
  39.1 3.4 %collective-permute-start.34 = (bf16[2,16,256]{2,1,0:T(8,128)(2,1)S(1)}, bf16[2,16,256]{2,1,0:T(8,128)(2,1)S(1)}, u32[]{:S(2)}, u32[]{:S(2)}) collective-permute-start(bf16[2,16,256]{2,1,0:T(8,128)(2,1)S(1)} %slice_bitcast_fusion), channel_id=1, source_target_pairs={{320,256},{321,257},{322,258},{323,259},{324,260},{325,261},{326,2... | collective-permute-start | bytes 49160 | tf_op jit(solution)/shard_map/ppermute | solution.py:211
  39.8 3.4 %collective-permute-start.29 = (bf16[2,16,256]{2,1,0:T(8,128)(2,1)S(1)}, bf16[2,16,256]{2,1,0:T(8,128)(2,1)S(1)}, u32[]{:S(2)}, u32[]{:S(2)}) collective-permute-start(bf16[2,16,256]{2,1,0:T(8,128)(2,1)S(1)} %get-tuple-element.40), channel_id=1, source_target_pairs={{194,324},{195,325},{196,322},{197,323},{198,328},{199,329},{200,3... | collective-permute-start | bytes 49160 | tf_op jit(solution)/shard_map/ppermute | solution.py:211
  40.5 2.7 %collective-permute-start.30 = (bf16[2,16,256]{2,1,0:T(8,128)(2,1)S(1)}, bf16[2,16,256]{2,1,0:T(8,128)(2,1)S(1)}, u32[]{:S(2)}, u32[]{:S(2)}) collective-permute-start(bf16[2,16,256]{2,1,0:T(8,128)(2,1)S(1)} %get-tuple-element.40), channel_id=1, source_target_pairs={{193,322},{194,321},{195,324},{196,323},{197,326},{198,325},{199,3... | collective-permute-start | bytes 49160 | tf_op jit(solution)/shard_map/ppermute | solution.py:211
  41.1 2.0 %collective-permute-start.31 = (bf16[2,16,256]{2,1,0:T(8,128)(2,1)S(1)}, bf16[2,16,256]{2,1,0:T(8,128)(2,1)S(1)}, u32[]{:S(2)}, u32[]{:S(2)}) collective-permute-start(bf16[2,16,256]{2,1,0:T(8,128)(2,1)S(1)} %get-tuple-element.40), channel_id=1, source_target_pairs={{192,322},{193,323},{194,320},{195,321},{196,326},{197,327},{198,3... | collective-permute-start | bytes 49160 | tf_op jit(solution)/shard_map/ppermute | solution.py:211
  41.8 1.4 %collective-permute-start.32 = (bf16[2,16,256]{2,1,0:T(8,128)(2,1)S(1)}, bf16[2,16,256]{2,1,0:T(8,128)(2,1)S(1)}, u32[]{:S(2)}, u32[]{:S(2)}) collective-permute-start(bf16[2,16,256]{2,1,0:T(8,128)(2,1)S(1)} %get-tuple-element.40), channel_id=1, source_target_pairs={{192,321},{193,320},{194,323},{195,322},{196,325},{197,324},{198,3... | collective-permute-start | bytes 49160 | tf_op jit(solution)/shard_map/ppermute | solution.py:211
  42.5 0.7 collective-permute-start.33
  43.2 3.4 %collective-permute-start.35 = (bf16[2,16,256]{2,1,0:T(8,128)(2,1)S(1)}, bf16[2,16,256]{2,1,0:T(8,128)(2,1)S(1)}, u32[]{:S(2)}, u32[]{:S(2)}) collective-permute-start(bf16[2,16,256]{2,1,0:T(8,128)(2,1)S(1)} %get-tuple-element.44), channel_id=1, source_target_pairs={{322,452},{323,453},{324,450},{325,451},{326,456},{327,457},{328,4... | collective-permute-start | bytes 49160 | tf_op jit(solution)/shard_map/ppermute | solution.py:211
  43.9 2.7 %collective-permute-start.36 = (bf16[2,16,256]{2,1,0:T(8,128)(2,1)S(1)}, bf16[2,16,256]{2,1,0:T(8,128)(2,1)S(1)}, u32[]{:S(2)}, u32[]{:S(2)}) collective-permute-start(bf16[2,16,256]{2,1,0:T(8,128)(2,1)S(1)} %get-tuple-element.44), channel_id=1, source_target_pairs={{321,450},{322,449},{323,452},{324,451},{325,454},{326,453},{327,4... | collective-permute-start | bytes 49160 | tf_op jit(solution)/shard_map/ppermute | solution.py:211
  44.6 2.0 %collective-permute-start.37 = (bf16[2,16,256]{2,1,0:T(8,128)(2,1)S(1)}, bf16[2,16,256]{2,1,0:T(8,128)(2,1)S(1)}, u32[]{:S(2)}, u32[]{:S(2)}) collective-permute-start(bf16[2,16,256]{2,1,0:T(8,128)(2,1)S(1)} %get-tuple-element.44), channel_id=1, source_target_pairs={{320,450},{321,451},{322,448},{323,449},{324,454},{325,455},{326,4... | collective-permute-start | bytes 49160 | tf_op jit(solution)/shard_map/ppermute | solution.py:211
  45.2 1.4 %collective-permute-start.38 = (bf16[2,16,256]{2,1,0:T(8,128)(2,1)S(1)}, bf16[2,16,256]{2,1,0:T(8,128)(2,1)S(1)}, u32[]{:S(2)}, u32[]{:S(2)}) collective-permute-start(bf16[2,16,256]{2,1,0:T(8,128)(2,1)S(1)} %get-tuple-element.44), channel_id=1, source_target_pairs={{320,449},{321,448},{322,451},{323,450},{324,453},{325,452},{326,4... | collective-permute-start | bytes 49160 | tf_op jit(solution)/shard_map/ppermute | solution.py:211
  45.9 0.7 collective-permute-start.39
  46.7 2.7 %collective-permute-start.40 = (bf16[2,16,256]{2,1,0:T(8,128)(2,1)S(1)}, bf16[2,16,256]{2,1,0:T(8,128)(2,1)S(1)}, u32[]{:S(2)}, u32[]{:S(2)}) collective-permute-start(bf16[2,16,256]{2,1,0:T(8,128)(2,1)S(1)} %get-tuple-element.47), channel_id=1, source_target_pairs={{129,66},{130,65},{131,68},{132,67},{133,70},{134,69},{135,72},{13... | collective-permute-start | bytes 49160 | tf_op jit(solution)/shard_map/ppermute | solution.py:211
  47.3 2.0 %collective-permute-start.41 = (bf16[2,16,256]{2,1,0:T(8,128)(2,1)S(1)}, bf16[2,16,256]{2,1,0:T(8,128)(2,1)S(1)}, u32[]{:S(2)}, u32[]{:S(2)}) collective-permute-start(bf16[2,16,256]{2,1,0:T(8,128)(2,1)S(1)} %get-tuple-element.47), channel_id=1, source_target_pairs={{128,65},{129,64},{130,67},{131,66},{132,69},{133,68},{134,71},{13... | collective-permute-start | bytes 49160 | tf_op jit(solution)/shard_map/ppermute | solution.py:211
  48.0 1.4 %collective-permute-start.42 = (bf16[2,16,256]{2,1,0:T(8,128)(2,1)S(1)}, bf16[2,16,256]{2,1,0:T(8,128)(2,1)S(1)}, u32[]{:S(2)}, u32[]{:S(2)}) collective-permute-start(bf16[2,16,256]{2,1,0:T(8,128)(2,1)S(1)} %get-tuple-element.47), channel_id=1, source_target_pairs={{128,64},{129,65},{130,66},{131,67},{132,68},{133,69},{134,70},{13... | collective-permute-start | bytes 49160 | tf_op jit(solution)/shard_map/ppermute | solution.py:211
  48.7 0.7 collective-permute-start.43
  49.4 58.1 %collective-permute-start.44 = (bf16[2,16,256]{2,1,0:T(8,128)(2,1)S(1)}, bf16[2,16,256]{2,1,0:T(8,128)(2,1)S(1)}, u32[]{:S(2)}, u32[]{:S(2)}) collective-permute-start(bf16[2,16,256]{2,1,0:T(8,128)(2,1)S(1)} %chosen_kernel.1.kept_ref), channel_id=1, source_target_pairs={{65,2},{66,1},{67,4},{68,3},{69,6},{70,5},{71,8},{72,7},{73,10},{7... | collective-permute-start | bytes 49160 | tf_op jit(solution)/shard_map/ppermute | solution.py:211
  50.7 56.8 %collective-permute-start.45 = (bf16[2,16,256]{2,1,0:T(8,128)(2,1)S(1)}, bf16[2,16,256]{2,1,0:T(8,128)(2,1)S(1)}, u32[]{:S(2)}, u32[]{:S(2)}) collective-permute-start(bf16[2,16,256]{2,1,0:T(8,128)(2,1)S(1)} %chosen_kernel.1.kept_ref), channel_id=1, source_target_pairs={{64,1},{65,0},{66,3},{67,2},{68,5},{69,4},{70,7},{71,6},{72,9},{73... | collective-permute-start | bytes 49160 | tf_op jit(solution)/shard_map/ppermute | solution.py:211
  52.0 55.5 %collective-permute-start.46 = (bf16[2,16,256]{2,1,0:T(8,128)(2,1)S(1)}, bf16[2,16,256]{2,1,0:T(8,128)(2,1)S(1)}, u32[]{:S(2)}, u32[]{:S(2)}) collective-permute-start(bf16[2,16,256]{2,1,0:T(8,128)(2,1)S(1)} %chosen_kernel.1.kept_ref), channel_id=1, source_target_pairs={{64,0},{65,1},{66,2},{67,3},{68,4},{69,5},{70,6},{71,7},{72,8},{73... | collective-permute-start | bytes 49160 | tf_op jit(solution)/shard_map/ppermute | solution.py:211

commit v7 on v6

--- a/solution.py
+++ b/solution.py
@@ -103,12 +103,11 @@
 
 def down_two_kernel(
     layer, first_ref, far_ref, second_ref, near_ref, same_ref, other_far_ref, other_same_ref, other_near_ref,
-    dense_ref, field_ref, next_ref, kept_ref, sent_ref, down_ref, both_ref, *rest,
+    dense_ref, field_ref, next_ref, kept_ref, sent_ref, passed_ref, send_ref, down_ref, wait_ref, mid_ref, pairs_ref,
 ):
-    *more_refs, pairs_ref = rest
     down_ref[...] = kept_ref[...]
-    for ref in more_refs[1:]:
-        ref[...] = sent_ref[...]
+    wait_ref[...] = sent_ref[...]
+    mid_ref[...] = passed_ref[...]
 
     @pl.when(lax.axis_index("depth") == layer)
     def _():
@@ -125,24 +124,19 @@
         window = [plus(field, trace) for field, trace in zip(fields, traces)]
         trace = applied(window, dense_ref).astype(jnp.bfloat16)
         down_ref[...] = trace
-        if more_refs:
-            send_ref, wait_ref = more_refs
-            send_ref[...] = plus(next_ref[...], trace)
-            wait_ref[...] = window[1]
-        both_ref[0] = trace
-        both_ref[1] = traces[1]
-
-
-def turn_kernel(layer, far_ref, near_ref, both_ref, dense_ref, wait_ref, kept_ref, send_ref, up_ref, down_ref):
-    up_ref[...] = kept_ref[...]
+        send_ref[...] = plus(next_ref[...], trace)
+        wait_ref[...] = window[1]
+        mid_ref[...] = traces[1]
+
+
+def turn_kernel(layer, far_ref, near_ref, same_ref, dense_ref, wait_ref, kept_ref, send_ref, down_ref):
     down_ref[...] = kept_ref[...]
 
     @pl.when(lax.axis_index("depth") == layer)
     def _():
-        down_ref[...] = both_ref[1]
-        window = (far_ref[0], both_ref[0], near_ref[0])
-        trace = plus(both_ref[1], applied(window, dense_ref))
-        up_ref[...] = trace
+        window = (far_ref[...], same_ref[...], near_ref[...])
+        trace = applied(window, dense_ref).astype(jnp.bfloat16)
+        down_ref[...] = trace
         send_ref[...] = plus(wait_ref[...], trace)
 
 
@@ -165,23 +159,20 @@
         send_ref[...] = trace if lone else plus(wait_ref[...], trace)
 
 
-def chosen_kernel(layers, up_ref, returned_ref, out_ref):
-    layer = lax.axis_index("depth")
-    out_ref[...] = up_ref[...]
-
-    @pl.when(functools.reduce(jnp.logical_or, [layer == k for k in layers]))
-    def _():
-        out_ref[...] = returned_ref[...]
-
-
-def last_kernel(passed, far_ref, near_ref, same_ref, dense_ref, down_ref, below_ref, kept_ref, up_out_ref, down_out_ref):
+def last_kernel(
+    passed, returned, far_ref, near_ref, same_ref, dense_ref, down_ref, below_ref, kept_ref, back_ref, up_out_ref, down_out_ref
+):
     layer = lax.axis_index("depth")
     up_out_ref[...] = kept_ref[...]
     down_out_ref[...] = down_ref[...]
 
-    @pl.when(layer == passed)
+    @pl.when(functools.reduce(jnp.logical_or, [layer == k for k in passed]))
     def _():
         down_out_ref[...] = below_ref[...]
+
+    @pl.when(functools.reduce(jnp.logical_or, [layer == k for k in returned]))
+    def _():
+        up_out_ref[...] = back_ref[...]
 
     @pl.when(layer == 0)
     def _():
@@ -199,7 +190,7 @@
     _, sources, width = field.shape
     count, parts, size, _ = blocks.shape[1:]
     rows = width // size
-    top, split = layers - 1, layers // 2 - 1
+    top, split = layers - 1, layers // 2 - 2
 
     def sent(value, steps, place):
         pairs = [
@@ -225,12 +216,12 @@
     def second(j):
         return j - 2 if j % 4 > 1 else j + 2
 
-    rounds = [(k, k + 1) for k in range(split)] + [(k, k + 2) for k in range(split, top, 2)]
-    rounds += [(top, top - 1)] + [(k, k - 2) for k in range(top - 1, 2, -2)] + [(2, 1), (1, 0)]
+    rounds = [(k, k + 1) for k in range(split)] + [(k, k + 2) for k in range(split, top - 1, 2)]
+    rounds += [(top - 1, top)] + [(k, k - 2) for k in range(top, 1, -2)] + [(1, 0)]
     wide, narrow = {step: [step] for step in rounds}, {step: [step] for step in rounds}
     if layers == 8:
-        narrow |= {step: [(2, 3), (7, 6)] for step in ((2, 3), (7, 6))}
-        for shared in ([(5, 7), (4, 2)], [(3, 5), (6, 4)]):
+        narrow |= {step: [(0, 1), (6, 7)] for step in ((0, 1), (6, 7))}
+        for shared in ([(2, 4), (7, 5)], [(4, 6), (3, 1)]):
             narrow |= {step: shared for step in shared}
             wide |= {step: shared for step in shared}
 
@@ -288,7 +279,7 @@
             name="hold",
         )(value, *others)
 
-    ups = [(k + 1, k) for k in range(2, top - 1, 2)]
+    ups = [(k + 1, k) for k in range(1, top, 2)]
     downs = [(k, k + 1) for k in range(split + 1, top, 2)]
     given = [*ups, *downs]
     send, down = field, jnp.zeros(field.shape, jnp.bfloat16)
@@ -296,7 +287,7 @@
     for layer in range(split + 1):
         if layer == 1:
             following = hold(following, other_same)
-        if layer == split:
+        if layer == 2:
             following = hold(following, other_near)
         shift = 1 if layer == 2 else 0
         parts = [*window[shift:], *window[:shift]]
@@ -306,29 +297,28 @@
         if layer == 0:
             [load] = step(later_kernel, (payload,), ([k for k, _ in given],), dense, following, send)
             other_far, other_near, other_same = (sent(load, given, place) for place in (far, near, same))
-    for layer in range(split + 2, top + 1, 2):
-        following = hold(following, other_far) if layer < top else following
+    wait, mid = send, jnp.zeros(field.shape, jnp.bfloat16)
+    for layer in range(split + 2, top, 2):
+        following = hold(following, other_far) if layer == split + 2 else following
         window = moved_two(send, layer - 2, layer)
-        down, both, *more = step(
-            down_two_kernel, (one, two, one, one)[: 4 if layer < top else 2], (layer,), *window,
-            other_far, other_same, other_near, dense, field, following, down, send, pairs=True,
+        send, down, wait, mid = step(
+            down_two_kernel, (one,) * 4, (layer,), *window, other_far, other_same, other_near, dense,
+            field, following, down, wait, mid, pairs=True,
         )
-        if layer < top:
-            send, kept = more
-            wait, below = sent(kept, [(2, 4), (5, 6)], same), sent(both[1], [(5, 4)], same)
-    window = moved(both, top, top - 1)
-    send, up, down = step(turn_kernel, (one,) * 3, (top - 1,), *window, dense, wait, down)
-    back = jnp.zeros(field.shape, jnp.bfloat16)
-    for layer in range(top - 3, 1, -2):
+    window = moved(send, top - 1, top)
+    wait = sent(wait, [(1, 3), (4, 5), (6, 7)], same)
+    below = sent(mid, [(4, 3), (6, 5)], same)
+    send, down = step(turn_kernel, (one, one), (top,), *window, dense, wait, down)
+    up, back = down, jnp.zeros(field.shape, jnp.bfloat16)
+    for layer in range(top - 2, 0, -2):
         window = moved_two(send, layer + 2, layer)
         send, up, back = step(
-            up_two_kernel, (one,) * 3, (layer, layer == 2), *window, other_far, other_same, other_near, dense,
+            up_two_kernel, (one,) * 3, (layer, layer == 1), *window, other_far, other_same, other_near, dense,
             down, below, wait, up, back, pairs=True,
         )
-    returned = sent(back, [(to_k, k) for k, to_k in ups], same)
-    [up] = step(up_kernel, (one,), (1,), *moved(send, 2, 1), dense, down, up)
-    [up] = step(chosen_kernel, (one,), ([k for k, _ in ups],), up, returned)
-    up, down = step(last_kernel, (one, one), (split + 1,), *moved(up, 1, 0), dense, down, below, up)
+    window = moved(send, 1, 0)
+    back = sent(back, [(to_k, k) for k, to_k in ups], same)
+    up, down = step(last_kernel, (one, one), ([3, 5], [k for k, _ in ups]), *window, dense, down, below, up, back)
     return (down.reshape(forcing.shape), up.reshape(forcing.shape))
 
 

time: 109 us -> 121 us (1.11)
  the two profiles are of different devices: /device:TPU:62 before, /device:TPU:322 now
where the time goes in v7:
time: 121 us; the launch traced here: 120 us
  starting transfers between devices  58.1 us (48%)
  waiting for transfers between devices  55.2 us (46%)
  local copies, waits for them, and re-layouts  3.1 us (3%)
  Pallas kernels  2.09 us (2%)
  between operations  1.42 us (1%)
    ppermute x46, starting transfers between devices, sent(): return lax.ppermute(value, AXES, pairs)  58.1 us
    ppermute x46, waiting for transfers between devices, sent(): return lax.ppermute(value, AXES, pairs)  55.2 us
    unnamed x8, local copies, waits for them, and re-layouts  3.1 us
  transfers between devices with their start and end apart: 46, of which 8 were waited for; matrix products, arithmetic and copies ran while one was open for 0% of the time, Pallas kernels for 1%

profile of v7, /device:TPU:322, one launch (start us, length us, event | category | flops | bytes accessed | tf_op | source)
XLA Modules:
  0.0 120.0 jit_solution(13681692145049580279)
XLA Ops:
  0.6 1.9 %collective-permute-start = (bf16[2,16,256]{2,1,0:T(8,128)(2,1)}, bf16[2,16,256]{2,1,0:T(8,128)(2,1)S(1)}, u32[]{:S(2)}, u32[]{:S(2)}) collective-permute-start(bf16[2,16,256]{2,1,0:T(8,128)(2,1)} %bitcast.5), channel_id=1, source_target_pairs={{64,0},{65,1},{66,2},{67,3},{68,4},{69,5},{70,6},{71,7},{72,8},{73... | collective-permute-start | bytes 49160 | tf_op jit(solution)/shard_map/ppermute | solution.py:202
  2.6 0.7 collective-permute-start.1
  3.2 0.7 collective-permute-start.2
  3.9 0.6 copy-done.3
  4.6 0.0 copy-start.2
  4.6 0.6 copy-done.2
  5.2 1.1 copy-done
  6.4 1.1 dense.1.refs_3_.dense_ref
  7.4 0.0 copy-start.1
  7.5 0.7 copy-done.1
  8.2 0.1 later_kernel.1
  8.2 2.5 %collective-permute-start.3 = (bf16[784,512]{1,0:T(8,128)(2,1)S(1)}, bf16[784,512]{1,0:T(8,128)(2,1)S(1)}, u32[]{:S(2)}, u32[]{:S(2)}) collective-permute-start(bf16[784,512]{1,0:T(8,128)(2,1)S(1)} %later_kernel.1), channel_id=1, source_target_pairs={{128,64},{129,65},{130,66},{131,67},{132,68},{133,69},{134,70},{13... | collective-permute-start | bytes 2408456 | tf_op jit(solution)/shard_map/ppermute | solution.py:202
  10.8 2.3 %collective-permute-start.4 = (bf16[784,512]{1,0:T(8,128)(2,1)S(1)}, bf16[784,512]{1,0:T(8,128)(2,1)S(1)}, u32[]{:S(2)}, u32[]{:S(2)}) collective-permute-start(bf16[784,512]{1,0:T(8,128)(2,1)S(1)} %later_kernel.1), channel_id=1, source_target_pairs={{128,65},{129,64},{130,67},{131,66},{132,69},{133,68},{134,71},{13... | collective-permute-start | bytes 2408456 | tf_op jit(solution)/shard_map/ppermute | solution.py:202
  13.1 3.2 %collective-permute-start.16 = (bf16[784,512]{1,0:T(8,128)(2,1)S(1)}, bf16[784,512]{1,0:T(8,128)(2,1)S(1)}, u32[]{:S(2)}, u32[]{:S(2)}) collective-permute-start(bf16[784,512]{1,0:T(8,128)(2,1)S(1)} %later_kernel.1), channel_id=1, source_target_pairs={{129,66},{130,65},{131,68},{132,67},{133,70},{134,69},{135,72},{13... | collective-permute-start | bytes 2408456 | tf_op jit(solution)/shard_map/ppermute | solution.py:202
  16.2 0.7 collective-permute-start.5
  16.9 0.7 collective-permute-start.6
  17.6 20.0 %collective-permute-done.3.refs_0_.other_same_ref = bf16[784,512]{1,0:T(8,128)(2,1)S(1)} collective-permute-done((bf16[784,512]{1,0:T(8,128)(2,1)S(1)}, bf16[784,512]{1,0:T(8,128)(2,1)S(1)}, u32[]{:S(2)}, u32[]{:S(2)}) %collective-permute-start.3) | collective-permute-done | bytes 802848 | tf_op jit(solution)/shard_map/ppermute | solution.py:202
  37.6 0.7 collective-permute-start.7
  38.3 1.3 %collective-permute-start.10 = (bf16[2,16,256]{2,1,0:T(8,128)(2,1)S(1)}, bf16[2,16,256]{2,1,0:T(8,128)(2,1)S(1)}, u32[]{:S(2)}, u32[]{:S(2)}) collective-permute-start(bf16[2,16,256]{2,1,0:T(8,128)(2,1)S(1)} %get-tuple-element.31.refs_5_), channel_id=1, source_target_pairs={{65,130},{66,129},{67,132},{68,131},{69,134},{70,133},{71,136},{72... | collective-permute-start | bytes 49160 | tf_op jit(solution)/shard_map/ppermute | solution.py:202
  39.6 1.3 %collective-permute-start.8 = (bf16[2,16,256]{2,1,0:T(8,128)(2,1)S(1)}, bf16[2,16,256]{2,1,0:T(8,128)(2,1)S(1)}, u32[]{:S(2)}, u32[]{:S(2)}) collective-permute-start(bf16[2,16,256]{2,1,0:T(8,128)(2,1)S(1)} %get-tuple-element.31.refs_5_), channel_id=1, source_target_pairs={{64,129},{65,128},{66,131},{67,130},{68,133},{69,132},{70,135},{71... | collective-permute-start | bytes 49160 | tf_op jit(solution)/shard_map/ppermute | solution.py:202
  40.9 1.3 %collective-permute-start.9 = (bf16[2,16,256]{2,1,0:T(8,128)(2,1)S(1)}, bf16[2,16,256]{2,1,0:T(8,128)(2,1)S(1)}, u32[]{:S(2)}, u32[]{:S(2)}) collective-permute-start(bf16[2,16,256]{2,1,0:T(8,128)(2,1)S(1)} %get-tuple-element.31.refs_5_), channel_id=1, source_target_pairs={{64,128},{65,129},{66,130},{67,131},{68,132},{69,133},{70,134},{71... | collective-permute-start | bytes 49160 | tf_op jit(solution)/shard_map/ppermute | solution.py:202
  42.2 14.8 %collective-permute-done.10.refs_2_ = bf16[2,16,256]{2,1,0:T(8,128)(2,1)S(1)} collective-permute-done((bf16[2,16,256]{2,1,0:T(8,128)(2,1)S(1)}, bf16[2,16,256]{2,1,0:T(8,128)(2,1)S(1)}, u32[]{:S(2)}, u32[]{:S(2)}) %collective-permute-start.10) | collective-permute-done | bytes 16416 | tf_op jit(solution)/shard_map/ppermute | solution.py:202
  57.0 0.5 collective-permute-done.9.refs_1_
  57.5 0.2 down_kernel.5
  57.7 1.3 %collective-permute-start.11 = (bf16[2,16,256]{2,1,0:T(8,128)(2,1)S(1)}, bf16[2,16,256]{2,1,0:T(8,128)(2,1)S(1)}, u32[]{:S(2)}, u32[]{:S(2)}) collective-permute-start(bf16[2,16,256]{2,1,0:T(8,128)(2,1)S(1)} %get-tuple-element.33.sent_ref), channel_id=1, source_target_pairs={{130,260},{131,261},{132,258},{133,259},{134,264},{135,265},{136,2... | collective-permute-start | bytes 49160 | tf_op jit(solution)/shard_map/ppermute | solution.py:202
  59.0 1.3 %collective-permute-start.12 = (bf16[2,16,256]{2,1,0:T(8,128)(2,1)S(1)}, bf16[2,16,256]{2,1,0:T(8,128)(2,1)S(1)}, u32[]{:S(2)}, u32[]{:S(2)}) collective-permute-start(bf16[2,16,256]{2,1,0:T(8,128)(2,1)S(1)} %get-tuple-element.33.sent_ref), channel_id=1, source_target_pairs={{129,258},{130,257},{131,260},{132,259},{133,262},{134,261},{135,2... | collective-permute-start | bytes 49160 | tf_op jit(solution)/shard_map/ppermute | solution.py:202
  60.3 1.3 %collective-permute-start.13 = (bf16[2,16,256]{2,1,0:T(8,128)(2,1)S(1)}, bf16[2,16,256]{2,1,0:T(8,128)(2,1)S(1)}, u32[]{:S(2)}, u32[]{:S(2)}) collective-permute-start(bf16[2,16,256]{2,1,0:T(8,128)(2,1)S(1)} %get-tuple-element.33.sent_ref), channel_id=1, source_target_pairs={{128,258},{129,259},{130,256},{131,257},{132,262},{133,263},{134,2... | collective-permute-start | bytes 49160 | tf_op jit(solution)/shard_map/ppermute | solution.py:202
  61.6 1.3 %collective-permute-start.14 = (bf16[2,16,256]{2,1,0:T(8,128)(2,1)S(1)}, bf16[2,16,256]{2,1,0:T(8,128)(2,1)S(1)}, u32[]{:S(2)}, u32[]{:S(2)}) collective-permute-start(bf16[2,16,256]{2,1,0:T(8,128)(2,1)S(1)} %get-tuple-element.33.sent_ref), channel_id=1, source_target_pairs={{128,257},{129,256},{130,259},{131,258},{132,261},{133,260},{134,2... | collective-permute-start | bytes 49160 | tf_op jit(solution)/shard_map/ppermute | solution.py:202
  62.9 1.3 %collective-permute-start.15 = (bf16[2,16,256]{2,1,0:T(8,128)(2,1)S(1)}, bf16[2,16,256]{2,1,0:T(8,128)(2,1)S(1)}, u32[]{:S(2)}, u32[]{:S(2)}) collective-permute-start(bf16[2,16,256]{2,1,0:T(8,128)(2,1)S(1)} %get-tuple-element.33.sent_ref), channel_id=1, source_target_pairs={{128,256},{129,257},{130,258},{131,259},{132,260},{133,261},{134,2... | collective-permute-start | bytes 49160 | tf_op jit(solution)/shard_map/ppermute | solution.py:202
  64.3 0.1 collective-permute-done.14.near_ref
  64.3 1.3 %collective-permute-done.15.same_ref = bf16[2,16,256]{2,1,0:T(8,128)(2,1)S(1)} collective-permute-done((bf16[2,16,256]{2,1,0:T(8,128)(2,1)S(1)}, bf16[2,16,256]{2,1,0:T(8,128)(2,1)S(1)}, u32[]{:S(2)}, u32[]{:S(2)}) %collective-permute-start.15) | collective-permute-done | bytes 16416 | tf_op jit(solution)/shard_map/ppermute | solution.py:202
  65.6 0.7 collective-permute-start.17
  66.3 0.7 collective-permute-start.18
  67.0 0.7 collective-permute-start.19
  67.6 0.7 collective-permute-start.20
  68.3 0.7 collective-permute-start.21
  69.1 0.7 collective-permute-start.22
  69.7 0.7 collective-permute-start.23
  70.4 0.7 collective-permute-start.24
  71.1 0.7 collective-permute-start.25
  71.7 0.7 collective-permute-start.31
  72.5 12.7 %collective-permute-start.26 = (bf16[2,16,256]{2,1,0:T(8,128)(2,1)S(1)}, bf16[2,16,256]{2,1,0:T(8,128)(2,1)S(1)}, u32[]{:S(2)}, u32[]{:S(2)}) collective-permute-start(bf16[2,16,256]{2,1,0:T(8,128)(2,1)S(1)} %get-tuple-element.42), channel_id=1, source_target_pairs={{130,260},{131,261},{132,258},{133,259},{134,264},{135,265},{136,2... | collective-permute-start | bytes 49160 | tf_op jit(solution)/shard_map/ppermute | solution.py:202
  85.2 1.5 %collective-permute-start.27 = (bf16[2,16,256]{2,1,0:T(8,128)(2,1)S(1)}, bf16[2,16,256]{2,1,0:T(8,128)(2,1)S(1)}, u32[]{:S(2)}, u32[]{:S(2)}) collective-permute-start(bf16[2,16,256]{2,1,0:T(8,128)(2,1)S(1)} %get-tuple-element.42), channel_id=1, source_target_pairs={{129,258},{130,257},{131,260},{132,259},{133,262},{134,261},{135,2... | collective-permute-start | bytes 49160 | tf_op jit(solution)/shard_map/ppermute | solution.py:202
  86.7 1.3 %collective-permute-start.28 = (bf16[2,16,256]{2,1,0:T(8,128)(2,1)S(1)}, bf16[2,16,256]{2,1,0:T(8,128)(2,1)S(1)}, u32[]{:S(2)}, u32[]{:S(2)}) collective-permute-start(bf16[2,16,256]{2,1,0:T(8,128)(2,1)S(1)} %get-tuple-element.42), channel_id=1, source_target_pairs={{128,258},{129,259},{130,256},{131,257},{132,262},{133,263},{134,2... | collective-permute-start | bytes 49160 | tf_op jit(solution)/shard_map/ppermute | solution.py:202
  88.0 1.3 %collective-permute-start.29 = (bf16[2,16,256]{2,1,0:T(8,128)(2,1)S(1)}, bf16[2,16,256]{2,1,0:T(8,128)(2,1)S(1)}, u32[]{:S(2)}, u32[]{:S(2)}) collective-permute-start(bf16[2,16,256]{2,1,0:T(8,128)(2,1)S(1)} %get-tuple-element.42), channel_id=1, source_target_pairs={{128,257},{129,256},{130,259},{131,258},{132,261},{133,260},{134,2... | collective-permute-start | bytes 49160 | tf_op jit(solution)/shard_map/ppermute | solution.py:202
  89.3 1.3 %collective-permute-start.30 = (bf16[2,16,256]{2,1,0:T(8,128)(2,1)S(1)}, bf16[2,16,256]{2,1,0:T(8,128)(2,1)S(1)}, u32[]{:S(2)}, u32[]{:S(2)}) collective-permute-start(bf16[2,16,256]{2,1,0:T(8,128)(2,1)S(1)} %get-tuple-element.42), channel_id=1, source_target_pairs={{128,256},{129,257},{130,258},{131,259},{132,260},{133,261},{134,2... | collective-permute-start | bytes 49160 | tf_op jit(solution)/shard_map/ppermute | solution.py:202
  90.6 0.1 collective-permute-done.29.near_ref
  90.7 1.3 %collective-permute-done.30.same_ref = bf16[2,16,256]{2,1,0:T(8,128)(2,1)S(1)} collective-permute-done((bf16[2,16,256]{2,1,0:T(8,128)(2,1)S(1)}, bf16[2,16,256]{2,1,0:T(8,128)(2,1)S(1)}, u32[]{:S(2)}, u32[]{:S(2)}) %collective-permute-start.30) | collective-permute-done | bytes 16416 | tf_op jit(solution)/shard_map/ppermute | solution.py:202
  92.0 0.7 collective-permute-start.32
  92.7 0.7 collective-permute-start.33
  93.4 0.7 collective-permute-start.34
  94.0 0.7 collective-permute-start.35
  94.7 0.7 collective-permute-start.36
  95.5 0.7 collective-permute-start.37
  96.1 0.7 collective-permute-start.38
  96.8 0.7 collective-permute-start.39
  97.5 0.7 collective-permute-start.40
  98.1 0.7 collective-permute-start.41
  98.9 0.7 collective-permute-start.42
  99.6 0.7 collective-permute-start.43
  100.2 0.7 collective-permute-start.44
  100.9 1.3 %collective-permute-start.45 = (bf16[2,16,256]{2,1,0:T(8,128)(2,1)S(1)}, bf16[2,16,256]{2,1,0:T(8,128)(2,1)S(1)}, u32[]{:S(2)}, u32[]{:S(2)}) collective-permute-start(bf16[2,16,256]{2,1,0:T(8,128)(2,1)S(1)} %get-tuple-element.53), channel_id=1, source_target_pairs={{64,128},{65,129},{66,130},{67,131},{68,132},{69,133},{70,134},{71... | collective-permute-start | bytes 49160 | tf_op jit(solution)/shard_map/ppermute | solution.py:202
  102.2 17.1 %collective-permute-done.45.back_ref = bf16[2,16,256]{2,1,0:T(8,128)(2,1)S(1)} collective-permute-done((bf16[2,16,256]{2,1,0:T(8,128)(2,1)S(1)}, bf16[2,16,256]{2,1,0:T(8,128)(2,1)S(1)}, u32[]{:S(2)}, u32[]{:S(2)}) %collective-permute-start.45) | collective-permute-done | bytes 16416 | tf_op jit(solution)/shard_map/ppermute | solution.py:202
  119.4 0.6 last_kernel.1
  (53 shorter events, 0.2 us)
Async XLA Ops:
  0.6 6.8 %collective-permute-start = (bf16[2,16,256]{2,1,0:T(8,128)(2,1)}, bf16[2,16,256]{2,1,0:T(8,128)(2,1)S(1)}, u32[]{:S(2)}, u32[]{:S(2)}) collective-permute-start(bf16[2,16,256]{2,1,0:T(8,128)(2,1)} %bitcast.5), channel_id=1, source_target_pairs={{64,0},{65,1},{66,2},{67,3},{68,4},{69,5},{70,6},{71,7},{72,8},{73... | collective-permute-start | bytes 49160 | tf_op jit(solution)/shard_map/ppermute | solution.py:202
  2.6 4.9 %collective-permute-start.1 = (bf16[2,16,256]{2,1,0:T(8,128)(2,1)}, bf16[2,16,256]{2,1,0:T(8,128)(2,1)S(1)}, u32[]{:S(2)}, u32[]{:S(2)}) collective-permute-start(bf16[2,16,256]{2,1,0:T(8,128)(2,1)} %bitcast.6), channel_id=1, source_target_pairs={{1,2},{2,1},{3,4},{4,3},{5,6},{6,5},{7,8},{8,7},{9,10},{10,9},{11,... | collective-permute-start | bytes 49160 | tf_op jit(solution)/shard_map/ppermute | solution.py:202
  3.2 4.2 %collective-permute-start.2 = (bf16[2,16,256]{2,1,0:T(8,128)(2,1)}, bf16[2,16,256]{2,1,0:T(8,128)(2,1)S(1)}, u32[]{:S(2)}, u32[]{:S(2)}) collective-permute-start(bf16[2,16,256]{2,1,0:T(8,128)(2,1)} %bitcast.7), channel_id=1, source_target_pairs={{0,1},{1,0},{2,3},{3,2},{4,5},{5,4},{6,7},{7,6},{8,9},{9,8},{10,11... | collective-permute-start | bytes 49160 | tf_op jit(solution)/shard_map/ppermute | solution.py:202
  3.9 0.7 copy-start.3
  4.6 0.7 copy-start.2
  5.2 1.1 copy-start
  7.4 0.7 copy-start.1
  8.2 29.4 %collective-permute-start.3 = (bf16[784,512]{1,0:T(8,128)(2,1)S(1)}, bf16[784,512]{1,0:T(8,128)(2,1)S(1)}, u32[]{:S(2)}, u32[]{:S(2)}) collective-permute-start(bf16[784,512]{1,0:T(8,128)(2,1)S(1)} %later_kernel.1), channel_id=1, source_target_pairs={{128,64},{129,65},{130,66},{131,67},{132,68},{133,69},{134,70},{13... | collective-permute-start | bytes 2408456 | tf_op jit(solution)/shard_map/ppermute | solution.py:202
  10.8 31.4 %collective-permute-start.4 = (bf16[784,512]{1,0:T(8,128)(2,1)S(1)}, bf16[784,512]{1,0:T(8,128)(2,1)S(1)}, u32[]{:S(2)}, u32[]{:S(2)}) collective-permute-start(bf16[784,512]{1,0:T(8,128)(2,1)S(1)} %later_kernel.1), channel_id=1, source_target_pairs={{128,65},{129,64},{130,67},{131,66},{132,69},{133,68},{134,71},{13... | collective-permute-start | bytes 2408456 | tf_op jit(solution)/shard_map/ppermute | solution.py:202
  13.1 49.8 %collective-permute-start.16 = (bf16[784,512]{1,0:T(8,128)(2,1)S(1)}, bf16[784,512]{1,0:T(8,128)(2,1)S(1)}, u32[]{:S(2)}, u32[]{:S(2)}) collective-permute-start(bf16[784,512]{1,0:T(8,128)(2,1)S(1)} %later_kernel.1), channel_id=1, source_target_pairs={{129,66},{130,65},{131,68},{132,67},{133,70},{134,69},{135,72},{13... | collective-permute-start | bytes 2408456 | tf_op jit(solution)/shard_map/ppermute | solution.py:202
  16.2 22.0 %collective-permute-start.5 = (bf16[2,16,256]{2,1,0:T(8,128)(2,1)S(1)}, bf16[2,16,256]{2,1,0:T(8,128)(2,1)S(1)}, u32[]{:S(2)}, u32[]{:S(2)}) collective-permute-start(bf16[2,16,256]{2,1,0:T(8,128)(2,1)S(1)} %get-tuple-element.29._after.refs_5_), channel_id=1, source_target_pairs={{1,66},{2,65},{3,68},{4,67},{5,70},{6,69},{7,72},{8,71},{9,74},{10... | collective-permute-start | bytes 49160 | tf_op jit(solution)/shard_map/ppermute | solution.py:202
  16.9 21.4 %collective-permute-start.6 = (bf16[2,16,256]{2,1,0:T(8,128)(2,1)S(1)}, bf16[2,16,256]{2,1,0:T(8,128)(2,1)S(1)}, u32[]{:S(2)}, u32[]{:S(2)}) collective-permute-start(bf16[2,16,256]{2,1,0:T(8,128)(2,1)S(1)} %get-tuple-element.29._after.refs_5_), channel_id=1, source_target_pairs={{0,65},{1,64},{2,67},{3,66},{4,69},{5,68},{6,71},{7,70},{8,73},{9,... | collective-permute-start | bytes 49160 | tf_op jit(solution)/shard_map/ppermute | solution.py:202
  37.6 0.7 collective-permute-start.7
  38.3 18.7 %collective-permute-start.10 = (bf16[2,16,256]{2,1,0:T(8,128)(2,1)S(1)}, bf16[2,16,256]{2,1,0:T(8,128)(2,1)S(1)}, u32[]{:S(2)}, u32[]{:S(2)}) collective-permute-start(bf16[2,16,256]{2,1,0:T(8,128)(2,1)S(1)} %get-tuple-element.31.refs_5_), channel_id=1, source_target_pairs={{65,130},{66,129},{67,132},{68,131},{69,134},{70,133},{71,136},{72... | collective-permute-start | bytes 49160 | tf_op jit(solution)/shard_map/ppermute | solution.py:202
  39.6 17.4 %collective-permute-start.8 = (bf16[2,16,256]{2,1,0:T(8,128)(2,1)S(1)}, bf16[2,16,256]{2,1,0:T(8,128)(2,1)S(1)}, u32[]{:S(2)}, u32[]{:S(2)}) collective-permute-start(bf16[2,16,256]{2,1,0:T(8,128)(2,1)S(1)} %get-tuple-element.31.refs_5_), channel_id=1, source_target_pairs={{64,129},{65,128},{66,131},{67,130},{68,133},{69,132},{70,135},{71... | collective-permute-start | bytes 49160 | tf_op jit(solution)/shard_map/ppermute | solution.py:202
  40.9 16.5 %collective-permute-start.9 = (bf16[2,16,256]{2,1,0:T(8,128)(2,1)S(1)}, bf16[2,16,256]{2,1,0:T(8,128)(2,1)S(1)}, u32[]{:S(2)}, u32[]{:S(2)}) collective-permute-start(bf16[2,16,256]{2,1,0:T(8,128)(2,1)S(1)} %get-tuple-element.31.refs_5_), channel_id=1, source_target_pairs={{64,128},{65,129},{66,130},{67,131},{68,132},{69,133},{70,134},{71... | collective-permute-start | bytes 49160 | tf_op jit(solution)/shard_map/ppermute | solution.py:202
  57.7 6.5 %collective-permute-start.11 = (bf16[2,16,256]{2,1,0:T(8,128)(2,1)S(1)}, bf16[2,16,256]{2,1,0:T(8,128)(2,1)S(1)}, u32[]{:S(2)}, u32[]{:S(2)}) collective-permute-start(bf16[2,16,256]{2,1,0:T(8,128)(2,1)S(1)} %get-tuple-element.33.sent_ref), channel_id=1, source_target_pairs={{130,260},{131,261},{132,258},{133,259},{134,264},{135,265},{136,2... | collective-permute-start | bytes 49160 | tf_op jit(solution)/shard_map/ppermute | solution.py:202
  59.0 5.2 %collective-permute-start.12 = (bf16[2,16,256]{2,1,0:T(8,128)(2,1)S(1)}, bf16[2,16,256]{2,1,0:T(8,128)(2,1)S(1)}, u32[]{:S(2)}, u32[]{:S(2)}) collective-permute-start(bf16[2,16,256]{2,1,0:T(8,128)(2,1)S(1)} %get-tuple-element.33.sent_ref), channel_id=1, source_target_pairs={{129,258},{130,257},{131,260},{132,259},{133,262},{134,261},{135,2... | collective-permute-start | bytes 49160 | tf_op jit(solution)/shard_map/ppermute | solution.py:202
  60.3 3.9 %collective-permute-start.13 = (bf16[2,16,256]{2,1,0:T(8,128)(2,1)S(1)}, bf16[2,16,256]{2,1,0:T(8,128)(2,1)S(1)}, u32[]{:S(2)}, u32[]{:S(2)}) collective-permute-start(bf16[2,16,256]{2,1,0:T(8,128)(2,1)S(1)} %get-tuple-element.33.sent_ref), channel_id=1, source_target_pairs={{128,258},{129,259},{130,256},{131,257},{132,262},{133,263},{134,2... | collective-permute-start | bytes 49160 | tf_op jit(solution)/shard_map/ppermute | solution.py:202
  61.6 2.7 %collective-permute-start.14 = (bf16[2,16,256]{2,1,0:T(8,128)(2,1)S(1)}, bf16[2,16,256]{2,1,0:T(8,128)(2,1)S(1)}, u32[]{:S(2)}, u32[]{:S(2)}) collective-permute-start(bf16[2,16,256]{2,1,0:T(8,128)(2,1)S(1)} %get-tuple-element.33.sent_ref), channel_id=1, source_target_pairs={{128,257},{129,256},{130,259},{131,258},{132,261},{133,260},{134,2... | collective-permute-start | bytes 49160 | tf_op jit(solution)/shard_map/ppermute | solution.py:202
  62.9 2.7 %collective-permute-start.15 = (bf16[2,16,256]{2,1,0:T(8,128)(2,1)S(1)}, bf16[2,16,256]{2,1,0:T(8,128)(2,1)S(1)}, u32[]{:S(2)}, u32[]{:S(2)}) collective-permute-start(bf16[2,16,256]{2,1,0:T(8,128)(2,1)S(1)} %get-tuple-element.33.sent_ref), channel_id=1, source_target_pairs={{128,256},{129,257},{130,258},{131,259},{132,260},{133,261},{134,2... | collective-permute-start | bytes 49160 | tf_op jit(solution)/shard_map/ppermute | solution.py:202
  65.6 3.3 %collective-permute-start.17 = (bf16[2,16,256]{2,1,0:T(8,128)(2,1)S(1)}, bf16[2,16,256]{2,1,0:T(8,128)(2,1)S(1)}, u32[]{:S(2)}, u32[]{:S(2)}) collective-permute-start(bf16[2,16,256]{2,1,0:T(8,128)(2,1)S(1)} %get-tuple-element.35), channel_id=1, source_target_pairs={{258,388},{259,389},{260,386},{261,387},{262,392},{263,393},{264,3... | collective-permute-start | bytes 49160 | tf_op jit(solution)/shard_map/ppermute | solution.py:202
  66.3 2.7 %collective-permute-start.18 = (bf16[2,16,256]{2,1,0:T(8,128)(2,1)S(1)}, bf16[2,16,256]{2,1,0:T(8,128)(2,1)S(1)}, u32[]{:S(2)}, u32[]{:S(2)}) collective-permute-start(bf16[2,16,256]{2,1,0:T(8,128)(2,1)S(1)} %get-tuple-element.35), channel_id=1, source_target_pairs={{257,386},{258,385},{259,388},{260,387},{261,390},{262,389},{263,3... | collective-permute-start | bytes 49160 | tf_op jit(solution)/shard_map/ppermute | solution.py:202
  67.0 2.0 %collective-permute-start.19 = (bf16[2,16,256]{2,1,0:T(8,128)(2,1)S(1)}, bf16[2,16,256]{2,1,0:T(8,128)(2,1)S(1)}, u32[]{:S(2)}, u32[]{:S(2)}) collective-permute-start(bf16[2,16,256]{2,1,0:T(8,128)(2,1)S(1)} %get-tuple-element.35), channel_id=1, source_target_pairs={{256,386},{257,387},{258,384},{259,385},{260,390},{261,391},{262,3... | collective-permute-start | bytes 49160 | tf_op jit(solution)/shard_map/ppermute | solution.py:202
  67.6 1.4 %collective-permute-start.20 = (bf16[2,16,256]{2,1,0:T(8,128)(2,1)S(1)}, bf16[2,16,256]{2,1,0:T(8,128)(2,1)S(1)}, u32[]{:S(2)}, u32[]{:S(2)}) collective-permute-start(bf16[2,16,256]{2,1,0:T(8,128)(2,1)S(1)} %get-tuple-element.35), channel_id=1, source_target_pairs={{256,385},{257,384},{258,387},{259,386},{260,389},{261,388},{262,3... | collective-permute-start | bytes 49160 | tf_op jit(solution)/shard_map/ppermute | solution.py:202
  68.3 0.7 collective-permute-start.21
  69.1 3.4 %collective-permute-start.22 = (bf16[2,16,256]{2,1,0:T(8,128)(2,1)S(1)}, bf16[2,16,256]{2,1,0:T(8,128)(2,1)S(1)}, u32[]{:S(2)}, u32[]{:S(2)}) collective-permute-start(bf16[2,16,256]{2,1,0:T(8,128)(2,1)S(1)} %get-tuple-element.39), channel_id=1, source_target_pairs={{385,450},{386,449},{387,452},{388,451},{389,454},{390,453},{391,4... | collective-permute-start | bytes 49160 | tf_op jit(solution)/shard_map/ppermute | solution.py:202
  69.7 2.7 %collective-permute-start.23 = (bf16[2,16,256]{2,1,0:T(8,128)(2,1)S(1)}, bf16[2,16,256]{2,1,0:T(8,128)(2,1)S(1)}, u32[]{:S(2)}, u32[]{:S(2)}) collective-permute-start(bf16[2,16,256]{2,1,0:T(8,128)(2,1)S(1)} %get-tuple-element.39), channel_id=1, source_target_pairs={{0,65},{1,64},{2,67},{3,66},{4,69},{5,68},{6,71},{7,70},{8,73},{9,... | collective-permute-start | bytes 49160 | tf_op jit(solution)/shard_map/ppermute | solution.py:202
  70.4 2.0 %collective-permute-start.24 = (bf16[2,16,256]{2,1,0:T(8,128)(2,1)S(1)}, bf16[2,16,256]{2,1,0:T(8,128)(2,1)S(1)}, u32[]{:S(2)}, u32[]{:S(2)}) collective-permute-start(bf16[2,16,256]{2,1,0:T(8,128)(2,1)S(1)} %get-tuple-element.39), channel_id=1, source_target_pairs={{0,64},{1,65},{2,66},{3,67},{4,68},{5,69},{6,70},{7,71},{8,72},{9,... | collective-permute-start | bytes 49160 | tf_op jit(solution)/shard_map/ppermute | solution.py:202
  71.1 1.4 %collective-permute-start.25 = (bf16[2,16,256]{2,1,0:T(8,128)(2,1)S(1)}, bf16[2,16,256]{2,1,0:T(8,128)(2,1)S(1)}, u32[]{:S(2)}, u32[]{:S(2)}) collective-permute-start(bf16[2,16,256]{2,1,0:T(8,128)(2,1)S(1)} %get-tuple-element.40), channel_id=1, source_target_pairs={{64,192},{65,193},{66,194},{67,195},{68,196},{69,197},{70,198},{71... | collective-permute-start | bytes 49160 | tf_op jit(solution)/shard_map/ppermute | solution.py:202
  71.7 17.6 %collective-permute-start.31 = (bf16[2,16,256]{2,1,0:T(8,128)(2,1)S(1)}, bf16[2,16,256]{2,1,0:T(8,128)(2,1)S(1)}, u32[]{:S(2)}, u32[]{:S(2)}) collective-permute-start(bf16[2,16,256]{2,1,0:T(8,128)(2,1)S(1)} %get-tuple-element.44), channel_id=1, source_target_pairs={{256,192},{257,193},{258,194},{259,195},{260,196},{261,197},{262,1... | collective-permute-start | bytes 49160 | tf_op jit(solution)/shard_map/ppermute | solution.py:202
  72.5 18.1 %collective-permute-start.26 = (bf16[2,16,256]{2,1,0:T(8,128)(2,1)S(1)}, bf16[2,16,256]{2,1,0:T(8,128)(2,1)S(1)}, u32[]{:S(2)}, u32[]{:S(2)}) collective-permute-start(bf16[2,16,256]{2,1,0:T(8,128)(2,1)S(1)} %get-tuple-element.42), channel_id=1, source_target_pairs={{130,260},{131,261},{132,258},{133,259},{134,264},{135,265},{136,2... | collective-permute-start | bytes 49160 | tf_op jit(solution)/shard_map/ppermute | solution.py:202
  85.2 5.5 %collective-permute-start.27 = (bf16[2,16,256]{2,1,0:T(8,128)(2,1)S(1)}, bf16[2,16,256]{2,1,0:T(8,128)(2,1)S(1)}, u32[]{:S(2)}, u32[]{:S(2)}) collective-permute-start(bf16[2,16,256]{2,1,0:T(8,128)(2,1)S(1)} %get-tuple-element.42), channel_id=1, source_target_pairs={{129,258},{130,257},{131,260},{132,259},{133,262},{134,261},{135,2... | collective-permute-start | bytes 49160 | tf_op jit(solution)/shard_map/ppermute | solution.py:202
  86.7 3.9 %collective-permute-start.28 = (bf16[2,16,256]{2,1,0:T(8,128)(2,1)S(1)}, bf16[2,16,256]{2,1,0:T(8,128)(2,1)S(1)}, u32[]{:S(2)}, u32[]{:S(2)}) collective-permute-start(bf16[2,16,256]{2,1,0:T(8,128)(2,1)S(1)} %get-tuple-element.42), channel_id=1, source_target_pairs={{128,258},{129,259},{130,256},{131,257},{132,262},{133,263},{134,2... | collective-permute-start | bytes 49160 | tf_op jit(solution)/shard_map/ppermute | solution.py:202
  88.0 2.7 %collective-permute-start.29 = (bf16[2,16,256]{2,1,0:T(8,128)(2,1)S(1)}, bf16[2,16,256]{2,1,0:T(8,128)(2,1)S(1)}, u32[]{:S(2)}, u32[]{:S(2)}) collective-permute-start(bf16[2,16,256]{2,1,0:T(8,128)(2,1)S(1)} %get-tuple-element.42), channel_id=1, source_target_pairs={{128,257},{129,256},{130,259},{131,258},{132,261},{133,260},{134,2... | collective-permute-start | bytes 49160 | tf_op jit(solution)/shard_map/ppermute | solution.py:202
  89.3 2.7 %collective-permute-start.30 = (bf16[2,16,256]{2,1,0:T(8,128)(2,1)S(1)}, bf16[2,16,256]{2,1,0:T(8,128)(2,1)S(1)}, u32[]{:S(2)}, u32[]{:S(2)}) collective-permute-start(bf16[2,16,256]{2,1,0:T(8,128)(2,1)S(1)} %get-tuple-element.42), channel_id=1, source_target_pairs={{128,256},{129,257},{130,258},{131,259},{132,260},{133,261},{134,2... | collective-permute-start | bytes 49160 | tf_op jit(solution)/shard_map/ppermute | solution.py:202
  92.0 3.3 %collective-permute-start.32 = (bf16[2,16,256]{2,1,0:T(8,128)(2,1)S(1)}, bf16[2,16,256]{2,1,0:T(8,128)(2,1)S(1)}, u32[]{:S(2)}, u32[]{:S(2)}) collective-permute-start(bf16[2,16,256]{2,1,0:T(8,128)(2,1)S(1)} %get-tuple-element.45), channel_id=1, source_target_pairs={{322,196},{323,197},{324,194},{325,195},{326,200},{327,201},{328,1... | collective-permute-start | bytes 49160 | tf_op jit(solution)/shard_map/ppermute | solution.py:202
  92.7 2.7 %collective-permute-start.33 = (bf16[2,16,256]{2,1,0:T(8,128)(2,1)S(1)}, bf16[2,16,256]{2,1,0:T(8,128)(2,1)S(1)}, u32[]{:S(2)}, u32[]{:S(2)}) collective-permute-start(bf16[2,16,256]{2,1,0:T(8,128)(2,1)S(1)} %get-tuple-element.45), channel_id=1, source_target_pairs={{321,194},{322,193},{323,196},{324,195},{325,198},{326,197},{327,2... | collective-permute-start | bytes 49160 | tf_op jit(solution)/shard_map/ppermute | solution.py:202
  93.4 2.0 %collective-permute-start.34 = (bf16[2,16,256]{2,1,0:T(8,128)(2,1)S(1)}, bf16[2,16,256]{2,1,0:T(8,128)(2,1)S(1)}, u32[]{:S(2)}, u32[]{:S(2)}) collective-permute-start(bf16[2,16,256]{2,1,0:T(8,128)(2,1)S(1)} %get-tuple-element.45), channel_id=1, source_target_pairs={{320,194},{321,195},{322,192},{323,193},{324,198},{325,199},{326,1... | collective-permute-start | bytes 49160 | tf_op jit(solution)/shard_map/ppermute | solution.py:202
  94.0 1.4 %collective-permute-start.35 = (bf16[2,16,256]{2,1,0:T(8,128)(2,1)S(1)}, bf16[2,16,256]{2,1,0:T(8,128)(2,1)S(1)}, u32[]{:S(2)}, u32[]{:S(2)}) collective-permute-start(bf16[2,16,256]{2,1,0:T(8,128)(2,1)S(1)} %get-tuple-element.45), channel_id=1, source_target_pairs={{320,193},{321,192},{322,195},{323,194},{324,197},{325,196},{326,1... | collective-permute-start | bytes 49160 | tf_op jit(solution)/shard_map/ppermute | solution.py:202
  94.7 0.7 collective-permute-start.36
  95.5 3.4 %collective-permute-start.37 = (bf16[2,16,256]{2,1,0:T(8,128)(2,1)S(1)}, bf16[2,16,256]{2,1,0:T(8,128)(2,1)S(1)}, u32[]{:S(2)}, u32[]{:S(2)}) collective-permute-start(bf16[2,16,256]{2,1,0:T(8,128)(2,1)S(1)} %get-tuple-element.48), channel_id=1, source_target_pairs={{258,388},{259,389},{260,386},{261,387},{262,392},{263,393},{264,3... | collective-permute-start | bytes 49160 | tf_op jit(solution)/shard_map/ppermute | solution.py:202
  96.1 2.7 %collective-permute-start.38 = (bf16[2,16,256]{2,1,0:T(8,128)(2,1)S(1)}, bf16[2,16,256]{2,1,0:T(8,128)(2,1)S(1)}, u32[]{:S(2)}, u32[]{:S(2)}) collective-permute-start(bf16[2,16,256]{2,1,0:T(8,128)(2,1)S(1)} %get-tuple-element.48), channel_id=1, source_target_pairs={{257,386},{258,385},{259,388},{260,387},{261,390},{262,389},{263,3... | collective-permute-start | bytes 49160 | tf_op jit(solution)/shard_map/ppermute | solution.py:202
  96.8 2.0 %collective-permute-start.39 = (bf16[2,16,256]{2,1,0:T(8,128)(2,1)S(1)}, bf16[2,16,256]{2,1,0:T(8,128)(2,1)S(1)}, u32[]{:S(2)}, u32[]{:S(2)}) collective-permute-start(bf16[2,16,256]{2,1,0:T(8,128)(2,1)S(1)} %get-tuple-element.48), channel_id=1, source_target_pairs={{256,386},{257,387},{258,384},{259,385},{260,390},{261,391},{262,3... | collective-permute-start | bytes 49160 | tf_op jit(solution)/shard_map/ppermute | solution.py:202
  97.5 1.4 %collective-permute-start.40 = (bf16[2,16,256]{2,1,0:T(8,128)(2,1)S(1)}, bf16[2,16,256]{2,1,0:T(8,128)(2,1)S(1)}, u32[]{:S(2)}, u32[]{:S(2)}) collective-permute-start(bf16[2,16,256]{2,1,0:T(8,128)(2,1)S(1)} %get-tuple-element.48), channel_id=1, source_target_pairs={{256,385},{257,384},{258,387},{259,386},{260,389},{261,388},{262,3... | collective-permute-start | bytes 49160 | tf_op jit(solution)/shard_map/ppermute | solution.py:202
  98.1 0.7 collective-permute-start.41
  98.9 3.3 %collective-permute-start.42 = (bf16[2,16,256]{2,1,0:T(8,128)(2,1)S(1)}, bf16[2,16,256]{2,1,0:T(8,128)(2,1)S(1)}, u32[]{:S(2)}, u32[]{:S(2)}) collective-permute-start(bf16[2,16,256]{2,1,0:T(8,128)(2,1)S(1)} %get-tuple-element.51), channel_id=1, source_target_pairs={{65,2},{66,1},{67,4},{68,3},{69,6},{70,5},{71,8},{72,7},{73,10},{7... | collective-permute-start | bytes 49160 | tf_op jit(solution)/shard_map/ppermute | solution.py:202
  99.6 2.7 %collective-permute-start.43 = (bf16[2,16,256]{2,1,0:T(8,128)(2,1)S(1)}, bf16[2,16,256]{2,1,0:T(8,128)(2,1)S(1)}, u32[]{:S(2)}, u32[]{:S(2)}) collective-permute-start(bf16[2,16,256]{2,1,0:T(8,128)(2,1)S(1)} %get-tuple-element.51), channel_id=1, source_target_pairs={{64,1},{65,0},{66,3},{67,2},{68,5},{69,4},{70,7},{71,6},{72,9},{73... | collective-permute-start | bytes 49160 | tf_op jit(solution)/shard_map/ppermute | solution.py:202
  100.2 2.0 %collective-permute-start.44 = (bf16[2,16,256]{2,1,0:T(8,128)(2,1)S(1)}, bf16[2,16,256]{2,1,0:T(8,128)(2,1)S(1)}, u32[]{:S(2)}, u32[]{:S(2)}) collective-permute-start(bf16[2,16,256]{2,1,0:T(8,128)(2,1)S(1)} %get-tuple-element.51), channel_id=1, source_target_pairs={{64,0},{65,1},{66,2},{67,3},{68,4},{69,5},{70,6},{71,7},{72,8},{73... | collective-permute-start | bytes 49160 | tf_op jit(solution)/shard_map/ppermute | solution.py:202
  100.9 18.5 %collective-permute-start.45 = (bf16[2,16,256]{2,1,0:T(8,128)(2,1)S(1)}, bf16[2,16,256]{2,1,0:T(8,128)(2,1)S(1)}, u32[]{:S(2)}, u32[]{:S(2)}) collective-permute-start(bf16[2,16,256]{2,1,0:T(8,128)(2,1)S(1)} %get-tuple-element.53), channel_id=1, source_target_pairs={{64,128},{65,129},{66,130},{67,131},{68,132},{69,133},{70,134},{71... | collective-permute-start | bytes 49160 | tf_op jit(solution)/shard_map/ppermute | solution.py:202

commit v8 on v6

--- a/solution.py
+++ b/solution.py
@@ -103,10 +103,11 @@
 
 def down_two_kernel(
     layer, first_ref, far_ref, second_ref, near_ref, same_ref, other_far_ref, other_same_ref, other_near_ref,
-    dense_ref, field_ref, next_ref, kept_ref, sent_ref, down_ref, both_ref, *rest,
+    dense_ref, field_ref, next_ref, kept_ref, sent_ref, passed_ref, down_ref, mid_ref, *rest,
 ):
     *more_refs, pairs_ref = rest
     down_ref[...] = kept_ref[...]
+    mid_ref[...] = passed_ref[...]
     for ref in more_refs[1:]:
         ref[...] = sent_ref[...]
 
@@ -129,19 +130,20 @@
             send_ref, wait_ref = more_refs
             send_ref[...] = plus(next_ref[...], trace)
             wait_ref[...] = window[1]
-        both_ref[0] = trace
-        both_ref[1] = traces[1]
-
-
-def turn_kernel(layer, far_ref, near_ref, both_ref, dense_ref, wait_ref, kept_ref, send_ref, up_ref, down_ref):
+        mid_ref[...] = traces[1]
+
+
+def turn_kernel(
+    layer, far_ref, near_ref, same_ref, dense_ref, below_ref, wait_ref, kept_ref, send_ref, up_ref, down_ref
+):
     up_ref[...] = kept_ref[...]
     down_ref[...] = kept_ref[...]
 
     @pl.when(lax.axis_index("depth") == layer)
     def _():
-        down_ref[...] = both_ref[1]
-        window = (far_ref[0], both_ref[0], near_ref[0])
-        trace = plus(both_ref[1], applied(window, dense_ref))
+        down_ref[...] = below_ref[...]
+        window = (far_ref[...], same_ref[...], near_ref[...])
+        trace = plus(below_ref[...], applied(window, dense_ref))
         up_ref[...] = trace
         send_ref[...] = plus(wait_ref[...], trace)
 
@@ -306,18 +308,20 @@
         if layer == 0:
             [load] = step(later_kernel, (payload,), ([k for k, _ in given],), dense, following, send)
             other_far, other_near, other_same = (sent(load, given, place) for place in (far, near, same))
+    mid = jnp.zeros(field.shape, jnp.bfloat16)
     for layer in range(split + 2, top + 1, 2):
         following = hold(following, other_far) if layer < top else following
         window = moved_two(send, layer - 2, layer)
-        down, both, *more = step(
-            down_two_kernel, (one, two, one, one)[: 4 if layer < top else 2], (layer,), *window,
-            other_far, other_same, other_near, dense, field, following, down, send, pairs=True,
+        down, mid, *more = step(
+            down_two_kernel, (one,) * (4 if layer < top else 2), (layer,), *window,
+            other_far, other_same, other_near, dense, field, following, down, send, mid, pairs=True,
         )
         if layer < top:
             send, kept = more
-            wait, below = sent(kept, [(2, 4), (5, 6)], same), sent(both[1], [(5, 4)], same)
-    window = moved(both, top, top - 1)
-    send, up, down = step(turn_kernel, (one,) * 3, (top - 1,), *window, dense, wait, down)
+            wait = sent(kept, [(2, 4), (5, 6)], same)
+    window = moved(down, top, top - 1)
+    below = sent(mid, [(5, 4), (7, 6)], same)
+    send, up, down = step(turn_kernel, (one,) * 3, (top - 1,), *window, dense, below, wait, down)
     back = jnp.zeros(field.shape, jnp.bfloat16)
     for layer in range(top - 3, 1, -2):
         window = moved_two(send, layer + 2, layer)

time: 109 us -> 109 us (level)
  no operation moved by 1% of the time
where the time goes in v8:
time: 109 us
  waiting for transfers between devices  55.6 us (51%)
  starting transfers between devices  46.3 us (42%)
  local copies, waits for them, and re-layouts  2.78 us (3%)
  Pallas kernels  2.38 us (2%)
  between operations  1.48 us (1%)
    ppermute x47, waiting for transfers between devices, sent(): return lax.ppermute(value, AXES, pairs)  55.6 us
    ppermute x47, starting transfers between devices, sent(): return lax.ppermute(value, AXES, pairs)  46.3 us
    unnamed x8, local copies, waits for them, and re-layouts  2.78 us
  transfers between devices with their start and end apart: 47, of which 4 were waited for; matrix products, arithmetic and copies ran while one was open for 0% of the time, Pallas kernels for 1%

profile of v8, /device:TPU:62, one launch (start us, length us, event | category | flops | bytes accessed | tf_op | source)
XLA Modules:
  0.0 108.5 jit_solution(5001883593122174296)
XLA Ops:
  0.6 1.3 %collective-permute-start = (bf16[2,16,256]{2,1,0:T(8,128)(2,1)}, bf16[2,16,256]{2,1,0:T(8,128)(2,1)S(1)}, u32[]{:S(2)}, u32[]{:S(2)}) collective-permute-start(bf16[2,16,256]{2,1,0:T(8,128)(2,1)} %bitcast.5), channel_id=1, source_target_pairs={{64,0},{65,1},{66,2},{67,3},{68,4},{69,5},{70,6},{71,7},{72,8},{73... | collective-permute-start | bytes 49160 | tf_op jit(solution)/shard_map/ppermute | solution.py:213
  1.9 10.0 %collective-permute-start.1 = (bf16[2,16,256]{2,1,0:T(8,128)(2,1)}, bf16[2,16,256]{2,1,0:T(8,128)(2,1)S(1)}, u32[]{:S(2)}, u32[]{:S(2)}) collective-permute-start(bf16[2,16,256]{2,1,0:T(8,128)(2,1)} %bitcast.6), channel_id=1, source_target_pairs={{1,2},{2,1},{3,4},{4,3},{5,6},{6,5},{7,8},{8,7},{9,10},{10,9},{11,... | collective-permute-start | bytes 49160 | tf_op jit(solution)/shard_map/ppermute | solution.py:213
  12.0 1.9 %collective-permute-start.2 = (bf16[2,16,256]{2,1,0:T(8,128)(2,1)}, bf16[2,16,256]{2,1,0:T(8,128)(2,1)S(1)}, u32[]{:S(2)}, u32[]{:S(2)}) collective-permute-start(bf16[2,16,256]{2,1,0:T(8,128)(2,1)} %bitcast.7), channel_id=1, source_target_pairs={{0,1},{1,0},{2,3},{3,2},{4,5},{5,4},{6,7},{7,6},{8,9},{9,8},{10,11... | collective-permute-start | bytes 49160 | tf_op jit(solution)/shard_map/ppermute | solution.py:213
  13.9 0.6 copy-done.3
  14.6 0.0 copy-start.2
  14.6 0.6 copy-done.2
  15.2 1.1 %copy-done = bf16[1,12,2,128,128]{4,3,2,1,0:T(8,128)(2,1)S(1)} copy-done((bf16[1,12,2,128,128]{4,3,2,1,0:T(8,128)(2,1)S(1)}, bf16[1,12,2,128,128]{4,3,2,1,0:T(8,128)(2,1)}, u32[]{:S(2)}) %copy-start) | copy-done | bytes 786456
  16.4 1.1 dense.1.refs_3_.dense_ref
  17.4 0.0 copy-start.1
  17.5 0.3 collective-permute-done.2.refs_1_
  17.8 0.3 copy-done.1
  18.2 0.2 down_kernel.4
  18.4 0.7 collective-permute-start.3
  19.2 0.7 collective-permute-start.4
  19.9 0.7 collective-permute-start.19
  20.6 1.3 %collective-permute-start.5 = (bf16[2,16,256]{2,1,0:T(8,128)(2,1)S(1)}, bf16[2,16,256]{2,1,0:T(8,128)(2,1)S(1)}, u32[]{:S(2)}, u32[]{:S(2)}) collective-permute-start(bf16[2,16,256]{2,1,0:T(8,128)(2,1)S(1)} %get-tuple-element.27._after.refs_5_), channel_id=1, source_target_pairs={{1,66},{2,65},{3,68},{4,67},{5,70},{6,69},{7,72},{8,71},{9,74},{10... | collective-permute-start | bytes 49160 | tf_op jit(solution)/shard_map/ppermute | solution.py:213
  21.9 1.3 %collective-permute-start.6 = (bf16[2,16,256]{2,1,0:T(8,128)(2,1)S(1)}, bf16[2,16,256]{2,1,0:T(8,128)(2,1)S(1)}, u32[]{:S(2)}, u32[]{:S(2)}) collective-permute-start(bf16[2,16,256]{2,1,0:T(8,128)(2,1)S(1)} %get-tuple-element.27._after.refs_5_), channel_id=1, source_target_pairs={{0,65},{1,64},{2,67},{3,66},{4,69},{5,68},{6,71},{7,70},{8,73},{9,... | collective-permute-start | bytes 49160 | tf_op jit(solution)/shard_map/ppermute | solution.py:213
  23.2 0.0 collective-permute-done.3.refs_0_.other_same_ref
  23.2 1.3 %collective-permute-start.7 = (bf16[2,16,256]{2,1,0:T(8,128)(2,1)S(1)}, bf16[2,16,256]{2,1,0:T(8,128)(2,1)S(1)}, u32[]{:S(2)}, u32[]{:S(2)}) collective-permute-start(bf16[2,16,256]{2,1,0:T(8,128)(2,1)S(1)} %get-tuple-element.27._after.refs_5_), channel_id=1, source_target_pairs={{0,64},{1,65},{2,66},{3,67},{4,68},{5,69},{6,70},{7,71},{8,72},{9,... | collective-permute-start | bytes 49160 | tf_op jit(solution)/shard_map/ppermute | solution.py:213
  24.5 0.0 collective-permute-done.5.refs_0_
  24.5 0.1 collective-permute-done.6.refs_1_
  24.6 0.7 collective-permute-done.7.refs_2_
  25.3 0.7 collective-permute-start.10
  26.0 0.7 collective-permute-start.8
  26.7 0.7 collective-permute-start.9
  27.3 0.0 collective-permute-done.10.refs_2_
  27.3 0.0 collective-permute-done.8.refs_0_
  27.4 0.7 collective-permute-start.11
  28.1 0.7 collective-permute-start.12
  28.7 0.7 collective-permute-start.13
  29.5 0.7 collective-permute-start.14
  30.2 0.7 collective-permute-start.15
  30.8 0.7 collective-permute-start.16
  31.5 0.7 collective-permute-start.17
  32.2 0.7 collective-permute-start.18
  32.9 0.7 collective-permute-start.20
  33.6 0.7 collective-permute-start.21
  34.3 0.7 collective-permute-start.22
  34.9 0.7 collective-permute-start.23
  35.6 0.7 collective-permute-start.24
  36.3 0.7 collective-permute-start.29
  37.0 0.7 collective-permute-start.25
  37.7 0.7 collective-permute-start.26
  38.4 0.7 collective-permute-start.27
  39.0 0.7 collective-permute-start.28
  39.8 0.7 collective-permute-start.30
  40.5 0.7 collective-permute-start.31
  41.1 0.7 collective-permute-start.32
  41.8 0.7 collective-permute-start.33
  42.5 0.7 collective-permute-start.34
  43.2 0.7 collective-permute-start.35
  43.9 0.7 collective-permute-start.36
  44.6 0.7 collective-permute-start.37
  45.2 0.7 collective-permute-start.38
  45.9 0.7 collective-permute-start.39
  46.7 0.7 collective-permute-start.40
  47.3 0.7 collective-permute-start.41
  48.0 0.7 collective-permute-start.42
  48.7 0.7 collective-permute-start.43
  49.4 1.3 %collective-permute-start.44 = (bf16[2,16,256]{2,1,0:T(8,128)(2,1)S(1)}, bf16[2,16,256]{2,1,0:T(8,128)(2,1)S(1)}, u32[]{:S(2)}, u32[]{:S(2)}) collective-permute-start(bf16[2,16,256]{2,1,0:T(8,128)(2,1)S(1)} %chosen_kernel.1.kept_ref), channel_id=1, source_target_pairs={{65,2},{66,1},{67,4},{68,3},{69,6},{70,5},{71,8},{72,7},{73,10},{7... | collective-permute-start | bytes 49160 | tf_op jit(solution)/shard_map/ppermute | solution.py:213
  50.7 1.3 %collective-permute-start.45 = (bf16[2,16,256]{2,1,0:T(8,128)(2,1)S(1)}, bf16[2,16,256]{2,1,0:T(8,128)(2,1)S(1)}, u32[]{:S(2)}, u32[]{:S(2)}) collective-permute-start(bf16[2,16,256]{2,1,0:T(8,128)(2,1)S(1)} %chosen_kernel.1.kept_ref), channel_id=1, source_target_pairs={{64,1},{65,0},{66,3},{67,2},{68,5},{69,4},{70,7},{71,6},{72,9},{73... | collective-permute-start | bytes 49160 | tf_op jit(solution)/shard_map/ppermute | solution.py:213
  52.0 1.3 %collective-permute-start.46 = (bf16[2,16,256]{2,1,0:T(8,128)(2,1)S(1)}, bf16[2,16,256]{2,1,0:T(8,128)(2,1)S(1)}, u32[]{:S(2)}, u32[]{:S(2)}) collective-permute-start(bf16[2,16,256]{2,1,0:T(8,128)(2,1)S(1)} %chosen_kernel.1.kept_ref), channel_id=1, source_target_pairs={{64,0},{65,1},{66,2},{67,3},{68,4},{69,5},{70,6},{71,7},{72,8},{73... | collective-permute-start | bytes 49160 | tf_op jit(solution)/shard_map/ppermute | solution.py:213
  53.3 54.3 %collective-permute-done.44.far_ref = bf16[2,16,256]{2,1,0:T(8,128)(2,1)S(1)} collective-permute-done((bf16[2,16,256]{2,1,0:T(8,128)(2,1)S(1)}, bf16[2,16,256]{2,1,0:T(8,128)(2,1)S(1)}, u32[]{:S(2)}, u32[]{:S(2)}) %collective-permute-start.44) | collective-permute-done | bytes 16416 | tf_op jit(solution)/shard_map/ppermute | solution.py:213
  107.7 0.9 last_kernel.1
  (57 shorter events, 0.3 us)
Async XLA Ops:
  0.6 16.8 %collective-permute-start = (bf16[2,16,256]{2,1,0:T(8,128)(2,1)}, bf16[2,16,256]{2,1,0:T(8,128)(2,1)S(1)}, u32[]{:S(2)}, u32[]{:S(2)}) collective-permute-start(bf16[2,16,256]{2,1,0:T(8,128)(2,1)} %bitcast.5), channel_id=1, source_target_pairs={{64,0},{65,1},{66,2},{67,3},{68,4},{69,5},{70,6},{71,7},{72,8},{73... | collective-permute-start | bytes 49160 | tf_op jit(solution)/shard_map/ppermute | solution.py:213
  1.9 15.5 %collective-permute-start.1 = (bf16[2,16,256]{2,1,0:T(8,128)(2,1)}, bf16[2,16,256]{2,1,0:T(8,128)(2,1)S(1)}, u32[]{:S(2)}, u32[]{:S(2)}) collective-permute-start(bf16[2,16,256]{2,1,0:T(8,128)(2,1)} %bitcast.6), channel_id=1, source_target_pairs={{1,2},{2,1},{3,4},{4,3},{5,6},{6,5},{7,8},{8,7},{9,10},{10,9},{11,... | collective-permute-start | bytes 49160 | tf_op jit(solution)/shard_map/ppermute | solution.py:213
  12.0 5.8 %collective-permute-start.2 = (bf16[2,16,256]{2,1,0:T(8,128)(2,1)}, bf16[2,16,256]{2,1,0:T(8,128)(2,1)S(1)}, u32[]{:S(2)}, u32[]{:S(2)}) collective-permute-start(bf16[2,16,256]{2,1,0:T(8,128)(2,1)} %bitcast.7), channel_id=1, source_target_pairs={{0,1},{1,0},{2,3},{3,2},{4,5},{5,4},{6,7},{7,6},{8,9},{9,8},{10,11... | collective-permute-start | bytes 49160 | tf_op jit(solution)/shard_map/ppermute | solution.py:213
  13.9 0.7 copy-start.3
  14.6 0.7 copy-start.2
  15.2 1.1 %copy-start = (bf16[1,12,2,128,128]{4,3,2,1,0:T(8,128)(2,1)S(1)}, bf16[1,12,2,128,128]{4,3,2,1,0:T(8,128)(2,1)}, u32[]{:S(2)}) copy-start(bf16[1,12,2,128,128]{4,3,2,1,0:T(8,128)(2,1)} %param.5) | copy-start | bytes 2359300
  17.4 0.7 copy-start.1
  18.4 4.8 %collective-permute-start.3 = (bf16[784,512]{1,0:T(8,128)(2,1)S(1)}, bf16[784,512]{1,0:T(8,128)(2,1)S(1)}, u32[]{:S(2)}, u32[]{:S(2)}) collective-permute-start(bf16[784,512]{1,0:T(8,128)(2,1)S(1)} %later_kernel.1), channel_id=1, source_target_pairs={{192,128},{193,129},{194,130},{195,131},{196,132},{197,133},{198,1... | collective-permute-start | bytes 2408456 | tf_op jit(solution)/shard_map/ppermute | solution.py:213
  19.2 10.2 %collective-permute-start.4 = (bf16[784,512]{1,0:T(8,128)(2,1)S(1)}, bf16[784,512]{1,0:T(8,128)(2,1)S(1)}, u32[]{:S(2)}, u32[]{:S(2)}) collective-permute-start(bf16[784,512]{1,0:T(8,128)(2,1)S(1)} %later_kernel.1), channel_id=1, source_target_pairs={{192,129},{193,128},{194,131},{195,130},{196,133},{197,132},{198,1... | collective-permute-start | bytes 2408456 | tf_op jit(solution)/shard_map/ppermute | solution.py:213
  19.9 12.3 %collective-permute-start.19 = (bf16[784,512]{1,0:T(8,128)(2,1)S(1)}, bf16[784,512]{1,0:T(8,128)(2,1)S(1)}, u32[]{:S(2)}, u32[]{:S(2)}) collective-permute-start(bf16[784,512]{1,0:T(8,128)(2,1)S(1)} %later_kernel.1), channel_id=1, source_target_pairs={{193,130},{194,129},{195,132},{196,131},{197,134},{198,133},{199,1... | collective-permute-start | bytes 2408456 | tf_op jit(solution)/shard_map/ppermute | solution.py:213
  20.6 3.9 %collective-permute-start.5 = (bf16[2,16,256]{2,1,0:T(8,128)(2,1)S(1)}, bf16[2,16,256]{2,1,0:T(8,128)(2,1)S(1)}, u32[]{:S(2)}, u32[]{:S(2)}) collective-permute-start(bf16[2,16,256]{2,1,0:T(8,128)(2,1)S(1)} %get-tuple-element.27._after.refs_5_), channel_id=1, source_target_pairs={{1,66},{2,65},{3,68},{4,67},{5,70},{6,69},{7,72},{8,71},{9,74},{10... | collective-permute-start | bytes 49160 | tf_op jit(solution)/shard_map/ppermute | solution.py:213
  21.9 2.7 %collective-permute-start.6 = (bf16[2,16,256]{2,1,0:T(8,128)(2,1)S(1)}, bf16[2,16,256]{2,1,0:T(8,128)(2,1)S(1)}, u32[]{:S(2)}, u32[]{:S(2)}) collective-permute-start(bf16[2,16,256]{2,1,0:T(8,128)(2,1)S(1)} %get-tuple-element.27._after.refs_5_), channel_id=1, source_target_pairs={{0,65},{1,64},{2,67},{3,66},{4,69},{5,68},{6,71},{7,70},{8,73},{9,... | collective-permute-start | bytes 49160 | tf_op jit(solution)/shard_map/ppermute | solution.py:213
  23.2 2.1 %collective-permute-start.7 = (bf16[2,16,256]{2,1,0:T(8,128)(2,1)S(1)}, bf16[2,16,256]{2,1,0:T(8,128)(2,1)S(1)}, u32[]{:S(2)}, u32[]{:S(2)}) collective-permute-start(bf16[2,16,256]{2,1,0:T(8,128)(2,1)S(1)} %get-tuple-element.27._after.refs_5_), channel_id=1, source_target_pairs={{0,64},{1,65},{2,66},{3,67},{4,68},{5,69},{6,70},{7,71},{8,72},{9,... | collective-permute-start | bytes 49160 | tf_op jit(solution)/shard_map/ppermute | solution.py:213
  25.3 2.0 %collective-permute-start.10 = (bf16[2,16,256]{2,1,0:T(8,128)(2,1)S(1)}, bf16[2,16,256]{2,1,0:T(8,128)(2,1)S(1)}, u32[]{:S(2)}, u32[]{:S(2)}) collective-permute-start(bf16[2,16,256]{2,1,0:T(8,128)(2,1)S(1)} %get-tuple-element.29.refs_5_), channel_id=1, source_target_pairs={{65,130},{66,129},{67,132},{68,131},{69,134},{70,133},{71,136},{72... | collective-permute-start | bytes 49160 | tf_op jit(solution)/shard_map/ppermute | solution.py:213
  26.0 1.4 %collective-permute-start.8 = (bf16[2,16,256]{2,1,0:T(8,128)(2,1)S(1)}, bf16[2,16,256]{2,1,0:T(8,128)(2,1)S(1)}, u32[]{:S(2)}, u32[]{:S(2)}) collective-permute-start(bf16[2,16,256]{2,1,0:T(8,128)(2,1)S(1)} %get-tuple-element.29.refs_5_), channel_id=1, source_target_pairs={{64,129},{65,128},{66,131},{67,130},{68,133},{69,132},{70,135},{71... | collective-permute-start | bytes 49160 | tf_op jit(solution)/shard_map/ppermute | solution.py:213
  26.7 0.7 collective-permute-start.9
  27.4 2.0 %collective-permute-start.11 = (bf16[2,16,256]{2,1,0:T(8,128)(2,1)S(1)}, bf16[2,16,256]{2,1,0:T(8,128)(2,1)S(1)}, u32[]{:S(2)}, u32[]{:S(2)}) collective-permute-start(bf16[2,16,256]{2,1,0:T(8,128)(2,1)S(1)} %get-tuple-element.31.refs_5_), channel_id=1, source_target_pairs={{129,194},{130,193},{131,196},{132,195},{133,198},{134,197},{135,2... | collective-permute-start | bytes 49160 | tf_op jit(solution)/shard_map/ppermute | solution.py:213
  28.1 1.4 %collective-permute-start.12 = (bf16[2,16,256]{2,1,0:T(8,128)(2,1)S(1)}, bf16[2,16,256]{2,1,0:T(8,128)(2,1)S(1)}, u32[]{:S(2)}, u32[]{:S(2)}) collective-permute-start(bf16[2,16,256]{2,1,0:T(8,128)(2,1)S(1)} %get-tuple-element.31.refs_5_), channel_id=1, source_target_pairs={{128,193},{129,192},{130,195},{131,194},{132,197},{133,196},{134,1... | collective-permute-start | bytes 49160 | tf_op jit(solution)/shard_map/ppermute | solution.py:213
  28.7 0.7 collective-permute-start.13
  29.5 3.4 %collective-permute-start.14 = (bf16[2,16,256]{2,1,0:T(8,128)(2,1)S(1)}, bf16[2,16,256]{2,1,0:T(8,128)(2,1)S(1)}, u32[]{:S(2)}, u32[]{:S(2)}) collective-permute-start(bf16[2,16,256]{2,1,0:T(8,128)(2,1)S(1)} %get-tuple-element.33.sent_ref), channel_id=1, source_target_pairs={{194,324},{195,325},{196,322},{197,323},{198,328},{199,329},{200,3... | collective-permute-start | bytes 49160 | tf_op jit(solution)/shard_map/ppermute | solution.py:213
  30.2 2.7 %collective-permute-start.15 = (bf16[2,16,256]{2,1,0:T(8,128)(2,1)S(1)}, bf16[2,16,256]{2,1,0:T(8,128)(2,1)S(1)}, u32[]{:S(2)}, u32[]{:S(2)}) collective-permute-start(bf16[2,16,256]{2,1,0:T(8,128)(2,1)S(1)} %get-tuple-element.33.sent_ref), channel_id=1, source_target_pairs={{193,322},{194,321},{195,324},{196,323},{197,326},{198,325},{199,3... | collective-permute-start | bytes 49160 | tf_op jit(solution)/shard_map/ppermute | solution.py:213
  30.8 2.1 %collective-permute-start.16 = (bf16[2,16,256]{2,1,0:T(8,128)(2,1)S(1)}, bf16[2,16,256]{2,1,0:T(8,128)(2,1)S(1)}, u32[]{:S(2)}, u32[]{:S(2)}) collective-permute-start(bf16[2,16,256]{2,1,0:T(8,128)(2,1)S(1)} %get-tuple-element.33.sent_ref), channel_id=1, source_target_pairs={{192,322},{193,323},{194,320},{195,321},{196,326},{197,327},{198,3... | collective-permute-start | bytes 49160 | tf_op jit(solution)/shard_map/ppermute | solution.py:213
  31.5 1.4 %collective-permute-start.17 = (bf16[2,16,256]{2,1,0:T(8,128)(2,1)S(1)}, bf16[2,16,256]{2,1,0:T(8,128)(2,1)S(1)}, u32[]{:S(2)}, u32[]{:S(2)}) collective-permute-start(bf16[2,16,256]{2,1,0:T(8,128)(2,1)S(1)} %get-tuple-element.33.sent_ref), channel_id=1, source_target_pairs={{192,321},{193,320},{194,323},{195,322},{196,325},{197,324},{198,3... | collective-permute-start | bytes 49160 | tf_op jit(solution)/shard_map/ppermute | solution.py:213
  32.2 0.7 collective-permute-start.18
  32.9 3.4 %collective-permute-start.20 = (bf16[2,16,256]{2,1,0:T(8,128)(2,1)S(1)}, bf16[2,16,256]{2,1,0:T(8,128)(2,1)S(1)}, u32[]{:S(2)}, u32[]{:S(2)}) collective-permute-start(bf16[2,16,256]{2,1,0:T(8,128)(2,1)S(1)} %get-tuple-element.35.sent_ref), channel_id=1, source_target_pairs={{322,452},{323,453},{324,450},{325,451},{326,456},{327,457},{328,4... | collective-permute-start | bytes 49160 | tf_op jit(solution)/shard_map/ppermute | solution.py:213
  33.6 3.4 %collective-permute-start.21 = (bf16[2,16,256]{2,1,0:T(8,128)(2,1)S(1)}, bf16[2,16,256]{2,1,0:T(8,128)(2,1)S(1)}, u32[]{:S(2)}, u32[]{:S(2)}) collective-permute-start(bf16[2,16,256]{2,1,0:T(8,128)(2,1)S(1)} %get-tuple-element.35.sent_ref), channel_id=1, source_target_pairs={{321,450},{322,449},{323,452},{324,451},{325,454},{326,453},{327,4... | collective-permute-start | bytes 49160 | tf_op jit(solution)/shard_map/ppermute | solution.py:213
  34.3 2.7 %collective-permute-start.22 = (bf16[2,16,256]{2,1,0:T(8,128)(2,1)S(1)}, bf16[2,16,256]{2,1,0:T(8,128)(2,1)S(1)}, u32[]{:S(2)}, u32[]{:S(2)}) collective-permute-start(bf16[2,16,256]{2,1,0:T(8,128)(2,1)S(1)} %get-tuple-element.35.sent_ref), channel_id=1, source_target_pairs={{320,450},{321,451},{322,448},{323,449},{324,454},{325,455},{326,4... | collective-permute-start | bytes 49160 | tf_op jit(solution)/shard_map/ppermute | solution.py:213
  34.9 2.0 %collective-permute-start.23 = (bf16[2,16,256]{2,1,0:T(8,128)(2,1)S(1)}, bf16[2,16,256]{2,1,0:T(8,128)(2,1)S(1)}, u32[]{:S(2)}, u32[]{:S(2)}) collective-permute-start(bf16[2,16,256]{2,1,0:T(8,128)(2,1)S(1)} %get-tuple-element.35.sent_ref), channel_id=1, source_target_pairs={{320,449},{321,448},{322,451},{323,450},{324,453},{325,452},{326,4... | collective-permute-start | bytes 49160 | tf_op jit(solution)/shard_map/ppermute | solution.py:213
  35.6 1.4 %collective-permute-start.24 = (bf16[2,16,256]{2,1,0:T(8,128)(2,1)S(1)}, bf16[2,16,256]{2,1,0:T(8,128)(2,1)S(1)}, u32[]{:S(2)}, u32[]{:S(2)}) collective-permute-start(bf16[2,16,256]{2,1,0:T(8,128)(2,1)S(1)} %get-tuple-element.35.sent_ref), channel_id=1, source_target_pairs={{320,448},{321,449},{322,450},{323,451},{324,452},{325,453},{326,4... | collective-permute-start | bytes 49160 | tf_op jit(solution)/shard_map/ppermute | solution.py:213
  36.3 3.4 %collective-permute-start.29 = (bf16[2,16,256]{2,1,0:T(8,128)(2,1)S(1)}, bf16[2,16,256]{2,1,0:T(8,128)(2,1)S(1)}, u32[]{:S(2)}, u32[]{:S(2)}) collective-permute-start(bf16[2,16,256]{2,1,0:T(8,128)(2,1)S(1)} %get-tuple-element.40), channel_id=1, source_target_pairs={{128,256},{129,257},{130,258},{131,259},{132,260},{133,261},{134,2... | collective-permute-start | bytes 49160 | tf_op jit(solution)/shard_map/ppermute | solution.py:213
  37.0 2.7 %collective-permute-start.25 = (bf16[2,16,256]{2,1,0:T(8,128)(2,1)S(1)}, bf16[2,16,256]{2,1,0:T(8,128)(2,1)S(1)}, u32[]{:S(2)}, u32[]{:S(2)}) collective-permute-start(bf16[2,16,256]{2,1,0:T(8,128)(2,1)S(1)} %get-tuple-element.38.kept_ref), channel_id=1, source_target_pairs={{449,386},{450,385},{451,388},{452,387},{453,390},{454,389},{455,3... | collective-permute-start | bytes 49160 | tf_op jit(solution)/shard_map/ppermute | solution.py:213
  37.7 2.0 %collective-permute-start.26 = (bf16[2,16,256]{2,1,0:T(8,128)(2,1)S(1)}, bf16[2,16,256]{2,1,0:T(8,128)(2,1)S(1)}, u32[]{:S(2)}, u32[]{:S(2)}) collective-permute-start(bf16[2,16,256]{2,1,0:T(8,128)(2,1)S(1)} %get-tuple-element.38.kept_ref), channel_id=1, source_target_pairs={{128,193},{129,192},{130,195},{131,194},{132,197},{133,196},{134,1... | collective-permute-start | bytes 49160 | tf_op jit(solution)/shard_map/ppermute | solution.py:213
  38.4 1.4 %collective-permute-start.27 = (bf16[2,16,256]{2,1,0:T(8,128)(2,1)S(1)}, bf16[2,16,256]{2,1,0:T(8,128)(2,1)S(1)}, u32[]{:S(2)}, u32[]{:S(2)}) collective-permute-start(bf16[2,16,256]{2,1,0:T(8,128)(2,1)S(1)} %get-tuple-element.38.kept_ref), channel_id=1, source_target_pairs={{128,192},{129,193},{130,194},{131,195},{132,196},{133,197},{134,1... | collective-permute-start | bytes 49160 | tf_op jit(solution)/shard_map/ppermute | solution.py:213
  39.0 0.7 collective-permute-start.28
  39.8 3.4 %collective-permute-start.30 = (bf16[2,16,256]{2,1,0:T(8,128)(2,1)S(1)}, bf16[2,16,256]{2,1,0:T(8,128)(2,1)S(1)}, u32[]{:S(2)}, u32[]{:S(2)}) collective-permute-start(bf16[2,16,256]{2,1,0:T(8,128)(2,1)S(1)} %get-tuple-element.41), channel_id=1, source_target_pairs={{194,324},{195,325},{196,322},{197,323},{198,328},{199,329},{200,3... | collective-permute-start | bytes 49160 | tf_op jit(solution)/shard_map/ppermute | solution.py:213
  40.5 2.7 %collective-permute-start.31 = (bf16[2,16,256]{2,1,0:T(8,128)(2,1)S(1)}, bf16[2,16,256]{2,1,0:T(8,128)(2,1)S(1)}, u32[]{:S(2)}, u32[]{:S(2)}) collective-permute-start(bf16[2,16,256]{2,1,0:T(8,128)(2,1)S(1)} %get-tuple-element.41), channel_id=1, source_target_pairs={{193,322},{194,321},{195,324},{196,323},{197,326},{198,325},{199,3... | collective-permute-start | bytes 49160 | tf_op jit(solution)/shard_map/ppermute | solution.py:213
  41.1 2.0 %collective-permute-start.32 = (bf16[2,16,256]{2,1,0:T(8,128)(2,1)S(1)}, bf16[2,16,256]{2,1,0:T(8,128)(2,1)S(1)}, u32[]{:S(2)}, u32[]{:S(2)}) collective-permute-start(bf16[2,16,256]{2,1,0:T(8,128)(2,1)S(1)} %get-tuple-element.41), channel_id=1, source_target_pairs={{192,322},{193,323},{194,320},{195,321},{196,326},{197,327},{198,3... | collective-permute-start | bytes 49160 | tf_op jit(solution)/shard_map/ppermute | solution.py:213
  41.8 1.4 %collective-permute-start.33 = (bf16[2,16,256]{2,1,0:T(8,128)(2,1)S(1)}, bf16[2,16,256]{2,1,0:T(8,128)(2,1)S(1)}, u32[]{:S(2)}, u32[]{:S(2)}) collective-permute-start(bf16[2,16,256]{2,1,0:T(8,128)(2,1)S(1)} %get-tuple-element.41), channel_id=1, source_target_pairs={{192,321},{193,320},{194,323},{195,322},{196,325},{197,324},{198,3... | collective-permute-start | bytes 49160 | tf_op jit(solution)/shard_map/ppermute | solution.py:213
  42.5 0.7 collective-permute-start.34
  43.2 3.4 %collective-permute-start.35 = (bf16[2,16,256]{2,1,0:T(8,128)(2,1)S(1)}, bf16[2,16,256]{2,1,0:T(8,128)(2,1)S(1)}, u32[]{:S(2)}, u32[]{:S(2)}) collective-permute-start(bf16[2,16,256]{2,1,0:T(8,128)(2,1)S(1)} %get-tuple-element.44), channel_id=1, source_target_pairs={{322,452},{323,453},{324,450},{325,451},{326,456},{327,457},{328,4... | collective-permute-start | bytes 49160 | tf_op jit(solution)/shard_map/ppermute | solution.py:213
  43.9 2.7 %collective-permute-start.36 = (bf16[2,16,256]{2,1,0:T(8,128)(2,1)S(1)}, bf16[2,16,256]{2,1,0:T(8,128)(2,1)S(1)}, u32[]{:S(2)}, u32[]{:S(2)}) collective-permute-start(bf16[2,16,256]{2,1,0:T(8,128)(2,1)S(1)} %get-tuple-element.44), channel_id=1, source_target_pairs={{321,450},{322,449},{323,452},{324,451},{325,454},{326,453},{327,4... | collective-permute-start | bytes 49160 | tf_op jit(solution)/shard_map/ppermute | solution.py:213
  44.6 2.0 %collective-permute-start.37 = (bf16[2,16,256]{2,1,0:T(8,128)(2,1)S(1)}, bf16[2,16,256]{2,1,0:T(8,128)(2,1)S(1)}, u32[]{:S(2)}, u32[]{:S(2)}) collective-permute-start(bf16[2,16,256]{2,1,0:T(8,128)(2,1)S(1)} %get-tuple-element.44), channel_id=1, source_target_pairs={{320,450},{321,451},{322,448},{323,449},{324,454},{325,455},{326,4... | collective-permute-start | bytes 49160 | tf_op jit(solution)/shard_map/ppermute | solution.py:213
  45.2 1.4 %collective-permute-start.38 = (bf16[2,16,256]{2,1,0:T(8,128)(2,1)S(1)}, bf16[2,16,256]{2,1,0:T(8,128)(2,1)S(1)}, u32[]{:S(2)}, u32[]{:S(2)}) collective-permute-start(bf16[2,16,256]{2,1,0:T(8,128)(2,1)S(1)} %get-tuple-element.44), channel_id=1, source_target_pairs={{320,449},{321,448},{322,451},{323,450},{324,453},{325,452},{326,4... | collective-permute-start | bytes 49160 | tf_op jit(solution)/shard_map/ppermute | solution.py:213
  45.9 0.7 collective-permute-start.39
  46.7 2.7 %collective-permute-start.40 = (bf16[2,16,256]{2,1,0:T(8,128)(2,1)S(1)}, bf16[2,16,256]{2,1,0:T(8,128)(2,1)S(1)}, u32[]{:S(2)}, u32[]{:S(2)}) collective-permute-start(bf16[2,16,256]{2,1,0:T(8,128)(2,1)S(1)} %get-tuple-element.47), channel_id=1, source_target_pairs={{129,66},{130,65},{131,68},{132,67},{133,70},{134,69},{135,72},{13... | collective-permute-start | bytes 49160 | tf_op jit(solution)/shard_map/ppermute | solution.py:213
  47.3 2.0 %collective-permute-start.41 = (bf16[2,16,256]{2,1,0:T(8,128)(2,1)S(1)}, bf16[2,16,256]{2,1,0:T(8,128)(2,1)S(1)}, u32[]{:S(2)}, u32[]{:S(2)}) collective-permute-start(bf16[2,16,256]{2,1,0:T(8,128)(2,1)S(1)} %get-tuple-element.47), channel_id=1, source_target_pairs={{128,65},{129,64},{130,67},{131,66},{132,69},{133,68},{134,71},{13... | collective-permute-start | bytes 49160 | tf_op jit(solution)/shard_map/ppermute | solution.py:213
  48.0 1.4 %collective-permute-start.42 = (bf16[2,16,256]{2,1,0:T(8,128)(2,1)S(1)}, bf16[2,16,256]{2,1,0:T(8,128)(2,1)S(1)}, u32[]{:S(2)}, u32[]{:S(2)}) collective-permute-start(bf16[2,16,256]{2,1,0:T(8,128)(2,1)S(1)} %get-tuple-element.47), channel_id=1, source_target_pairs={{128,64},{129,65},{130,66},{131,67},{132,68},{133,69},{134,70},{13... | collective-permute-start | bytes 49160 | tf_op jit(solution)/shard_map/ppermute | solution.py:213
  48.7 0.7 collective-permute-start.43
  49.4 58.2 %collective-permute-start.44 = (bf16[2,16,256]{2,1,0:T(8,128)(2,1)S(1)}, bf16[2,16,256]{2,1,0:T(8,128)(2,1)S(1)}, u32[]{:S(2)}, u32[]{:S(2)}) collective-permute-start(bf16[2,16,256]{2,1,0:T(8,128)(2,1)S(1)} %chosen_kernel.1.kept_ref), channel_id=1, source_target_pairs={{65,2},{66,1},{67,4},{68,3},{69,6},{70,5},{71,8},{72,7},{73,10},{7... | collective-permute-start | bytes 49160 | tf_op jit(solution)/shard_map/ppermute | solution.py:213
  50.7 56.9 %collective-permute-start.45 = (bf16[2,16,256]{2,1,0:T(8,128)(2,1)S(1)}, bf16[2,16,256]{2,1,0:T(8,128)(2,1)S(1)}, u32[]{:S(2)}, u32[]{:S(2)}) collective-permute-start(bf16[2,16,256]{2,1,0:T(8,128)(2,1)S(1)} %chosen_kernel.1.kept_ref), channel_id=1, source_target_pairs={{64,1},{65,0},{66,3},{67,2},{68,5},{69,4},{70,7},{71,6},{72,9},{73... | collective-permute-start | bytes 49160 | tf_op jit(solution)/shard_map/ppermute | solution.py:213
  52.0 55.6 %collective-permute-start.46 = (bf16[2,16,256]{2,1,0:T(8,128)(2,1)S(1)}, bf16[2,16,256]{2,1,0:T(8,128)(2,1)S(1)}, u32[]{:S(2)}, u32[]{:S(2)}) collective-permute-start(bf16[2,16,256]{2,1,0:T(8,128)(2,1)S(1)} %chosen_kernel.1.kept_ref), channel_id=1, source_target_pairs={{64,0},{65,1},{66,2},{67,3},{68,4},{69,5},{70,6},{71,7},{72,8},{73... | collective-permute-start | bytes 49160 | tf_op jit(solution)/shard_map/ppermute | solution.py:213

commit v9 on v8

--- a/solution.py
+++ b/solution.py
@@ -102,9 +102,11 @@
 
 
 def down_two_kernel(
-    layer, first_ref, far_ref, second_ref, near_ref, same_ref, other_far_ref, other_same_ref, other_near_ref,
+    layer, swapped, first_ref, far_ref, second_ref, near_ref, same_ref, other_far_ref, other_same_ref, other_near_ref,
     dense_ref, field_ref, next_ref, kept_ref, sent_ref, passed_ref, down_ref, mid_ref, *rest,
 ):
+    if swapped:
+        first_ref, far_ref = far_ref, first_ref
     *more_refs, pairs_ref = rest
     down_ref[...] = kept_ref[...]
     mid_ref[...] = passed_ref[...]
@@ -149,9 +151,11 @@
 
 
 def up_two_kernel(
-    layer, lone, first_ref, far_ref, second_ref, near_ref, same_ref, other_far_ref, other_same_ref, other_near_ref,
+    layer, lone, swapped, first_ref, far_ref, second_ref, near_ref, same_ref, other_far_ref, other_same_ref, other_near_ref,
     dense_ref, down_ref, below_ref, wait_ref, kept_ref, other_ref, send_ref, up_ref, back_ref, pairs_ref,
 ):
+    if swapped:
+        first_ref, far_ref = far_ref, first_ref
     up_ref[...] = kept_ref[...]
     back_ref[...] = other_ref[...]
 
@@ -242,9 +246,9 @@
 
     def moved_two(value, k, to_k):
         outer, inner = wide[k, to_k], narrow[k, to_k]
+        long = [sent(value, outer, first), sent(value, outer, far)]
         return (
-            sent(value, outer, first),
-            sent(value, outer, far),
+            *(long[::-1] if to_k in (2, top) else long),
             sent(value, outer, second),
             sent(value, inner, near),
             sent(value, inner, same),
@@ -313,7 +317,7 @@
         following = hold(following, other_far) if layer < top else following
         window = moved_two(send, layer - 2, layer)
         down, mid, *more = step(
-            down_two_kernel, (one,) * (4 if layer < top else 2), (layer,), *window,
+            down_two_kernel, (one,) * (4 if layer < top else 2), (layer, layer == top), *window,
             other_far, other_same, other_near, dense, field, following, down, send, mid, pairs=True,
         )
         if layer < top:
@@ -326,7 +330,7 @@
     for layer in range(top - 3, 1, -2):
         window = moved_two(send, layer + 2, layer)
         send, up, back = step(
-            up_two_kernel, (one,) * 3, (layer, layer == 2), *window, other_far, other_same, other_near, dense,
+            up_two_kernel, (one,) * 3, (layer, layer == 2, layer == 2), *window, other_far, other_same, other_near, dense,
             down, below, wait, up, back, pairs=True,
         )
     returned = sent(back, [(to_k, k) for k, to_k in ups], same)

time: 109 us -> 110 us (level)
  no operation moved by 1% of the time
where the time goes in v9:
time: 110 us
  waiting for transfers between devices  56.6 us (51%)
  starting transfers between devices  46.3 us (42%)
  local copies, waits for them, and re-layouts  2.78 us (3%)
  Pallas kernels  2.37 us (2%)
  between operations  1.48 us (1%)
    ppermute x47, waiting for transfers between devices, sent(): return lax.ppermute(value, AXES, pairs)  56.6 us
    ppermute x47, starting transfers between devices, sent(): return lax.ppermute(value, AXES, pairs)  46.3 us
    unnamed x8, local copies, waits for them, and re-layouts  2.78 us
  transfers between devices with their start and end apart: 47, of which 4 were waited for; matrix products, arithmetic and copies ran while one was open for 0% of the time, Pallas kernels for 1%

profile of v9, /device:TPU:62, one launch (start us, length us, event | category | flops | bytes accessed | tf_op | source)
XLA Modules:
  0.0 109.5 jit_solution(7796969550060371620)
XLA Ops:
  0.6 1.3 %collective-permute-start = (bf16[2,16,256]{2,1,0:T(8,128)(2,1)}, bf16[2,16,256]{2,1,0:T(8,128)(2,1)S(1)}, u32[]{:S(2)}, u32[]{:S(2)}) collective-permute-start(bf16[2,16,256]{2,1,0:T(8,128)(2,1)} %bitcast.5), channel_id=1, source_target_pairs={{64,0},{65,1},{66,2},{67,3},{68,4},{69,5},{70,6},{71,7},{72,8},{73... | collective-permute-start | bytes 49160 | tf_op jit(solution)/shard_map/ppermute | solution.py:217
  1.9 10.0 %collective-permute-start.1 = (bf16[2,16,256]{2,1,0:T(8,128)(2,1)}, bf16[2,16,256]{2,1,0:T(8,128)(2,1)S(1)}, u32[]{:S(2)}, u32[]{:S(2)}) collective-permute-start(bf16[2,16,256]{2,1,0:T(8,128)(2,1)} %bitcast.6), channel_id=1, source_target_pairs={{1,2},{2,1},{3,4},{4,3},{5,6},{6,5},{7,8},{8,7},{9,10},{10,9},{11,... | collective-permute-start | bytes 49160 | tf_op jit(solution)/shard_map/ppermute | solution.py:217
  12.0 1.9 %collective-permute-start.2 = (bf16[2,16,256]{2,1,0:T(8,128)(2,1)}, bf16[2,16,256]{2,1,0:T(8,128)(2,1)S(1)}, u32[]{:S(2)}, u32[]{:S(2)}) collective-permute-start(bf16[2,16,256]{2,1,0:T(8,128)(2,1)} %bitcast.7), channel_id=1, source_target_pairs={{0,1},{1,0},{2,3},{3,2},{4,5},{5,4},{6,7},{7,6},{8,9},{9,8},{10,11... | collective-permute-start | bytes 49160 | tf_op jit(solution)/shard_map/ppermute | solution.py:217
  13.9 0.6 copy-done.3
  14.6 0.0 copy-start.2
  14.6 0.6 copy-done.2
  15.2 1.1 %copy-done = bf16[1,12,2,128,128]{4,3,2,1,0:T(8,128)(2,1)S(1)} copy-done((bf16[1,12,2,128,128]{4,3,2,1,0:T(8,128)(2,1)S(1)}, bf16[1,12,2,128,128]{4,3,2,1,0:T(8,128)(2,1)}, u32[]{:S(2)}) %copy-start) | copy-done | bytes 786456
  16.4 1.1 dense.1.refs_3_.dense_ref
  17.4 0.0 copy-start.1
  17.5 0.0 collective-permute-done.1.refs_0_
  17.5 0.3 collective-permute-done.2.refs_1_
  17.8 0.3 copy-done.1
  18.2 0.2 down_kernel.4
  18.4 0.7 collective-permute-start.3
  19.2 0.7 collective-permute-start.4
  19.9 0.7 collective-permute-start.19
  20.6 1.3 %collective-permute-start.5 = (bf16[2,16,256]{2,1,0:T(8,128)(2,1)S(1)}, bf16[2,16,256]{2,1,0:T(8,128)(2,1)S(1)}, u32[]{:S(2)}, u32[]{:S(2)}) collective-permute-start(bf16[2,16,256]{2,1,0:T(8,128)(2,1)S(1)} %get-tuple-element.27._after.refs_5_), channel_id=1, source_target_pairs={{1,66},{2,65},{3,68},{4,67},{5,70},{6,69},{7,72},{8,71},{9,74},{10... | collective-permute-start | bytes 49160 | tf_op jit(solution)/shard_map/ppermute | solution.py:217
  21.9 1.3 %collective-permute-start.6 = (bf16[2,16,256]{2,1,0:T(8,128)(2,1)S(1)}, bf16[2,16,256]{2,1,0:T(8,128)(2,1)S(1)}, u32[]{:S(2)}, u32[]{:S(2)}) collective-permute-start(bf16[2,16,256]{2,1,0:T(8,128)(2,1)S(1)} %get-tuple-element.27._after.refs_5_), channel_id=1, source_target_pairs={{0,65},{1,64},{2,67},{3,66},{4,69},{5,68},{6,71},{7,70},{8,73},{9,... | collective-permute-start | bytes 49160 | tf_op jit(solution)/shard_map/ppermute | solution.py:217
  23.2 0.0 collective-permute-done.3.refs_0_.other_same_ref
  23.2 1.3 %collective-permute-start.7 = (bf16[2,16,256]{2,1,0:T(8,128)(2,1)S(1)}, bf16[2,16,256]{2,1,0:T(8,128)(2,1)S(1)}, u32[]{:S(2)}, u32[]{:S(2)}) collective-permute-start(bf16[2,16,256]{2,1,0:T(8,128)(2,1)S(1)} %get-tuple-element.27._after.refs_5_), channel_id=1, source_target_pairs={{0,64},{1,65},{2,66},{3,67},{4,68},{5,69},{6,70},{7,71},{8,72},{9,... | collective-permute-start | bytes 49160 | tf_op jit(solution)/shard_map/ppermute | solution.py:217
  24.5 0.0 collective-permute-done.5.refs_0_
  24.5 0.1 collective-permute-done.6.refs_1_
  24.6 0.7 collective-permute-done.7.refs_2_
  25.3 0.7 collective-permute-start.10
  26.0 0.7 collective-permute-start.8
  26.7 0.7 collective-permute-start.9
  27.3 0.0 collective-permute-done.10.refs_2_
  27.4 0.7 collective-permute-start.11
  28.1 0.7 collective-permute-start.12
  28.7 0.7 collective-permute-start.13
  29.5 0.7 collective-permute-start.14
  30.2 0.7 collective-permute-start.15
  30.8 0.7 collective-permute-start.16
  31.5 0.7 collective-permute-start.17
  32.2 0.7 collective-permute-start.18
  32.9 0.7 collective-permute-start.20
  33.6 0.7 collective-permute-start.21
  34.3 0.7 collective-permute-start.22
  34.9 0.7 collective-permute-start.23
  35.6 0.7 collective-permute-start.24
  36.3 0.7 collective-permute-start.29
  37.0 0.7 collective-permute-start.25
  37.7 0.7 collective-permute-start.26
  38.4 0.7 collective-permute-start.27
  39.0 0.7 collective-permute-start.28
  39.8 0.7 collective-permute-start.30
  40.5 0.7 collective-permute-start.31
  41.1 0.7 collective-permute-start.32
  41.8 0.7 collective-permute-start.33
  42.5 0.7 collective-permute-start.34
  43.2 0.7 collective-permute-start.35
  43.9 0.7 collective-permute-start.36
  44.6 0.7 collective-permute-start.37
  45.2 0.7 collective-permute-start.38
  45.9 0.7 collective-permute-start.39
  46.7 0.7 collective-permute-start.40
  47.3 0.7 collective-permute-start.41
  48.0 0.7 collective-permute-start.42
  48.7 0.7 collective-permute-start.43
  49.4 1.3 %collective-permute-start.44 = (bf16[2,16,256]{2,1,0:T(8,128)(2,1)S(1)}, bf16[2,16,256]{2,1,0:T(8,128)(2,1)S(1)}, u32[]{:S(2)}, u32[]{:S(2)}) collective-permute-start(bf16[2,16,256]{2,1,0:T(8,128)(2,1)S(1)} %chosen_kernel.1.kept_ref), channel_id=1, source_target_pairs={{65,2},{66,1},{67,4},{68,3},{69,6},{70,5},{71,8},{72,7},{73,10},{7... | collective-permute-start | bytes 49160 | tf_op jit(solution)/shard_map/ppermute | solution.py:217
  50.7 1.3 %collective-permute-start.45 = (bf16[2,16,256]{2,1,0:T(8,128)(2,1)S(1)}, bf16[2,16,256]{2,1,0:T(8,128)(2,1)S(1)}, u32[]{:S(2)}, u32[]{:S(2)}) collective-permute-start(bf16[2,16,256]{2,1,0:T(8,128)(2,1)S(1)} %chosen_kernel.1.kept_ref), channel_id=1, source_target_pairs={{64,1},{65,0},{66,3},{67,2},{68,5},{69,4},{70,7},{71,6},{72,9},{73... | collective-permute-start | bytes 49160 | tf_op jit(solution)/shard_map/ppermute | solution.py:217
  52.0 1.3 %collective-permute-start.46 = (bf16[2,16,256]{2,1,0:T(8,128)(2,1)S(1)}, bf16[2,16,256]{2,1,0:T(8,128)(2,1)S(1)}, u32[]{:S(2)}, u32[]{:S(2)}) collective-permute-start(bf16[2,16,256]{2,1,0:T(8,128)(2,1)S(1)} %chosen_kernel.1.kept_ref), channel_id=1, source_target_pairs={{64,0},{65,1},{66,2},{67,3},{68,4},{69,5},{70,6},{71,7},{72,8},{73... | collective-permute-start | bytes 49160 | tf_op jit(solution)/shard_map/ppermute | solution.py:217
  53.3 55.3 %collective-permute-done.44.far_ref = bf16[2,16,256]{2,1,0:T(8,128)(2,1)S(1)} collective-permute-done((bf16[2,16,256]{2,1,0:T(8,128)(2,1)S(1)}, bf16[2,16,256]{2,1,0:T(8,128)(2,1)S(1)}, u32[]{:S(2)}, u32[]{:S(2)}) %collective-permute-start.44) | collective-permute-done | bytes 16416 | tf_op jit(solution)/shard_map/ppermute | solution.py:217
  108.6 0.9 last_kernel.1
  (57 shorter events, 0.3 us)
Async XLA Ops:
  0.6 16.8 %collective-permute-start = (bf16[2,16,256]{2,1,0:T(8,128)(2,1)}, bf16[2,16,256]{2,1,0:T(8,128)(2,1)S(1)}, u32[]{:S(2)}, u32[]{:S(2)}) collective-permute-start(bf16[2,16,256]{2,1,0:T(8,128)(2,1)} %bitcast.5), channel_id=1, source_target_pairs={{64,0},{65,1},{66,2},{67,3},{68,4},{69,5},{70,6},{71,7},{72,8},{73... | collective-permute-start | bytes 49160 | tf_op jit(solution)/shard_map/ppermute | solution.py:217
  1.9 15.5 %collective-permute-start.1 = (bf16[2,16,256]{2,1,0:T(8,128)(2,1)}, bf16[2,16,256]{2,1,0:T(8,128)(2,1)S(1)}, u32[]{:S(2)}, u32[]{:S(2)}) collective-permute-start(bf16[2,16,256]{2,1,0:T(8,128)(2,1)} %bitcast.6), channel_id=1, source_target_pairs={{1,2},{2,1},{3,4},{4,3},{5,6},{6,5},{7,8},{8,7},{9,10},{10,9},{11,... | collective-permute-start | bytes 49160 | tf_op jit(solution)/shard_map/ppermute | solution.py:217
  12.0 5.8 %collective-permute-start.2 = (bf16[2,16,256]{2,1,0:T(8,128)(2,1)}, bf16[2,16,256]{2,1,0:T(8,128)(2,1)S(1)}, u32[]{:S(2)}, u32[]{:S(2)}) collective-permute-start(bf16[2,16,256]{2,1,0:T(8,128)(2,1)} %bitcast.7), channel_id=1, source_target_pairs={{0,1},{1,0},{2,3},{3,2},{4,5},{5,4},{6,7},{7,6},{8,9},{9,8},{10,11... | collective-permute-start | bytes 49160 | tf_op jit(solution)/shard_map/ppermute | solution.py:217
  13.9 0.7 copy-start.3
  14.6 0.7 copy-start.2
  15.2 1.1 %copy-start = (bf16[1,12,2,128,128]{4,3,2,1,0:T(8,128)(2,1)S(1)}, bf16[1,12,2,128,128]{4,3,2,1,0:T(8,128)(2,1)}, u32[]{:S(2)}) copy-start(bf16[1,12,2,128,128]{4,3,2,1,0:T(8,128)(2,1)} %param.5) | copy-start | bytes 2359300
  17.4 0.7 copy-start.1
  18.4 4.8 %collective-permute-start.3 = (bf16[784,512]{1,0:T(8,128)(2,1)S(1)}, bf16[784,512]{1,0:T(8,128)(2,1)S(1)}, u32[]{:S(2)}, u32[]{:S(2)}) collective-permute-start(bf16[784,512]{1,0:T(8,128)(2,1)S(1)} %later_kernel.1), channel_id=1, source_target_pairs={{192,128},{193,129},{194,130},{195,131},{196,132},{197,133},{198,1... | collective-permute-start | bytes 2408456 | tf_op jit(solution)/shard_map/ppermute | solution.py:217
  19.2 10.2 %collective-permute-start.4 = (bf16[784,512]{1,0:T(8,128)(2,1)S(1)}, bf16[784,512]{1,0:T(8,128)(2,1)S(1)}, u32[]{:S(2)}, u32[]{:S(2)}) collective-permute-start(bf16[784,512]{1,0:T(8,128)(2,1)S(1)} %later_kernel.1), channel_id=1, source_target_pairs={{192,129},{193,128},{194,131},{195,130},{196,133},{197,132},{198,1... | collective-permute-start | bytes 2408456 | tf_op jit(solution)/shard_map/ppermute | solution.py:217
  19.9 12.3 %collective-permute-start.19 = (bf16[784,512]{1,0:T(8,128)(2,1)S(1)}, bf16[784,512]{1,0:T(8,128)(2,1)S(1)}, u32[]{:S(2)}, u32[]{:S(2)}) collective-permute-start(bf16[784,512]{1,0:T(8,128)(2,1)S(1)} %later_kernel.1), channel_id=1, source_target_pairs={{193,130},{194,129},{195,132},{196,131},{197,134},{198,133},{199,1... | collective-permute-start | bytes 2408456 | tf_op jit(solution)/shard_map/ppermute | solution.py:217
  20.6 3.9 %collective-permute-start.5 = (bf16[2,16,256]{2,1,0:T(8,128)(2,1)S(1)}, bf16[2,16,256]{2,1,0:T(8,128)(2,1)S(1)}, u32[]{:S(2)}, u32[]{:S(2)}) collective-permute-start(bf16[2,16,256]{2,1,0:T(8,128)(2,1)S(1)} %get-tuple-element.27._after.refs_5_), channel_id=1, source_target_pairs={{1,66},{2,65},{3,68},{4,67},{5,70},{6,69},{7,72},{8,71},{9,74},{10... | collective-permute-start | bytes 49160 | tf_op jit(solution)/shard_map/ppermute | solution.py:217
  21.9 2.7 %collective-permute-start.6 = (bf16[2,16,256]{2,1,0:T(8,128)(2,1)S(1)}, bf16[2,16,256]{2,1,0:T(8,128)(2,1)S(1)}, u32[]{:S(2)}, u32[]{:S(2)}) collective-permute-start(bf16[2,16,256]{2,1,0:T(8,128)(2,1)S(1)} %get-tuple-element.27._after.refs_5_), channel_id=1, source_target_pairs={{0,65},{1,64},{2,67},{3,66},{4,69},{5,68},{6,71},{7,70},{8,73},{9,... | collective-permute-start | bytes 49160 | tf_op jit(solution)/shard_map/ppermute | solution.py:217
  23.2 2.1 %collective-permute-start.7 = (bf16[2,16,256]{2,1,0:T(8,128)(2,1)S(1)}, bf16[2,16,256]{2,1,0:T(8,128)(2,1)S(1)}, u32[]{:S(2)}, u32[]{:S(2)}) collective-permute-start(bf16[2,16,256]{2,1,0:T(8,128)(2,1)S(1)} %get-tuple-element.27._after.refs_5_), channel_id=1, source_target_pairs={{0,64},{1,65},{2,66},{3,67},{4,68},{5,69},{6,70},{7,71},{8,72},{9,... | collective-permute-start | bytes 49160 | tf_op jit(solution)/shard_map/ppermute | solution.py:217
  25.3 2.0 %collective-permute-start.10 = (bf16[2,16,256]{2,1,0:T(8,128)(2,1)S(1)}, bf16[2,16,256]{2,1,0:T(8,128)(2,1)S(1)}, u32[]{:S(2)}, u32[]{:S(2)}) collective-permute-start(bf16[2,16,256]{2,1,0:T(8,128)(2,1)S(1)} %get-tuple-element.29.refs_5_), channel_id=1, source_target_pairs={{65,130},{66,129},{67,132},{68,131},{69,134},{70,133},{71,136},{72... | collective-permute-start | bytes 49160 | tf_op jit(solution)/shard_map/ppermute | solution.py:217
  26.0 1.4 %collective-permute-start.8 = (bf16[2,16,256]{2,1,0:T(8,128)(2,1)S(1)}, bf16[2,16,256]{2,1,0:T(8,128)(2,1)S(1)}, u32[]{:S(2)}, u32[]{:S(2)}) collective-permute-start(bf16[2,16,256]{2,1,0:T(8,128)(2,1)S(1)} %get-tuple-element.29.refs_5_), channel_id=1, source_target_pairs={{64,129},{65,128},{66,131},{67,130},{68,133},{69,132},{70,135},{71... | collective-permute-start | bytes 49160 | tf_op jit(solution)/shard_map/ppermute | solution.py:217
  26.7 0.7 collective-permute-start.9
  27.4 2.0 %collective-permute-start.11 = (bf16[2,16,256]{2,1,0:T(8,128)(2,1)S(1)}, bf16[2,16,256]{2,1,0:T(8,128)(2,1)S(1)}, u32[]{:S(2)}, u32[]{:S(2)}) collective-permute-start(bf16[2,16,256]{2,1,0:T(8,128)(2,1)S(1)} %get-tuple-element.31.refs_5_), channel_id=1, source_target_pairs={{129,194},{130,193},{131,196},{132,195},{133,198},{134,197},{135,2... | collective-permute-start | bytes 49160 | tf_op jit(solution)/shard_map/ppermute | solution.py:217
  28.1 1.4 %collective-permute-start.12 = (bf16[2,16,256]{2,1,0:T(8,128)(2,1)S(1)}, bf16[2,16,256]{2,1,0:T(8,128)(2,1)S(1)}, u32[]{:S(2)}, u32[]{:S(2)}) collective-permute-start(bf16[2,16,256]{2,1,0:T(8,128)(2,1)S(1)} %get-tuple-element.31.refs_5_), channel_id=1, source_target_pairs={{128,193},{129,192},{130,195},{131,194},{132,197},{133,196},{134,1... | collective-permute-start | bytes 49160 | tf_op jit(solution)/shard_map/ppermute | solution.py:217
  28.7 0.7 collective-permute-start.13
  29.5 3.4 %collective-permute-start.14 = (bf16[2,16,256]{2,1,0:T(8,128)(2,1)S(1)}, bf16[2,16,256]{2,1,0:T(8,128)(2,1)S(1)}, u32[]{:S(2)}, u32[]{:S(2)}) collective-permute-start(bf16[2,16,256]{2,1,0:T(8,128)(2,1)S(1)} %get-tuple-element.33.sent_ref), channel_id=1, source_target_pairs={{194,324},{195,325},{196,322},{197,323},{198,328},{199,329},{200,3... | collective-permute-start | bytes 49160 | tf_op jit(solution)/shard_map/ppermute | solution.py:217
  30.2 2.7 %collective-permute-start.15 = (bf16[2,16,256]{2,1,0:T(8,128)(2,1)S(1)}, bf16[2,16,256]{2,1,0:T(8,128)(2,1)S(1)}, u32[]{:S(2)}, u32[]{:S(2)}) collective-permute-start(bf16[2,16,256]{2,1,0:T(8,128)(2,1)S(1)} %get-tuple-element.33.sent_ref), channel_id=1, source_target_pairs={{193,322},{194,321},{195,324},{196,323},{197,326},{198,325},{199,3... | collective-permute-start | bytes 49160 | tf_op jit(solution)/shard_map/ppermute | solution.py:217
  30.8 2.1 %collective-permute-start.16 = (bf16[2,16,256]{2,1,0:T(8,128)(2,1)S(1)}, bf16[2,16,256]{2,1,0:T(8,128)(2,1)S(1)}, u32[]{:S(2)}, u32[]{:S(2)}) collective-permute-start(bf16[2,16,256]{2,1,0:T(8,128)(2,1)S(1)} %get-tuple-element.33.sent_ref), channel_id=1, source_target_pairs={{192,322},{193,323},{194,320},{195,321},{196,326},{197,327},{198,3... | collective-permute-start | bytes 49160 | tf_op jit(solution)/shard_map/ppermute | solution.py:217
  31.5 1.4 %collective-permute-start.17 = (bf16[2,16,256]{2,1,0:T(8,128)(2,1)S(1)}, bf16[2,16,256]{2,1,0:T(8,128)(2,1)S(1)}, u32[]{:S(2)}, u32[]{:S(2)}) collective-permute-start(bf16[2,16,256]{2,1,0:T(8,128)(2,1)S(1)} %get-tuple-element.33.sent_ref), channel_id=1, source_target_pairs={{192,321},{193,320},{194,323},{195,322},{196,325},{197,324},{198,3... | collective-permute-start | bytes 49160 | tf_op jit(solution)/shard_map/ppermute | solution.py:217
  32.2 0.7 collective-permute-start.18
  32.9 3.4 %collective-permute-start.20 = (bf16[2,16,256]{2,1,0:T(8,128)(2,1)S(1)}, bf16[2,16,256]{2,1,0:T(8,128)(2,1)S(1)}, u32[]{:S(2)}, u32[]{:S(2)}) collective-permute-start(bf16[2,16,256]{2,1,0:T(8,128)(2,1)S(1)} %get-tuple-element.35.sent_ref), channel_id=1, source_target_pairs={{321,450},{322,449},{323,452},{324,451},{325,454},{326,453},{327,4... | collective-permute-start | bytes 49160 | tf_op jit(solution)/shard_map/ppermute | solution.py:217
  33.6 3.4 %collective-permute-start.21 = (bf16[2,16,256]{2,1,0:T(8,128)(2,1)S(1)}, bf16[2,16,256]{2,1,0:T(8,128)(2,1)S(1)}, u32[]{:S(2)}, u32[]{:S(2)}) collective-permute-start(bf16[2,16,256]{2,1,0:T(8,128)(2,1)S(1)} %get-tuple-element.35.sent_ref), channel_id=1, source_target_pairs={{322,452},{323,453},{324,450},{325,451},{326,456},{327,457},{328,4... | collective-permute-start | bytes 49160 | tf_op jit(solution)/shard_map/ppermute | solution.py:217
  34.3 2.7 %collective-permute-start.22 = (bf16[2,16,256]{2,1,0:T(8,128)(2,1)S(1)}, bf16[2,16,256]{2,1,0:T(8,128)(2,1)S(1)}, u32[]{:S(2)}, u32[]{:S(2)}) collective-permute-start(bf16[2,16,256]{2,1,0:T(8,128)(2,1)S(1)} %get-tuple-element.35.sent_ref), channel_id=1, source_target_pairs={{320,450},{321,451},{322,448},{323,449},{324,454},{325,455},{326,4... | collective-permute-start | bytes 49160 | tf_op jit(solution)/shard_map/ppermute | solution.py:217
  34.9 2.0 %collective-permute-start.23 = (bf16[2,16,256]{2,1,0:T(8,128)(2,1)S(1)}, bf16[2,16,256]{2,1,0:T(8,128)(2,1)S(1)}, u32[]{:S(2)}, u32[]{:S(2)}) collective-permute-start(bf16[2,16,256]{2,1,0:T(8,128)(2,1)S(1)} %get-tuple-element.35.sent_ref), channel_id=1, source_target_pairs={{320,449},{321,448},{322,451},{323,450},{324,453},{325,452},{326,4... | collective-permute-start | bytes 49160 | tf_op jit(solution)/shard_map/ppermute | solution.py:217
  35.6 1.4 %collective-permute-start.24 = (bf16[2,16,256]{2,1,0:T(8,128)(2,1)S(1)}, bf16[2,16,256]{2,1,0:T(8,128)(2,1)S(1)}, u32[]{:S(2)}, u32[]{:S(2)}) collective-permute-start(bf16[2,16,256]{2,1,0:T(8,128)(2,1)S(1)} %get-tuple-element.35.sent_ref), channel_id=1, source_target_pairs={{320,448},{321,449},{322,450},{323,451},{324,452},{325,453},{326,4... | collective-permute-start | bytes 49160 | tf_op jit(solution)/shard_map/ppermute | solution.py:217
  36.3 3.4 %collective-permute-start.29 = (bf16[2,16,256]{2,1,0:T(8,128)(2,1)S(1)}, bf16[2,16,256]{2,1,0:T(8,128)(2,1)S(1)}, u32[]{:S(2)}, u32[]{:S(2)}) collective-permute-start(bf16[2,16,256]{2,1,0:T(8,128)(2,1)S(1)} %get-tuple-element.40), channel_id=1, source_target_pairs={{128,256},{129,257},{130,258},{131,259},{132,260},{133,261},{134,2... | collective-permute-start | bytes 49160 | tf_op jit(solution)/shard_map/ppermute | solution.py:217
  37.0 2.7 %collective-permute-start.25 = (bf16[2,16,256]{2,1,0:T(8,128)(2,1)S(1)}, bf16[2,16,256]{2,1,0:T(8,128)(2,1)S(1)}, u32[]{:S(2)}, u32[]{:S(2)}) collective-permute-start(bf16[2,16,256]{2,1,0:T(8,128)(2,1)S(1)} %get-tuple-element.38.kept_ref), channel_id=1, source_target_pairs={{449,386},{450,385},{451,388},{452,387},{453,390},{454,389},{455,3... | collective-permute-start | bytes 49160 | tf_op jit(solution)/shard_map/ppermute | solution.py:217
  37.7 2.0 %collective-permute-start.26 = (bf16[2,16,256]{2,1,0:T(8,128)(2,1)S(1)}, bf16[2,16,256]{2,1,0:T(8,128)(2,1)S(1)}, u32[]{:S(2)}, u32[]{:S(2)}) collective-permute-start(bf16[2,16,256]{2,1,0:T(8,128)(2,1)S(1)} %get-tuple-element.38.kept_ref), channel_id=1, source_target_pairs={{128,193},{129,192},{130,195},{131,194},{132,197},{133,196},{134,1... | collective-permute-start | bytes 49160 | tf_op jit(solution)/shard_map/ppermute | solution.py:217
  38.4 1.4 %collective-permute-start.27 = (bf16[2,16,256]{2,1,0:T(8,128)(2,1)S(1)}, bf16[2,16,256]{2,1,0:T(8,128)(2,1)S(1)}, u32[]{:S(2)}, u32[]{:S(2)}) collective-permute-start(bf16[2,16,256]{2,1,0:T(8,128)(2,1)S(1)} %get-tuple-element.38.kept_ref), channel_id=1, source_target_pairs={{128,192},{129,193},{130,194},{131,195},{132,196},{133,197},{134,1... | collective-permute-start | bytes 49160 | tf_op jit(solution)/shard_map/ppermute | solution.py:217
  39.0 0.7 collective-permute-start.28
  39.8 3.4 %collective-permute-start.30 = (bf16[2,16,256]{2,1,0:T(8,128)(2,1)S(1)}, bf16[2,16,256]{2,1,0:T(8,128)(2,1)S(1)}, u32[]{:S(2)}, u32[]{:S(2)}) collective-permute-start(bf16[2,16,256]{2,1,0:T(8,128)(2,1)S(1)} %get-tuple-element.41), channel_id=1, source_target_pairs={{194,324},{195,325},{196,322},{197,323},{198,328},{199,329},{200,3... | collective-permute-start | bytes 49160 | tf_op jit(solution)/shard_map/ppermute | solution.py:217
  40.5 2.7 %collective-permute-start.31 = (bf16[2,16,256]{2,1,0:T(8,128)(2,1)S(1)}, bf16[2,16,256]{2,1,0:T(8,128)(2,1)S(1)}, u32[]{:S(2)}, u32[]{:S(2)}) collective-permute-start(bf16[2,16,256]{2,1,0:T(8,128)(2,1)S(1)} %get-tuple-element.41), channel_id=1, source_target_pairs={{193,322},{194,321},{195,324},{196,323},{197,326},{198,325},{199,3... | collective-permute-start | bytes 49160 | tf_op jit(solution)/shard_map/ppermute | solution.py:217
  41.1 2.0 %collective-permute-start.32 = (bf16[2,16,256]{2,1,0:T(8,128)(2,1)S(1)}, bf16[2,16,256]{2,1,0:T(8,128)(2,1)S(1)}, u32[]{:S(2)}, u32[]{:S(2)}) collective-permute-start(bf16[2,16,256]{2,1,0:T(8,128)(2,1)S(1)} %get-tuple-element.41), channel_id=1, source_target_pairs={{192,322},{193,323},{194,320},{195,321},{196,326},{197,327},{198,3... | collective-permute-start | bytes 49160 | tf_op jit(solution)/shard_map/ppermute | solution.py:217
  41.8 1.4 %collective-permute-start.33 = (bf16[2,16,256]{2,1,0:T(8,128)(2,1)S(1)}, bf16[2,16,256]{2,1,0:T(8,128)(2,1)S(1)}, u32[]{:S(2)}, u32[]{:S(2)}) collective-permute-start(bf16[2,16,256]{2,1,0:T(8,128)(2,1)S(1)} %get-tuple-element.41), channel_id=1, source_target_pairs={{192,321},{193,320},{194,323},{195,322},{196,325},{197,324},{198,3... | collective-permute-start | bytes 49160 | tf_op jit(solution)/shard_map/ppermute | solution.py:217
  42.5 0.7 collective-permute-start.34
  43.2 3.4 %collective-permute-start.35 = (bf16[2,16,256]{2,1,0:T(8,128)(2,1)S(1)}, bf16[2,16,256]{2,1,0:T(8,128)(2,1)S(1)}, u32[]{:S(2)}, u32[]{:S(2)}) collective-permute-start(bf16[2,16,256]{2,1,0:T(8,128)(2,1)S(1)} %get-tuple-element.44), channel_id=1, source_target_pairs={{321,450},{322,449},{323,452},{324,451},{325,454},{326,453},{327,4... | collective-permute-start | bytes 49160 | tf_op jit(solution)/shard_map/ppermute | solution.py:217
  43.9 2.7 %collective-permute-start.36 = (bf16[2,16,256]{2,1,0:T(8,128)(2,1)S(1)}, bf16[2,16,256]{2,1,0:T(8,128)(2,1)S(1)}, u32[]{:S(2)}, u32[]{:S(2)}) collective-permute-start(bf16[2,16,256]{2,1,0:T(8,128)(2,1)S(1)} %get-tuple-element.44), channel_id=1, source_target_pairs={{322,452},{323,453},{324,450},{325,451},{326,456},{327,457},{328,4... | collective-permute-start | bytes 49160 | tf_op jit(solution)/shard_map/ppermute | solution.py:217
  44.6 2.0 %collective-permute-start.37 = (bf16[2,16,256]{2,1,0:T(8,128)(2,1)S(1)}, bf16[2,16,256]{2,1,0:T(8,128)(2,1)S(1)}, u32[]{:S(2)}, u32[]{:S(2)}) collective-permute-start(bf16[2,16,256]{2,1,0:T(8,128)(2,1)S(1)} %get-tuple-element.44), channel_id=1, source_target_pairs={{320,450},{321,451},{322,448},{323,449},{324,454},{325,455},{326,4... | collective-permute-start | bytes 49160 | tf_op jit(solution)/shard_map/ppermute | solution.py:217
  45.2 1.4 %collective-permute-start.38 = (bf16[2,16,256]{2,1,0:T(8,128)(2,1)S(1)}, bf16[2,16,256]{2,1,0:T(8,128)(2,1)S(1)}, u32[]{:S(2)}, u32[]{:S(2)}) collective-permute-start(bf16[2,16,256]{2,1,0:T(8,128)(2,1)S(1)} %get-tuple-element.44), channel_id=1, source_target_pairs={{320,449},{321,448},{322,451},{323,450},{324,453},{325,452},{326,4... | collective-permute-start | bytes 49160 | tf_op jit(solution)/shard_map/ppermute | solution.py:217
  45.9 0.7 collective-permute-start.39
  46.7 2.7 %collective-permute-start.40 = (bf16[2,16,256]{2,1,0:T(8,128)(2,1)S(1)}, bf16[2,16,256]{2,1,0:T(8,128)(2,1)S(1)}, u32[]{:S(2)}, u32[]{:S(2)}) collective-permute-start(bf16[2,16,256]{2,1,0:T(8,128)(2,1)S(1)} %get-tuple-element.47), channel_id=1, source_target_pairs={{129,66},{130,65},{131,68},{132,67},{133,70},{134,69},{135,72},{13... | collective-permute-start | bytes 49160 | tf_op jit(solution)/shard_map/ppermute | solution.py:217
  47.3 2.0 %collective-permute-start.41 = (bf16[2,16,256]{2,1,0:T(8,128)(2,1)S(1)}, bf16[2,16,256]{2,1,0:T(8,128)(2,1)S(1)}, u32[]{:S(2)}, u32[]{:S(2)}) collective-permute-start(bf16[2,16,256]{2,1,0:T(8,128)(2,1)S(1)} %get-tuple-element.47), channel_id=1, source_target_pairs={{128,65},{129,64},{130,67},{131,66},{132,69},{133,68},{134,71},{13... | collective-permute-start | bytes 49160 | tf_op jit(solution)/shard_map/ppermute | solution.py:217
  48.0 1.4 %collective-permute-start.42 = (bf16[2,16,256]{2,1,0:T(8,128)(2,1)S(1)}, bf16[2,16,256]{2,1,0:T(8,128)(2,1)S(1)}, u32[]{:S(2)}, u32[]{:S(2)}) collective-permute-start(bf16[2,16,256]{2,1,0:T(8,128)(2,1)S(1)} %get-tuple-element.47), channel_id=1, source_target_pairs={{128,64},{129,65},{130,66},{131,67},{132,68},{133,69},{134,70},{13... | collective-permute-start | bytes 49160 | tf_op jit(solution)/shard_map/ppermute | solution.py:217
  48.7 0.7 collective-permute-start.43
  49.4 59.2 %collective-permute-start.44 = (bf16[2,16,256]{2,1,0:T(8,128)(2,1)S(1)}, bf16[2,16,256]{2,1,0:T(8,128)(2,1)S(1)}, u32[]{:S(2)}, u32[]{:S(2)}) collective-permute-start(bf16[2,16,256]{2,1,0:T(8,128)(2,1)S(1)} %chosen_kernel.1.kept_ref), channel_id=1, source_target_pairs={{65,2},{66,1},{67,4},{68,3},{69,6},{70,5},{71,8},{72,7},{73,10},{7... | collective-permute-start | bytes 49160 | tf_op jit(solution)/shard_map/ppermute | solution.py:217
  50.7 57.9 %collective-permute-start.45 = (bf16[2,16,256]{2,1,0:T(8,128)(2,1)S(1)}, bf16[2,16,256]{2,1,0:T(8,128)(2,1)S(1)}, u32[]{:S(2)}, u32[]{:S(2)}) collective-permute-start(bf16[2,16,256]{2,1,0:T(8,128)(2,1)S(1)} %chosen_kernel.1.kept_ref), channel_id=1, source_target_pairs={{64,1},{65,0},{66,3},{67,2},{68,5},{69,4},{70,7},{71,6},{72,9},{73... | collective-permute-start | bytes 49160 | tf_op jit(solution)/shard_map/ppermute | solution.py:217
  52.0 56.6 %collective-permute-start.46 = (bf16[2,16,256]{2,1,0:T(8,128)(2,1)S(1)}, bf16[2,16,256]{2,1,0:T(8,128)(2,1)S(1)}, u32[]{:S(2)}, u32[]{:S(2)}) collective-permute-start(bf16[2,16,256]{2,1,0:T(8,128)(2,1)S(1)} %chosen_kernel.1.kept_ref), channel_id=1, source_target_pairs={{64,0},{65,1},{66,2},{67,3},{68,4},{69,5},{70,6},{71,7},{72,8},{73... | collective-permute-start | bytes 49160 | tf_op jit(solution)/shard_map/ppermute | solution.py:217
